TPU v7x, 32 devices: a whole 2x2x4 slice. The times are simulated.
32 devices in a mesh: groups: 2 (over x), seq: 16 (over z, y, core).
Axes of the slice: x: 2, y: 2, z: 4, core: 2. Of those that a mesh axis runs over, the one named last changes fastest.
Arguments:
- inputs: bfloat16 [8192, 1536], P(('groups', 'seq')), parts along dimension 0, may hold values from -6 to 6
- norm_gain: float32 [1536], replicated, may hold values from 0.1 to 1.9
- dilated_weight: bfloat16 [3, 1536, 768], P(None, 'seq'), may hold values from -0.09375 to 0.09375
- point_weight: bfloat16 [768, 1536], replicated, may hold values from -0.21875 to 0.21875
- cotangent: bfloat16 [8192, 1536], P(('groups', 'seq')), parts along dimension 0, may hold values from -6 to 6
Outputs:
- outputs: bfloat16 [8192, 1536], P(('groups', 'seq')), parts along dimension 0
- input_grad: bfloat16 [8192, 1536], P(('groups', 'seq')), parts along dimension 0
- dilated_grad: float32 [6, 1536, 768], P('groups', 'seq'), parts along dimension 0
- point_grad: float32 [1536, 1536], P('groups', 'seq'), parts along dimension 0
There are 2 independent parts, one for each index of `groups`. A program takes and returns all parts, laid end to end along the dimension named above; an argument that names none is the same for every part. Nothing has to cross between parts.
All inputs are finite; a program needn't handle non-finite values.
Results may differ from a plain program's by a relative error of at most 0.0053.
Values may be sent and summed in bfloat16 or wider, within the bound.
No kernel may reach another device: no remote copies, remote signals or barrier semaphores. Data moves between devices by JAX's collectives and lax.ppermute only.
A program may use at most 128 MiB of HBM per device.

v0:
```python
import math

import jax
import jax.numpy as jnp
from jax import lax
from jax.sharding import PartitionSpec as P

HOPS = 1


root_coef = math.sqrt(2.0 / math.pi)


def from_behind(value, axis, by):
    size = lax.axis_size(axis)
    pairs = [(i, i + by) for i in range(size) if 0 <= i + by < size]
    return lax.ppermute(value, axis, pairs)


def gelu_value(v):
    return 0.5 * v * (1.0 + jnp.tanh(root_coef * (v + 0.044715 * v * v * v)))


def gelu_slope(v):
    inner = jnp.tanh(root_coef * (v + 0.044715 * v * v * v))
    return 0.5 * (1.0 + inner) + 0.5 * v * (1.0 - inner * inner) * root_coef * (
        1.0 + 3.0 * 0.044715 * v * v
    )


def rows_product(left, right):
    return lax.dot_general(
        left, right, (((0,), (0,)), ((), ())), preferred_element_type=jnp.float32
    )


def transposed_product(left, weight):
    return lax.dot_general(
        left, weight, (((1,), (1,)), ((), ())), preferred_element_type=jnp.float32
    )


def local(inputs, norm_gain, dilated_weight, point_weight, cotangent):
    xfull = inputs.astype(jnp.float32)
    ratio = lax.rsqrt(jnp.mean(xfull * xfull, axis=-1, keepdims=True) + 1e-06)
    normed = xfull * ratio * norm_gain
    act = gelu_value(normed).astype(jnp.bfloat16)
    act_ahead = from_behind(act, "seq", -HOPS)
    act_behind = from_behind(act, "seq", HOPS)
    taps_whole = lax.all_gather(dilated_weight, "seq", axis=1, tiled=True)
    pre = jnp.dot(act, taps_whole[1], preferred_element_type=jnp.float32)
    pre = pre + jnp.dot(act_behind, taps_whole[0], preferred_element_type=jnp.float32)
    pre = pre + jnp.dot(act_ahead, taps_whole[2], preferred_element_type=jnp.float32)
    branch = gelu_value(pre).astype(jnp.bfloat16)
    outputs = (xfull + jnp.dot(branch, point_weight, preferred_element_type=jnp.float32)).astype(
        jnp.bfloat16
    )
    branch_grad = transposed_product(cotangent, point_weight)
    pre_grad = (branch_grad * gelu_slope(pre)).astype(jnp.bfloat16)
    point_share = lax.psum_scatter(
        rows_product(branch, cotangent), "seq", scatter_dimension=1, tiled=True
    )
    grad_ahead = from_behind(pre_grad, "seq", -HOPS)
    grad_behind = from_behind(pre_grad, "seq", HOPS)
    act_grad = transposed_product(pre_grad, taps_whole[1])
    act_grad = act_grad + transposed_product(grad_ahead, taps_whole[0])
    act_grad = act_grad + transposed_product(grad_behind, taps_whole[2])
    scaled = act_grad * gelu_slope(normed) * norm_gain
    inner = jnp.mean(scaled * xfull, axis=-1, keepdims=True)
    input_grad = (
        cotangent.astype(jnp.float32) + ratio * scaled - xfull * ratio * ratio * ratio * inner
    ).astype(jnp.bfloat16)
    tap_terms = jnp.stack(
        [
            rows_product(act_behind, pre_grad),
            rows_product(act, pre_grad),
            rows_product(act_ahead, pre_grad),
        ]
    )
    dilated_share = lax.psum_scatter(tap_terms, "seq", scatter_dimension=1, tiled=True)
    return (outputs, input_grad, dilated_share, point_share)


def solution(mesh):
    placed = (
        P(("groups", "seq"), None),
        P(),
        P(None, "seq", None),
        P(),
        P(("groups", "seq"), None),
    )
    return jax.shard_map(
        local,
        mesh=mesh,
        in_specs=placed,
        out_specs=(
            P(("groups", "seq"), None),
            P(("groups", "seq"), None),
            P("groups", "seq", None),
            P("groups", "seq"),
        ),
        check_vma=False,
    )
```

profile of v0, /device:TPU:9, one launch (start us, length us, event | category | flops | bytes accessed | tf_op | source)
XLA Modules:
  0.0 335.2 jit_solution(5972888151832841149)
XLA Ops:
  8.0 1.4 fusion.23
  9.4 2.3 fusion.12
  11.7 3.7 %collective-permute-start = (bf16[256,1536]{1,0:T(8,128)(2,1)}, bf16[256,1536]{1,0:T(8,128)(2,1)}, u32[]{:S(2)}, u32[]{:S(2)}) collective-permute-start(bf16[256,1536]{1,0:T(8,128)(2,1)} %fusion.12), channel_id=1, source_target_pairs={{0,1},{1,2},{2,3},{3,4},{4,5},{5,6},{6,7},{7,8},{8,9},{9,10},{10,1... | collective-permute-start | bytes 2359304 | tf_op jit(solution)/shard_map/ppermute | solution.py:17
  15.4 1.9 collective-permute-start.1
  17.3 67.6 %all-gather.2.cloned.1.call-done = bf16[3,1536,768]{2,1,0:T(8,128)(2,1)} async-done(((bf16[3,96,768]{2,1,0:T(8,128)(2,1)}), bf16[3,1536,768]{2,1,0:T(8,128)(2,1)}) %all-gather.2.cloned.1.call-update) | async-done | bytes 7077904 | tf_op jit(solution)/shard_map/all_gather | solution.py:50
  85.0 2.7 fusion.4
  87.7 2.7 fusion.26
  90.4 2.8 fusion.25
  94.0 3.1 fusion.34
  97.2 2.4 fusion.33
  99.6 4.1 %convolution_bitcast_fusion.1 = f32[1,1536,768]{2,1,0:T(8,128)} fusion(bf16[256,1536]{1,0:T(8,128)(2,1)} %fusion.12, bf16[256,768]{1,0:T(8,128)(2,1)S(1)} %fusion.33), kind=kOutput, calls=%fused_computation.2 | convolution fusion | flops 603979776 | bytes 5898240 | tf_op jit(solution)/shard_map/dot_general | solution.py:32
  103.7 4.3 %convolution_bitcast_fusion = f32[1,1536,768]{2,1,0:T(8,128)} fusion(bf16[256,1536]{1,0:T(8,128)(2,1)} %collective-permute-done.1, bf16[256,768]{1,0:T(8,128)(2,1)S(1)} %fusion.33), kind=kOutput, calls=%fused_computation.1 | convolution fusion | flops 603979776 | bytes 5898240 | tf_op jit(solution)/shard_map/dot_general | solution.py:32
  108.0 4.1 %convolution_bitcast_fusion.2 = f32[1,1536,768]{2,1,0:T(8,128)} fusion(bf16[256,1536]{1,0:T(8,128)(2,1)} %collective-permute-done, bf16[256,768]{1,0:T(8,128)(2,1)S(1)} %fusion.33), kind=kOutput, calls=%fused_computation.3 | convolution fusion | flops 603979776 | bytes 5898240 | tf_op jit(solution)/shard_map/dot_general | solution.py:32
  112.1 11.7 %pad_maximum_fusion = f32[3,1536,768]{2,1,0:T(8,128)} fusion(f32[1,1536,768]{2,1,0:T(8,128)} %convolution_bitcast_fusion, f32[1,1536,768]{2,1,0:T(8,128)} %convolution_bitcast_fusion.1, f32[1,1536,768]{2,1,0:T(8,128)} %convolution_bitcast_fusion.2), kind=kLoop, calls=%fused_computation | loop fusion | flops 7077888 | bytes 28311552 | tf_op jit(solution)/shard_map/stack | solution.py:73
  123.9 2.4 collective-permute-start.3
  126.3 2.1 collective-permute-start.2
  128.4 2.8 fusion.2
  131.2 2.5 fusion.3
  133.7 14.0 %collective-permute-done.2 = bf16[256,768]{1,0:T(8,128)(2,1)S(1)} collective-permute-done((bf16[256,768]{1,0:T(8,128)(2,1)S(1)}, bf16[256,768]{1,0:T(8,128)(2,1)S(1)}, u32[]{:S(2)}, u32[]{:S(2)}) %collective-permute-start.2) | collective-permute-done | bytes 393248 | tf_op jit(solution)/shard_map/ppermute | solution.py:17
  147.7 2.5 convolution_add_fusion.1
  150.3 3.7 %fusion.24 = (f32[256]{0:T(256)S(1)}, f32[256,1536]{1,0:T(8,128)S(1)}) fusion(bf16[256,1536]{1,0:T(8,128)(2,1)S(1)} %copy-done.1, f32[1536]{0:T(1024)S(1)} %copy-done.5, f32[256]{0:T(256)S(1)} %add_rsqrt_fusion, f32[256,1536]{1,0:T(8,128)S(1)} %convolution_add_fusion.1, bf16[256,768]{1,0:T(8,128)(2,1)S(1)} %collective-permute-done.3, ...), kind=kOutput, calls=%fused_computation.39 | convolution fusion | flops 613809920 | bytes 6692864 | tf_op jit(solution)/shard_map/dot_general | solution.py:38
  154.0 1.5 fusion.19
  155.4 22.5 %reduce-scatter.5.cloned.1.call-done = f32[768,96]{0,1:T(8,128)} async-done(((f32[768,1536]{0,1:T(8,128)}), f32[768,96]{0,1:T(8,128)}) %reduce-scatter.5.cloned.1.call-update) | async-done | bytes 294928 | tf_op jit(solution)/shard_map/reduce_scatter | solution.py:60
  177.9 150.8 %reduce-scatter.3.cloned.1.call-done = f32[3,96,768]{2,1,0:T(8,128)} async-done(((f32[3,1536,768]{2,1,0:T(8,128)}), f32[3,96,768]{2,1,0:T(8,128)}) %reduce-scatter.3.cloned.1.call-update) | async-done | bytes 884752 | tf_op jit(solution)/shard_map/reduce_scatter | solution.py:80
  (23 shorter events, 1.8 us)
Async XLA Ops:
  7.2 90.1 %copy-start = (bf16[768,1536]{1,0:T(8,128)(2,1)S(1)}, bf16[768,1536]{1,0:T(8,128)(2,1)}, u32[]{:S(2)}) copy-start(bf16[768,1536]{1,0:T(8,128)(2,1)} %param.8) | copy-start | bytes 7077892
  7.2 2.2 copy-start.1
  7.2 77.8 %all-gather.2.cloned.1.call-start = ((), (), s32[]{:S(2)}) async-start(), calls=%async_computation.2 | async-start | bytes 7520256 | tf_op jit(solution)/shard_map/all_gather | solution.py:50
  7.9 170.0 %reduce-scatter.5.cloned.1.call-start = ((), (), s32[]{:S(2)}) async-start(), calls=%async_computation.4 | async-start | bytes 5013504 | tf_op jit(solution)/shard_map/reduce_scatter | solution.py:60
  11.7 76.0 %collective-permute-start = (bf16[256,1536]{1,0:T(8,128)(2,1)}, bf16[256,1536]{1,0:T(8,128)(2,1)}, u32[]{:S(2)}, u32[]{:S(2)}) collective-permute-start(bf16[256,1536]{1,0:T(8,128)(2,1)} %fusion.12), channel_id=1, source_target_pairs={{0,1},{1,2},{2,3},{3,4},{4,5},{5,6},{6,7},{7,8},{8,9},{9,10},{10,1... | collective-permute-start | bytes 2359304 | tf_op jit(solution)/shard_map/ppermute | solution.py:17
  15.4 75.0 %collective-permute-start.1 = (bf16[256,1536]{1,0:T(8,128)(2,1)}, bf16[256,1536]{1,0:T(8,128)(2,1)}, u32[]{:S(2)}, u32[]{:S(2)}) collective-permute-start(bf16[256,1536]{1,0:T(8,128)(2,1)} %fusion.12), channel_id=1, source_target_pairs={{1,0},{2,1},{3,2},{4,3},{5,4},{6,5},{7,6},{8,7},{9,8},{10,9},{11,1... | collective-permute-start | bytes 2359304 | tf_op jit(solution)/shard_map/ppermute | solution.py:17
  90.4 3.7 %copy-start.2 = (bf16[256,1536]{1,0:T(8,128)(2,1)S(1)}, bf16[256,1536]{1,0:T(8,128)(2,1)}, u32[]{:S(2)}) copy-start(bf16[256,1536]{1,0:T(8,128)(2,1)} %param.9) | copy-start | bytes 2359300
  93.2 0.9 copy-start.4
  97.2 231.5 %reduce-scatter.3.cloned.1.call-start = ((), (), s32[]{:S(2)}) async-start(), calls=%async_computation.3 | async-start | bytes 15040512 | tf_op jit(solution)/shard_map/reduce_scatter | solution.py:80
  123.9 26.4 %collective-permute-start.3 = (bf16[256,768]{1,0:T(8,128)(2,1)S(1)}, bf16[256,768]{1,0:T(8,128)(2,1)S(1)}, u32[]{:S(2)}, u32[]{:S(2)}) collective-permute-start(bf16[256,768]{1,0:T(8,128)(2,1)S(1)} %fusion.33), channel_id=1, source_target_pairs={{0,1},{1,2},{2,3},{3,4},{4,5},{5,6},{6,7},{7,8},{8,9},{9,10},{10,1... | collective-permute-start | bytes 1179656 | tf_op jit(solution)/shard_map/ppermute | solution.py:17
  126.3 21.4 %collective-permute-start.2 = (bf16[256,768]{1,0:T(8,128)(2,1)S(1)}, bf16[256,768]{1,0:T(8,128)(2,1)S(1)}, u32[]{:S(2)}, u32[]{:S(2)}) collective-permute-start(bf16[256,768]{1,0:T(8,128)(2,1)S(1)} %fusion.33), channel_id=1, source_target_pairs={{1,0},{2,1},{3,2},{4,3},{5,4},{6,5},{7,6},{8,7},{9,8},{10,9},{11,1... | collective-permute-start | bytes 1179656 | tf_op jit(solution)/shard_map/ppermute | solution.py:17
  133.7 16.5 %copy-start.5 = (f32[1536]{0:T(1024)S(1)}, f32[1536]{0:T(1024)}, u32[]{:S(2)}) copy-start(f32[1536]{0:T(1024)} %param.6) | copy-start | bytes 18436
  150.2 3.7 %copy-start.3 = (bf16[256,1536]{1,0:T(8,128)(2,1)S(1)}, bf16[256,1536]{1,0:T(8,128)(2,1)}, u32[]{:S(2)}) copy-start(bf16[256,1536]{1,0:T(8,128)(2,1)} %param.9) | copy-start | bytes 2359300
Sparse Core Ops, SparseCore 0:
  10.3 74.6 all-gather.1
  97.3 80.5 reduce-scatter.4
  183.3 145.4 reduce-scatter.2
where the time goes:
time: 338 us; the launch traced here: 335 us
  waiting for transfers between devices  256 us (76%)
  matrix products  37.6 us (11%)
  other arithmetic  16.9 us (5%)
  between operations  13.9 us (4%)
  starting transfers between devices  10.3 us (3%)
    reduce_scatter x1, waiting for transfers between devices, local(): lax.psum_scatter(tap_terms, 'seq', scatter_dimension=1, tiled=True)  151 us
    all_gather x1, waiting for transfers between devices, local(): taps_whole = lax.all_gather(dilated_weight, 'seq', axis=1, tiled=True)  67.6 us
    reduce_scatter x1, waiting for transfers between devices, local(): lax.psum_scatter(rows_product(branch, cotangent), 'seq', scatter_dimensio...  22.5 us
    dot_general x4, matrix products, rows_product(): lax.dot_general(left, right, (((0,), (0,)), ((), ())), preferred_element_...  15.6 us
    ppermute x4, waiting for transfers between devices, from_behind(): return lax.ppermute(value, axis, pairs)  14 us
    another operation x1, other arithmetic, local(): jnp.stack([rows_product(act_behind, pre_grad), rows_product(act, pre_grad...  11.7 us
    dot_general x4, matrix products, transposed_product(): lax.dot_general(left, weight, (((1,), (1,)), ((), ())), preferred_element...  11.1 us
    ppermute x4, starting transfers between devices, from_behind(): return lax.ppermute(value, axis, pairs)  10.1 us
  transfers between devices with their start and end apart: 7, of which 4 were waited for; matrix products, arithmetic and copies ran while one was open for 15% of the time, Pallas kernels for 0%

commit v1 on v0

v1 whole, which is shorter than its diff:
```python
import math

import jax
import jax.numpy as jnp
from jax import lax
from jax.sharding import PartitionSpec as P

root_coef = math.sqrt(2.0 / math.pi)
bf16 = jnp.bfloat16
f32 = jnp.float32


def gelu_value(v):
    return 0.5 * v * (1.0 + jnp.tanh(root_coef * (v + 0.044715 * v * v * v)))


def gelu_slope(v):
    inner = jnp.tanh(root_coef * (v + 0.044715 * v * v * v))
    return 0.5 * (1.0 + inner) + 0.5 * v * (1.0 - inner * inner) * root_coef * (
        1.0 + 3.0 * 0.044715 * v * v
    )


def product(left, right):
    return jnp.dot(left, right, preferred_element_type=f32)


def transposed_product(left, weight):
    return lax.dot_general(
        left, weight, (((1,), (1,)), ((), ())), preferred_element_type=f32
    )


def in_order(first, mine, other, axis):
    return jnp.where(
        first,
        jnp.concatenate([mine, other], axis),
        jnp.concatenate([other, mine], axis),
    )


def local(inputs, norm_gain, dilated_weight, point_weight, cotangent):
    size = lax.axis_size("seq")
    depth = size // 4
    me = lax.axis_index("seq")
    core = me % 2
    y = (me // 2) % 2
    z = me // 4
    rows, channels = inputs.shape
    own = dilated_weight.shape[1]
    hidden = dilated_weight.shape[2]
    half = hidden // 2
    block = 2 * own

    def send(value, target):
        pairs = [(i, target(i)) for i in range(size)]
        return lax.ppermute(value, "seq", [p for p in pairs if 0 <= p[1] < size])

    def to_core(value):
        return send(value, lambda i: i ^ 1)

    def to_y(value):
        return send(value, lambda i: i ^ 2)

    def to_z(value, by):
        return send(value, lambda i: (i + 4 * by) % size)

    def cut(value, start, length, axis):
        return lax.dynamic_slice_in_dim(value, start, length, axis)

    mine = cut(dilated_weight, core * half, half, 2)
    theirs = cut(dilated_weight, (1 - core) * half, half, 2)
    chip_taps = in_order(core == 0, mine, to_core(theirs), 1)
    columns = [chip_taps] + [to_z(chip_taps, d) for d in range(1, depth)]
    beside = [to_y(c) for c in columns]
    taps = jnp.zeros((3, channels, half), bf16)
    for d in range(depth):
        source = (z - d) % depth
        taps = lax.dynamic_update_slice_in_dim(
            taps, columns[d], (source * 2 + y) * block, 1
        )
        taps = lax.dynamic_update_slice_in_dim(
            taps, beside[d], (source * 2 + 1 - y) * block, 1
        )

    xfull = inputs.astype(f32)
    ratio = lax.rsqrt(jnp.mean(xfull * xfull, axis=-1, keepdims=True) + 1e-06)
    normed = xfull * ratio * norm_gain
    act = gelu_value(normed).astype(bf16)
    edge = send(act, lambda i: i + 1 if i % 2 else i - 1)
    act_inner = in_order(core == 0, act, to_core(act), 0)
    edge_other = to_core(edge)
    low = jnp.where(core == 0, edge, edge_other)
    high = jnp.where(core == 0, edge_other, edge)
    act_wide = jnp.concatenate([low, act_inner, high], 0)

    cot = in_order(core == 0, cotangent, to_core(cotangent), 0)
    point_rows = cut(point_weight, core * half, half, 0)
    branch_grad = transposed_product(cot, point_rows)

    act_turned = act_wide.T.reshape(depth, 2, block, 4 * rows)
    far_part = lax.dynamic_slice(
        act_turned,
        (0, 1 - y, 0, (y * 2 + core) * rows),
        (depth, 1, block, rows),
    ).reshape(depth * block, rows)
    far = to_y(far_part)
    far = in_order(core == 0, far, to_core(far), 1)
    near = cut(act_turned, y, 1, 1).reshape(depth * block, 4 * rows)
    act_row = in_order(y == 0, near, far, 1)

    pre = product(act_wide[: 2 * rows], taps[0])
    pre = pre + product(act_wide[rows : 3 * rows], taps[1])
    pre = pre + product(act_wide[2 * rows :], taps[2])
    branch = gelu_value(pre).astype(bf16)
    pre_grad = (branch_grad * gelu_slope(pre)).astype(bf16)

    grad_row = in_order(y == 0, pre_grad, to_y(pre_grad), 0)
    grad_low = send(pre_grad[rows:], lambda i: i + 2)
    grad_high = send(pre_grad[:rows], lambda i: i - 2)

    def spread(partial):
        total = lax.dynamic_index_in_dim(partial, z, 0, keepdims=False)
        for d in range(1, depth):
            piece = lax.dynamic_index_in_dim(
                partial, (z + d) % depth, 0, keepdims=False
            )
            total = total + to_z(piece.astype(bf16), d).astype(f32)
        return total

    tap_terms = jnp.stack(
        [
            product(act_row[:, k * rows : (k + 4) * rows], grad_row).reshape(
                depth, block, half
            )
            for k in range(3)
        ],
        1,
    )
    tap_sum = spread(tap_terms)

    cot_turned = cot.T.reshape(depth, 2, block, 2 * rows)

    def point_term(parity):
        picked = cut(cot_turned, parity, 1, 1).reshape(depth * block, 2 * rows)
        return product(picked, branch).reshape(depth, block, half)

    point_terms = point_term(y) + to_y(point_term(1 - y).astype(bf16)).astype(f32)
    point_sum = spread(point_terms)

    branch_other = to_core(cut(branch, (1 - core) * rows, rows, 0))
    branch_own = in_order(
        core == 0, cut(branch, core * rows, rows, 0), branch_other, 1
    )
    outputs = (xfull + product(branch_own, point_weight)).astype(bf16)

    grad_wide = jnp.concatenate([grad_low, pre_grad, grad_high], 0)
    act_grad = transposed_product(grad_wide[2 * rows :], taps[0])
    act_grad = act_grad + transposed_product(grad_wide[rows : 3 * rows], taps[1])
    act_grad = act_grad + transposed_product(grad_wide[: 2 * rows], taps[2])
    act_grad = cut(act_grad, core * rows, rows, 0) + to_core(
        cut(act_grad, (1 - core) * rows, rows, 0)
    )
    scaled = act_grad * gelu_slope(normed) * norm_gain
    inner = jnp.mean(scaled * xfull, axis=-1, keepdims=True)
    input_grad = (
        cotangent.astype(f32) + ratio * scaled - xfull * ratio * ratio * ratio * inner
    ).astype(bf16)

    sums = jnp.concatenate([tap_sum, point_sum[None]], 0)
    sums = in_order(
        core == 0,
        cut(sums, core * own, own, 1),
        to_core(cut(sums, (1 - core) * own, own, 1)),
        2,
    )
    return (outputs, input_grad, sums[:3], sums[3].T)


def solution(mesh):
    placed = (
        P(("groups", "seq"), None),
        P(),
        P(None, "seq", None),
        P(),
        P(("groups", "seq"), None),
    )
    return jax.shard_map(
        local,
        mesh=mesh,
        in_specs=placed,
        out_specs=(
            P(("groups", "seq"), None),
            P(("groups", "seq"), None),
            P("groups", "seq", None),
            P("groups", "seq"),
        ),
        check_vma=False,
    )
```

time: 338 us -> 212 us (0.63)
  waiting for transfers between devices: 256 us -> 96.2 us
  local copies, waits for them, and re-layouts: 0.91 us -> 31.2 us
  starting transfers between devices: 10.3 us -> 37.3 us
  between operations: 13.9 us -> 1.02 us
  matrix products: 37.6 us -> 27.8 us
    reduce_scatter x2 -> x0, waiting for transfers between devices: 173 us -> none  [the longest x1 151 us: local(): lax.psum_scatter(tap_terms, 'seq', scatter_dimension=1, tiled=True)]
    ppermute x4 -> x27, waiting for transfers between devices: 14 us -> 96.2 us  [send(): return lax.ppermute(value, 'seq', [p for p in pairs if 0 <= p[1] < size])]
    all_gather x1 -> x0, waiting for transfers between devices: 67.6 us -> none  [local(): taps_whole = lax.all_gather(dilated_weight, 'seq', axis=1, tiled=True)]
    ppermute x4 -> x27, starting transfers between devices: 10.1 us -> 37.3 us  [send(): return lax.ppermute(value, 'seq', [p for p in pairs if 0 <= p[1] < size])]
    dynamic_update_slice x0 -> x7, local copies, waits for them, and re-layouts: none -> 12.9 us  [the longest x4 7.37 us: local(): lax.dynamic_update_slice_in_dim(taps, beside[d], (source * 2 + 1 - y) * b...]
    another operation x1, other arithmetic: 11.7 us -> 0.24 us  [local(): jnp.stack([product(act_row[:, k * rows:(k + 4) * rows], grad_row).reshape...]
    dot_general x8 -> x9, matrix products: 26.6 us -> 18.1 us  [product(): return jnp.dot(left, right, preferred_element_type=f32)]
    transpose x0 -> x3, local copies, waits for them, and re-layouts: none -> 7.92 us  [the longest x1 4.62 us: local(): act_turned = act_wide.T.reshape(depth, 2, block, 4 * rows)]
  transfers between devices with their start and end apart: 7 -> 27, of which waited for: 4 -> 9; matrix products, arithmetic and copies ran while one was open for 15% -> 29% of each run, Pallas kernels for 0% -> 0%
where the time goes in v1:
time: 212 us; the launch traced here: 211 us
  waiting for transfers between devices  96.2 us (45%)
  starting transfers between devices  37.3 us (18%)
  local copies, waits for them, and re-layouts  31.2 us (15%)
  matrix products  27.8 us (13%)
  other arithmetic  17.3 us (8%)
    ppermute x27, waiting for transfers between devices, send(): return lax.ppermute(value, 'seq', [p for p in pairs if 0 <= p[1] < size])  96.2 us
    ppermute x27, starting transfers between devices, send(): return lax.ppermute(value, 'seq', [p for p in pairs if 0 <= p[1] < size])  37.3 us
    dot_general x9, matrix products, product(): return jnp.dot(left, right, preferred_element_type=f32)  18.1 us
    dot_general x4, matrix products, transposed_product(): lax.dot_general(left, weight, (((1,), (1,)), ((), ())), preferred_element...  9.71 us
    dynamic_update_slice x4, local copies, waits for them, and re-layouts, local(): lax.dynamic_update_slice_in_dim(taps, beside[d], (source * 2 + 1 - y) * b...  7.37 us
    dynamic_update_slice x3, local copies, waits for them, and re-layouts, local(): lax.dynamic_update_slice_in_dim(taps, columns[d], (source * 2 + y) * bloc...  5.52 us
    transpose x1, local copies, waits for them, and re-layouts, local(): act_turned = act_wide.T.reshape(depth, 2, block, 4 * rows)  4.62 us
  transfers between devices with their start and end apart: 27, of which 9 were waited for; matrix products, arithmetic and copies ran while one was open for 29% of the time, Pallas kernels for 0%

profile of v1, /device:TPU:9, one launch (start us, length us, event | category | flops | bytes accessed | tf_op | source)
XLA Modules:
  0.0 210.8 jit_solution(9363355042332155578)
XLA Ops:
  12.1 3.0 %collective-permute-start = (bf16[256,1536]{1,0:T(8,128)(2,1)}, bf16[256,1536]{1,0:T(8,128)(2,1)}, u32[]{:S(2)}, u32[]{:S(2)}) collective-permute-start(bf16[256,1536]{1,0:T(8,128)(2,1)} %fusion.7), channel_id=1, source_target_pairs={{1,2},{2,1},{3,4},{4,3},{5,6},{6,5},{7,8},{8,7},{9,10},{10,9},{11,... | collective-permute-start | bytes 2359304 | tf_op jit(solution)/shard_map/ppermute | solution.py:57
  15.2 4.4 %collective-permute-done.4 = bf16[3,192,384]{2,1,0:T(8,128)(2,1)} collective-permute-done((bf16[3,192,384]{2,1,0:T(8,128)(2,1)}, bf16[3,192,384]{2,1,0:T(8,128)(2,1)}, u32[]{:S(2)}, u32[]{:S(2)}) %collective-permute-start.4) | collective-permute-done | bytes 442400 | tf_op jit(solution)/shard_map/ppermute | solution.py:57
  19.6 2.3 %collective-permute-start.7 = (bf16[3,192,384]{2,1,0:T(8,128)(2,1)}, bf16[3,192,384]{2,1,0:T(8,128)(2,1)}, u32[]{:S(2)}, u32[]{:S(2)}) collective-permute-start(bf16[3,192,384]{2,1,0:T(8,128)(2,1)} %get-tuple-element.7), channel_id=1, source_target_pairs={{0,8},{1,9},{2,10},{3,11},{4,12},{5,13},{6,14},{7,15},{8,0},{9,1},... | collective-permute-start | bytes 1327112 | tf_op jit(solution)/shard_map/ppermute | solution.py:57
  26.5 24.5 %collective-permute-done.7 = bf16[3,192,384]{2,1,0:T(8,128)(2,1)} collective-permute-done((bf16[3,192,384]{2,1,0:T(8,128)(2,1)}, bf16[3,192,384]{2,1,0:T(8,128)(2,1)}, u32[]{:S(2)}, u32[]{:S(2)}) %collective-permute-start.7) | collective-permute-done | bytes 442400 | tf_op jit(solution)/shard_map/ppermute | solution.py:57
  51.0 7.0 %collective-permute-start.6 = (bf16[3,192,384]{2,1,0:T(8,128)(2,1)}, bf16[3,192,384]{2,1,0:T(8,128)(2,1)}, u32[]{:S(2)}, u32[]{:S(2)}) collective-permute-start(bf16[3,192,384]{2,1,0:T(8,128)(2,1)} %collective-permute-done.5), channel_id=1, source_target_pairs={{0,2},{1,3},{2,0},{3,1},{4,6},{5,7},{6,4},{7,5},{8,10},{9,11},{10,... | collective-permute-start | bytes 1327112 | tf_op jit(solution)/shard_map/ppermute | solution.py:57
  59.4 3.0 %fusion.71 = bf16[1536,512]{0,1:T(8,128)(2,1)} fusion(bf16[256,1536]{1,0:T(8,128)(2,1)S(1)} %copy-done.6, bf16[256,1536]{1,0:T(8,128)(2,1)} %collective-permute-done.12, pred[]{:T(512)S(6)} %eq.27), kind=kLoop, calls=%fused_computation.114 | loop fusion | flops 7077888 | bytes 3145729 | tf_op jit(solution)/shard_map/transpose | solution.py:142
  62.4 2.6 %copy.18 = bf16[1536,512]{1,0:T(8,128)(2,1)} copy(bf16[1536,512]{0,1:T(8,128)(2,1)} %fusion.71) | data formatting | bytes 3145728 | tf_op jit(solution)/shard_map/transpose | solution.py:142
  65.0 2.4 %collective-permute-start.1 = (bf16[256,1536]{1,0:T(8,128)(2,1)}, bf16[256,1536]{1,0:T(8,128)(2,1)S(1)}, u32[]{:S(2)}, u32[]{:S(2)}) collective-permute-start(bf16[256,1536]{1,0:T(8,128)(2,1)} %collective-permute-done), channel_id=1, source_target_pairs={{0,1},{1,0},{2,3},{3,2},{4,5},{5,4},{6,7},{7,6},{8,9},{9,8},{10,11... | collective-permute-start | bytes 2359304 | tf_op jit(solution)/shard_map/ppermute | solution.py:57
  67.4 2.3 %maximum_select_fusion.1 = bf16[512,1536]{1,0:T(8,128)(2,1)S(1)} fusion(bf16[256,1536]{1,0:T(8,128)(2,1)} %collective-permute-done.2, bf16[256,1536]{1,0:T(8,128)(2,1)} %fusion.7, pred[]{:T(512)S(6)} %eq.27), kind=kLoop, calls=%fused_computation.44 | loop fusion | flops 7077888 | bytes 3145729 | tf_op jit(solution)/shard_map/jit(_where)/select_n | solution.py:35
  73.4 5.2 %collective-permute-done.8 = bf16[3,192,384]{2,1,0:T(8,128)(2,1)} collective-permute-done((bf16[3,192,384]{2,1,0:T(8,128)(2,1)}, bf16[3,192,384]{2,1,0:T(8,128)(2,1)}, u32[]{:S(2)}, u32[]{:S(2)}) %collective-permute-start.8) | collective-permute-done | bytes 442400 | tf_op jit(solution)/shard_map/ppermute | solution.py:57
  82.2 3.1 %collective-permute-done.10 = bf16[3,192,384]{2,1,0:T(8,128)(2,1)} collective-permute-done((bf16[3,192,384]{2,1,0:T(8,128)(2,1)}, bf16[3,192,384]{2,1,0:T(8,128)(2,1)}, u32[]{:S(2)}, u32[]{:S(2)}) %collective-permute-start.10) | collective-permute-done | bytes 442400 | tf_op jit(solution)/shard_map/ppermute | solution.py:57
  90.8 2.2 %fusion.28 = f32[512,384]{1,0:T(8,128)S(1)} fusion(bf16[256,1536]{1,0:T(8,128)(2,1)S(1)} %get-tuple-element.12, bf16[512,1536]{1,0:T(8,128)(2,1)S(1)} %maximum_select_fusion.1, bf16[3,1536,384]{2,1,0:T(8,128)(2,1)} %constant_dynamic-update-slice_fusion), kind=kOutput, calls=%fused_computation.39 | convolution fusion | flops 607125504 | bytes 4325376 | tf_op jit(solution)/shard_map/dot_general | solution.py:25
  94.9 2.5 %multiply_convert_fusion = (bf16[512,384]{1,0:T(8,128)(2,1)S(1)}, f32[512,384]{1,0:T(8,128)S(1)}) fusion(f32[512,384]{1,0:T(8,128)S(1)} %fusion.28, f32[512,384]{1,0:T(8,128)S(1)} %fusion.37, bf16[3,1536,384]{2,1,0:T(8,128)(2,1)} %constant_dynamic-update-slice_fusion, bf16[512,1536]{1,0:T(8,128)(2,1)S(1)} %maximum_select_fusion.1, ...), kind=kOutput, calls=%fused_computation.84 | convolution fusion | flops 609288192 | bytes 6291456 | tf_op jit(solution)/shard_map/dot_general | solution.py:25
  97.4 2.8 %fusion.34 = bf16[512,384]{1,0:T(8,128)(2,1)S(1)} fusion(bf16[768,1536]{1,0:T(8,128)(2,1)S(1)} %copy-done, s32[]{:T(128)S(6)} %select_n.205, f32[512,384]{1,0:T(8,128)S(1)} %get-tuple-element.25, bf16[256,1536]{1,0:T(8,128)(2,1)} %collective-permute-done.12, bf16[256,1536]{1,0:T(8,128)(2,1)S(1)} %copy-done.7, pred[]{:T(512)S(6)} %eq.27), kind=kOutput, calls=%fused_computation.54 | convolution fusion | flops 614793216 | bytes 3932165 | tf_op jit(solution)/shard_map/dot_general | solution.py:29
  104.3 4.6 %copy.14 = bf16[1536,1024]{1,0:T(8,128)(2,1)} copy(bf16[1536,1024]{0,1:T(8,128)(2,1)} %maximum_bitcast_fusion) | data formatting | bytes 6291456 | tf_op jit(solution)/shard_map/transpose | solution.py:101
  113.4 3.5 %collective-permute-start.14 = (bf16[256,384]{1,0:T(8,128)(2,1)}, bf16[256,384]{1,0:T(8,128)(2,1)S(1)}, u32[]{:S(2)}, u32[]{:S(2)}) collective-permute-start(bf16[256,384]{1,0:T(8,128)(2,1)} %get-tuple-element.21), channel_id=1, source_target_pairs={{0,2},{1,3},{2,4},{3,5},{4,6},{5,7},{6,8},{7,9},{8,10},{9,11},{10,... | collective-permute-start | bytes 589832 | tf_op jit(solution)/shard_map/ppermute | solution.py:57
  119.5 20.2 %collective-permute-done.13 = bf16[256,384]{1,0:T(8,128)(2,1)S(1)} collective-permute-done((bf16[256,384]{1,0:T(8,128)(2,1)}, bf16[256,384]{1,0:T(8,128)(2,1)S(1)}, u32[]{:S(2)}, u32[]{:S(2)}) %collective-permute-start.13) | collective-permute-done | bytes 196640 | tf_op jit(solution)/shard_map/ppermute | solution.py:57
  139.7 2.3 %fusion.36 = f32[512,1536]{1,0:T(8,128)S(1)} fusion(bf16[3,1536,384]{2,1,0:T(8,128)(2,1)} %constant_dynamic-update-slice_fusion, bf16[256,384]{1,0:T(8,128)(2,1)S(1)} %collective-permute-done.13, bf16[512,384]{1,0:T(8,128)(2,1)S(1)} %fusion.34), kind=kOutput, calls=%fused_computation.63 | convolution fusion | flops 604766208 | bytes 4915200 | tf_op jit(solution)/shard_map/dot_general | solution.py:29
  142.0 2.3 %fusion.38 = f32[512,1536]{1,0:T(8,128)S(1)} fusion(bf16[3,1536,384]{2,1,0:T(8,128)(2,1)} %constant_dynamic-update-slice_fusion, bf16[512,384]{1,0:T(8,128)(2,1)S(1)} %fusion.34, bf16[256,384]{1,0:T(8,128)(2,1)S(1)} %collective-permute-done.14), kind=kOutput, calls=%fused_computation.65 | convolution fusion | flops 604766208 | bytes 4915200 | tf_op jit(solution)/shard_map/dot_general | solution.py:29
  144.3 2.3 %fusion = f32[512,1536]{1,0:T(8,128)S(1)} fusion(f32[512,1536]{1,0:T(8,128)S(1)} %fusion.38, f32[512,1536]{1,0:T(8,128)S(1)} %fusion.36, bf16[512,384]{1,0:T(8,128)(2,1)S(1)} %fusion.34, bf16[3,1536,384]{2,1,0:T(8,128)(2,1)} %constant_dynamic-update-slice_fusion), kind=kOutput, calls=%fused_computation.2 | convolution fusion | flops 605552640 | bytes 11010048 | tf_op jit(solution)/shard_map/dot_general | solution.py:29
  150.9 3.4 %collective-permute-start.24 = (bf16[192,384]{1,0:T(8,128)(2,1)S(1)}, bf16[192,384]{1,0:T(8,128)(2,1)S(1)}, u32[]{:S(2)}, u32[]{:S(2)}) collective-permute-start(bf16[192,384]{1,0:T(8,128)(2,1)S(1)} %get-tuple-element.17), channel_id=1, source_target_pairs={{0,8},{1,9},{2,10},{3,11},{4,12},{5,13},{6,14},{7,15},{8,0},{9,1},... | collective-permute-start | bytes 442376 | tf_op jit(solution)/shard_map/ppermute | solution.py:57
  167.2 18.0 %collective-permute-done.25 = bf16[192,384]{1,0:T(8,128)(2,1)S(1)} collective-permute-done((bf16[192,384]{1,0:T(8,128)(2,1)S(1)}, bf16[192,384]{1,0:T(8,128)(2,1)S(1)}, u32[]{:S(2)}, u32[]{:S(2)}) %collective-permute-start.25) | collective-permute-done | bytes 147488 | tf_op jit(solution)/shard_map/ppermute | solution.py:57
  185.2 15.6 %collective-permute-done.20 = bf16[3,192,384]{2,1,0:T(8,128)(2,1)S(1)} collective-permute-done((bf16[3,192,384]{2,1,0:T(8,128)(2,1)S(1)}, bf16[3,192,384]{2,1,0:T(8,128)(2,1)S(1)}, u32[]{:S(2)}, u32[]{:S(2)}) %collective-permute-start.20) | collective-permute-done | bytes 442400 | tf_op jit(solution)/shard_map/ppermute | solution.py:57
  200.9 4.1 %collective-permute-done.21 = bf16[3,192,384]{2,1,0:T(8,128)(2,1)S(1)} collective-permute-done((bf16[3,192,384]{2,1,0:T(8,128)(2,1)S(1)}, bf16[3,192,384]{2,1,0:T(8,128)(2,1)S(1)}, u32[]{:S(2)}, u32[]{:S(2)}) %collective-permute-start.21) | collective-permute-done | bytes 442400 | tf_op jit(solution)/shard_map/ppermute | solution.py:57
  (105 shorter events, 66.1 us)
Async XLA Ops:
  2.7 55.3 %collective-permute-start.12 = (bf16[256,1536]{1,0:T(8,128)(2,1)}, bf16[256,1536]{1,0:T(8,128)(2,1)}, u32[]{:S(2)}, u32[]{:S(2)}) collective-permute-start(bf16[256,1536]{1,0:T(8,128)(2,1)} %param.9), channel_id=1, source_target_pairs={{0,1},{1,0},{2,3},{3,2},{4,5},{5,4},{6,7},{7,6},{8,9},{9,8},{10,11... | collective-permute-start | bytes 2359304 | tf_op jit(solution)/shard_map/ppermute | solution.py:57
  8.0 11.6 %collective-permute-start.4 = (bf16[3,192,384]{2,1,0:T(8,128)(2,1)}, bf16[3,192,384]{2,1,0:T(8,128)(2,1)}, u32[]{:S(2)}, u32[]{:S(2)}) collective-permute-start(bf16[3,192,384]{2,1,0:T(8,128)(2,1)} %get-tuple-element.7), channel_id=1, source_target_pairs={{0,2},{1,3},{2,0},{3,1},{4,6},{5,7},{6,4},{7,5},{8,10},{9,11},{10,... | collective-permute-start | bytes 1327112 | tf_op jit(solution)/shard_map/ppermute | solution.py:57
  9.2 12.7 %collective-permute-start.5 = (bf16[3,192,384]{2,1,0:T(8,128)(2,1)}, bf16[3,192,384]{2,1,0:T(8,128)(2,1)}, u32[]{:S(2)}, u32[]{:S(2)}) collective-permute-start(bf16[3,192,384]{2,1,0:T(8,128)(2,1)} %get-tuple-element.7), channel_id=1, source_target_pairs={{0,4},{1,5},{2,6},{3,7},{4,8},{5,9},{6,10},{7,11},{8,12},{9,13},{1... | collective-permute-start | bytes 1327112 | tf_op jit(solution)/shard_map/ppermute | solution.py:57
  12.1 52.9 %collective-permute-start = (bf16[256,1536]{1,0:T(8,128)(2,1)}, bf16[256,1536]{1,0:T(8,128)(2,1)}, u32[]{:S(2)}, u32[]{:S(2)}) collective-permute-start(bf16[256,1536]{1,0:T(8,128)(2,1)} %fusion.7), channel_id=1, source_target_pairs={{1,2},{2,1},{3,4},{4,3},{5,6},{6,5},{7,8},{8,7},{9,10},{10,9},{11,... | collective-permute-start | bytes 2359304 | tf_op jit(solution)/shard_map/ppermute | solution.py:57
  15.1 52.3 %collective-permute-start.2 = (bf16[256,1536]{1,0:T(8,128)(2,1)}, bf16[256,1536]{1,0:T(8,128)(2,1)}, u32[]{:S(2)}, u32[]{:S(2)}) collective-permute-start(bf16[256,1536]{1,0:T(8,128)(2,1)} %fusion.7), channel_id=1, source_target_pairs={{0,1},{1,0},{2,3},{3,2},{4,5},{5,4},{6,7},{7,6},{8,9},{9,8},{10,11... | collective-permute-start | bytes 2359304 | tf_op jit(solution)/shard_map/ppermute | solution.py:57
  19.6 31.4 %collective-permute-start.7 = (bf16[3,192,384]{2,1,0:T(8,128)(2,1)}, bf16[3,192,384]{2,1,0:T(8,128)(2,1)}, u32[]{:S(2)}, u32[]{:S(2)}) collective-permute-start(bf16[3,192,384]{2,1,0:T(8,128)(2,1)} %get-tuple-element.7), channel_id=1, source_target_pairs={{0,8},{1,9},{2,10},{3,11},{4,12},{5,13},{6,14},{7,15},{8,0},{9,1},... | collective-permute-start | bytes 1327112 | tf_op jit(solution)/shard_map/ppermute | solution.py:57
  21.9 36.1 %collective-permute-start.9 = (bf16[3,192,384]{2,1,0:T(8,128)(2,1)}, bf16[3,192,384]{2,1,0:T(8,128)(2,1)}, u32[]{:S(2)}, u32[]{:S(2)}) collective-permute-start(bf16[3,192,384]{2,1,0:T(8,128)(2,1)} %get-tuple-element.7), channel_id=1, source_target_pairs={{0,12},{1,13},{2,14},{3,15},{4,0},{5,1},{6,2},{7,3},{8,4},{9,5},{1... | collective-permute-start | bytes 1327112 | tf_op jit(solution)/shard_map/ppermute | solution.py:57
  51.0 18.8 %collective-permute-start.6 = (bf16[3,192,384]{2,1,0:T(8,128)(2,1)}, bf16[3,192,384]{2,1,0:T(8,128)(2,1)}, u32[]{:S(2)}, u32[]{:S(2)}) collective-permute-start(bf16[3,192,384]{2,1,0:T(8,128)(2,1)} %collective-permute-done.5), channel_id=1, source_target_pairs={{0,2},{1,3},{2,0},{3,1},{4,6},{5,7},{6,4},{7,5},{8,10},{9,11},{10,... | collective-permute-start | bytes 1327112 | tf_op jit(solution)/shard_map/ppermute | solution.py:57
  58.0 20.6 %collective-permute-start.8 = (bf16[3,192,384]{2,1,0:T(8,128)(2,1)}, bf16[3,192,384]{2,1,0:T(8,128)(2,1)}, u32[]{:S(2)}, u32[]{:S(2)}) collective-permute-start(bf16[3,192,384]{2,1,0:T(8,128)(2,1)} %collective-permute-done.7), channel_id=1, source_target_pairs={{0,2},{1,3},{2,0},{3,1},{4,6},{5,7},{6,4},{7,5},{8,10},{9,11},{10,... | collective-permute-start | bytes 1327112 | tf_op jit(solution)/shard_map/ppermute | solution.py:57
  58.0 27.3 %collective-permute-start.10 = (bf16[3,192,384]{2,1,0:T(8,128)(2,1)}, bf16[3,192,384]{2,1,0:T(8,128)(2,1)}, u32[]{:S(2)}, u32[]{:S(2)}) collective-permute-start(bf16[3,192,384]{2,1,0:T(8,128)(2,1)} %collective-permute-done.9), channel_id=1, source_target_pairs={{0,2},{1,3},{2,0},{3,1},{4,6},{5,7},{6,4},{7,5},{8,10},{9,11},{10,... | collective-permute-start | bytes 1327112 | tf_op jit(solution)/shard_map/ppermute | solution.py:57
  65.0 24.4 %collective-permute-start.1 = (bf16[256,1536]{1,0:T(8,128)(2,1)}, bf16[256,1536]{1,0:T(8,128)(2,1)S(1)}, u32[]{:S(2)}, u32[]{:S(2)}) collective-permute-start(bf16[256,1536]{1,0:T(8,128)(2,1)} %collective-permute-done), channel_id=1, source_target_pairs={{0,1},{1,0},{2,3},{3,2},{4,5},{5,4},{6,7},{7,6},{8,9},{9,8},{10,11... | collective-permute-start | bytes 2359304 | tf_op jit(solution)/shard_map/ppermute | solution.py:57
  100.3 55.0 %collective-permute-start.18 = (bf16[512,384]{1,0:T(8,128)(2,1)S(1)}, bf16[512,384]{1,0:T(8,128)(2,1)}, u32[]{:S(2)}, u32[]{:S(2)}) collective-permute-start(bf16[512,384]{1,0:T(8,128)(2,1)S(1)} %fusion.34), channel_id=1, source_target_pairs={{0,2},{1,3},{2,0},{3,1},{4,6},{5,7},{6,4},{7,5},{8,10},{9,11},{10,... | collective-permute-start | bytes 1179656 | tf_op jit(solution)/shard_map/ppermute | solution.py:57
  104.3 43.2 %collective-permute-start.22 = (bf16[4,192,384]{2,1,0:T(8,128)(2,1)}, bf16[4,192,384]{2,1,0:T(8,128)(2,1)}, u32[]{:S(2)}, u32[]{:S(2)}) collective-permute-start(bf16[4,192,384]{2,1,0:T(8,128)(2,1)} %convolution_convert_fusion), channel_id=1, source_target_pairs={{0,2},{1,3},{2,0},{3,1},{4,6},{5,7},{6,4},{7,5},{8,10},{9,11},{10,... | collective-permute-start | bytes 1769480 | tf_op jit(solution)/shard_map/ppermute | solution.py:57
  109.9 37.4 %collective-permute-start.16 = (bf16[768,256]{1,0:T(8,128)(2,1)S(1)}, bf16[768,256]{1,0:T(8,128)(2,1)S(1)}, u32[]{:S(2)}, u32[]{:S(2)}) collective-permute-start(bf16[768,256]{1,0:T(8,128)(2,1)S(1)} %bitcast.87), channel_id=1, source_target_pairs={{0,2},{1,3},{2,0},{3,1},{4,6},{5,7},{6,4},{7,5},{8,10},{9,11},{10,... | collective-permute-start | bytes 1179656 | tf_op jit(solution)/shard_map/ppermute | solution.py:57
  111.4 28.3 %collective-permute-start.13 = (bf16[256,384]{1,0:T(8,128)(2,1)}, bf16[256,384]{1,0:T(8,128)(2,1)S(1)}, u32[]{:S(2)}, u32[]{:S(2)}) collective-permute-start(bf16[256,384]{1,0:T(8,128)(2,1)} %get-tuple-element.20), channel_id=1, source_target_pairs={{2,0},{3,1},{4,2},{5,3},{6,4},{7,5},{8,6},{9,7},{10,8},{11,9},{12,... | collective-permute-start | bytes 589832 | tf_op jit(solution)/shard_map/ppermute | solution.py:57
  113.4 28.6 %collective-permute-start.14 = (bf16[256,384]{1,0:T(8,128)(2,1)}, bf16[256,384]{1,0:T(8,128)(2,1)S(1)}, u32[]{:S(2)}, u32[]{:S(2)}) collective-permute-start(bf16[256,384]{1,0:T(8,128)(2,1)} %get-tuple-element.21), channel_id=1, source_target_pairs={{0,2},{1,3},{2,4},{3,5},{4,6},{5,7},{6,8},{7,9},{8,10},{9,11},{10,... | collective-permute-start | bytes 589832 | tf_op jit(solution)/shard_map/ppermute | solution.py:57
  139.7 22.9 %collective-permute-start.11 = (bf16[256,384]{1,0:T(8,128)(2,1)S(1)}, bf16[256,384]{1,0:T(8,128)(2,1)S(1)}, u32[]{:S(2)}, u32[]{:S(2)}) collective-permute-start(bf16[256,384]{1,0:T(8,128)(2,1)S(1)} %get-tuple-element.23), channel_id=1, source_target_pairs={{0,1},{1,0},{2,3},{3,2},{4,5},{5,4},{6,7},{7,6},{8,9},{9,8},{10,11... | collective-permute-start | bytes 589832 | tf_op jit(solution)/shard_map/ppermute | solution.py:57
  146.8 59.1 %collective-permute-start.15 = (f32[256,1536]{1,0:T(8,128)S(1)}, f32[256,1536]{1,0:T(8,128)S(1)}, u32[]{:S(2)}, u32[]{:S(2)}) collective-permute-start(f32[256,1536]{1,0:T(8,128)S(1)} %constant_dynamic-slice_fusion.2), channel_id=1, source_target_pairs={{0,1},{1,0},{2,3},{3,2},{4,5},{5,4},{6,7},{7,6},{8,9},{9,8},{10,11... | collective-permute-start | bytes 4718600 | tf_op jit(solution)/shard_map/ppermute | solution.py:57
  149.8 13.9 %collective-permute-start.23 = (bf16[192,384]{1,0:T(8,128)(2,1)S(1)}, bf16[192,384]{1,0:T(8,128)(2,1)S(1)}, u32[]{:S(2)}, u32[]{:S(2)}) collective-permute-start(bf16[192,384]{1,0:T(8,128)(2,1)S(1)} %get-tuple-element.15), channel_id=1, source_target_pairs={{0,4},{1,5},{2,6},{3,7},{4,8},{5,9},{6,10},{7,11},{8,12},{9,13},{1... | collective-permute-start | bytes 442376 | tf_op jit(solution)/shard_map/ppermute | solution.py:57
  150.9 14.6 %collective-permute-start.24 = (bf16[192,384]{1,0:T(8,128)(2,1)S(1)}, bf16[192,384]{1,0:T(8,128)(2,1)S(1)}, u32[]{:S(2)}, u32[]{:S(2)}) collective-permute-start(bf16[192,384]{1,0:T(8,128)(2,1)S(1)} %get-tuple-element.17), channel_id=1, source_target_pairs={{0,8},{1,9},{2,10},{3,11},{4,12},{5,13},{6,14},{7,15},{8,0},{9,1},... | collective-permute-start | bytes 442376 | tf_op jit(solution)/shard_map/ppermute | solution.py:57
  155.3 29.9 %collective-permute-start.25 = (bf16[192,384]{1,0:T(8,128)(2,1)S(1)}, bf16[192,384]{1,0:T(8,128)(2,1)S(1)}, u32[]{:S(2)}, u32[]{:S(2)}) collective-permute-start(bf16[192,384]{1,0:T(8,128)(2,1)S(1)} %get-tuple-element.16), channel_id=1, source_target_pairs={{0,12},{1,13},{2,14},{3,15},{4,0},{5,1},{6,2},{7,3},{8,4},{9,5},{1... | collective-permute-start | bytes 442376 | tf_op jit(solution)/shard_map/ppermute | solution.py:57
  162.6 22.7 %collective-permute-start.19 = (bf16[3,192,384]{2,1,0:T(8,128)(2,1)S(1)}, bf16[3,192,384]{2,1,0:T(8,128)(2,1)S(1)}, u32[]{:S(2)}, u32[]{:S(2)}) collective-permute-start(bf16[3,192,384]{2,1,0:T(8,128)(2,1)S(1)} %get-tuple-element.8), channel_id=1, source_target_pairs={{0,4},{1,5},{2,6},{3,7},{4,8},{5,9},{6,10},{7,11},{8,12},{9,13},{1... | collective-permute-start | bytes 1327112 | tf_op jit(solution)/shard_map/ppermute | solution.py:57
  163.7 37.2 %collective-permute-start.20 = (bf16[3,192,384]{2,1,0:T(8,128)(2,1)S(1)}, bf16[3,192,384]{2,1,0:T(8,128)(2,1)S(1)}, u32[]{:S(2)}, u32[]{:S(2)}) collective-permute-start(bf16[3,192,384]{2,1,0:T(8,128)(2,1)S(1)} %get-tuple-element.10), channel_id=1, source_target_pairs={{0,8},{1,9},{2,10},{3,11},{4,12},{5,13},{6,14},{7,15},{8,0},{9,1},... | collective-permute-start | bytes 1327112 | tf_op jit(solution)/shard_map/ppermute | solution.py:57
  165.5 39.5 %collective-permute-start.21 = (bf16[3,192,384]{2,1,0:T(8,128)(2,1)S(1)}, bf16[3,192,384]{2,1,0:T(8,128)(2,1)S(1)}, u32[]{:S(2)}, u32[]{:S(2)}) collective-permute-start(bf16[3,192,384]{2,1,0:T(8,128)(2,1)S(1)} %get-tuple-element.9), channel_id=1, source_target_pairs={{0,12},{1,13},{2,14},{3,15},{4,0},{5,1},{6,2},{7,3},{8,4},{9,5},{1... | collective-permute-start | bytes 1327112 | tf_op jit(solution)/shard_map/ppermute | solution.py:57
  (15 other events, 175.6 us)

commit v2 on v1

v2 whole, which is shorter than its diff:
```python
import functools
import math

import jax
import jax.numpy as jnp
from jax import lax
from jax.experimental import pallas as pl
from jax.experimental.pallas import tpu as pltpu
from jax.sharding import PartitionSpec as P

root_coef = math.sqrt(2.0 / math.pi)
bf16 = jnp.bfloat16
f32 = jnp.float32


def gelu_value(v):
    return 0.5 * v * (1.0 + jnp.tanh(root_coef * (v + 0.044715 * v * v * v)))


def gelu_slope(v):
    inner = jnp.tanh(root_coef * (v + 0.044715 * v * v * v))
    return 0.5 * (1.0 + inner) + 0.5 * v * (1.0 - inner * inner) * root_coef * (
        1.0 + 3.0 * 0.044715 * v * v
    )


def product(left, right):
    return jnp.dot(left, right, preferred_element_type=f32)


def transposed_product(left, weight):
    return lax.dot_general(
        left, weight, (((1,), (1,)), ((), ())), preferred_element_type=f32
    )


def in_order(first, mine, other, axis):
    return jnp.where(
        first,
        jnp.concatenate([mine, other], axis),
        jnp.concatenate([other, mine], axis),
    )


MIB = 1024 * 1024


def position():
    me = lax.axis_index("seq")
    return me // 4, (me // 2) % 2, me % 2


def fetch(pairs, sems):
    copies = [
        pltpu.make_async_copy(src, dst, sems.at[i]) for i, (src, dst) in enumerate(pairs)
    ]
    for copy in copies:
        copy.start()
    for copy in copies:
        copy.wait()


def tap_copies(pieces, whole):
    z, y, _ = position()
    depth = len(pieces) // 2
    block = pieces[0].shape[1]
    pairs = []
    for i, piece in enumerate(pieces):
        source = lax.rem(z + depth - i % depth, depth)
        side = y if i < depth else 1 - y
        start = pl.multiple_of((source * 2 + side) * block, block)
        pairs.append((piece, whole.at[:, pl.ds(start, block), :]))
    return pairs


def forward_kernel(count, *refs):
    pieces = refs[:count]
    act, act_other, edge, edge_other, slope_in = refs[count : count + 5]
    branch, grad, wide, taps, sems = refs[count + 5 :]
    _, _, core = position()
    rows = act.shape[0]

    def at(start):
        return wide.at[pl.ds(pl.multiple_of(start * rows, rows), rows), :]

    fetch(
        [
            (act, at(1 + core)),
            (act_other, at(2 - core)),
            (edge, at(3 * core)),
            (edge_other, at(3 - 3 * core)),
        ]
        + tap_copies(pieces, taps),
        sems,
    )
    for part in range(2):
        pre = product(wide[pl.ds(part * rows, rows), :], taps[0])
        pre = pre + product(wide[pl.ds((part + 1) * rows, rows), :], taps[1])
        pre = pre + product(wide[pl.ds((part + 2) * rows, rows), :], taps[2])
        here = pl.ds(part * rows, rows)
        branch[here, :] = gelu_value(pre).astype(bf16)
        grad[here, :] = (slope_in[here, :] * gelu_slope(pre)).astype(bf16)


def terms_kernel(depth, near, far, far_other, mine, other, *refs):
    outs = refs[:depth]
    wide, grads, sems = refs[depth:]
    z, y, core = position()
    rows = far.shape[-1]
    span = mine.shape[0]

    def at(start):
        return wide.at[:, :, pl.ds(pl.multiple_of(start * rows, rows), rows)]

    fetch(
        [
            (
                near.at[:, y],
                wide.at[:, :, pl.ds(pl.multiple_of(y * 2 * rows, 2 * rows), 4 * rows)],
            ),
            (far, at((1 - y) * 4 + core)),
            (far_other, at((1 - y) * 4 + 1 - core)),
            (mine, grads.at[pl.ds(pl.multiple_of(y * span, span), span), :]),
            (other, grads.at[pl.ds(pl.multiple_of((1 - y) * span, span), span), :]),
        ],
        sems,
    )
    for i in range(depth):
        d = (i + 1) % depth
        target = lax.rem(z + d, depth)
        for k in range(3):
            outs[d][k] = product(
                wide[target, :, pl.ds(k * rows, 4 * rows)], grads[...]
            ).astype(outs[d].dtype)


def point_kernel(depth, turned, branch, *outs):
    z, _, _ = position()
    for i in range(depth):
        d = (i + 1) % depth
        target = lax.rem(z + d, depth)
        outs[d][...] = product(turned[target], branch[...]).astype(outs[d].dtype)


def backward_kernel(count, *refs):
    pieces = refs[:count]
    low, grad, high = refs[count : count + 3]
    mine, other, wide, taps, sems = refs[count + 3 :]
    _, _, core = position()
    rows = low.shape[0]
    fetch(
        [
            (low, wide.at[pl.ds(0, rows), :]),
            (grad, wide.at[pl.ds(rows, 2 * rows), :]),
            (high, wide.at[pl.ds(3 * rows, rows), :]),
        ]
        + tap_copies(pieces, taps),
        sems,
    )
    for out, part in ((other, 1 - core), (mine, core)):
        total = None
        for k in range(3):
            start = pl.multiple_of((part + 2 - k) * rows, rows)
            term = transposed_product(wide[pl.ds(start, rows), :], taps[k])
            total = term if total is None else total + term
        out[...] = total


def call(kernel, outs, args, specs, scratch, flops, limit):
    nbytes = sum(a.size * a.dtype.itemsize for a in args) + sum(
        math.prod(s) * jnp.dtype(t).itemsize for s, t in outs
    )
    return pl.pallas_call(
        kernel,
        out_shape=[jax.ShapeDtypeStruct(s, t) for s, t in outs],
        in_specs=[pl.BlockSpec(memory_space=m) for m in specs],
        out_specs=[pl.BlockSpec(memory_space=pltpu.VMEM)] * len(outs),
        scratch_shapes=scratch,
        compiler_params=pltpu.CompilerParams(vmem_limit_bytes=limit * MIB),
        cost_estimate=pl.CostEstimate(
            flops=flops, bytes_accessed=nbytes, transcendentals=0
        ),
    )(*args)


def local(inputs, norm_gain, dilated_weight, point_weight, cotangent):
    size = lax.axis_size("seq")
    depth = size // 4
    z, y, core = position()
    rows, channels = inputs.shape
    own = dilated_weight.shape[1]
    hidden = dilated_weight.shape[2]
    half = hidden // 2
    block = 2 * own
    span = 2 * rows

    def send(value, target):
        pairs = [(i, target(i)) for i in range(size)]
        return lax.ppermute(value, "seq", [p for p in pairs if 0 <= p[1] < size])

    def to_core(value):
        return send(value, lambda i: i ^ 1)

    def to_y(value):
        return send(value, lambda i: i ^ 2)

    def to_z(value, by):
        return send(value, lambda i: (i + 4 * by) % size)

    def cut(value, start, length, axis):
        return lax.dynamic_slice_in_dim(value, start, length, axis)

    mine = cut(dilated_weight, core * half, half, 2)
    theirs = cut(dilated_weight, (1 - core) * half, half, 2)
    chip_taps = in_order(core == 0, mine, to_core(theirs), 1)
    pieces = [chip_taps] + [to_z(chip_taps, d) for d in range(1, depth)]
    pieces = pieces + [to_y(c) for c in pieces]

    xfull = inputs.astype(f32)
    ratio = lax.rsqrt(jnp.mean(xfull * xfull, axis=-1, keepdims=True) + 1e-06)
    normed = xfull * ratio * norm_gain
    act = gelu_value(normed).astype(bf16)
    edge = send(act, lambda i: i + 1 if i % 2 else i - 1)
    act_other = to_core(act)
    edge_other = to_core(edge)

    cot_other = to_core(cotangent)
    cot = in_order(core == 0, cotangent, cot_other, 0)
    point_rows = cut(point_weight, core * half, half, 0)
    branch_grad = transposed_product(cot, point_rows)
    cot_turned = cot.T.reshape(depth, 2 * block, span)

    act_wide = jnp.concatenate(
        [
            jnp.where(core == 0, edge, edge_other),
            in_order(core == 0, act, act_other, 0),
            jnp.where(core == 0, edge_other, edge),
        ],
        0,
    )
    act_turned = act_wide.T.reshape(depth, 2, block, 4 * rows)
    far = to_y(
        lax.dynamic_slice(
            act_turned,
            (0, 1 - y, 0, (y * 2 + core) * rows),
            (depth, 1, block, rows),
        ).reshape(depth, block, rows)
    )
    far_other = to_core(far)

    count = len(pieces)
    branch, pre_grad = call(
        functools.partial(forward_kernel, count),
        [((span, half), bf16)] * 2,
        [*pieces, act, act_other, edge, edge_other, branch_grad],
        [pl.ANY] * (count + 4) + [pltpu.VMEM],
        [
            pltpu.VMEM((4 * rows, channels), bf16),
            pltpu.VMEM((3, channels, half), bf16),
            pltpu.SemaphoreType.DMA((count + 4,)),
        ],
        6 * span * channels * half,
        24,
    )

    grad_far = to_y(pre_grad)
    grad_low = send(pre_grad[rows:], lambda i: i + 2)
    grad_high = send(pre_grad[:rows], lambda i: i - 2)

    def gathered(terms):
        total = terms[0]
        for d in range(1, depth):
            total = total + to_z(terms[d], d).astype(f32)
        return total

    point_terms = call(
        functools.partial(point_kernel, depth),
        [((2 * block, half), bf16 if d else f32) for d in range(depth)],
        [cot_turned, branch],
        [pltpu.VMEM] * 2,
        [],
        2 * span * channels * half,
        16,
    )
    point_sum = gathered(point_terms)

    tap_terms = call(
        functools.partial(terms_kernel, depth),
        [((3, block, half), bf16 if d else f32) for d in range(depth)],
        [act_turned, far, far_other, pre_grad, grad_far],
        [pl.ANY] * 5,
        [
            pltpu.VMEM((depth, block, 6 * rows), bf16),
            pltpu.VMEM((2 * span, half), bf16),
            pltpu.SemaphoreType.DMA((5,)),
        ],
        6 * span * channels * half,
        24,
    )
    tap_sum = gathered(tap_terms)

    point_sum = cut(point_sum, y * block, block, 0) + to_y(
        cut(point_sum, (1 - y) * block, block, 0).astype(bf16)
    ).astype(f32)

    branch_other = to_core(cut(branch, (1 - core) * rows, rows, 0))
    branch_own = in_order(
        core == 0, cut(branch, core * rows, rows, 0), branch_other, 1
    )
    outputs = (xfull + product(branch_own, point_weight)).astype(bf16)

    act_grad, act_grad_other = call(
        functools.partial(backward_kernel, count),
        [((rows, channels), f32)] * 2,
        [*pieces, grad_low, pre_grad, grad_high],
        [pl.ANY] * (count + 3),
        [
            pltpu.VMEM((4 * rows, half), bf16),
            pltpu.VMEM((3, channels, half), bf16),
            pltpu.SemaphoreType.DMA((count + 3,)),
        ],
        6 * span * channels * half,
        24,
    )
    act_grad = act_grad + to_core(act_grad_other)
    scaled = act_grad * gelu_slope(normed) * norm_gain
    inner = jnp.mean(scaled * xfull, axis=-1, keepdims=True)
    input_grad = (
        cotangent.astype(f32) + ratio * scaled - xfull * ratio * ratio * ratio * inner
    ).astype(bf16)

    sums = jnp.concatenate([tap_sum, point_sum[None]], 0)
    sums = in_order(
        core == 0,
        cut(sums, core * own, own, 1),
        to_core(cut(sums, (1 - core) * own, own, 1)),
        2,
    )
    return (outputs, input_grad, sums[:3], sums[3].T)


def solution(mesh):
    placed = (
        P(("groups", "seq"), None),
        P(),
        P(None, "seq", None),
        P(),
        P(("groups", "seq"), None),
    )
    return jax.shard_map(
        local,
        mesh=mesh,
        in_specs=placed,
        out_specs=(
            P(("groups", "seq"), None),
            P(("groups", "seq"), None),
            P("groups", "seq", None),
            P("groups", "seq"),
        ),
        check_vma=False,
    )
```

time: 212 us -> 207 us (0.976)
  matrix products: 27.8 us -> 5.53 us
  Pallas kernels: 0 us -> 16.6 us
  local copies, waits for them, and re-layouts: 31.2 us -> 18.8 us
  starting transfers between devices: 37.3 us -> 46.5 us
  other arithmetic: 17.3 us -> 19.8 us
  waiting for transfers between devices: 96.2 us -> 98.4 us
    pallas_call x0 -> x4, Pallas kernels: none -> 16.6 us  [call(): pl.pallas_call(kernel, out_shape=[jax.ShapeDtypeStruct(s, t) for s, t in...]
    dot_general x9 -> x1, matrix products: 18.1 us -> 1.66 us  [product(): return jnp.dot(left, right, preferred_element_type=f32)]
    dynamic_update_slice x7 -> x0, local copies, waits for them, and re-layouts: 12.9 us -> none  [the longest x4 7.37 us: local(): lax.dynamic_update_slice_in_dim(taps, beside[d], (source * 2 + 1 - y) * b...]
    ppermute x27, starting transfers between devices: 37.3 us -> 46.5 us  [send(): return lax.ppermute(value, 'seq', [p for p in pairs if 0 <= p[1] < size])]
    dot_general x4 -> x1, matrix products: 9.71 us -> 3.87 us  [transposed_product(): lax.dot_general(left, weight, (((1,), (1,)), ((), ())), preferred_element...]
    unnamed x24 -> x16, local copies, waits for them, and re-layouts: 1.39 us -> 4.33 us
    ppermute x27, waiting for transfers between devices: 96.2 us -> 98.4 us  [send(): return lax.ppermute(value, 'seq', [p for p in pairs if 0 <= p[1] < size])]
  transfers between devices with their start and end apart: 27 -> 27, of which waited for: 9 -> 10; matrix products, arithmetic and copies ran while one was open for 29% -> 17% of each run, Pallas kernels for 0% -> 8%
where the time goes in v2:
time: 207 us; the launch traced here: 206 us
  waiting for transfers between devices  98.4 us (48%)
  starting transfers between devices  46.5 us (22%)
  other arithmetic  19.8 us (10%)
  local copies, waits for them, and re-layouts  18.8 us (9%)
  Pallas kernels  16.6 us (8%)
  matrix products  5.53 us (3%)
    ppermute x27, waiting for transfers between devices, send(): return lax.ppermute(value, 'seq', [p for p in pairs if 0 <= p[1] < size])  98.4 us
    ppermute x27, starting transfers between devices, send(): return lax.ppermute(value, 'seq', [p for p in pairs if 0 <= p[1] < size])  46.5 us
    pallas_call x4, Pallas kernels, call(): pl.pallas_call(kernel, out_shape=[jax.ShapeDtypeStruct(s, t) for s, t in...  16.6 us
    transpose x1, local copies, waits for them, and re-layouts, local(): act_turned = act_wide.T.reshape(depth, 2, block, 4 * rows)  4.64 us
    unnamed x16, local copies, waits for them, and re-layouts  4.33 us
  transfers between devices with their start and end apart: 27, of which 10 were waited for; matrix products, arithmetic and copies ran while one was open for 17% of the time, Pallas kernels for 8%

profile of v2, /device:TPU:9, one launch (start us, length us, event | category | flops | bytes accessed | tf_op | source)
XLA Modules:
  0.0 206.3 jit_solution(1217932518889567332)
XLA Ops:
  4.0 3.7 %collective-permute-start.9 = (bf16[256,1536]{1,0:T(8,128)(2,1)S(1)}, bf16[256,1536]{1,0:T(8,128)(2,1)}, u32[]{:S(2)}, u32[]{:S(2)}) collective-permute-start(bf16[256,1536]{1,0:T(8,128)(2,1)S(1)} %fusion.6.refs_8_), channel_id=1, source_target_pairs={{1,2},{2,1},{3,4},{4,3},{5,6},{6,5},{7,8},{8,7},{9,10},{10,9},{11,... | collective-permute-start | bytes 2359304 | tf_op jit(solution)/shard_map/ppermute | solution.py:199
  10.1 15.8 %collective-permute-done.9.refs_10_ = bf16[256,1536]{1,0:T(8,128)(2,1)} collective-permute-done((bf16[256,1536]{1,0:T(8,128)(2,1)S(1)}, bf16[256,1536]{1,0:T(8,128)(2,1)}, u32[]{:S(2)}, u32[]{:S(2)}) %collective-permute-start.9) | collective-permute-done | bytes 786464 | tf_op jit(solution)/shard_map/ppermute | solution.py:199
  31.6 3.9 %fusion.21.refs_12_ = f32[512,384]{1,0:T(8,128)} fusion(bf16[768,1536]{1,0:T(8,128)(2,1)S(1)} %copy-done, s32[]{:T(128)S(6)} %select_n.97, bf16[256,1536]{1,0:T(8,128)(2,1)} %collective-permute-done.11, bf16[256,1536]{1,0:T(8,128)(2,1)} %param.9, pred[]{:T(512)S(6)} %eq.5), kind=kOutput, calls=%fused_computation.35 | convolution fusion | flops 611057664 | bytes 3538949 | tf_op jit(solution)/shard_map/dot_general | solution.py:32
  35.5 3.9 %collective-permute-done.1.refs_1_ = bf16[3,192,384]{2,1,0:T(8,128)(2,1)} collective-permute-done((bf16[3,192,384]{2,1,0:T(8,128)(2,1)}, bf16[3,192,384]{2,1,0:T(8,128)(2,1)}, u32[]{:S(2)}, u32[]{:S(2)}) %collective-permute-start.1) | collective-permute-done | bytes 442400 | tf_op jit(solution)/shard_map/ppermute | solution.py:199
  41.8 25.1 %collective-permute-done.2.refs_2_ = bf16[3,192,384]{2,1,0:T(8,128)(2,1)} collective-permute-done((bf16[3,192,384]{2,1,0:T(8,128)(2,1)}, bf16[3,192,384]{2,1,0:T(8,128)(2,1)}, u32[]{:S(2)}, u32[]{:S(2)}) %collective-permute-start.2) | collective-permute-done | bytes 442400 | tf_op jit(solution)/shard_map/ppermute | solution.py:199
  76.5 4.6 %copy.9 = bf16[1536,1024]{1,0:T(8,128)(2,1)} copy(bf16[1536,1024]{0,1:T(8,128)(2,1)} %maximum_bitcast_fusion) | data formatting | bytes 6291456 | tf_op jit(solution)/shard_map/transpose | solution.py:241
  84.4 4.5 %collective-permute-done.6.refs_6_ = bf16[3,192,384]{2,1,0:T(8,128)(2,1)} collective-permute-done((bf16[3,192,384]{2,1,0:T(8,128)(2,1)}, bf16[3,192,384]{2,1,0:T(8,128)(2,1)}, u32[]{:S(2)}, u32[]{:S(2)}) %collective-permute-start.6) | collective-permute-done | bytes 442400 | tf_op jit(solution)/shard_map/ppermute | solution.py:199
  88.9 9.5 %collective-permute-done.7.refs_7_ = bf16[3,192,384]{2,1,0:T(8,128)(2,1)} collective-permute-done((bf16[3,192,384]{2,1,0:T(8,128)(2,1)}, bf16[3,192,384]{2,1,0:T(8,128)(2,1)}, u32[]{:S(2)}, u32[]{:S(2)}) %collective-permute-start.7) | collective-permute-done | bytes 442400 | tf_op jit(solution)/shard_map/ppermute | solution.py:199
  99.5 5.8 %shard_map.84 = (bf16[512,384]{1,0:T(8,128)(2,1)S(1)}, bf16[512,384]{1,0:T(8,128)(2,1)S(1)}) custom-call(bf16[3,192,384]{2,1,0:T(8,128)(2,1)} %maximum_select_fusion.3.refs_0_, bf16[3,192,384]{2,1,0:T(8,128)(2,1)} %collective-permute-done.1.refs_1_, bf16[3,192,384]{2,1,0:T(8,128)(2,1)} %collective-permute-done.2.refs_2_, ...), custom_call_target="tpu_custom_call" | custom-call | flops 1811939328 | bytes 8257536 | tf_op jit(solution)/shard_map/pallas_call | solution.py:173
  106.9 3.0 %collective-permute-start.13 = (bf16[256,384]{1,0:T(8,128)(2,1)}, bf16[256,384]{1,0:T(8,128)(2,1)S(1)}, u32[]{:S(2)}, u32[]{:S(2)}) collective-permute-start(bf16[256,384]{1,0:T(8,128)(2,1)} %get-tuple-element.37), channel_id=1, source_target_pairs={{0,2},{1,3},{2,4},{3,5},{4,6},{5,7},{6,8},{7,9},{8,10},{9,11},{10,... | collective-permute-start | bytes 589832 | tf_op jit(solution)/shard_map/ppermute | solution.py:199
  109.9 3.1 %collective-permute-start.14 = (bf16[256,384]{1,0:T(8,128)(2,1)}, bf16[256,384]{1,0:T(8,128)(2,1)}, u32[]{:S(2)}, u32[]{:S(2)}) collective-permute-start(bf16[256,384]{1,0:T(8,128)(2,1)} %get-tuple-element.36), channel_id=1, source_target_pairs={{2,0},{3,1},{4,2},{5,3},{6,4},{7,5},{8,6},{9,7},{10,8},{11,9},{12,... | collective-permute-start | bytes 589832 | tf_op jit(solution)/shard_map/ppermute | solution.py:199
  113.1 3.5 %fusion.31 = bf16[1536,512]{0,1:T(8,128)(2,1)} fusion(bf16[256,1536]{1,0:T(8,128)(2,1)} %param.9, bf16[256,1536]{1,0:T(8,128)(2,1)} %collective-permute-done.11, pred[]{:T(512)S(6)} %eq.5), kind=kLoop, calls=%fused_computation.55 | loop fusion | flops 7077888 | bytes 3145729 | tf_op jit(solution)/shard_map/transpose | solution.py:231
  116.6 2.6 %copy.10 = bf16[1536,512]{1,0:T(8,128)(2,1)} copy(bf16[1536,512]{0,1:T(8,128)(2,1)} %fusion.31) | data formatting | bytes 3145728 | tf_op jit(solution)/shard_map/transpose | solution.py:231
  123.1 3.1 %collective-permute-start.23 = (bf16[384,384]{1,0:T(8,128)(2,1)}, bf16[384,384]{1,0:T(8,128)(2,1)}, u32[]{:S(2)}, u32[]{:S(2)}) collective-permute-start(bf16[384,384]{1,0:T(8,128)(2,1)} %get-tuple-element.26), channel_id=1, source_target_pairs={{0,8},{1,9},{2,10},{3,11},{4,12},{5,13},{6,14},{7,15},{8,0},{9,1},... | collective-permute-start | bytes 884744 | tf_op jit(solution)/shard_map/ppermute | solution.py:199
  129.7 4.6 %collective-permute-start.17 = (bf16[4,192,256]{2,1,0:T(8,128)(2,1)}, bf16[4,192,256]{2,1,0:T(8,128)(2,1)S(1)}, u32[]{:S(2)}, u32[]{:S(2)}) collective-permute-start(bf16[4,192,256]{2,1,0:T(8,128)(2,1)} %collective-permute-done.16.far), channel_id=1, source_target_pairs={{0,1},{1,0},{2,3},{3,2},{4,5},{5,4},{6,7},{7,6},{8,9},{9,8},{10,11... | collective-permute-start | bytes 1179656 | tf_op jit(solution)/shard_map/ppermute | solution.py:199
  134.4 5.4 %shard_map.85 = (f32[256,1536]{1,0:T(8,128)S(1)}, f32[256,1536]{1,0:T(8,128)S(1)}) custom-call(bf16[3,192,384]{2,1,0:T(8,128)(2,1)} %maximum_select_fusion.3.refs_0_, bf16[3,192,384]{2,1,0:T(8,128)(2,1)} %collective-permute-done.1.refs_1_, bf16[3,192,384]{2,1,0:T(8,128)(2,1)} %collective-permute-done.2.refs_2_, ...), custom_call_target="tpu_custom_call" | custom-call | flops 1811939328 | bytes 7471104 | tf_op jit(solution)/shard_map/pallas_call | solution.py:173
  139.8 6.7 %collective-permute-start.12 = (bf16[256,384]{1,0:T(8,128)(2,1)S(1)}, bf16[256,384]{1,0:T(8,128)(2,1)S(1)}, u32[]{:S(2)}, u32[]{:S(2)}) collective-permute-start(bf16[256,384]{1,0:T(8,128)(2,1)S(1)} %get-tuple-element.39), channel_id=1, source_target_pairs={{0,1},{1,0},{2,3},{3,2},{4,5},{5,4},{6,7},{7,6},{8,9},{9,8},{10,11... | collective-permute-start | bytes 589832 | tf_op jit(solution)/shard_map/ppermute | solution.py:199
  146.5 3.2 %collective-permute-start.15 = (f32[256,1536]{1,0:T(8,128)S(1)}, f32[256,1536]{1,0:T(8,128)S(1)}, u32[]{:S(2)}, u32[]{:S(2)}) collective-permute-start(f32[256,1536]{1,0:T(8,128)S(1)} %get-tuple-element.19), channel_id=1, source_target_pairs={{0,1},{1,0},{2,3},{3,2},{4,5},{5,4},{6,7},{7,6},{8,9},{9,8},{10,11... | collective-permute-start | bytes 4718600 | tf_op jit(solution)/shard_map/ppermute | solution.py:199
  149.6 3.4 %collective-permute-done.24 = bf16[384,384]{1,0:T(8,128)(2,1)} collective-permute-done((bf16[384,384]{1,0:T(8,128)(2,1)}, bf16[384,384]{1,0:T(8,128)(2,1)}, u32[]{:S(2)}, u32[]{:S(2)}) %collective-permute-start.24) | collective-permute-done | bytes 294944 | tf_op jit(solution)/shard_map/ppermute | solution.py:199
  155.3 3.9 %shard_map.86 = (f32[3,192,384]{2,1,0:T(8,128)S(1)}, bf16[3,192,384]{2,1,0:T(8,128)(2,1)S(1)}, bf16[3,192,384]{2,1,0:T(8,128)(2,1)S(1)}, bf16[3,192,384]{2,1,0:T(8,128)(2,1)S(1)}) custom-call(bf16[4,2,192,1024]{3,2,1,0:T(8,128)(2,1)S(1)} %bitcast.16, bf16[4,192,256]{2,1,0:T(8,128)(2,1)} %collective-permute-done.16.far, ...), custom_call_target="tpu_custom_call" | custom-call | flops 1811939328 | bytes 6930432 | tf_op jit(solution)/shard_map/pallas_call | solution.py:173
  163.4 6.7 %collective-permute-done.19 = bf16[3,192,384]{2,1,0:T(8,128)(2,1)S(1)} collective-permute-done((bf16[3,192,384]{2,1,0:T(8,128)(2,1)S(1)}, bf16[3,192,384]{2,1,0:T(8,128)(2,1)S(1)}, u32[]{:S(2)}, u32[]{:S(2)}) %collective-permute-start.19) | collective-permute-done | bytes 442400 | tf_op jit(solution)/shard_map/ppermute | solution.py:199
  170.2 26.6 %collective-permute-done.20 = bf16[3,192,384]{2,1,0:T(8,128)(2,1)S(1)} collective-permute-done((bf16[3,192,384]{2,1,0:T(8,128)(2,1)S(1)}, bf16[3,192,384]{2,1,0:T(8,128)(2,1)S(1)}, u32[]{:S(2)}, u32[]{:S(2)}) %collective-permute-start.20) | collective-permute-done | bytes 442400 | tf_op jit(solution)/shard_map/ppermute | solution.py:199
  196.7 2.7 %collective-permute-done.21 = bf16[3,192,384]{2,1,0:T(8,128)(2,1)S(1)} collective-permute-done((bf16[3,192,384]{2,1,0:T(8,128)(2,1)S(1)}, bf16[3,192,384]{2,1,0:T(8,128)(2,1)S(1)}, u32[]{:S(2)}, u32[]{:S(2)}) %collective-permute-start.21) | collective-permute-done | bytes 442400 | tf_op jit(solution)/shard_map/ppermute | solution.py:199
  201.9 2.6 %fusion.15 = bf16[256,1536]{1,0:T(8,128)(2,1)} fusion(bf16[256,1536]{1,0:T(8,128)(2,1)S(1)} %copy-done.6, f32[256,1536]{1,0:T(8,128)S(1)} %get-tuple-element.29, bf16[256,1536]{1,0:T(8,128)(2,1)} %param.9, f32[256]{0:T(256)S(1)} %broadcast_multiply_fusion, f32[256]{0:T(256)S(1)} %add_rsqrt_fusion), kind=kLoop, calls=%fused_computation.22 | loop fusion | flops 3932160 | bytes 3934208 | tf_op jit(solution)/shard_map/convert_element_type | solution.py:330
  (77 shorter events, 47.6 us)
Async XLA Ops:
  4.0 21.9 %collective-permute-start.9 = (bf16[256,1536]{1,0:T(8,128)(2,1)S(1)}, bf16[256,1536]{1,0:T(8,128)(2,1)}, u32[]{:S(2)}, u32[]{:S(2)}) collective-permute-start(bf16[256,1536]{1,0:T(8,128)(2,1)S(1)} %fusion.6.refs_8_), channel_id=1, source_target_pairs={{1,2},{2,1},{3,4},{4,3},{5,6},{6,5},{7,8},{8,7},{9,10},{10,9},{11,... | collective-permute-start | bytes 2359304 | tf_op jit(solution)/shard_map/ppermute | solution.py:199
  7.7 22.4 %collective-permute-start.11 = (bf16[256,1536]{1,0:T(8,128)(2,1)}, bf16[256,1536]{1,0:T(8,128)(2,1)}, u32[]{:S(2)}, u32[]{:S(2)}) collective-permute-start(bf16[256,1536]{1,0:T(8,128)(2,1)} %param.9), channel_id=1, source_target_pairs={{0,1},{1,0},{2,3},{3,2},{4,5},{5,4},{6,7},{7,6},{8,9},{9,8},{10,11... | collective-permute-start | bytes 2359304 | tf_op jit(solution)/shard_map/ppermute | solution.py:199
  9.6 16.3 %collective-permute-start = (bf16[3,96,384]{2,1,0:T(8,128)(2,1)}, bf16[3,96,384]{2,1,0:T(8,128)(2,1)}, u32[]{:S(2)}, u32[]{:S(2)}) collective-permute-start(bf16[3,96,384]{2,1,0:T(8,128)(2,1)} %get-tuple-element.35), channel_id=1, source_target_pairs={{0,1},{1,0},{2,3},{3,2},{4,5},{5,4},{6,7},{7,6},{8,9},{9,8},{10,11... | collective-permute-start | bytes 663560 | tf_op jit(solution)/shard_map/ppermute | solution.py:199
  10.1 61.3 %collective-permute-start.8 = (bf16[256,1536]{1,0:T(8,128)(2,1)S(1)}, bf16[256,1536]{1,0:T(8,128)(2,1)}, u32[]{:S(2)}, u32[]{:S(2)}) collective-permute-start(bf16[256,1536]{1,0:T(8,128)(2,1)S(1)} %fusion.6.refs_8_), channel_id=1, source_target_pairs={{0,1},{1,0},{2,3},{3,2},{4,5},{5,4},{6,7},{7,6},{8,9},{9,8},{10,11... | collective-permute-start | bytes 2359304 | tf_op jit(solution)/shard_map/ppermute | solution.py:199
  25.9 47.3 %collective-permute-start.10 = (bf16[256,1536]{1,0:T(8,128)(2,1)}, bf16[256,1536]{1,0:T(8,128)(2,1)}, u32[]{:S(2)}, u32[]{:S(2)}) collective-permute-start(bf16[256,1536]{1,0:T(8,128)(2,1)} %collective-permute-done.9.refs_10_), channel_id=1, source_target_pairs={{0,1},{1,0},{2,3},{3,2},{4,5},{5,4},{6,7},{7,6},{8,9},{9,8},{10,11... | collective-permute-start | bytes 2359304 | tf_op jit(solution)/shard_map/ppermute | solution.py:199
  27.9 11.5 %collective-permute-start.1 = (bf16[3,192,384]{2,1,0:T(8,128)(2,1)}, bf16[3,192,384]{2,1,0:T(8,128)(2,1)}, u32[]{:S(2)}, u32[]{:S(2)}) collective-permute-start(bf16[3,192,384]{2,1,0:T(8,128)(2,1)} %maximum_select_fusion.3.refs_0_), channel_id=1, source_target_pairs={{0,4},{1,5},{2,6},{3,7},{4,8},{5,9},{6,10},{7,11},{8,12},{9,13},{1... | collective-permute-start | bytes 1327112 | tf_op jit(solution)/shard_map/ppermute | solution.py:199
  29.2 37.8 %collective-permute-start.2 = (bf16[3,192,384]{2,1,0:T(8,128)(2,1)}, bf16[3,192,384]{2,1,0:T(8,128)(2,1)}, u32[]{:S(2)}, u32[]{:S(2)}) collective-permute-start(bf16[3,192,384]{2,1,0:T(8,128)(2,1)} %maximum_select_fusion.3.refs_0_), channel_id=1, source_target_pairs={{0,8},{1,9},{2,10},{3,11},{4,12},{5,13},{6,14},{7,15},{8,0},{9,1},... | collective-permute-start | bytes 1327112 | tf_op jit(solution)/shard_map/ppermute | solution.py:199
  30.2 39.4 %collective-permute-start.3 = (bf16[3,192,384]{2,1,0:T(8,128)(2,1)}, bf16[3,192,384]{2,1,0:T(8,128)(2,1)}, u32[]{:S(2)}, u32[]{:S(2)}) collective-permute-start(bf16[3,192,384]{2,1,0:T(8,128)(2,1)} %maximum_select_fusion.3.refs_0_), channel_id=1, source_target_pairs={{0,12},{1,13},{2,14},{3,15},{4,0},{5,1},{6,2},{7,3},{8,4},{9,5},{1... | collective-permute-start | bytes 1327112 | tf_op jit(solution)/shard_map/ppermute | solution.py:199
  39.4 45.0 %collective-permute-start.4 = (bf16[3,192,384]{2,1,0:T(8,128)(2,1)}, bf16[3,192,384]{2,1,0:T(8,128)(2,1)}, u32[]{:S(2)}, u32[]{:S(2)}) collective-permute-start(bf16[3,192,384]{2,1,0:T(8,128)(2,1)} %maximum_select_fusion.3.refs_0_), channel_id=1, source_target_pairs={{0,2},{1,3},{2,0},{3,1},{4,6},{5,7},{6,4},{7,5},{8,10},{9,11},{10,... | collective-permute-start | bytes 1327112 | tf_op jit(solution)/shard_map/ppermute | solution.py:199
  66.9 17.5 %collective-permute-start.5 = (bf16[3,192,384]{2,1,0:T(8,128)(2,1)}, bf16[3,192,384]{2,1,0:T(8,128)(2,1)}, u32[]{:S(2)}, u32[]{:S(2)}) collective-permute-start(bf16[3,192,384]{2,1,0:T(8,128)(2,1)} %collective-permute-done.1.refs_1_), channel_id=1, source_target_pairs={{0,2},{1,3},{2,0},{3,1},{4,6},{5,7},{6,4},{7,5},{8,10},{9,11},{10,... | collective-permute-start | bytes 1327112 | tf_op jit(solution)/shard_map/ppermute | solution.py:199
  69.6 19.3 %collective-permute-start.6 = (bf16[3,192,384]{2,1,0:T(8,128)(2,1)}, bf16[3,192,384]{2,1,0:T(8,128)(2,1)}, u32[]{:S(2)}, u32[]{:S(2)}) collective-permute-start(bf16[3,192,384]{2,1,0:T(8,128)(2,1)} %collective-permute-done.2.refs_2_), channel_id=1, source_target_pairs={{0,2},{1,3},{2,0},{3,1},{4,6},{5,7},{6,4},{7,5},{8,10},{9,11},{10,... | collective-permute-start | bytes 1327112 | tf_op jit(solution)/shard_map/ppermute | solution.py:199
  71.4 27.0 %collective-permute-start.7 = (bf16[3,192,384]{2,1,0:T(8,128)(2,1)}, bf16[3,192,384]{2,1,0:T(8,128)(2,1)}, u32[]{:S(2)}, u32[]{:S(2)}) collective-permute-start(bf16[3,192,384]{2,1,0:T(8,128)(2,1)} %collective-permute-done.3.refs_3_), channel_id=1, source_target_pairs={{0,2},{1,3},{2,0},{3,1},{4,6},{5,7},{6,4},{7,5},{8,10},{9,11},{10,... | collective-permute-start | bytes 1327112 | tf_op jit(solution)/shard_map/ppermute | solution.py:199
  83.0 46.8 %collective-permute-start.16 = (bf16[4,192,256]{2,1,0:T(8,128)(2,1)}, bf16[4,192,256]{2,1,0:T(8,128)(2,1)}, u32[]{:S(2)}, u32[]{:S(2)}) collective-permute-start(bf16[4,192,256]{2,1,0:T(8,128)(2,1)} %dynamic-slice_bitcast_fusion), channel_id=1, source_target_pairs={{0,2},{1,3},{2,0},{3,1},{4,6},{5,7},{6,4},{7,5},{8,10},{9,11},{10,... | collective-permute-start | bytes 1179656 | tf_op jit(solution)/shard_map/ppermute | solution.py:199
  106.9 19.3 %collective-permute-start.13 = (bf16[256,384]{1,0:T(8,128)(2,1)}, bf16[256,384]{1,0:T(8,128)(2,1)S(1)}, u32[]{:S(2)}, u32[]{:S(2)}) collective-permute-start(bf16[256,384]{1,0:T(8,128)(2,1)} %get-tuple-element.37), channel_id=1, source_target_pairs={{0,2},{1,3},{2,4},{3,5},{4,6},{5,7},{6,8},{7,9},{8,10},{9,11},{10,... | collective-permute-start | bytes 589832 | tf_op jit(solution)/shard_map/ppermute | solution.py:199
  109.9 18.8 %collective-permute-start.14 = (bf16[256,384]{1,0:T(8,128)(2,1)}, bf16[256,384]{1,0:T(8,128)(2,1)}, u32[]{:S(2)}, u32[]{:S(2)}) collective-permute-start(bf16[256,384]{1,0:T(8,128)(2,1)} %get-tuple-element.36), channel_id=1, source_target_pairs={{2,0},{3,1},{4,2},{5,3},{6,4},{7,5},{8,6},{9,7},{10,8},{11,9},{12,... | collective-permute-start | bytes 589832 | tf_op jit(solution)/shard_map/ppermute | solution.py:199
  123.1 16.6 %collective-permute-start.22 = (bf16[384,384]{1,0:T(8,128)(2,1)}, bf16[384,384]{1,0:T(8,128)(2,1)}, u32[]{:S(2)}, u32[]{:S(2)}) collective-permute-start(bf16[384,384]{1,0:T(8,128)(2,1)} %get-tuple-element.25), channel_id=1, source_target_pairs={{0,4},{1,5},{2,6},{3,7},{4,8},{5,9},{6,10},{7,11},{8,12},{9,13},{1... | collective-permute-start | bytes 884744 | tf_op jit(solution)/shard_map/ppermute | solution.py:199
  123.1 23.3 %collective-permute-start.23 = (bf16[384,384]{1,0:T(8,128)(2,1)}, bf16[384,384]{1,0:T(8,128)(2,1)}, u32[]{:S(2)}, u32[]{:S(2)}) collective-permute-start(bf16[384,384]{1,0:T(8,128)(2,1)} %get-tuple-element.26), channel_id=1, source_target_pairs={{0,8},{1,9},{2,10},{3,11},{4,12},{5,13},{6,14},{7,15},{8,0},{9,1},... | collective-permute-start | bytes 884744 | tf_op jit(solution)/shard_map/ppermute | solution.py:199
  126.2 26.7 %collective-permute-start.24 = (bf16[384,384]{1,0:T(8,128)(2,1)}, bf16[384,384]{1,0:T(8,128)(2,1)}, u32[]{:S(2)}, u32[]{:S(2)}) collective-permute-start(bf16[384,384]{1,0:T(8,128)(2,1)} %get-tuple-element.27), channel_id=1, source_target_pairs={{0,12},{1,13},{2,14},{3,15},{4,0},{5,1},{6,2},{7,3},{8,4},{9,5},{1... | collective-permute-start | bytes 884744 | tf_op jit(solution)/shard_map/ppermute | solution.py:199
  128.8 26.5 %collective-permute-start.18 = (bf16[512,384]{1,0:T(8,128)(2,1)S(1)}, bf16[512,384]{1,0:T(8,128)(2,1)S(1)}, u32[]{:S(2)}, u32[]{:S(2)}) collective-permute-start(bf16[512,384]{1,0:T(8,128)(2,1)S(1)} %get-tuple-element.17.refs_9_.mine), channel_id=1, source_target_pairs={{0,2},{1,3},{2,0},{3,1},{4,6},{5,7},{6,4},{7,5},{8,10},{9,11},{10,... | collective-permute-start | bytes 1179656 | tf_op jit(solution)/shard_map/ppermute | solution.py:199
  129.7 25.6 %collective-permute-start.17 = (bf16[4,192,256]{2,1,0:T(8,128)(2,1)}, bf16[4,192,256]{2,1,0:T(8,128)(2,1)S(1)}, u32[]{:S(2)}, u32[]{:S(2)}) collective-permute-start(bf16[4,192,256]{2,1,0:T(8,128)(2,1)} %collective-permute-done.16.far), channel_id=1, source_target_pairs={{0,1},{1,0},{2,3},{3,2},{4,5},{5,4},{6,7},{7,6},{8,9},{9,8},{10,11... | collective-permute-start | bytes 1179656 | tf_op jit(solution)/shard_map/ppermute | solution.py:199
  139.8 20.6 %collective-permute-start.12 = (bf16[256,384]{1,0:T(8,128)(2,1)S(1)}, bf16[256,384]{1,0:T(8,128)(2,1)S(1)}, u32[]{:S(2)}, u32[]{:S(2)}) collective-permute-start(bf16[256,384]{1,0:T(8,128)(2,1)S(1)} %get-tuple-element.39), channel_id=1, source_target_pairs={{0,1},{1,0},{2,3},{3,2},{4,5},{5,4},{6,7},{7,6},{8,9},{9,8},{10,11... | collective-permute-start | bytes 589832 | tf_op jit(solution)/shard_map/ppermute | solution.py:199
  146.5 53.8 %collective-permute-start.15 = (f32[256,1536]{1,0:T(8,128)S(1)}, f32[256,1536]{1,0:T(8,128)S(1)}, u32[]{:S(2)}, u32[]{:S(2)}) collective-permute-start(f32[256,1536]{1,0:T(8,128)S(1)} %get-tuple-element.19), channel_id=1, source_target_pairs={{0,1},{1,0},{2,3},{3,2},{4,5},{5,4},{6,7},{7,6},{8,9},{9,8},{10,11... | collective-permute-start | bytes 4718600 | tf_op jit(solution)/shard_map/ppermute | solution.py:199
  159.3 37.5 %collective-permute-start.20 = (bf16[3,192,384]{2,1,0:T(8,128)(2,1)S(1)}, bf16[3,192,384]{2,1,0:T(8,128)(2,1)S(1)}, u32[]{:S(2)}, u32[]{:S(2)}) collective-permute-start(bf16[3,192,384]{2,1,0:T(8,128)(2,1)S(1)} %get-tuple-element.22), channel_id=1, source_target_pairs={{0,8},{1,9},{2,10},{3,11},{4,12},{5,13},{6,14},{7,15},{8,0},{9,1},... | collective-permute-start | bytes 1327112 | tf_op jit(solution)/shard_map/ppermute | solution.py:199
  160.3 39.0 %collective-permute-start.21 = (bf16[3,192,384]{2,1,0:T(8,128)(2,1)S(1)}, bf16[3,192,384]{2,1,0:T(8,128)(2,1)S(1)}, u32[]{:S(2)}, u32[]{:S(2)}) collective-permute-start(bf16[3,192,384]{2,1,0:T(8,128)(2,1)S(1)} %get-tuple-element.23), channel_id=1, source_target_pairs={{0,12},{1,13},{2,14},{3,15},{4,0},{5,1},{6,2},{7,3},{8,4},{9,5},{1... | collective-permute-start | bytes 1327112 | tf_op jit(solution)/shard_map/ppermute | solution.py:199
  (11 other events, 89.3 us)

commit v3 on v2

--- a/solution.py
+++ b/solution.py
@@ -22,6 +22,10 @@
     return 0.5 * (1.0 + inner) + 0.5 * v * (1.0 - inner * inner) * root_coef * (
         1.0 + 3.0 * 0.044715 * v * v
     )
+
+
+def after(value, *others):
+    return lax.optimization_barrier((value, *others))[0]
 
 
 def product(left, right):
@@ -60,20 +64,25 @@
         copy.wait()
 
 
-def tap_copies(pieces, whole):
+def tap_copies(places, pieces, whole):
     z, y, _ = position()
-    depth = len(pieces) // 2
-    block = pieces[0].shape[1]
+    parity = lax.rem(lax.axis_index("groups"), 2)
     pairs = []
-    for i, piece in enumerate(pieces):
-        source = lax.rem(z + depth - i % depth, depth)
-        side = y if i < depth else 1 - y
-        start = pl.multiple_of((source * 2 + side) * block, block)
-        pairs.append((piece, whole.at[:, pl.ds(start, block), :]))
+    for (shift, across, part), piece in zip(places, pieces):
+        size = piece.shape[1]
+        depth = lax.axis_size("seq") // 4
+        source = lax.rem(z + depth - shift, depth)
+        side = 1 - y if across else y
+        start = source * 2 + side
+        if part is not None:
+            start = start * 2 + (1 - parity if part else parity)
+        start = pl.multiple_of(start * size, size)
+        pairs.append((piece, whole.at[:, pl.ds(start, size), :]))
     return pairs
 
 
-def forward_kernel(count, *refs):
+def forward_kernel(places, *refs):
+    count = len(places)
     pieces = refs[:count]
     act, act_other, edge, edge_other, slope_in = refs[count : count + 5]
     branch, grad, wide, taps, sems = refs[count + 5 :]
@@ -90,7 +99,7 @@
             (edge, at(3 * core)),
             (edge_other, at(3 - 3 * core)),
         ]
-        + tap_copies(pieces, taps),
+        + tap_copies(places, pieces, taps),
         sems,
     )
     for part in range(2):
@@ -142,7 +151,8 @@
         outs[d][...] = product(turned[target], branch[...]).astype(outs[d].dtype)
 
 
-def backward_kernel(count, *refs):
+def backward_kernel(places, *refs):
+    count = len(places)
     pieces = refs[:count]
     low, grad, high = refs[count : count + 3]
     mine, other, wide, taps, sems = refs[count + 3 :]
@@ -154,7 +164,7 @@
             (grad, wide.at[pl.ds(rows, 2 * rows), :]),
             (high, wide.at[pl.ds(3 * rows, rows), :]),
         ]
-        + tap_copies(pieces, taps),
+        + tap_copies(places, pieces, taps),
         sems,
     )
     for out, part in ((other, 1 - core), (mine, core)):
@@ -207,24 +217,45 @@
     def to_z(value, by):
         return send(value, lambda i: (i + 4 * by) % size)
 
+    groups = lax.axis_size("groups")
+    halved = groups % 2 == 0 and own % 16 == 0
+
+    def to_x(value):
+        return lax.ppermute(value, "groups", [(g, g ^ 1) for g in range(groups)])
+
     def cut(value, start, length, axis):
         return lax.dynamic_slice_in_dim(value, start, length, axis)
 
     mine = cut(dilated_weight, core * half, half, 2)
     theirs = cut(dilated_weight, (1 - core) * half, half, 2)
-    chip_taps = in_order(core == 0, mine, to_core(theirs), 1)
-    pieces = [chip_taps] + [to_z(chip_taps, d) for d in range(1, depth)]
-    pieces = pieces + [to_y(c) for c in pieces]
-
+    swapped = to_core(theirs)
+    if halved:
+        parity = lax.axis_index("groups") % 2
+        start_piece = jnp.where(core == parity, mine, swapped)
+        rest_piece = jnp.where(core == parity, swapped, mine)
+    else:
+        start_piece = in_order(core == 0, mine, swapped, 1)
+    part = 0 if halved else None
+    along = [start_piece] + [to_z(start_piece, d) for d in range(1, depth)]
+    beside = [to_y(c) for c in along]
+    pieces = along + beside
+    places = [(d, False, part) for d in range(depth)]
+    places += [(d, True, part) for d in range(depth)]
+    if halved:
+        pieces = pieces + [rest_piece] + [to_x(c) for c in pieces[1:]]
+        places = places + [(d, across, 1) for d, across, _ in places]
+
+    inputs = after(inputs, theirs)
+    cotangent = after(cotangent, theirs)
     xfull = inputs.astype(f32)
     ratio = lax.rsqrt(jnp.mean(xfull * xfull, axis=-1, keepdims=True) + 1e-06)
     normed = xfull * ratio * norm_gain
     act = gelu_value(normed).astype(bf16)
     edge = send(act, lambda i: i + 1 if i % 2 else i - 1)
     act_other = to_core(act)
-    edge_other = to_core(edge)
-
-    cot_other = to_core(cotangent)
+    edge_other = to_core(after(edge, *beside[:2]))
+
+    cot_other = to_core(after(cotangent, start_piece))
     cot = in_order(core == 0, cotangent, cot_other, 0)
     point_rows = cut(point_weight, core * half, half, 0)
     branch_grad = transposed_product(cot, point_rows)
@@ -246,11 +277,12 @@
             (depth, 1, block, rows),
         ).reshape(depth, block, rows)
     )
+    branch_grad = after(branch_grad, cot_turned, act_turned)
     far_other = to_core(far)
 
     count = len(pieces)
     branch, pre_grad = call(
-        functools.partial(forward_kernel, count),
+        functools.partial(forward_kernel, places),
         [((span, half), bf16)] * 2,
         [*pieces, act, act_other, edge, edge_other, branch_grad],
         [pl.ANY] * (count + 4) + [pltpu.VMEM],
@@ -264,13 +296,17 @@
     )
 
     grad_far = to_y(pre_grad)
-    grad_low = send(pre_grad[rows:], lambda i: i + 2)
-    grad_high = send(pre_grad[:rows], lambda i: i - 2)
-
-    def gathered(terms):
+    grad_edge = after(pre_grad, grad_far)
+    grad_low = send(grad_edge[rows:], lambda i: i + 2)
+    grad_high = send(grad_edge[:rows], lambda i: i - 2)
+
+    def sent(terms):
+        return [terms[0]] + [to_z(terms[d], d) for d in range(1, depth)]
+
+    def added(terms):
         total = terms[0]
-        for d in range(1, depth):
-            total = total + to_z(terms[d], d).astype(f32)
+        for term in terms[1:]:
+            total = total + term.astype(f32)
         return total
 
     point_terms = call(
@@ -282,7 +318,7 @@
         2 * span * channels * half,
         16,
     )
-    point_sum = gathered(point_terms)
+    point_parts = sent(point_terms)
 
     tap_terms = call(
         functools.partial(terms_kernel, depth),
@@ -297,12 +333,10 @@
         6 * span * channels * half,
         24,
     )
-    tap_sum = gathered(tap_terms)
-
-    point_sum = cut(point_sum, y * block, block, 0) + to_y(
-        cut(point_sum, (1 - y) * block, block, 0).astype(bf16)
-    ).astype(f32)
-
+    tap_parts = sent(tap_terms)
+    tap_sum = added(tap_parts)
+
+    branch = after(branch, tap_terms[0])
     branch_other = to_core(cut(branch, (1 - core) * rows, rows, 0))
     branch_own = in_order(
         core == 0, cut(branch, core * rows, rows, 0), branch_other, 1
@@ -310,9 +344,9 @@
     outputs = (xfull + product(branch_own, point_weight)).astype(bf16)
 
     act_grad, act_grad_other = call(
-        functools.partial(backward_kernel, count),
+        functools.partial(backward_kernel, places),
         [((rows, channels), f32)] * 2,
-        [*pieces, grad_low, pre_grad, grad_high],
+        [*pieces, grad_low, after(pre_grad, tap_terms[0]), grad_high],
         [pl.ANY] * (count + 3),
         [
             pltpu.VMEM((4 * rows, half), bf16),
@@ -322,6 +356,11 @@
         6 * span * channels * half,
         24,
     )
+    point_sum = added([after(term, act_grad_other) for term in point_parts])
+    point_sum = cut(point_sum, y * block, block, 0) + to_y(
+        cut(point_sum, (1 - y) * block, block, 0).astype(bf16)
+    ).astype(f32)
+
     act_grad = act_grad + to_core(act_grad_other)
     scaled = act_grad * gelu_slope(normed) * norm_gain
     inner = jnp.mean(scaled * xfull, axis=-1, keepdims=True)

time: 207 us -> 197 us (0.952)
  the two profiles are of different devices: /device:TPU:9 before, /device:TPU:29 now
where the time goes in v3:
time: 197 us; the launch traced here: 196 us
  starting transfers between devices  70 us (36%)
  waiting for transfers between devices  61.2 us (31%)
  local copies, waits for them, and re-layouts  21.4 us (11%)
  other arithmetic  19.7 us (10%)
  Pallas kernels  17.6 us (9%)
  matrix products  5.64 us (3%)
    ppermute x27, starting transfers between devices, send(): return lax.ppermute(value, 'seq', [p for p in pairs if 0 <= p[1] < size])  64.4 us
    ppermute x27, waiting for transfers between devices, send(): return lax.ppermute(value, 'seq', [p for p in pairs if 0 <= p[1] < size])  54.7 us
    pallas_call x4, Pallas kernels, call(): pl.pallas_call(kernel, out_shape=[jax.ShapeDtypeStruct(s, t) for s, t in...  17.6 us
    unnamed x38, local copies, waits for them, and re-layouts  9.08 us
    ppermute x7, waiting for transfers between devices, to_x(): return lax.ppermute(value, 'groups', [(g, g ^ 1) for g in range(groups)])  6.49 us
    ppermute x7, starting transfers between devices, to_x(): return lax.ppermute(value, 'groups', [(g, g ^ 1) for g in range(groups)])  5.61 us
    transpose x1, local copies, waits for them, and re-layouts, local(): act_turned = act_wide.T.reshape(depth, 2, block, 4 * rows)  4.67 us
    dot_general x1, matrix products, transposed_product(): lax.dot_general(left, weight, (((1,), (1,)), ((), ())), preferred_element...  3.96 us
  transfers between devices with their start and end apart: 34, of which 9 were waited for; matrix products, arithmetic and copies ran while one was open for 17% of the time, Pallas kernels for 9%

profile of v3, /device:TPU:29, one launch (start us, length us, event | category | flops | bytes accessed | tf_op | source)
XLA Modules:
  0.0 196.4 jit_solution(6430423558771873053)
XLA Ops:
  7.9 1.8 broadcast_select_fusion.2
  11.0 11.8 %collective-permute-done.1.refs_1_ = bf16[3,96,384]{2,1,0:T(8,128)(2,1)} collective-permute-done((bf16[3,96,384]{2,1,0:T(8,128)(2,1)}, bf16[3,96,384]{2,1,0:T(8,128)(2,1)}, u32[]{:S(2)}, u32[]{:S(2)}) %collective-permute-start.1) | collective-permute-done | bytes 221216 | tf_op jit(solution)/shard_map/ppermute | solution.py:209
  22.8 11.0 %collective-permute-start.3 = (bf16[3,96,384]{2,1,0:T(8,128)(2,1)}, bf16[3,96,384]{2,1,0:T(8,128)(2,1)}, u32[]{:S(2)}, u32[]{:S(2)}) collective-permute-start(bf16[3,96,384]{2,1,0:T(8,128)(2,1)} %get-tuple-element.59.refs_0_), channel_id=1, source_target_pairs={{0,12},{1,13},{2,14},{3,15},{4,0},{5,1},{6,2},{7,3},{8,4},{9,5},{1... | collective-permute-start | bytes 663560 | tf_op jit(solution)/shard_map/ppermute | solution.py:209
  36.1 3.2 %collective-permute-done.3.refs_3_ = bf16[3,96,384]{2,1,0:T(8,128)(2,1)} collective-permute-done((bf16[3,96,384]{2,1,0:T(8,128)(2,1)}, bf16[3,96,384]{2,1,0:T(8,128)(2,1)}, u32[]{:S(2)}, u32[]{:S(2)}) %collective-permute-start.3) | collective-permute-done | bytes 221216 | tf_op jit(solution)/shard_map/ppermute | solution.py:209
  40.6 3.0 %maximum_select_fusion.1 = bf16[512,1536]{1,0:T(8,128)(2,1)} fusion(bf16[256,1536]{1,0:T(8,128)(2,1)} %collective-permute-done.15.refs_17_, bf16[256,1536]{1,0:T(8,128)(2,1)S(1)} %fusion.6.refs_16_, pred[]{:T(512)S(6)} %eq.8), kind=kLoop, calls=%fused_computation.29 | loop fusion | flops 7077888 | bytes 3145729 | tf_op jit(solution)/shard_map/jit(_where)/select_n | solution.py:42
  43.9 2.9 %fusion.31 = bf16[1536,512]{0,1:T(8,128)(2,1)} fusion(bf16[256,1536]{1,0:T(8,128)(2,1)S(1)} %copy-done.15, bf16[256,1536]{1,0:T(8,128)(2,1)} %collective-permute-done.18, pred[]{:T(512)S(6)} %eq.8), kind=kLoop, calls=%fused_computation.54 | loop fusion | flops 7077888 | bytes 3145729 | tf_op jit(solution)/shard_map/transpose | solution.py:262
  46.8 2.7 %copy.12 = bf16[1536,512]{1,0:T(8,128)(2,1)} copy(bf16[1536,512]{0,1:T(8,128)(2,1)} %fusion.31) | data formatting | bytes 3145728 | tf_op jit(solution)/shard_map/transpose | solution.py:262
  49.5 4.0 %fusion.21.refs_20_ = f32[512,384]{1,0:T(8,128)} fusion(bf16[768,1536]{1,0:T(8,128)(2,1)S(1)} %copy-done, s32[]{:T(128)S(6)} %select_n.107, bf16[256,1536]{1,0:T(8,128)(2,1)} %collective-permute-done.18, bf16[256,1536]{1,0:T(8,128)(2,1)} %param.9, pred[]{:T(512)S(6)} %eq.8), kind=kOutput, calls=%fused_computation.35 | convolution fusion | flops 611057664 | bytes 3538949 | tf_op jit(solution)/shard_map/dot_general | solution.py:36
  57.6 2.2 %collective-permute-done.6.refs_6_ = bf16[3,96,384]{2,1,0:T(8,128)(2,1)} collective-permute-done((bf16[3,96,384]{2,1,0:T(8,128)(2,1)}, bf16[3,96,384]{2,1,0:T(8,128)(2,1)}, u32[]{:S(2)}, u32[]{:S(2)}) %collective-permute-start.6) | collective-permute-done | bytes 221216 | tf_op jit(solution)/shard_map/ppermute | solution.py:209
  62.7 1.8 maximum_bitcast_fusion
  64.5 4.7 %copy.13 = bf16[1536,1024]{1,0:T(8,128)(2,1)} copy(bf16[1536,1024]{0,1:T(8,128)(2,1)} %maximum_bitcast_fusion) | data formatting | bytes 6291456 | tf_op jit(solution)/shard_map/transpose | solution.py:272
  71.7 1.7 collective-permute-done.13.refs_14_
  73.5 4.7 %collective-permute-done.14.refs_15_ = bf16[3,96,384]{2,1,0:T(8,128)(2,1)} collective-permute-done((bf16[3,96,384]{2,1,0:T(8,128)(2,1)}, bf16[3,96,384]{2,1,0:T(8,128)(2,1)}, u32[]{:S(2)}, u32[]{:S(2)}) %collective-permute-start.14) | collective-permute-done | bytes 221216 | tf_op jit(solution)/shard_map/ppermute | solution.py:224
  79.4 6.6 %shard_map.84 = (bf16[512,384]{1,0:T(8,128)(2,1)S(1)}, bf16[512,384]{1,0:T(8,128)(2,1)}) custom-call(bf16[3,96,384]{2,1,0:T(8,128)(2,1)} %get-tuple-element.59.refs_0_, bf16[3,96,384]{2,1,0:T(8,128)(2,1)} %collective-permute-done.1.refs_1_, bf16[3,96,384]{2,1,0:T(8,128)(2,1)} %collective-permute-done.2.refs_2_, ...), custom_call_target="tpu_custom_call" | custom-call | flops 1811939328 | bytes 8257536 | tf_op jit(solution)/shard_map/pallas_call | solution.py:183
  87.4 6.1 %collective-permute-start.20 = (bf16[4,192,256]{2,1,0:T(8,128)(2,1)}, bf16[4,192,256]{2,1,0:T(8,128)(2,1)S(1)}, u32[]{:S(2)}, u32[]{:S(2)}) collective-permute-start(bf16[4,192,256]{2,1,0:T(8,128)(2,1)} %collective-permute-done.19.far), channel_id=1, source_target_pairs={{0,1},{1,0},{2,3},{3,2},{4,5},{5,4},{6,7},{7,6},{8,9},{9,8},{10,11... | collective-permute-start | bytes 1179656 | tf_op jit(solution)/shard_map/ppermute | solution.py:209
  95.9 4.0 %collective-permute-start.24 = (bf16[256,384]{1,0:T(8,128)(2,1)S(1)}, bf16[256,384]{1,0:T(8,128)(2,1)S(1)}, u32[]{:S(2)}, u32[]{:S(2)}) collective-permute-start(bf16[256,384]{1,0:T(8,128)(2,1)S(1)} %get-tuple-element.60), channel_id=1, source_target_pairs={{2,0},{3,1},{4,2},{5,3},{6,4},{7,5},{8,6},{9,7},{10,8},{11,9},{12,... | collective-permute-start | bytes 589832 | tf_op jit(solution)/shard_map/ppermute | solution.py:209
  103.3 4.6 %collective-permute-start.29 = (bf16[384,384]{1,0:T(8,128)(2,1)S(1)}, bf16[384,384]{1,0:T(8,128)(2,1)S(1)}, u32[]{:S(2)}, u32[]{:S(2)}) collective-permute-start(bf16[384,384]{1,0:T(8,128)(2,1)S(1)} %get-tuple-element.46), channel_id=1, source_target_pairs={{0,4},{1,5},{2,6},{3,7},{4,8},{5,9},{6,10},{7,11},{8,12},{9,13},{1... | collective-permute-start | bytes 884744 | tf_op jit(solution)/shard_map/ppermute | solution.py:209
  109.5 1.9 copy-done.1
  111.4 4.8 %shard_map.85 = (f32[3,192,384]{2,1,0:T(8,128)S(1)}, bf16[3,192,384]{2,1,0:T(8,128)(2,1)}, bf16[3,192,384]{2,1,0:T(8,128)(2,1)}, bf16[3,192,384]{2,1,0:T(8,128)(2,1)}) custom-call(bf16[4,2,192,1024]{3,2,1,0:T(8,128)(2,1)S(1)} %bitcast.16, bf16[4,192,256]{2,1,0:T(8,128)(2,1)} %collective-permute-done.19.far, ...), custom_call_target="tpu_custom_call" | custom-call | flops 1811939328 | bytes 6930432 | tf_op jit(solution)/shard_map/pallas_call | solution.py:183
  117.1 5.3 %shard_map.86 = (f32[256,1536]{1,0:T(8,128)S(1)}, f32[256,1536]{1,0:T(8,128)S(1)}) custom-call(bf16[3,96,384]{2,1,0:T(8,128)(2,1)} %get-tuple-element.59.refs_0_, bf16[3,96,384]{2,1,0:T(8,128)(2,1)} %collective-permute-done.1.refs_1_, bf16[3,96,384]{2,1,0:T(8,128)(2,1)} %collective-permute-done.2.refs_2_, ...), custom_call_target="tpu_custom_call" | custom-call | flops 1811939328 | bytes 7471104 | tf_op jit(solution)/shard_map/pallas_call | solution.py:183
  123.5 8.9 %collective-permute-done.30 = bf16[384,384]{1,0:T(8,128)(2,1)S(1)} collective-permute-done((bf16[384,384]{1,0:T(8,128)(2,1)S(1)}, bf16[384,384]{1,0:T(8,128)(2,1)S(1)}, u32[]{:S(2)}, u32[]{:S(2)}) %collective-permute-start.30) | collective-permute-done | bytes 294944 | tf_op jit(solution)/shard_map/ppermute | solution.py:209
  132.5 13.8 %collective-permute-start.27 = (bf16[3,192,384]{2,1,0:T(8,128)(2,1)}, bf16[3,192,384]{2,1,0:T(8,128)(2,1)}, u32[]{:S(2)}, u32[]{:S(2)}) collective-permute-start(bf16[3,192,384]{2,1,0:T(8,128)(2,1)} %get-tuple-element.42), channel_id=1, source_target_pairs={{0,8},{1,9},{2,10},{3,11},{4,12},{5,13},{6,14},{7,15},{8,0},{9,1},... | collective-permute-start | bytes 1327112 | tf_op jit(solution)/shard_map/ppermute | solution.py:209
  148.7 8.0 %collective-permute-start.25 = (f32[256,1536]{1,0:T(8,128)}, f32[256,1536]{1,0:T(8,128)S(1)}, u32[]{:S(2)}, u32[]{:S(2)}) collective-permute-start(f32[256,1536]{1,0:T(8,128)} %copy-done.11), channel_id=1, source_target_pairs={{0,1},{1,0},{2,3},{3,2},{4,5},{5,4},{6,7},{7,6},{8,9},{9,8},{10,11... | collective-permute-start | bytes 4718600 | tf_op jit(solution)/shard_map/ppermute | solution.py:209
  157.7 27.4 %collective-permute-done.27 = bf16[3,192,384]{2,1,0:T(8,128)(2,1)} collective-permute-done((bf16[3,192,384]{2,1,0:T(8,128)(2,1)}, bf16[3,192,384]{2,1,0:T(8,128)(2,1)}, u32[]{:S(2)}, u32[]{:S(2)}) %collective-permute-start.27) | collective-permute-done | bytes 442400 | tf_op jit(solution)/shard_map/ppermute | solution.py:209
  (113 shorter events, 48.7 us)
Async XLA Ops:
  5.3 28.5 %collective-permute-start.16 = (bf16[256,1536]{1,0:T(8,128)(2,1)S(1)}, bf16[256,1536]{1,0:T(8,128)(2,1)}, u32[]{:S(2)}, u32[]{:S(2)}) collective-permute-start(bf16[256,1536]{1,0:T(8,128)(2,1)S(1)} %fusion.6.refs_16_), channel_id=1, source_target_pairs={{1,2},{2,1},{3,4},{4,3},{5,6},{6,5},{7,8},{8,7},{9,10},{10,9},{11,... | collective-permute-start | bytes 2359304 | tf_op jit(solution)/shard_map/ppermute | solution.py:209
  6.9 32.5 %collective-permute-start.15 = (bf16[256,1536]{1,0:T(8,128)(2,1)S(1)}, bf16[256,1536]{1,0:T(8,128)(2,1)}, u32[]{:S(2)}, u32[]{:S(2)}) collective-permute-start(bf16[256,1536]{1,0:T(8,128)(2,1)S(1)} %fusion.6.refs_16_), channel_id=1, source_target_pairs={{0,1},{1,0},{2,3},{3,2},{4,5},{5,4},{6,7},{7,6},{8,9},{9,8},{10,11... | collective-permute-start | bytes 2359304 | tf_op jit(solution)/shard_map/ppermute | solution.py:209
  9.8 33.9 %collective-permute-start.18 = (bf16[256,1536]{1,0:T(8,128)(2,1)}, bf16[256,1536]{1,0:T(8,128)(2,1)}, u32[]{:S(2)}, u32[]{:S(2)}) collective-permute-start(bf16[256,1536]{1,0:T(8,128)(2,1)} %param.9), channel_id=1, source_target_pairs={{0,1},{1,0},{2,3},{3,2},{4,5},{5,4},{6,7},{7,6},{8,9},{9,8},{10,11... | collective-permute-start | bytes 2359304 | tf_op jit(solution)/shard_map/ppermute | solution.py:209
  9.8 13.0 %collective-permute-start.1 = (bf16[3,96,384]{2,1,0:T(8,128)(2,1)}, bf16[3,96,384]{2,1,0:T(8,128)(2,1)}, u32[]{:S(2)}, u32[]{:S(2)}) collective-permute-start(bf16[3,96,384]{2,1,0:T(8,128)(2,1)} %get-tuple-element.59.refs_0_), channel_id=1, source_target_pairs={{0,4},{1,5},{2,6},{3,7},{4,8},{5,9},{6,10},{7,11},{8,12},{9,13},{1... | collective-permute-start | bytes 663560 | tf_op jit(solution)/shard_map/ppermute | solution.py:209
  22.8 16.5 %collective-permute-start.3 = (bf16[3,96,384]{2,1,0:T(8,128)(2,1)}, bf16[3,96,384]{2,1,0:T(8,128)(2,1)}, u32[]{:S(2)}, u32[]{:S(2)}) collective-permute-start(bf16[3,96,384]{2,1,0:T(8,128)(2,1)} %get-tuple-element.59.refs_0_), channel_id=1, source_target_pairs={{0,12},{1,13},{2,14},{3,15},{4,0},{5,1},{6,2},{7,3},{8,4},{9,5},{1... | collective-permute-start | bytes 663560 | tf_op jit(solution)/shard_map/ppermute | solution.py:209
  33.8 20.9 %collective-permute-start.17 = (bf16[256,1536]{1,0:T(8,128)(2,1)}, bf16[256,1536]{1,0:T(8,128)(2,1)}, u32[]{:S(2)}, u32[]{:S(2)}) collective-permute-start(bf16[256,1536]{1,0:T(8,128)(2,1)} %collective-permute-done.16.refs_18_), channel_id=1, source_target_pairs={{0,1},{1,0},{2,3},{3,2},{4,5},{5,4},{6,7},{7,6},{8,9},{9,8},{10,11... | collective-permute-start | bytes 2359304 | tf_op jit(solution)/shard_map/ppermute | solution.py:209
  35.4 18.1 %collective-permute-start.2 = (bf16[3,96,384]{2,1,0:T(8,128)(2,1)}, bf16[3,96,384]{2,1,0:T(8,128)(2,1)}, u32[]{:S(2)}, u32[]{:S(2)}) collective-permute-start(bf16[3,96,384]{2,1,0:T(8,128)(2,1)} %get-tuple-element.59.refs_0_), channel_id=1, source_target_pairs={{0,8},{1,9},{2,10},{3,11},{4,12},{5,13},{6,14},{7,15},{8,0},{9,1},... | collective-permute-start | bytes 663560 | tf_op jit(solution)/shard_map/ppermute | solution.py:209
  39.3 20.7 %collective-permute-start.7 = (bf16[3,96,384]{2,1,0:T(8,128)(2,1)}, bf16[3,96,384]{2,1,0:T(8,128)(2,1)}, u32[]{:S(2)}, u32[]{:S(2)}) collective-permute-start(bf16[3,96,384]{2,1,0:T(8,128)(2,1)} %collective-permute-done.3.refs_3_), channel_id=1, source_target_pairs={{0,2},{1,3},{2,0},{3,1},{4,6},{5,7},{6,4},{7,5},{8,10},{9,11},{10,... | collective-permute-start | bytes 663560 | tf_op jit(solution)/shard_map/ppermute | solution.py:209
  39.4 21.9 %collective-permute-start.10 = (bf16[3,96,384]{2,1,0:T(8,128)(2,1)}, bf16[3,96,384]{2,1,0:T(8,128)(2,1)}, u32[]{:S(2)}, u32[]{:S(2)}) collective-permute-start(bf16[3,96,384]{2,1,0:T(8,128)(2,1)} %collective-permute-done.3.refs_3_), channel_id=1, source_target_pairs={{0,16},{16,0},{1,17},{17,1},{2,18},{18,2},{3,19},{19,3},{4,20},{20... | collective-permute-start | bytes 663560 | tf_op jit(solution)/shard_map/ppermute | solution.py:224
  43.6 17.9 %collective-permute-start.11 = (bf16[3,96,384]{2,1,0:T(8,128)(2,1)}, bf16[3,96,384]{2,1,0:T(8,128)(2,1)}, u32[]{:S(2)}, u32[]{:S(2)}) collective-permute-start(bf16[3,96,384]{2,1,0:T(8,128)(2,1)} %collective-permute-done.4.refs_4_), channel_id=1, source_target_pairs={{0,16},{16,0},{1,17},{17,1},{2,18},{18,2},{3,19},{19,3},{4,20},{20... | collective-permute-start | bytes 663560 | tf_op jit(solution)/shard_map/ppermute | solution.py:224
  53.5 16.7 %collective-permute-start.8 = (bf16[3,96,384]{2,1,0:T(8,128)(2,1)}, bf16[3,96,384]{2,1,0:T(8,128)(2,1)}, u32[]{:S(2)}, u32[]{:S(2)}) collective-permute-start(bf16[3,96,384]{2,1,0:T(8,128)(2,1)} %collective-permute-done.1.refs_1_), channel_id=1, source_target_pairs={{0,16},{16,0},{1,17},{17,1},{2,18},{18,2},{3,19},{19,3},{4,20},{20... | collective-permute-start | bytes 663560 | tf_op jit(solution)/shard_map/ppermute | solution.py:224
  61.3 12.2 %collective-permute-start.13 = (bf16[3,96,384]{2,1,0:T(8,128)(2,1)}, bf16[3,96,384]{2,1,0:T(8,128)(2,1)}, u32[]{:S(2)}, u32[]{:S(2)}) collective-permute-start(bf16[3,96,384]{2,1,0:T(8,128)(2,1)} %collective-permute-done.6.refs_6_), channel_id=1, source_target_pairs={{0,16},{16,0},{1,17},{17,1},{2,18},{18,2},{3,19},{19,3},{4,20},{20... | collective-permute-start | bytes 663560 | tf_op jit(solution)/shard_map/ppermute | solution.py:224
  61.5 16.7 %collective-permute-start.14 = (bf16[3,96,384]{2,1,0:T(8,128)(2,1)}, bf16[3,96,384]{2,1,0:T(8,128)(2,1)}, u32[]{:S(2)}, u32[]{:S(2)}) collective-permute-start(bf16[3,96,384]{2,1,0:T(8,128)(2,1)} %collective-permute-done.7.refs_7_), channel_id=1, source_target_pairs={{0,16},{16,0},{1,17},{17,1},{2,18},{18,2},{3,19},{19,3},{4,20},{20... | collective-permute-start | bytes 663560 | tf_op jit(solution)/shard_map/ppermute | solution.py:224
  70.2 17.2 %collective-permute-start.19 = (bf16[4,192,256]{2,1,0:T(8,128)(2,1)S(1)}, bf16[4,192,256]{2,1,0:T(8,128)(2,1)}, u32[]{:S(2)}, u32[]{:S(2)}) collective-permute-start(bf16[4,192,256]{2,1,0:T(8,128)(2,1)S(1)} %dynamic-slice_bitcast_fusion), channel_id=1, source_target_pairs={{0,2},{1,3},{2,0},{3,1},{4,6},{5,7},{6,4},{7,5},{8,10},{9,11},{10,... | collective-permute-start | bytes 1179656 | tf_op jit(solution)/shard_map/ppermute | solution.py:209
  87.4 21.2 %collective-permute-start.20 = (bf16[4,192,256]{2,1,0:T(8,128)(2,1)}, bf16[4,192,256]{2,1,0:T(8,128)(2,1)S(1)}, u32[]{:S(2)}, u32[]{:S(2)}) collective-permute-start(bf16[4,192,256]{2,1,0:T(8,128)(2,1)} %collective-permute-done.19.far), channel_id=1, source_target_pairs={{0,1},{1,0},{2,3},{3,2},{4,5},{5,4},{6,7},{7,6},{8,9},{9,8},{10,11... | collective-permute-start | bytes 1179656 | tf_op jit(solution)/shard_map/ppermute | solution.py:209
  94.6 22.5 %collective-permute-start.23 = (bf16[256,384]{1,0:T(8,128)(2,1)S(1)}, bf16[256,384]{1,0:T(8,128)(2,1)S(1)}, u32[]{:S(2)}, u32[]{:S(2)}) collective-permute-start(bf16[256,384]{1,0:T(8,128)(2,1)S(1)} %get-tuple-element.61), channel_id=1, source_target_pairs={{0,2},{1,3},{2,4},{3,5},{4,6},{5,7},{6,8},{7,9},{8,10},{9,11},{10,... | collective-permute-start | bytes 589832 | tf_op jit(solution)/shard_map/ppermute | solution.py:209
  95.9 21.2 %collective-permute-start.24 = (bf16[256,384]{1,0:T(8,128)(2,1)S(1)}, bf16[256,384]{1,0:T(8,128)(2,1)S(1)}, u32[]{:S(2)}, u32[]{:S(2)}) collective-permute-start(bf16[256,384]{1,0:T(8,128)(2,1)S(1)} %get-tuple-element.60), channel_id=1, source_target_pairs={{2,0},{3,1},{4,2},{5,3},{6,4},{7,5},{8,6},{9,7},{10,8},{11,9},{12,... | collective-permute-start | bytes 589832 | tf_op jit(solution)/shard_map/ppermute | solution.py:209
  103.3 20.2 %collective-permute-start.29 = (bf16[384,384]{1,0:T(8,128)(2,1)S(1)}, bf16[384,384]{1,0:T(8,128)(2,1)S(1)}, u32[]{:S(2)}, u32[]{:S(2)}) collective-permute-start(bf16[384,384]{1,0:T(8,128)(2,1)S(1)} %get-tuple-element.46), channel_id=1, source_target_pairs={{0,4},{1,5},{2,6},{3,7},{4,8},{5,9},{6,10},{7,11},{8,12},{9,13},{1... | collective-permute-start | bytes 884744 | tf_op jit(solution)/shard_map/ppermute | solution.py:209
  107.9 24.6 %collective-permute-start.30 = (bf16[384,384]{1,0:T(8,128)(2,1)S(1)}, bf16[384,384]{1,0:T(8,128)(2,1)S(1)}, u32[]{:S(2)}, u32[]{:S(2)}) collective-permute-start(bf16[384,384]{1,0:T(8,128)(2,1)S(1)} %get-tuple-element.48), channel_id=1, source_target_pairs={{0,8},{1,9},{2,10},{3,11},{4,12},{5,13},{6,14},{7,15},{8,0},{9,1},... | collective-permute-start | bytes 884744 | tf_op jit(solution)/shard_map/ppermute | solution.py:209
  108.6 23.9 %collective-permute-start.31 = (bf16[384,384]{1,0:T(8,128)(2,1)S(1)}, bf16[384,384]{1,0:T(8,128)(2,1)S(1)}, u32[]{:S(2)}, u32[]{:S(2)}) collective-permute-start(bf16[384,384]{1,0:T(8,128)(2,1)S(1)} %get-tuple-element.50), channel_id=1, source_target_pairs={{0,12},{1,13},{2,14},{3,15},{4,0},{5,1},{6,2},{7,3},{8,4},{9,5},{1... | collective-permute-start | bytes 884744 | tf_op jit(solution)/shard_map/ppermute | solution.py:209
  132.5 25.3 %collective-permute-start.26 = (bf16[3,192,384]{2,1,0:T(8,128)(2,1)}, bf16[3,192,384]{2,1,0:T(8,128)(2,1)}, u32[]{:S(2)}, u32[]{:S(2)}) collective-permute-start(bf16[3,192,384]{2,1,0:T(8,128)(2,1)} %get-tuple-element.41), channel_id=1, source_target_pairs={{0,4},{1,5},{2,6},{3,7},{4,8},{5,9},{6,10},{7,11},{8,12},{9,13},{1... | collective-permute-start | bytes 1327112 | tf_op jit(solution)/shard_map/ppermute | solution.py:209
  132.5 52.6 %collective-permute-start.27 = (bf16[3,192,384]{2,1,0:T(8,128)(2,1)}, bf16[3,192,384]{2,1,0:T(8,128)(2,1)}, u32[]{:S(2)}, u32[]{:S(2)}) collective-permute-start(bf16[3,192,384]{2,1,0:T(8,128)(2,1)} %get-tuple-element.42), channel_id=1, source_target_pairs={{0,8},{1,9},{2,10},{3,11},{4,12},{5,13},{6,14},{7,15},{8,0},{9,1},... | collective-permute-start | bytes 1327112 | tf_op jit(solution)/shard_map/ppermute | solution.py:209
  146.2 38.9 %collective-permute-start.28 = (bf16[3,192,384]{2,1,0:T(8,128)(2,1)}, bf16[3,192,384]{2,1,0:T(8,128)(2,1)}, u32[]{:S(2)}, u32[]{:S(2)}) collective-permute-start(bf16[3,192,384]{2,1,0:T(8,128)(2,1)} %get-tuple-element.43), channel_id=1, source_target_pairs={{0,12},{1,13},{2,14},{3,15},{4,0},{5,1},{6,2},{7,3},{8,4},{9,5},{1... | collective-permute-start | bytes 1327112 | tf_op jit(solution)/shard_map/ppermute | solution.py:209
  148.7 44.6 %collective-permute-start.25 = (f32[256,1536]{1,0:T(8,128)}, f32[256,1536]{1,0:T(8,128)S(1)}, u32[]{:S(2)}, u32[]{:S(2)}) collective-permute-start(f32[256,1536]{1,0:T(8,128)} %copy-done.11), channel_id=1, source_target_pairs={{0,1},{1,0},{2,3},{3,2},{4,5},{5,4},{6,7},{7,6},{8,9},{9,8},{10,11... | collective-permute-start | bytes 4718600 | tf_op jit(solution)/shard_map/ppermute | solution.py:209
  (29 other events, 254.0 us)

commit v4 on v3

--- a/solution.py
+++ b/solution.py
@@ -84,49 +84,68 @@
 def forward_kernel(places, *refs):
     count = len(places)
     pieces = refs[:count]
-    act, act_other, edge, edge_other, slope_in = refs[count : count + 5]
-    branch, grad, wide, taps, sems = refs[count + 5 :]
+    act, act_other, edge, edge_other, slope, slope_other = refs[count : count + 6]
+    branch, grad, wide, taps, sems = refs[count + 6 :]
     _, _, core = position()
     rows = act.shape[0]
 
-    def at(start):
-        return wide.at[pl.ds(pl.multiple_of(start * rows, rows), rows), :]
+    def here(start):
+        return pl.ds(pl.multiple_of(start * rows, rows), rows)
 
     fetch(
         [
-            (act, at(1 + core)),
-            (act_other, at(2 - core)),
-            (edge, at(3 * core)),
-            (edge_other, at(3 - 3 * core)),
+            (act, wide.at[here(1 + core)]),
+            (act_other, wide.at[here(2 - core)]),
+            (edge, wide.at[here(3 * core)]),
+            (edge_other, wide.at[here(3 - 3 * core)]),
         ]
         + tap_copies(places, pieces, taps),
         sems,
     )
-    for part in range(2):
-        pre = product(wide[pl.ds(part * rows, rows), :], taps[0])
-        pre = pre + product(wide[pl.ds((part + 1) * rows, rows), :], taps[1])
-        pre = pre + product(wide[pl.ds((part + 2) * rows, rows), :], taps[2])
-        here = pl.ds(part * rows, rows)
-        branch[here, :] = gelu_value(pre).astype(bf16)
-        grad[here, :] = (slope_in[here, :] * gelu_slope(pre)).astype(bf16)
-
-
-def terms_kernel(depth, near, far, far_other, mine, other, *refs):
-    outs = refs[:depth]
-    wide, grads, sems = refs[depth:]
+    for part, slope_in in ((core, slope), (1 - core, slope_other)):
+        pre = product(wide[here(part)], taps[0])
+        pre = pre + product(wide[here(part + 1)], taps[1])
+        pre = pre + product(wide[here(part + 2)], taps[2])
+        branch[here(part)] = gelu_value(pre).astype(bf16)
+        grad[here(part)] = (slope_in[...] * gelu_slope(pre)).astype(bf16)
+
+
+def targets(depth, z):
+    if depth == 4:
+        return [
+            jnp.where(z == 0, 3, 0),
+            jnp.where(z < 2, z + 2, z - 2),
+            jnp.minimum(z + 1, 3),
+            jnp.maximum(z - 1, 0),
+            z,
+        ]
+    return [lax.rem(z + d, depth) for d in range(1, depth)] + [z]
+
+
+def target_types(depth):
+    if depth == 4:
+        return [bf16, f32, bf16, bf16, f32]
+    return [bf16] * (depth - 1) + [f32]
+
+
+def terms_kernel(depth, act, act_other, edge, edge_other, far, far_other, mine, other, *refs):
+    count = len(target_types(depth))
+    outs = refs[:count]
+    wide, grads, sems = refs[count:]
     z, y, core = position()
     rows = far.shape[-1]
     span = mine.shape[0]
+    first = y * 2
 
     def at(start):
         return wide.at[:, :, pl.ds(pl.multiple_of(start * rows, rows), rows)]
 
     fetch(
         [
-            (
-                near.at[:, y],
-                wide.at[:, :, pl.ds(pl.multiple_of(y * 2 * rows, 2 * rows), 4 * rows)],
-            ),
+            (act.at[:, y], at(first + 1 + core)),
+            (act_other.at[:, y], at(first + 2 - core)),
+            (edge.at[:, y], at(first + 3 * core)),
+            (edge_other.at[:, y], at(first + 3 - 3 * core)),
             (far, at((1 - y) * 4 + core)),
             (far_other, at((1 - y) * 4 + 1 - core)),
             (mine, grads.at[pl.ds(pl.multiple_of(y * span, span), span), :]),
@@ -134,21 +153,24 @@
         ],
         sems,
     )
-    for i in range(depth):
-        d = (i + 1) % depth
-        target = lax.rem(z + d, depth)
+    for out, target in zip(outs, targets(depth, z)):
         for k in range(3):
-            outs[d][k] = product(
+            out[k] = product(
                 wide[target, :, pl.ds(k * rows, 4 * rows)], grads[...]
-            ).astype(outs[d].dtype)
-
-
-def point_kernel(depth, turned, branch, *outs):
-    z, _, _ = position()
-    for i in range(depth):
-        d = (i + 1) % depth
-        target = lax.rem(z + d, depth)
-        outs[d][...] = product(turned[target], branch[...]).astype(outs[d].dtype)
+            ).astype(out.dtype)
+
+
+def point_kernel(depth, turned, turned_other, branch, *outs):
+    z, _, core = position()
+    rows = turned.shape[-1]
+
+    def here(start):
+        return pl.ds(pl.multiple_of(start * rows, rows), rows)
+
+    for out, target in zip(outs, targets(depth, z)):
+        total = product(turned[target], branch[here(core)])
+        total = total + product(turned_other[target], branch[here(1 - core)])
+        out[...] = total.astype(out.dtype)
 
 
 def backward_kernel(places, *refs):
@@ -226,8 +248,13 @@
     def cut(value, start, length, axis):
         return lax.dynamic_slice_in_dim(value, start, length, axis)
 
+    def turned(value):
+        return value.T.reshape(depth, 2, block, rows)
+
     mine = cut(dilated_weight, core * half, half, 2)
     theirs = cut(dilated_weight, (1 - core) * half, half, 2)
+    inputs = after(inputs, theirs)
+    cotangent = after(cotangent, theirs)
     swapped = to_core(theirs)
     if halved:
         parity = lax.axis_index("groups") % 2
@@ -235,9 +262,30 @@
         rest_piece = jnp.where(core == parity, swapped, mine)
     else:
         start_piece = in_order(core == 0, mine, swapped, 1)
+    along = [start_piece] + [to_z(start_piece, d) for d in range(1, depth)]
+
+    xfull = inputs.astype(f32)
+    ratio = lax.rsqrt(jnp.mean(xfull * xfull, axis=-1, keepdims=True) + 1e-06)
+    normed = xfull * ratio * norm_gain
+    act = gelu_value(normed).astype(bf16)
+    edge = send(act, lambda i: i + 1 if i % 2 else i - 1)
+    act_other = to_core(after(act, start_piece))
+    cot_other = to_core(after(cotangent, start_piece))
+    beside = [to_y(start_piece)]
+    *first, edge, act_other, cot_other, act_late, cot_late = lax.optimization_barrier(
+        (*along[1:], *beside, edge, act_other, cot_other, act, cotangent)
+    )
+    along = along[:1] + first[:-1]
+    beside = first[-1:]
+    point_rows = cut(point_weight, core * half, half, 0)
+    branch_grad = transposed_product(cot_late, point_rows)
+    branch_grad_other = transposed_product(cot_other, point_rows)
+    cot_turned = turned(cot_late)
+    cot_turned_other = turned(cot_other)
+    act_turned = turned(act_late)
+    act_turned_other = turned(act_other)
     part = 0 if halved else None
-    along = [start_piece] + [to_z(start_piece, d) for d in range(1, depth)]
-    beside = [to_y(c) for c in along]
+    beside += [to_y(piece) for piece in along[1:]]
     pieces = along + beside
     places = [(d, False, part) for d in range(depth)]
     places += [(d, True, part) for d in range(depth)]
@@ -245,47 +293,36 @@
         pieces = pieces + [rest_piece] + [to_x(c) for c in pieces[1:]]
         places = places + [(d, across, 1) for d, across, _ in places]
 
-    inputs = after(inputs, theirs)
-    cotangent = after(cotangent, theirs)
-    xfull = inputs.astype(f32)
-    ratio = lax.rsqrt(jnp.mean(xfull * xfull, axis=-1, keepdims=True) + 1e-06)
-    normed = xfull * ratio * norm_gain
-    act = gelu_value(normed).astype(bf16)
-    edge = send(act, lambda i: i + 1 if i % 2 else i - 1)
-    act_other = to_core(act)
-    edge_other = to_core(after(edge, *beside[:2]))
-
-    cot_other = to_core(after(cotangent, start_piece))
-    cot = in_order(core == 0, cotangent, cot_other, 0)
-    point_rows = cut(point_weight, core * half, half, 0)
-    branch_grad = transposed_product(cot, point_rows)
-    cot_turned = cot.T.reshape(depth, 2 * block, span)
-
-    act_wide = jnp.concatenate(
-        [
-            jnp.where(core == 0, edge, edge_other),
-            in_order(core == 0, act, act_other, 0),
-            jnp.where(core == 0, edge_other, edge),
-        ],
-        0,
-    )
-    act_turned = act_wide.T.reshape(depth, 2, block, 4 * rows)
+    edge_other = to_core(edge)
+    edge_turned = turned(edge)
     far = to_y(
-        lax.dynamic_slice(
-            act_turned,
-            (0, 1 - y, 0, (y * 2 + core) * rows),
-            (depth, 1, block, rows),
+        cut(
+            jnp.where(core == y, edge_turned, act_turned_other), 1 - y, 1, 1
         ).reshape(depth, block, rows)
     )
-    branch_grad = after(branch_grad, cot_turned, act_turned)
-    far_other = to_core(far)
+    edge_turned_other = turned(edge_other)
 
     count = len(pieces)
     branch, pre_grad = call(
         functools.partial(forward_kernel, places),
         [((span, half), bf16)] * 2,
-        [*pieces, act, act_other, edge, edge_other, branch_grad],
-        [pl.ANY] * (count + 4) + [pltpu.VMEM],
+        [
+            *pieces,
+            act,
+            act_other,
+            edge,
+            after(
+                edge_other,
+                edge_turned_other,
+                cot_turned,
+                cot_turned_other,
+                act_turned,
+                act_turned_other,
+            ),
+            branch_grad,
+            branch_grad_other,
+        ],
+        [pl.ANY] * (count + 4) + [pltpu.VMEM] * 2,
         [
             pltpu.VMEM((4 * rows, channels), bf16),
             pltpu.VMEM((3, channels, half), bf16),
@@ -296,24 +333,41 @@
     )
 
     grad_far = to_y(pre_grad)
-    grad_edge = after(pre_grad, grad_far)
-    grad_low = send(grad_edge[rows:], lambda i: i + 2)
-    grad_high = send(grad_edge[:rows], lambda i: i - 2)
+    far_other = to_core(after(far, pre_grad))
+
+    def line(value, pairs):
+        return lax.ppermute(
+            value,
+            "seq",
+            [(4 * a + i, 4 * b + i) for a, b in pairs for i in range(4)],
+        )
 
     def sent(terms):
-        return [terms[0]] + [to_z(terms[d], d) for d in range(1, depth)]
-
-    def added(terms):
-        total = terms[0]
-        for term in terms[1:]:
+        if depth != 4:
+            return [to_z(term, d + 1) for d, term in enumerate(terms[:-1])]
+        three, two, up, down, _ = terms
+        passing = line(three, [(0, 1), (3, 2)])
+        direct = line(two.astype(bf16), [(0, 2), (3, 1)])
+        up = line(up, [(0, 1), (1, 2), (2, 3)])
+        down = line(down, [(1, 0), (2, 1), (3, 2)])
+        joined = line((two + passing.astype(f32)).astype(bf16), [(1, 3), (2, 0)])
+        return [up, down, direct, joined]
+
+    def added(total, terms):
+        for term in terms:
             total = total + term.astype(f32)
         return total
 
+    types = target_types(depth)
     point_terms = call(
         functools.partial(point_kernel, depth),
-        [((2 * block, half), bf16 if d else f32) for d in range(depth)],
-        [cot_turned, branch],
-        [pltpu.VMEM] * 2,
+        [((2 * block, half), t) for t in types],
+        [
+            cot_turned.reshape(depth, 2 * block, rows),
+            cot_turned_other.reshape(depth, 2 * block, rows),
+            branch,
+        ],
+        [pltpu.VMEM] * 3,
         [],
         2 * span * channels * half,
         16,
@@ -322,31 +376,42 @@
 
     tap_terms = call(
         functools.partial(terms_kernel, depth),
-        [((3, block, half), bf16 if d else f32) for d in range(depth)],
-        [act_turned, far, far_other, pre_grad, grad_far],
-        [pl.ANY] * 5,
+        [((3, block, half), t) for t in types],
+        [
+            act_turned,
+            act_turned_other,
+            edge_turned,
+            edge_turned_other,
+            far,
+            far_other,
+            pre_grad,
+            grad_far,
+        ],
+        [pl.ANY] * 8,
         [
             pltpu.VMEM((depth, block, 6 * rows), bf16),
             pltpu.VMEM((2 * span, half), bf16),
-            pltpu.SemaphoreType.DMA((5,)),
+            pltpu.SemaphoreType.DMA((8,)),
         ],
         6 * span * channels * half,
         24,
     )
     tap_parts = sent(tap_terms)
-    tap_sum = added(tap_parts)
-
-    branch = after(branch, tap_terms[0])
+    first_parts = tap_parts[:-1]
+
+    pre_grad = after(pre_grad, *first_parts)
+    grad_low = send(pre_grad[rows:], lambda i: i + 2)
+    grad_high = send(pre_grad[:rows], lambda i: i - 2)
+    branch = after(branch, *first_parts)
     branch_other = to_core(cut(branch, (1 - core) * rows, rows, 0))
     branch_own = in_order(
         core == 0, cut(branch, core * rows, rows, 0), branch_other, 1
     )
     outputs = (xfull + product(branch_own, point_weight)).astype(bf16)
-
     act_grad, act_grad_other = call(
         functools.partial(backward_kernel, places),
         [((rows, channels), f32)] * 2,
-        [*pieces, grad_low, after(pre_grad, tap_terms[0]), grad_high],
+        [*pieces, grad_low, pre_grad, grad_high],
         [pl.ANY] * (count + 3),
         [
             pltpu.VMEM((4 * rows, half), bf16),
@@ -356,26 +421,34 @@
         6 * span * channels * half,
         24,
     )
-    point_sum = added([after(term, act_grad_other) for term in point_parts])
-    point_sum = cut(point_sum, y * block, block, 0) + to_y(
-        cut(point_sum, (1 - y) * block, block, 0).astype(bf16)
-    ).astype(f32)
-
-    act_grad = act_grad + to_core(act_grad_other)
+    act_grad = act_grad + to_core(after(act_grad_other, tap_parts[-1]))
     scaled = act_grad * gelu_slope(normed) * norm_gain
     inner = jnp.mean(scaled * xfull, axis=-1, keepdims=True)
     input_grad = (
         cotangent.astype(f32) + ratio * scaled - xfull * ratio * ratio * ratio * inner
     ).astype(bf16)
 
-    sums = jnp.concatenate([tap_sum, point_sum[None]], 0)
-    sums = in_order(
-        core == 0,
-        cut(sums, core * own, own, 1),
-        to_core(cut(sums, (1 - core) * own, own, 1)),
-        2,
-    )
-    return (outputs, input_grad, sums[:3], sums[3].T)
+    def halves(value, axis):
+        return in_order(
+            core == 0,
+            cut(value, core * own, own, axis),
+            to_core(cut(value, (1 - core) * own, own, axis)),
+            axis + 1,
+        )
+
+    point_sum = added(
+        point_terms[-1], [after(term, act_grad_other) for term in point_parts]
+    )
+    point_sum = cut(point_sum, y * block, block, 0) + to_y(
+        cut(point_sum, (1 - y) * block, block, 0).astype(bf16)
+    ).astype(f32)
+    point_grad = halves(point_sum, 0).T
+
+    tap_parts = list(
+        lax.optimization_barrier((*tap_parts, outputs, input_grad, point_grad))
+    )
+    tap_sum = added(tap_terms[-1], tap_parts[:-3])
+    return (*tap_parts[-3:-1], halves(tap_sum, 1), tap_parts[-1])
 
 
 def solution(mesh):

time: 197 us -> 209 us (1.061)
  the two profiles are of different devices: /device:TPU:29 before, /device:TPU:9 now
where the time goes in v4:
time: 209 us; the launch traced here: 204 us
  starting transfers between devices  76.2 us (36%)
  waiting for transfers between devices  54.3 us (26%)
  local copies, waits for them, and re-layouts  30 us (14%)
  Pallas kernels  19.3 us (9%)
  other arithmetic  18.8 us (9%)
  matrix products  4.73 us (2%)
    ppermute x22, starting transfers between devices, send(): return lax.ppermute(value, 'seq', [p for p in pairs if 0 <= p[1] < size])  37.8 us
    ppermute x22, waiting for transfers between devices, send(): return lax.ppermute(value, 'seq', [p for p in pairs if 0 <= p[1] < size])  37.2 us
    ppermute x10, starting transfers between devices, line(): lax.ppermute(value, 'seq', [(4 * a + i, 4 * b + i) for a, b in pairs for...  32.8 us
    pallas_call x4, Pallas kernels, call(): pl.pallas_call(kernel, out_shape=[jax.ShapeDtypeStruct(s, t) for s, t in...  19.3 us
    unnamed x66, local copies, waits for them, and re-layouts  14.1 us
    transpose x6, local copies, waits for them, and re-layouts, turned(): return value.T.reshape(depth, 2, block, rows)  12.8 us
    ppermute x7, waiting for transfers between devices, to_x(): return lax.ppermute(value, 'groups', [(g, g ^ 1) for g in range(groups)])  11.3 us
    ppermute x10, waiting for transfers between devices, line(): lax.ppermute(value, 'seq', [(4 * a + i, 4 * b + i) for a, b in pairs for...  5.83 us
  transfers between devices with their start and end apart: 39, of which 14 were waited for; matrix products, arithmetic and copies ran while one was open for 15% of the time, Pallas kernels for 7%

profile of v4, /device:TPU:9, one launch (start us, length us, event | category | flops | bytes accessed | tf_op | source)
XLA Modules:
  0.0 204.5 jit_solution(13386558690113998788)
XLA Ops:
  6.0 3.0 %collective-permute-start.5 = (bf16[256,1536]{1,0:T(8,128)(2,1)S(1)}, bf16[256,1536]{1,0:T(8,128)(2,1)}, u32[]{:S(2)}, u32[]{:S(2)}) collective-permute-start(bf16[256,1536]{1,0:T(8,128)(2,1)S(1)} %fusion.6.refs_16_), channel_id=1, source_target_pairs={{1,2},{2,1},{3,4},{4,3},{5,6},{6,5},{7,8},{8,7},{9,10},{10,9},{11,... | collective-permute-start | bytes 2359304 | tf_op jit(solution)/shard_map/ppermute | solution.py:231
  13.6 4.4 %collective-permute-done.1.refs_1_ = bf16[3,96,384]{2,1,0:T(8,128)(2,1)} collective-permute-done((bf16[3,96,384]{2,1,0:T(8,128)(2,1)S(1)}, bf16[3,96,384]{2,1,0:T(8,128)(2,1)}, u32[]{:S(2)}, u32[]{:S(2)}) %collective-permute-start.1) | collective-permute-done | bytes 221216 | tf_op jit(solution)/shard_map/ppermute | solution.py:231
  18.0 2.6 %collective-permute-start.3 = (bf16[3,96,384]{2,1,0:T(8,128)(2,1)S(1)}, bf16[3,96,384]{2,1,0:T(8,128)(2,1)}, u32[]{:S(2)}, u32[]{:S(2)}) collective-permute-start(bf16[3,96,384]{2,1,0:T(8,128)(2,1)S(1)} %get-tuple-element.97.refs_0_), channel_id=1, source_target_pairs={{0,12},{1,13},{2,14},{3,15},{4,0},{5,1},{6,2},{7,3},{8,4},{9,5},{1... | collective-permute-start | bytes 663560 | tf_op jit(solution)/shard_map/ppermute | solution.py:231
  20.6 8.2 %collective-permute-done.2.refs_2_ = bf16[3,96,384]{2,1,0:T(8,128)(2,1)} collective-permute-done((bf16[3,96,384]{2,1,0:T(8,128)(2,1)S(1)}, bf16[3,96,384]{2,1,0:T(8,128)(2,1)}, u32[]{:S(2)}, u32[]{:S(2)}) %collective-permute-start.2) | collective-permute-done | bytes 221216 | tf_op jit(solution)/shard_map/ppermute | solution.py:231
  28.8 9.3 %collective-permute-start.4 = (bf16[3,96,384]{2,1,0:T(8,128)(2,1)S(1)}, bf16[3,96,384]{2,1,0:T(8,128)(2,1)}, u32[]{:S(2)}, u32[]{:S(2)}) collective-permute-start(bf16[3,96,384]{2,1,0:T(8,128)(2,1)S(1)} %get-tuple-element.97.refs_0_), channel_id=1, source_target_pairs={{0,2},{1,3},{2,0},{3,1},{4,6},{5,7},{6,4},{7,5},{8,10},{9,11},{10,... | collective-permute-start | bytes 663560 | tf_op jit(solution)/shard_map/ppermute | solution.py:231
  38.9 2.9 %collective-permute-done.4.refs_4_ = bf16[3,96,384]{2,1,0:T(8,128)(2,1)} collective-permute-done((bf16[3,96,384]{2,1,0:T(8,128)(2,1)S(1)}, bf16[3,96,384]{2,1,0:T(8,128)(2,1)}, u32[]{:S(2)}, u32[]{:S(2)}) %collective-permute-start.4) | collective-permute-done | bytes 221216 | tf_op jit(solution)/shard_map/ppermute | solution.py:231
  70.4 4.7 %collective-permute-done.18.refs_14_ = bf16[3,96,384]{2,1,0:T(8,128)(2,1)} collective-permute-done((bf16[3,96,384]{2,1,0:T(8,128)(2,1)}, bf16[3,96,384]{2,1,0:T(8,128)(2,1)}, u32[]{:S(2)}, u32[]{:S(2)}) %collective-permute-start.18) | collective-permute-done | bytes 221216 | tf_op jit(solution)/shard_map/ppermute | solution.py:246
  75.1 4.7 %collective-permute-done.19.refs_15_ = bf16[3,96,384]{2,1,0:T(8,128)(2,1)} collective-permute-done((bf16[3,96,384]{2,1,0:T(8,128)(2,1)}, bf16[3,96,384]{2,1,0:T(8,128)(2,1)}, u32[]{:S(2)}, u32[]{:S(2)}) %collective-permute-start.19) | collective-permute-done | bytes 221216 | tf_op jit(solution)/shard_map/ppermute | solution.py:246
  84.8 5.8 %shard_map.84 = (bf16[512,384]{1,0:T(8,128)(2,1)S(1)}, bf16[512,384]{1,0:T(8,128)(2,1)S(1)}) custom-call(bf16[3,96,384]{2,1,0:T(8,128)(2,1)S(1)} %copy-done.11, bf16[3,96,384]{2,1,0:T(8,128)(2,1)} %collective-permute-done.1.refs_1_, bf16[3,96,384]{2,1,0:T(8,128)(2,1)} %collective-permute-done.2.refs_2_, bf16[3,96,384]{2,1,0:T(8,128)(2,1)} %collective-permute-done.3.refs_3_, ...), custom_call_target="tpu_custom_call" | custom-call | flops 1811939328 | bytes 8257536 | tf_op jit(solution)/shard_map/pallas_call | solution.py:205
  91.4 3.8 %collective-permute-start.20 = (bf16[4,192,256]{2,1,0:T(8,128)(2,1)}, bf16[4,192,256]{2,1,0:T(8,128)(2,1)S(1)}, u32[]{:S(2)}, u32[]{:S(2)}) collective-permute-start(bf16[4,192,256]{2,1,0:T(8,128)(2,1)} %collective-permute-done.9.far), channel_id=1, source_target_pairs={{0,1},{1,0},{2,3},{3,2},{4,5},{5,4},{6,7},{7,6},{8,9},{9,8},{10,11... | collective-permute-start | bytes 1179656 | tf_op jit(solution)/shard_map/ppermute | solution.py:231
  96.7 9.1 %collective-permute-done.21.other = bf16[512,384]{1,0:T(8,128)(2,1)S(1)} collective-permute-done((bf16[512,384]{1,0:T(8,128)(2,1)S(1)}, bf16[512,384]{1,0:T(8,128)(2,1)S(1)}, u32[]{:S(2)}, u32[]{:S(2)}) %collective-permute-start.21) | collective-permute-done | bytes 393248 | tf_op jit(solution)/shard_map/ppermute | solution.py:231
  105.8 5.1 %shard_map.85 = (bf16[3,192,384]{2,1,0:T(8,128)(2,1)S(1)}, f32[3,192,384]{2,1,0:T(8,128)S(1)}, bf16[3,192,384]{2,1,0:T(8,128)(2,1)}, bf16[3,192,384]{2,1,0:T(8,128)(2,1)}, f32[3,192,384]{2,1,0:T(8,128)S(1)}) custom-call(bf16[4,2,192,256]{3,2,1,0:T(8,128)(2,1)S(1)} %bitcast.25, bf16[4,2,192,256]{3,2,1,0:T(8,128)(2,1)S(1)} %bitcast.22, ...), custom_call_target="tpu_custom_call" | custom-call | flops 1811939328 | bytes 7815168 | tf_op jit(solution)/shard_map/pallas_call | solution.py:205
  112.3 3.7 %collective-permute-start.22 = (bf16[3,192,384]{2,1,0:T(8,128)(2,1)}, bf16[3,192,384]{2,1,0:T(8,128)(2,1)}, u32[]{:S(2)}, u32[]{:S(2)}) collective-permute-start(bf16[3,192,384]{2,1,0:T(8,128)(2,1)} %get-tuple-element.63), channel_id=1, source_target_pairs={{0,4},{1,5},{2,6},{3,7},{4,8},{5,9},{6,10},{7,11},{8,12},{9,13},{1... | collective-permute-start | bytes 1327112 | tf_op jit(solution)/shard_map/ppermute | solution.py:339
  115.9 3.3 %collective-permute-start.23 = (bf16[3,192,384]{2,1,0:T(8,128)(2,1)}, bf16[3,192,384]{2,1,0:T(8,128)(2,1)}, u32[]{:S(2)}, u32[]{:S(2)}) collective-permute-start(bf16[3,192,384]{2,1,0:T(8,128)(2,1)} %get-tuple-element.64), channel_id=1, source_target_pairs={{4,0},{5,1},{6,2},{7,3},{8,4},{9,5},{10,6},{11,7},{12,8},{13,9},{1... | collective-permute-start | bytes 1327112 | tf_op jit(solution)/shard_map/ppermute | solution.py:339
  119.2 5.5 %collective-permute-done.25 = bf16[3,192,384]{2,1,0:T(8,128)(2,1)S(1)} collective-permute-done((bf16[3,192,384]{2,1,0:T(8,128)(2,1)S(1)}, bf16[3,192,384]{2,1,0:T(8,128)(2,1)S(1)}, u32[]{:S(2)}, u32[]{:S(2)}) %collective-permute-start.25) | collective-permute-done | bytes 442400 | tf_op jit(solution)/shard_map/ppermute | solution.py:339
  138.2 5.2 %collective-permute-start.32 = (bf16[384,384]{1,0:T(8,128)(2,1)}, bf16[384,384]{1,0:T(8,128)(2,1)}, u32[]{:S(2)}, u32[]{:S(2)}) collective-permute-start(bf16[384,384]{1,0:T(8,128)(2,1)} %get-tuple-element.76), channel_id=1, source_target_pairs={{4,0},{5,1},{6,2},{7,3},{8,4},{9,5},{10,6},{11,7},{12,8},{13,9},{1... | collective-permute-start | bytes 884744 | tf_op jit(solution)/shard_map/ppermute | solution.py:339
  145.4 2.6 %collective-permute-start.26 = (bf16[3,192,384]{2,1,0:T(8,128)(2,1)S(1)}, bf16[3,192,384]{2,1,0:T(8,128)(2,1)}, u32[]{:S(2)}, u32[]{:S(2)}) collective-permute-start(bf16[3,192,384]{2,1,0:T(8,128)(2,1)S(1)} %copy-done.31), channel_id=1, source_target_pairs={{4,12},{5,13},{6,14},{7,15},{8,0},{9,1},{10,2},{11,3},{20,28},{21,... | collective-permute-start | bytes 1327112 | tf_op jit(solution)/shard_map/ppermute | solution.py:339
  148.0 3.0 %collective-permute-start.28 = (bf16[256,384]{1,0:T(8,128)(2,1)S(1)}, bf16[256,384]{1,0:T(8,128)(2,1)S(1)}, u32[]{:S(2)}, u32[]{:S(2)}) collective-permute-start(bf16[256,384]{1,0:T(8,128)(2,1)S(1)} %get-tuple-element.101), channel_id=1, source_target_pairs={{0,2},{1,3},{2,4},{3,5},{4,6},{5,7},{6,8},{7,9},{8,10},{9,11},{10,... | collective-permute-start | bytes 589832 | tf_op jit(solution)/shard_map/ppermute | solution.py:231
  151.1 3.1 %collective-permute-start.29 = (bf16[256,384]{1,0:T(8,128)(2,1)S(1)}, bf16[256,384]{1,0:T(8,128)(2,1)S(1)}, u32[]{:S(2)}, u32[]{:S(2)}) collective-permute-start(bf16[256,384]{1,0:T(8,128)(2,1)S(1)} %get-tuple-element.100), channel_id=1, source_target_pairs={{2,0},{3,1},{4,2},{5,3},{6,4},{7,5},{8,6},{9,7},{10,8},{11,9},{12,... | collective-permute-start | bytes 589832 | tf_op jit(solution)/shard_map/ppermute | solution.py:231
  155.1 5.4 %collective-permute-done.28.refs_16_ = bf16[256,384]{1,0:T(8,128)(2,1)S(1)} collective-permute-done((bf16[256,384]{1,0:T(8,128)(2,1)S(1)}, bf16[256,384]{1,0:T(8,128)(2,1)S(1)}, u32[]{:S(2)}, u32[]{:S(2)}) %collective-permute-start.28) | collective-permute-done | bytes 196640 | tf_op jit(solution)/shard_map/ppermute | solution.py:231
  160.5 10.8 %collective-permute-start.35 = (bf16[384,384]{1,0:T(8,128)(2,1)}, bf16[384,384]{1,0:T(8,128)(2,1)}, u32[]{:S(2)}, u32[]{:S(2)}) collective-permute-start(bf16[384,384]{1,0:T(8,128)(2,1)} %get-tuple-element.99), channel_id=1, source_target_pairs={{4,12},{5,13},{6,14},{7,15},{8,0},{9,1},{10,2},{11,3},{20,28},{21,... | collective-permute-start | bytes 884744 | tf_op jit(solution)/shard_map/ppermute | solution.py:339
  172.6 6.7 %shard_map.86 = (f32[256,1536]{1,0:T(8,128)S(1)}, f32[256,1536]{1,0:T(8,128)}) custom-call(bf16[3,96,384]{2,1,0:T(8,128)(2,1)S(1)} %copy-done.12, bf16[3,96,384]{2,1,0:T(8,128)(2,1)} %collective-permute-done.1.refs_1_, bf16[3,96,384]{2,1,0:T(8,128)(2,1)} %collective-permute-done.2.refs_2_, bf16[3,96,384]{2,1,0:T(8,128)(2,1)} %collective-permute-done.3.refs_3_, ...), custom_call_target="tpu_custom_call" | custom-call | flops 1811939328 | bytes 7471104 | tf_op jit(solution)/shard_map/pallas_call | solution.py:205
  187.7 2.6 %collective-permute-done.36 = bf16[192,384]{1,0:T(8,128)(2,1)S(1)} collective-permute-done((bf16[192,384]{1,0:T(8,128)(2,1)S(1)}, bf16[192,384]{1,0:T(8,128)(2,1)S(1)}, u32[]{:S(2)}, u32[]{:S(2)}) %collective-permute-start.36) | collective-permute-done | bytes 147488 | tf_op jit(solution)/shard_map/ppermute | solution.py:231
  195.5 3.0 %fusion.20 = (f32[256]{0:T(256)S(1)}, f32[256,1536]{1,0:T(8,128)S(1)}) fusion(bf16[256,1536]{1,0:T(8,128)(2,1)S(1)} %copy-done.26, f32[1536]{0:T(1024)S(1)} %copy-done.32, f32[256]{0:T(256)S(1)} %add_rsqrt_fusion, f32[256,1536]{1,0:T(8,128)S(1)} %copy-done.7, f32[256,1536]{1,0:T(8,128)} %collective-permute-done.30), kind=kLoop, calls=%fused_computation.26 | loop fusion | flops 9830144 | bytes 5513216 | tf_op jit(solution)/shard_map/reduce_sum | solution.py:426
  (154 shorter events, 84.6 us)
Async XLA Ops:
  6.0 35.8 %collective-permute-start.5 = (bf16[256,1536]{1,0:T(8,128)(2,1)S(1)}, bf16[256,1536]{1,0:T(8,128)(2,1)}, u32[]{:S(2)}, u32[]{:S(2)}) collective-permute-start(bf16[256,1536]{1,0:T(8,128)(2,1)S(1)} %fusion.6.refs_16_), channel_id=1, source_target_pairs={{1,2},{2,1},{3,4},{4,3},{5,6},{6,5},{7,8},{8,7},{9,10},{10,9},{11,... | collective-permute-start | bytes 2359304 | tf_op jit(solution)/shard_map/ppermute | solution.py:231
  10.8 31.0 %collective-permute-start.6 = (bf16[256,1536]{1,0:T(8,128)(2,1)S(1)}, bf16[256,1536]{1,0:T(8,128)(2,1)S(1)}, u32[]{:S(2)}, u32[]{:S(2)}) collective-permute-start(bf16[256,1536]{1,0:T(8,128)(2,1)S(1)} %fusion.6.refs_16_), channel_id=1, source_target_pairs={{0,1},{1,0},{2,3},{3,2},{4,5},{5,4},{6,7},{7,6},{8,9},{9,8},{10,11... | collective-permute-start | bytes 2359304 | tf_op jit(solution)/shard_map/ppermute | solution.py:231
  11.1 31.5 %collective-permute-start.7 = (bf16[256,1536]{1,0:T(8,128)(2,1)}, bf16[256,1536]{1,0:T(8,128)(2,1)S(1)}, u32[]{:S(2)}, u32[]{:S(2)}) collective-permute-start(bf16[256,1536]{1,0:T(8,128)(2,1)} %param.9), channel_id=1, source_target_pairs={{0,1},{1,0},{2,3},{3,2},{4,5},{5,4},{6,7},{7,6},{8,9},{9,8},{10,11... | collective-permute-start | bytes 2359304 | tf_op jit(solution)/shard_map/ppermute | solution.py:231
  12.6 16.3 %collective-permute-start.2 = (bf16[3,96,384]{2,1,0:T(8,128)(2,1)S(1)}, bf16[3,96,384]{2,1,0:T(8,128)(2,1)}, u32[]{:S(2)}, u32[]{:S(2)}) collective-permute-start(bf16[3,96,384]{2,1,0:T(8,128)(2,1)S(1)} %get-tuple-element.97.refs_0_), channel_id=1, source_target_pairs={{0,8},{1,9},{2,10},{3,11},{4,12},{5,13},{6,14},{7,15},{8,0},{9,1},... | collective-permute-start | bytes 663560 | tf_op jit(solution)/shard_map/ppermute | solution.py:231
  18.0 20.9 %collective-permute-start.3 = (bf16[3,96,384]{2,1,0:T(8,128)(2,1)S(1)}, bf16[3,96,384]{2,1,0:T(8,128)(2,1)}, u32[]{:S(2)}, u32[]{:S(2)}) collective-permute-start(bf16[3,96,384]{2,1,0:T(8,128)(2,1)S(1)} %get-tuple-element.97.refs_0_), channel_id=1, source_target_pairs={{0,12},{1,13},{2,14},{3,15},{4,0},{5,1},{6,2},{7,3},{8,4},{9,5},{1... | collective-permute-start | bytes 663560 | tf_op jit(solution)/shard_map/ppermute | solution.py:231
  28.8 12.9 %collective-permute-start.4 = (bf16[3,96,384]{2,1,0:T(8,128)(2,1)S(1)}, bf16[3,96,384]{2,1,0:T(8,128)(2,1)}, u32[]{:S(2)}, u32[]{:S(2)}) collective-permute-start(bf16[3,96,384]{2,1,0:T(8,128)(2,1)S(1)} %get-tuple-element.97.refs_0_), channel_id=1, source_target_pairs={{0,2},{1,3},{2,0},{3,1},{4,6},{5,7},{6,4},{7,5},{8,10},{9,11},{10,... | collective-permute-start | bytes 663560 | tf_op jit(solution)/shard_map/ppermute | solution.py:231
  43.5 21.1 %collective-permute-start.8 = (bf16[256,1536]{1,0:T(8,128)(2,1)}, bf16[256,1536]{1,0:T(8,128)(2,1)}, u32[]{:S(2)}, u32[]{:S(2)}) collective-permute-start(bf16[256,1536]{1,0:T(8,128)(2,1)} %collective-permute-done.5.refs_18_), channel_id=1, source_target_pairs={{0,1},{1,0},{2,3},{3,2},{4,5},{5,4},{6,7},{7,6},{8,9},{9,8},{10,11... | collective-permute-start | bytes 2359304 | tf_op jit(solution)/shard_map/ppermute | solution.py:231
  45.0 16.3 %collective-permute-start.13 = (bf16[3,96,384]{2,1,0:T(8,128)(2,1)}, bf16[3,96,384]{2,1,0:T(8,128)(2,1)}, u32[]{:S(2)}, u32[]{:S(2)}) collective-permute-start(bf16[3,96,384]{2,1,0:T(8,128)(2,1)} %collective-permute-done.1.refs_1_), channel_id=1, source_target_pairs={{0,16},{16,0},{1,17},{17,1},{2,18},{18,2},{3,19},{19,3},{4,20},{20... | collective-permute-start | bytes 663560 | tf_op jit(solution)/shard_map/ppermute | solution.py:246
  46.2 16.3 %collective-permute-start.14 = (bf16[3,96,384]{2,1,0:T(8,128)(2,1)}, bf16[3,96,384]{2,1,0:T(8,128)(2,1)}, u32[]{:S(2)}, u32[]{:S(2)}) collective-permute-start(bf16[3,96,384]{2,1,0:T(8,128)(2,1)} %collective-permute-done.2.refs_2_), channel_id=1, source_target_pairs={{0,16},{16,0},{1,17},{17,1},{2,18},{18,2},{3,19},{19,3},{4,20},{20... | collective-permute-start | bytes 663560 | tf_op jit(solution)/shard_map/ppermute | solution.py:246
  60.0 31.4 %collective-permute-start.9 = (bf16[4,192,256]{2,1,0:T(8,128)(2,1)}, bf16[4,192,256]{2,1,0:T(8,128)(2,1)}, u32[]{:S(2)}, u32[]{:S(2)}) collective-permute-start(bf16[4,192,256]{2,1,0:T(8,128)(2,1)} %fusion.25), channel_id=1, source_target_pairs={{0,2},{1,3},{2,0},{3,1},{4,6},{5,7},{6,4},{7,5},{8,10},{9,11},{10,... | collective-permute-start | bytes 1179656 | tf_op jit(solution)/shard_map/ppermute | solution.py:231
  64.7 15.2 %collective-permute-start.19 = (bf16[3,96,384]{2,1,0:T(8,128)(2,1)}, bf16[3,96,384]{2,1,0:T(8,128)(2,1)}, u32[]{:S(2)}, u32[]{:S(2)}) collective-permute-start(bf16[3,96,384]{2,1,0:T(8,128)(2,1)} %collective-permute-done.12.refs_7_), channel_id=1, source_target_pairs={{0,16},{16,0},{1,17},{17,1},{2,18},{18,2},{3,19},{19,3},{4,20},{20... | collective-permute-start | bytes 663560 | tf_op jit(solution)/shard_map/ppermute | solution.py:246
  111.0 13.8 %collective-permute-start.25 = (bf16[3,192,384]{2,1,0:T(8,128)(2,1)S(1)}, bf16[3,192,384]{2,1,0:T(8,128)(2,1)S(1)}, u32[]{:S(2)}, u32[]{:S(2)}) collective-permute-start(bf16[3,192,384]{2,1,0:T(8,128)(2,1)S(1)} %get-tuple-element.66), channel_id=1, source_target_pairs={{0,4},{1,5},{2,6},{3,7},{12,8},{13,9},{14,10},{15,11},{16,20},{17,... | collective-permute-start | bytes 1327112 | tf_op jit(solution)/shard_map/ppermute | solution.py:339
  112.3 31.1 %collective-permute-start.22 = (bf16[3,192,384]{2,1,0:T(8,128)(2,1)}, bf16[3,192,384]{2,1,0:T(8,128)(2,1)}, u32[]{:S(2)}, u32[]{:S(2)}) collective-permute-start(bf16[3,192,384]{2,1,0:T(8,128)(2,1)} %get-tuple-element.63), channel_id=1, source_target_pairs={{0,4},{1,5},{2,6},{3,7},{4,8},{5,9},{6,10},{7,11},{8,12},{9,13},{1... | collective-permute-start | bytes 1327112 | tf_op jit(solution)/shard_map/ppermute | solution.py:339
  115.9 29.4 %collective-permute-start.23 = (bf16[3,192,384]{2,1,0:T(8,128)(2,1)}, bf16[3,192,384]{2,1,0:T(8,128)(2,1)}, u32[]{:S(2)}, u32[]{:S(2)}) collective-permute-start(bf16[3,192,384]{2,1,0:T(8,128)(2,1)} %get-tuple-element.64), channel_id=1, source_target_pairs={{4,0},{5,1},{6,2},{7,3},{8,4},{9,5},{10,6},{11,7},{12,8},{13,9},{1... | collective-permute-start | bytes 1327112 | tf_op jit(solution)/shard_map/ppermute | solution.py:339
  125.9 22.1 %collective-permute-start.24 = (bf16[3,192,384]{2,1,0:T(8,128)(2,1)}, bf16[3,192,384]{2,1,0:T(8,128)(2,1)}, u32[]{:S(2)}, u32[]{:S(2)}) collective-permute-start(bf16[3,192,384]{2,1,0:T(8,128)(2,1)} %get-tuple-element.95), channel_id=1, source_target_pairs={{0,8},{1,9},{2,10},{3,11},{12,4},{13,5},{14,6},{15,7},{16,24},{17,... | collective-permute-start | bytes 1327112 | tf_op jit(solution)/shard_map/ppermute | solution.py:339
  136.7 14.3 %collective-permute-start.34 = (bf16[384,384]{1,0:T(8,128)(2,1)S(1)}, bf16[384,384]{1,0:T(8,128)(2,1)S(1)}, u32[]{:S(2)}, u32[]{:S(2)}) collective-permute-start(bf16[384,384]{1,0:T(8,128)(2,1)S(1)} %get-tuple-element.80), channel_id=1, source_target_pairs={{0,4},{1,5},{2,6},{3,7},{12,8},{13,9},{14,10},{15,11},{16,20},{17,... | collective-permute-start | bytes 884744 | tf_op jit(solution)/shard_map/ppermute | solution.py:339
  138.2 45.0 %collective-permute-start.32 = (bf16[384,384]{1,0:T(8,128)(2,1)}, bf16[384,384]{1,0:T(8,128)(2,1)}, u32[]{:S(2)}, u32[]{:S(2)}) collective-permute-start(bf16[384,384]{1,0:T(8,128)(2,1)} %get-tuple-element.76), channel_id=1, source_target_pairs={{4,0},{5,1},{6,2},{7,3},{8,4},{9,5},{10,6},{11,7},{12,8},{13,9},{1... | collective-permute-start | bytes 884744 | tf_op jit(solution)/shard_map/ppermute | solution.py:339
  143.4 39.8 %collective-permute-start.31 = (bf16[384,384]{1,0:T(8,128)(2,1)S(1)}, bf16[384,384]{1,0:T(8,128)(2,1)}, u32[]{:S(2)}, u32[]{:S(2)}) collective-permute-start(bf16[384,384]{1,0:T(8,128)(2,1)S(1)} %get-tuple-element.74), channel_id=1, source_target_pairs={{0,4},{1,5},{2,6},{3,7},{4,8},{5,9},{6,10},{7,11},{8,12},{9,13},{1... | collective-permute-start | bytes 884744 | tf_op jit(solution)/shard_map/ppermute | solution.py:339
  145.4 35.1 %collective-permute-start.26 = (bf16[3,192,384]{2,1,0:T(8,128)(2,1)S(1)}, bf16[3,192,384]{2,1,0:T(8,128)(2,1)}, u32[]{:S(2)}, u32[]{:S(2)}) collective-permute-start(bf16[3,192,384]{2,1,0:T(8,128)(2,1)S(1)} %copy-done.31), channel_id=1, source_target_pairs={{4,12},{5,13},{6,14},{7,15},{8,0},{9,1},{10,2},{11,3},{20,28},{21,... | collective-permute-start | bytes 1327112 | tf_op jit(solution)/shard_map/ppermute | solution.py:339
  148.0 12.5 %collective-permute-start.28 = (bf16[256,384]{1,0:T(8,128)(2,1)S(1)}, bf16[256,384]{1,0:T(8,128)(2,1)S(1)}, u32[]{:S(2)}, u32[]{:S(2)}) collective-permute-start(bf16[256,384]{1,0:T(8,128)(2,1)S(1)} %get-tuple-element.101), channel_id=1, source_target_pairs={{0,2},{1,3},{2,4},{3,5},{4,6},{5,7},{6,8},{7,9},{8,10},{9,11},{10,... | collective-permute-start | bytes 589832 | tf_op jit(solution)/shard_map/ppermute | solution.py:231
  151.1 20.2 %collective-permute-start.29 = (bf16[256,384]{1,0:T(8,128)(2,1)S(1)}, bf16[256,384]{1,0:T(8,128)(2,1)S(1)}, u32[]{:S(2)}, u32[]{:S(2)}) collective-permute-start(bf16[256,384]{1,0:T(8,128)(2,1)S(1)} %get-tuple-element.100), channel_id=1, source_target_pairs={{2,0},{3,1},{4,2},{5,3},{6,4},{7,5},{8,6},{9,7},{10,8},{11,9},{12,... | collective-permute-start | bytes 589832 | tf_op jit(solution)/shard_map/ppermute | solution.py:231
  160.5 22.7 %collective-permute-start.35 = (bf16[384,384]{1,0:T(8,128)(2,1)}, bf16[384,384]{1,0:T(8,128)(2,1)}, u32[]{:S(2)}, u32[]{:S(2)}) collective-permute-start(bf16[384,384]{1,0:T(8,128)(2,1)} %get-tuple-element.99), channel_id=1, source_target_pairs={{4,12},{5,13},{6,14},{7,15},{8,0},{9,1},{10,2},{11,3},{20,28},{21,... | collective-permute-start | bytes 884744 | tf_op jit(solution)/shard_map/ppermute | solution.py:339
  171.3 11.9 %collective-permute-start.33 = (bf16[384,384]{1,0:T(8,128)(2,1)}, bf16[384,384]{1,0:T(8,128)(2,1)}, u32[]{:S(2)}, u32[]{:S(2)}) collective-permute-start(bf16[384,384]{1,0:T(8,128)(2,1)} %get-tuple-element.98), channel_id=1, source_target_pairs={{0,8},{1,9},{2,10},{3,11},{12,4},{13,5},{14,6},{15,7},{16,24},{17,... | collective-permute-start | bytes 884744 | tf_op jit(solution)/shard_map/ppermute | solution.py:339
  180.5 15.0 %collective-permute-start.30 = (f32[256,1536]{1,0:T(8,128)}, f32[256,1536]{1,0:T(8,128)}, u32[]{:S(2)}, u32[]{:S(2)}) collective-permute-start(f32[256,1536]{1,0:T(8,128)} %get-tuple-element.72), channel_id=1, source_target_pairs={{0,1},{1,0},{2,3},{3,2},{4,5},{5,4},{6,7},{7,6},{8,9},{9,8},{10,11... | collective-permute-start | bytes 4718600 | tf_op jit(solution)/shard_map/ppermute | solution.py:231
  (48 other events, 477.5 us)

commit v5 on v0

v5 whole, which is shorter than its diff:
```python
import functools
import math

import jax
import jax.numpy as jnp
from jax import lax
from jax.experimental import pallas as pl
from jax.experimental.pallas import tpu as pltpu
from jax.sharding import PartitionSpec as P

root_coef = math.sqrt(2.0 / math.pi)
bf16 = jnp.bfloat16
f32 = jnp.float32
MIB = 1024 * 1024


def gelu_value(v):
    return 0.5 * v * (1.0 + jnp.tanh(root_coef * (v + 0.044715 * v * v * v)))


def gelu_slope(v):
    inner = jnp.tanh(root_coef * (v + 0.044715 * v * v * v))
    return 0.5 * (1.0 + inner) + 0.5 * v * (1.0 - inner * inner) * root_coef * (
        1.0 + 3.0 * 0.044715 * v * v
    )


def after(value, *others):
    return lax.optimization_barrier((value, *others))[0]


def product(left, right):
    return jnp.dot(left, right, preferred_element_type=f32)


def transposed_product(left, weight):
    return lax.dot_general(
        left, weight, (((1,), (1,)), ((), ())), preferred_element_type=f32
    )


def position():
    me = lax.axis_index("seq")
    return me // 4, lax.rem(me, 4)


def toggled(q, bit):
    low = lax.rem(q, 2)
    if bit == 0:
        return q
    if bit == 1:
        return q + 1 - 2 * low
    if bit == 2:
        return lax.rem(q + 2, 4)
    return 3 - q


def within(start, length):
    return pl.ds(pl.multiple_of(start * length, length), length)


def started(pairs, sems, first=0):
    copies = [
        pltpu.make_async_copy(src, dst, sems.at[first + i])
        for i, (src, dst) in enumerate(pairs)
    ]
    for copy in copies:
        copy.start()
    return copies


def finish(copies):
    for copy in copies:
        copy.wait()


def tap_pairs(pieces, packed):
    z, _ = position()
    depth = len(pieces)
    return [
        (piece, packed.at[:, lax.rem(z + depth - d, depth)])
        for d, piece in enumerate(pieces)
    ]


def unpack(packed, taps):
    _, depth, _, own, width = packed.shape
    quarter = width // 2
    for k in range(3):
        for i in range(2 * depth):
            for core in range(2):
                taps[k, pl.ds((2 * i + core) * own, own), :] = packed[
                    k, i // 2, i % 2, :, core * quarter : (core + 1) * quarter
                ]


def weight_kernel(depth, *refs):
    pieces = refs[:depth]
    acts = refs[depth : depth + 4]
    edge, edge_other = refs[depth + 4 : depth + 6]
    cots = refs[depth + 6 : depth + 10]
    point = refs[depth + 10]
    branch, grad = refs[depth + 11 : depth + 13]
    outs = refs[depth + 13 : -7]
    wide, wide_cot, packed, taps, grads, branches, sems = refs[-7:]
    z, q = position()
    rows = acts[0].shape[0]
    core = lax.rem(q, 2)
    first = started(
        [(act, wide.at[within(1 + toggled(q, m), rows)]) for m, act in enumerate(acts)]
        + [
            (edge, wide.at[within(5 * (1 - core), rows)]),
            (edge_other, wide.at[within(5 * core, rows)]),
        ]
        + tap_pairs(pieces, packed),
        sems,
    )
    second = started(
        [(cot, wide_cot.at[within(toggled(q, m), rows)]) for m, cot in enumerate(cots)],
        sems,
        len(first),
    )
    finish(first)
    unpack(packed, taps)
    finish(second)
    for part in range(4):
        here = pl.ds(part * rows, rows)
        slope = transposed_product(wide_cot[here], point[...])
        pre = product(wide[here], taps[0])
        pre = pre + product(wide[pl.ds((part + 1) * rows, rows)], taps[1])
        pre = pre + product(wide[pl.ds((part + 2) * rows, rows)], taps[2])
        value = gelu_value(pre)
        branch[here] = value.astype(bf16)
        branches[:, here] = value.T.astype(bf16)
        value = slope * gelu_slope(pre)
        grad[here] = value.astype(bf16)
        grads[:, here] = value.T.astype(bf16)
    width = wide.shape[1] // depth
    for i in range(depth):
        if len(outs) > 1:
            target = lax.rem(z + i + 1, depth)
            lanes = within(target, width)
            out = outs[(i + 1) % depth]
        else:
            lanes = pl.ds(i * width, width)
            out = outs[0].at[lax.rem(i + depth - z, depth)]
        for k in range(3):
            out[k] = product(
                grads[...], wide[pl.ds(k * rows, 4 * rows), lanes]
            ).astype(out.dtype)
        out[3] = product(branches[...], wide_cot[:, lanes]).astype(out.dtype)


def backward_kernel(depth, *refs):
    pieces = refs[:depth]
    low, grad, high = refs[depth : depth + 3]
    outs = refs[depth + 3 : depth + 7]
    wide, packed, taps, sems = refs[depth + 7 :]
    _, q = position()
    rows = low.shape[0]
    finish(
        started(
            [
                (low, wide.at[pl.ds(0, rows)]),
                (grad, wide.at[pl.ds(rows, 4 * rows)]),
                (high, wide.at[pl.ds(5 * rows, rows)]),
            ]
            + tap_pairs(pieces, packed),
            sems,
        )
    )
    unpack(packed, taps)
    for m in (1, 3, 2, 0):
        part = toggled(q, m)
        total = None
        for k in range(3):
            term = transposed_product(wide[within(part + 2 - k, rows)], taps[k])
            total = term if total is None else total + term
        outs[m][...] = total.astype(outs[m].dtype)


def final_kernel(*refs):
    parts = refs[:4]
    dilated, point, held = refs[4:]
    _, q = position()
    quarter = parts[0].shape[1]
    for m in range(4):
        held[m] = parts[m][...].astype(f32)
    for j in range(4):
        m = lax.rem(q + j, 2) + 2 * lax.rem(q // 2 + j // 2, 2)
        here = pl.ds(j * quarter, quarter)
        for k in range(3):
            dilated[k, :, here] = held[m, k].T
        point[here, :] = held[m, 3]


def call(kernel, outs, args, specs, scratch, flops, limit):
    nbytes = sum(a.size * a.dtype.itemsize for a in args) + sum(
        math.prod(s) * jnp.dtype(t).itemsize for s, t in outs
    )
    return pl.pallas_call(
        kernel,
        out_shape=[jax.ShapeDtypeStruct(s, t) for s, t in outs],
        in_specs=[pl.BlockSpec(memory_space=m) for m in specs],
        out_specs=[pl.BlockSpec(memory_space=pltpu.VMEM)] * len(outs),
        scratch_shapes=scratch,
        compiler_params=pltpu.CompilerParams(vmem_limit_bytes=limit * MIB),
        cost_estimate=pl.CostEstimate(
            flops=flops, bytes_accessed=nbytes, transcendentals=0
        ),
    )(*args)


def local(inputs, norm_gain, dilated_weight, point_weight, cotangent):
    size = lax.axis_size("seq")
    depth = size // 4
    z, q = position()
    core = q % 2
    y = q // 2
    rows, channels = inputs.shape
    own = dilated_weight.shape[1]
    hidden = dilated_weight.shape[2]
    quarter = hidden // 4
    flops = 8 * rows * channels * quarter

    def send(value, target):
        pairs = [(i, target(i)) for i in range(size)]
        return lax.ppermute(
            value, "seq", [p for p in pairs if p[1] is not None and 0 <= p[1] < size]
        )

    def cross(value, m):
        return send(value, lambda i: i ^ m)

    def to_z(value, by):
        return send(value, lambda i: (i + 4 * by) % size)

    def cut(value, start, length, axis):
        return lax.dynamic_slice_in_dim(value, start, length, axis)

    def in_order(first, mine, other, axis):
        return jnp.where(
            first,
            jnp.concatenate([mine, other], axis),
            jnp.concatenate([other, mine], axis),
        )

    quarters = [
        cut(dilated_weight, toggled(q, m) * quarter, quarter, 2) for m in range(4)
    ]
    inputs = after(inputs, *quarters[1:])
    cotangent = after(cotangent, *quarters[1:])
    got = [quarters[0]] + [cross(quarters[m], m) for m in range(1, 4)]
    same = in_order(core == 0, got[0], got[1], 2)
    other = in_order(core == 0, got[2], got[3], 2)
    start_piece = in_order(y == 0, same[:, None], other[:, None], 1)
    pieces = [start_piece] + [to_z(start_piece, d) for d in range(1, depth)]

    xfull = inputs.astype(f32)
    ratio = lax.rsqrt(jnp.mean(xfull * xfull, axis=-1, keepdims=True) + 1e-06)
    normed = xfull * ratio * norm_gain
    act = gelu_value(normed).astype(bf16)
    edge = send(
        act, lambda i: i + 4 if i % 4 == 3 else i - 4 if i % 4 == 0 else None
    )
    edge_across = send(
        edge, lambda i: i - 2 if i % 4 == 3 else i + 2 if i % 4 == 0 else None
    )
    edge = jnp.where(core == y, edge, edge_across)
    edge_other = cross(edge, 1)

    def around(value):
        across = cross(value, 2)
        return [value, cross(value, 1), across, cross(across, 1)]

    acts = around(act)
    cots = around(cotangent)
    point_rows = cut(point_weight, q * quarter, quarter, 0)

    width = channels // depth
    apart = width % 128 == 0
    outs = [((4, quarter, width), bf16 if d else f32) for d in range(depth)]
    if not apart:
        outs = [((depth, 4, quarter, width), f32)]
    branch, pre_grad, *terms = call(
        functools.partial(weight_kernel, depth),
        [((4 * rows, quarter), bf16)] * 2 + outs,
        [*pieces, *acts, edge, edge_other, *cots, point_rows],
        [pl.ANY] * (depth + 10) + [pltpu.VMEM],
        [
            pltpu.VMEM((6 * rows, channels), bf16),
            pltpu.VMEM((4 * rows, channels), bf16),
            pltpu.VMEM((3, depth, 2, own, 2 * quarter), bf16),
            pltpu.VMEM((3, channels, quarter), bf16),
            pltpu.VMEM((quarter, 4 * rows), bf16),
            pltpu.VMEM((quarter, 4 * rows), bf16),
            pltpu.SemaphoreType.DMA((depth + 10,)),
        ],
        8 * flops,
        40,
    )
    if not apart:
        terms = [terms[0][0]] + [terms[0][d].astype(bf16) for d in range(1, depth)]
    parts = [to_z(terms[d], d) for d in range(1, depth)]

    grad_low = send(pre_grad[3 * rows :], lambda i: i + 4)
    grad_high = send(pre_grad[:rows], lambda i: i - 4)
    shares = call(
        functools.partial(backward_kernel, depth),
        [((rows, channels), t) for t in (f32, bf16, f32, bf16)],
        [*pieces, grad_low, pre_grad, grad_high],
        [pl.ANY] * (depth + 3),
        [
            pltpu.VMEM((6 * rows, quarter), bf16),
            pltpu.VMEM((3, depth, 2, own, 2 * quarter), bf16),
            pltpu.VMEM((3, channels, quarter), bf16),
            pltpu.SemaphoreType.DMA((depth + 3,)),
        ],
        3 * flops,
        40,
    )
    mine = shares[0] + cross(shares[1], 1).astype(f32)
    far = shares[2] + cross(shares[3], 1).astype(f32)
    act_grad = mine + cross(far.astype(bf16), 2).astype(f32)
    scaled = act_grad * gelu_slope(normed) * norm_gain
    inner = jnp.mean(scaled * xfull, axis=-1, keepdims=True)
    input_grad = (
        cotangent.astype(f32) + ratio * scaled - xfull * ratio * ratio * ratio * inner
    ).astype(bf16)

    branch = branch.reshape(2, 2, rows, quarter)
    keep = cut(branch, core, 1, 1)[:, 0]
    chip = in_order(core == 0, keep, cross(cut(branch, 1 - core, 1, 1)[:, 0], 1), 2)
    keep = cut(chip, y, 1, 0)[0]
    full = in_order(y == 0, keep, cross(cut(chip, 1 - y, 1, 0)[0], 2), 1)
    outputs = (xfull + product(full, point_weight)).astype(bf16)

    total = terms[0]
    for part in parts:
        total = total + part.astype(f32)
    slices = [cut(total, toggled(q, m) * own, own, 2) for m in range(4)]
    slices = slices[:1] + [cross(slices[m].astype(bf16), m) for m in range(1, 4)]
    dilated_grad, point_grad = call(
        final_kernel,
        [((3, own, hidden), f32), ((hidden, own), f32)],
        slices,
        [pltpu.VMEM] * 4,
        [pltpu.VMEM((4, 4, quarter, own), f32)],
        1024,
        16,
    )
    return (outputs, input_grad, dilated_grad, point_grad)


def solution(mesh):
    placed = (
        P(("groups", "seq"), None),
        P(),
        P(None, "seq", None),
        P(),
        P(("groups", "seq"), None),
    )
    return jax.shard_map(
        local,
        mesh=mesh,
        in_specs=placed,
        out_specs=(
            P(("groups", "seq"), None),
            P(("groups", "seq"), None),
            P("groups", "seq", None),
            P("groups", "seq"),
        ),
        check_vma=False,
    )
```

time: 338 us -> 212 us (0.63)
  waiting for transfers between devices: 256 us -> 81 us
  starting transfers between devices: 10.3 us -> 87.8 us
  matrix products: 37.6 us -> 1.69 us
  Pallas kernels: 0 us -> 15.4 us
  between operations: 13.9 us -> 0.99 us
  local copies, waits for them, and re-layouts: 0.91 us -> 8.9 us
    reduce_scatter x2 -> x0, waiting for transfers between devices: 173 us -> none  [the longest x1 151 us: local(): lax.psum_scatter(tap_terms, 'seq', scatter_dimension=1, tiled=True)]
    ppermute x4 -> x28, starting transfers between devices: 10.1 us -> 87.8 us  [send(): lax.ppermute(value, 'seq', [p for p in pairs if p[1] is not None and 0 <=...]
    all_gather x1 -> x0, waiting for transfers between devices: 67.6 us -> none  [local(): taps_whole = lax.all_gather(dilated_weight, 'seq', axis=1, tiled=True)]
    ppermute x4 -> x28, waiting for transfers between devices: 14 us -> 81 us  [send(): lax.ppermute(value, 'seq', [p for p in pairs if p[1] is not None and 0 <=...]
    dot_general x12 -> x1, matrix products: 37.6 us -> 1.69 us  [product(): return jnp.dot(left, right, preferred_element_type=f32)]
    pallas_call x0 -> x3, Pallas kernels: none -> 15.4 us  [call(): pl.pallas_call(kernel, out_shape=[jax.ShapeDtypeStruct(s, t) for s, t in...]
    another operation x1 -> x0, other arithmetic: 11.7 us -> none  [local(): jnp.stack([rows_product(act_behind, pre_grad), rows_product(act, pre_grad...]
    select_n x0 -> x5, other arithmetic: none -> 5.28 us  [the longest x4 4.06 us: in_order(): jnp.where(first, jnp.concatenate([mine, other], axis), jnp.concatenate([o...]
  transfers between devices with their start and end apart: 7 -> 28, of which waited for: 4 -> 12; matrix products, arithmetic and copies ran while one was open for 15% -> 6% of each run, Pallas kernels for 0% -> 1%
where the time goes in v5:
time: 212 us; the launch traced here: 211 us
  starting transfers between devices  87.8 us (41%)
  waiting for transfers between devices  81 us (38%)
  other arithmetic  15.8 us (7%)
  Pallas kernels  15.4 us (7%)
  local copies, waits for them, and re-layouts  8.9 us (4%)
    ppermute x28, starting transfers between devices, send(): lax.ppermute(value, 'seq', [p for p in pairs if p[1] is not None and 0 <=...  87.8 us
    ppermute x28, waiting for transfers between devices, send(): lax.ppermute(value, 'seq', [p for p in pairs if p[1] is not None and 0 <=...  81 us
    pallas_call x3, Pallas kernels, call(): pl.pallas_call(kernel, out_shape=[jax.ShapeDtypeStruct(s, t) for s, t in...  15.4 us
  transfers between devices with their start and end apart: 28, of which 12 were waited for; matrix products, arithmetic and copies ran while one was open for 6% of the time, Pallas kernels for 1%

profile of v5, /device:TPU:9, one launch (start us, length us, event | category | flops | bytes accessed | tf_op | source)
XLA Modules:
  0.0 211.5 jit_solution(9180534226397653085)
XLA Ops:
  0.7 2.3 %dynamic-slice_bitcast_fusion.4 = (bf16[3,1,96,192]{3,2,1,0:T(8,128)(2,1)S(1)}, bf16[3,96,192]{2,1,0:T(8,128)(2,1)}, bf16[3,96,192]{2,1,0:T(8,128)(2,1)}, bf16[3,96,192]{2,1,0:T(8,128)(2,1)S(1)}) fusion(bf16[3,96,768]{2,1,0:T(8,128)(2,1)} %param.7, s32[]{:T(128)S(6)} %select_n.115, s32[]{:T(128)S(6)} %select_n.107, s32[]{:T(128)S(6)} %select_n.106, ...), kind=kLoop, calls=%fused_computation.48 | loop fusion | bytes 884752 | tf_op jit(solution)/shard_map/concatenate | solution.py:244
  8.9 14.2 %collective-permute-start = (bf16[3,96,192]{2,1,0:T(8,128)(2,1)}, bf16[3,96,192]{2,1,0:T(8,128)(2,1)}, u32[]{:S(2)}, u32[]{:S(2)}) collective-permute-start(bf16[3,96,192]{2,1,0:T(8,128)(2,1)} %get-tuple-element.47), channel_id=1, source_target_pairs={{0,1},{1,0},{2,3},{3,2},{4,5},{5,4},{6,7},{7,6},{8,9},{9,8},{10,11... | collective-permute-start | bytes 331784 | tf_op jit(solution)/shard_map/ppermute | solution.py:228
  27.6 28.8 %collective-permute-done.1 = bf16[3,96,192]{2,1,0:T(8,128)(2,1)} collective-permute-done((bf16[3,96,192]{2,1,0:T(8,128)(2,1)}, bf16[3,96,192]{2,1,0:T(8,128)(2,1)}, u32[]{:S(2)}, u32[]{:S(2)}) %collective-permute-start.1) | collective-permute-done | bytes 110624 | tf_op jit(solution)/shard_map/ppermute | solution.py:228
  59.1 2.9 %collective-permute-start.4 = (bf16[3,2,96,384]{3,2,1,0:T(8,128)(2,1)S(1)}, bf16[3,2,96,384]{3,2,1,0:T(8,128)(2,1)S(1)}, u32[]{:S(2)}, u32[]{:S(2)}) collective-permute-start(bf16[3,2,96,384]{3,2,1,0:T(8,128)(2,1)S(1)} %maximum_select_fusion.refs_0_), channel_id=1, source_target_pairs={{0,8},{1,9},{2,10},{3,11},{4,12},{5,13},{6,14},{7,15},{8,0},{9,1},... | collective-permute-start | bytes 1327112 | tf_op jit(solution)/shard_map/ppermute | solution.py:228
  65.3 28.0 %collective-permute-start.6 = (bf16[256,1536]{1,0:T(8,128)(2,1)}, bf16[256,1536]{1,0:T(8,128)(2,1)S(1)}, u32[]{:S(2)}, u32[]{:S(2)}) collective-permute-start(bf16[256,1536]{1,0:T(8,128)(2,1)} %fusion.6.refs_4_), channel_id=1, source_target_pairs={{0,1},{1,0},{2,3},{3,2},{4,5},{5,4},{6,7},{7,6},{8,9},{9,8},{10,11... | collective-permute-start | bytes 2359304 | tf_op jit(solution)/shard_map/ppermute | solution.py:228
  93.3 4.7 %collective-permute-start.12 = (bf16[256,1536]{1,0:T(8,128)(2,1)S(1)}, bf16[256,1536]{1,0:T(8,128)(2,1)S(1)}, u32[]{:S(2)}, u32[]{:S(2)}) collective-permute-start(bf16[256,1536]{1,0:T(8,128)(2,1)S(1)} %copy-done.4), channel_id=1, source_target_pairs={{0,1},{1,0},{2,3},{3,2},{4,5},{5,4},{6,7},{7,6},{8,9},{9,8},{10,11... | collective-permute-start | bytes 2359304 | tf_op jit(solution)/shard_map/ppermute | solution.py:228
  98.5 2.6 %collective-permute-done.5.refs_3_ = bf16[3,2,96,384]{3,2,1,0:T(8,128)(2,1)S(1)} collective-permute-done((bf16[3,2,96,384]{3,2,1,0:T(8,128)(2,1)S(1)}, bf16[3,2,96,384]{3,2,1,0:T(8,128)(2,1)S(1)}, u32[]{:S(2)}, u32[]{:S(2)}) %collective-permute-start.5) | collective-permute-done | bytes 442400 | tf_op jit(solution)/shard_map/ppermute | solution.py:228
  103.5 10.0 %shard_map.84 = (bf16[1024,192]{1,0:T(8,128)(2,1)S(1)}, bf16[1024,192]{1,0:T(8,128)(2,1)S(1)}, f32[4,192,384]{2,1,0:T(8,128)S(1)}, bf16[4,192,384]{2,1,0:T(8,128...) custom-call(bf16[3,2,96,384]{3,2,1,0:T(8,128)(2,1)S(1)} %maximum_select_fusion.refs_0_, ...), custom_call_target="tpu_custom_call" | custom-call | flops 4831838208 | bytes 13959168 | tf_op jit(solution)/shard_map/pallas_call | solution.py:201
  113.6 1.9 collective-permute-start.17
  115.5 3.5 %collective-permute-start.18 = (bf16[256,192]{1,0:T(8,128)(2,1)S(1)}, bf16[256,192]{1,0:T(8,128)(2,1)S(1)}, u32[]{:S(2)}, u32[]{:S(2)}) collective-permute-start(bf16[256,192]{1,0:T(8,128)(2,1)S(1)} %get-tuple-element.41), channel_id=1, source_target_pairs={{4,0},{5,1},{6,2},{7,3},{8,4},{9,5},{10,6},{11,7},{12,8},{13,9},{1... | collective-permute-start | bytes 294920 | tf_op jit(solution)/shard_map/ppermute | solution.py:228
  120.2 3.6 %collective-permute-done.18.refs_6_ = bf16[256,192]{1,0:T(8,128)(2,1)S(1)} collective-permute-done((bf16[256,192]{1,0:T(8,128)(2,1)S(1)}, bf16[256,192]{1,0:T(8,128)(2,1)S(1)}, u32[]{:S(2)}, u32[]{:S(2)}) %collective-permute-start.18) | collective-permute-done | bytes 98336 | tf_op jit(solution)/shard_map/ppermute | solution.py:228
  123.8 3.7 %shard_map.85 = (f32[256,1536]{1,0:T(8,128)S(1)}, bf16[256,1536]{1,0:T(8,128)(2,1)S(1)}, f32[256,1536]{1,0:T(8,128)S(1)}, bf16[256,1536]{1,0:T(8,128)(2,1)}) custom-call(bf16[3,2,96,384]{3,2,1,0:T(8,128)(2,1)S(1)} %maximum_select_fusion.refs_0_, bf16[3,2,96,384]{3,2,1,0:T(8,128)(2,1)S(1)} %collective-permute-done.3.refs_1_, ...), custom_call_target="tpu_custom_call" | custom-call | flops 1811939328 | bytes 7077888 | tf_op jit(solution)/shard_map/pallas_call | solution.py:201
  132.0 1.9 dynamic-slice_bitcast_fusion.1
  139.2 5.8 %collective-permute-start.16 = (bf16[256,384]{1,0:T(8,128)(2,1)S(1)}, bf16[256,384]{1,0:T(8,128)(2,1)S(1)}, u32[]{:S(2)}, u32[]{:S(2)}) collective-permute-start(bf16[256,384]{1,0:T(8,128)(2,1)S(1)} %get-tuple-element.50), channel_id=1, source_target_pairs={{0,2},{1,3},{2,0},{3,1},{4,6},{5,7},{6,4},{7,5},{8,10},{9,11},{10,... | collective-permute-start | bytes 589832 | tf_op jit(solution)/shard_map/ppermute | solution.py:228
  145.0 2.2 %add_convert_fusion = bf16[256,1536]{1,0:T(8,128)(2,1)} fusion(f32[256,1536]{1,0:T(8,128)S(1)} %copy-done.2, bf16[256,1536]{1,0:T(8,128)(2,1)} %collective-permute-done.20), kind=kLoop, calls=%fused_computation.27 | loop fusion | flops 1179648 | bytes 3145728 | tf_op jit(solution)/shard_map/convert_element_type | solution.py:324
  148.5 5.7 %collective-permute-start.21 = (bf16[256,1536]{1,0:T(8,128)(2,1)}, bf16[256,1536]{1,0:T(8,128)(2,1)}, u32[]{:S(2)}, u32[]{:S(2)}) collective-permute-start(bf16[256,1536]{1,0:T(8,128)(2,1)} %add_convert_fusion), channel_id=1, source_target_pairs={{0,2},{1,3},{2,0},{3,1},{4,6},{5,7},{6,4},{7,5},{8,10},{9,11},{10,... | collective-permute-start | bytes 2359304 | tf_op jit(solution)/shard_map/ppermute | solution.py:228
  154.2 31.6 %collective-permute-done.23 = bf16[4,192,384]{2,1,0:T(8,128)(2,1)S(1)} collective-permute-done((bf16[4,192,384]{2,1,0:T(8,128)(2,1)}, bf16[4,192,384]{2,1,0:T(8,128)(2,1)S(1)}, u32[]{:S(2)}, u32[]{:S(2)}) %collective-permute-start.23) | collective-permute-done | bytes 589856 | tf_op jit(solution)/shard_map/ppermute | solution.py:228
  185.8 2.1 collective-permute-done.24
  188.8 5.7 %collective-permute-start.26 = (bf16[4,192,96]{2,1,0:T(8,128)(2,1)S(1)}, bf16[4,192,96]{2,1,0:T(8,128)(2,1)S(1)}, u32[]{:S(2)}, u32[]{:S(2)}) collective-permute-start(bf16[4,192,96]{2,1,0:T(8,128)(2,1)S(1)} %get-tuple-element.39), channel_id=1, source_target_pairs={{0,2},{1,3},{2,0},{3,1},{4,6},{5,7},{6,4},{7,5},{8,10},{9,11},{10,... | collective-permute-start | bytes 442376 | tf_op jit(solution)/shard_map/ppermute | solution.py:228
  194.6 1.7 fusion
  196.5 3.2 %collective-permute-done.26.refs_2_ = bf16[4,192,96]{2,1,0:T(8,128)(2,1)S(1)} collective-permute-done((bf16[4,192,96]{2,1,0:T(8,128)(2,1)S(1)}, bf16[4,192,96]{2,1,0:T(8,128)(2,1)S(1)}, u32[]{:S(2)}, u32[]{:S(2)}) %collective-permute-start.26) | collective-permute-done | bytes 147488 | tf_op jit(solution)/shard_map/ppermute | solution.py:228
  199.7 4.2 %collective-permute-done.27.refs_3_ = bf16[4,192,96]{2,1,0:T(8,128)(2,1)S(1)} collective-permute-done((bf16[4,192,96]{2,1,0:T(8,128)(2,1)S(1)}, bf16[4,192,96]{2,1,0:T(8,128)(2,1)S(1)}, u32[]{:S(2)}, u32[]{:S(2)}) %collective-permute-start.27) | collective-permute-done | bytes 147488 | tf_op jit(solution)/shard_map/ppermute | solution.py:228
  204.0 1.6 shard_map.86
  206.5 3.5 %fusion.20 = (f32[256]{0:T(256)S(1)}, f32[256,1536]{1,0:T(8,128)S(1)}) fusion(bf16[256,1536]{1,0:T(8,128)(2,1)S(1)} %copy-done.14, f32[1536]{0:T(1024)S(1)} %copy-done.15, f32[256]{0:T(256)S(1)} %add_rsqrt_fusion, bf16[256,1536]{1,0:T(8,128)(2,1)} %collective-permute-done.21, f32[256,1536]{1,0:T(8,128)} %copy-done.3, ...), kind=kLoop, calls=%fused_computation.26 | loop fusion | flops 11009792 | bytes 5513216 | tf_op jit(solution)/shard_map/reduce_sum | solution.py:326
  (89 shorter events, 35.0 us)
Async XLA Ops:
  7.6 54.4 %collective-permute-start.10 = (bf16[256,1536]{1,0:T(8,128)(2,1)}, bf16[256,1536]{1,0:T(8,128)(2,1)}, u32[]{:S(2)}, u32[]{:S(2)}) collective-permute-start(bf16[256,1536]{1,0:T(8,128)(2,1)} %collective-permute-done.9), channel_id=1, source_target_pairs={{0,2},{3,1},{4,6},{7,5},{8,10},{11,9},{12,14},{15,13},{16,18},{19,... | collective-permute-start | bytes 2359304 | tf_op jit(solution)/shard_map/ppermute | solution.py:228
  8.9 16.0 %collective-permute-start = (bf16[3,96,192]{2,1,0:T(8,128)(2,1)}, bf16[3,96,192]{2,1,0:T(8,128)(2,1)}, u32[]{:S(2)}, u32[]{:S(2)}) collective-permute-start(bf16[3,96,192]{2,1,0:T(8,128)(2,1)} %get-tuple-element.47), channel_id=1, source_target_pairs={{0,1},{1,0},{2,3},{3,2},{4,5},{5,4},{6,7},{7,6},{8,9},{9,8},{10,11... | collective-permute-start | bytes 331784 | tf_op jit(solution)/shard_map/ppermute | solution.py:228
  23.1 74.9 %collective-permute-start.7 = (bf16[256,1536]{1,0:T(8,128)(2,1)}, bf16[256,1536]{1,0:T(8,128)(2,1)}, u32[]{:S(2)}, u32[]{:S(2)}) collective-permute-start(bf16[256,1536]{1,0:T(8,128)(2,1)} %fusion.6.refs_4_), channel_id=1, source_target_pairs={{0,2},{1,3},{2,0},{3,1},{4,6},{5,7},{6,4},{7,5},{8,10},{9,11},{10,... | collective-permute-start | bytes 2359304 | tf_op jit(solution)/shard_map/ppermute | solution.py:228
  23.1 33.3 %collective-permute-start.1 = (bf16[3,96,192]{2,1,0:T(8,128)(2,1)}, bf16[3,96,192]{2,1,0:T(8,128)(2,1)}, u32[]{:S(2)}, u32[]{:S(2)}) collective-permute-start(bf16[3,96,192]{2,1,0:T(8,128)(2,1)} %get-tuple-element.46), channel_id=1, source_target_pairs={{0,2},{1,3},{2,0},{3,1},{4,6},{5,7},{6,4},{7,5},{8,10},{9,11},{10,... | collective-permute-start | bytes 331784 | tf_op jit(solution)/shard_map/ppermute | solution.py:228
  24.6 31.9 %collective-permute-start.2 = (bf16[3,96,192]{2,1,0:T(8,128)(2,1)S(1)}, bf16[3,96,192]{2,1,0:T(8,128)(2,1)}, u32[]{:S(2)}, u32[]{:S(2)}) collective-permute-start(bf16[3,96,192]{2,1,0:T(8,128)(2,1)S(1)} %get-tuple-element.48), channel_id=1, source_target_pairs={{0,3},{1,2},{2,1},{3,0},{4,7},{5,6},{6,5},{7,4},{8,11},{9,10},{10,... | collective-permute-start | bytes 331784 | tf_op jit(solution)/shard_map/ppermute | solution.py:228
  24.9 73.0 %collective-permute-start.13 = (bf16[256,1536]{1,0:T(8,128)(2,1)S(1)}, bf16[256,1536]{1,0:T(8,128)(2,1)S(1)}, u32[]{:S(2)}, u32[]{:S(2)}) collective-permute-start(bf16[256,1536]{1,0:T(8,128)(2,1)S(1)} %copy-done.4), channel_id=1, source_target_pairs={{0,2},{1,3},{2,0},{3,1},{4,6},{5,7},{6,4},{7,5},{8,10},{9,11},{10,... | collective-permute-start | bytes 2359304 | tf_op jit(solution)/shard_map/ppermute | solution.py:228
  57.8 7.5 %collective-permute-start.3 = (bf16[3,2,96,384]{3,2,1,0:T(8,128)(2,1)S(1)}, bf16[3,2,96,384]{3,2,1,0:T(8,128)(2,1)S(1)}, u32[]{:S(2)}, u32[]{:S(2)}) collective-permute-start(bf16[3,2,96,384]{3,2,1,0:T(8,128)(2,1)S(1)} %maximum_select_fusion.refs_0_), channel_id=1, source_target_pairs={{0,4},{1,5},{2,6},{3,7},{4,8},{5,9},{6,10},{7,11},{8,12},{9,13},{1... | collective-permute-start | bytes 1327112 | tf_op jit(solution)/shard_map/ppermute | solution.py:228
  59.1 34.1 %collective-permute-start.4 = (bf16[3,2,96,384]{3,2,1,0:T(8,128)(2,1)S(1)}, bf16[3,2,96,384]{3,2,1,0:T(8,128)(2,1)S(1)}, u32[]{:S(2)}, u32[]{:S(2)}) collective-permute-start(bf16[3,2,96,384]{3,2,1,0:T(8,128)(2,1)S(1)} %maximum_select_fusion.refs_0_), channel_id=1, source_target_pairs={{0,8},{1,9},{2,10},{3,11},{4,12},{5,13},{6,14},{7,15},{8,0},{9,1},... | collective-permute-start | bytes 1327112 | tf_op jit(solution)/shard_map/ppermute | solution.py:228
  62.1 39.0 %collective-permute-start.5 = (bf16[3,2,96,384]{3,2,1,0:T(8,128)(2,1)S(1)}, bf16[3,2,96,384]{3,2,1,0:T(8,128)(2,1)S(1)}, u32[]{:S(2)}, u32[]{:S(2)}) collective-permute-start(bf16[3,2,96,384]{3,2,1,0:T(8,128)(2,1)S(1)} %maximum_select_fusion.refs_0_), channel_id=1, source_target_pairs={{0,12},{1,13},{2,14},{3,15},{4,0},{5,1},{6,2},{7,3},{8,4},{9,5},{1... | collective-permute-start | bytes 1327112 | tf_op jit(solution)/shard_map/ppermute | solution.py:228
  65.3 36.3 %collective-permute-start.6 = (bf16[256,1536]{1,0:T(8,128)(2,1)}, bf16[256,1536]{1,0:T(8,128)(2,1)S(1)}, u32[]{:S(2)}, u32[]{:S(2)}) collective-permute-start(bf16[256,1536]{1,0:T(8,128)(2,1)} %fusion.6.refs_4_), channel_id=1, source_target_pairs={{0,1},{1,0},{2,3},{3,2},{4,5},{5,4},{6,7},{7,6},{8,9},{9,8},{10,11... | collective-permute-start | bytes 2359304 | tf_op jit(solution)/shard_map/ppermute | solution.py:228
  93.3 8.4 %collective-permute-start.12 = (bf16[256,1536]{1,0:T(8,128)(2,1)S(1)}, bf16[256,1536]{1,0:T(8,128)(2,1)S(1)}, u32[]{:S(2)}, u32[]{:S(2)}) collective-permute-start(bf16[256,1536]{1,0:T(8,128)(2,1)S(1)} %copy-done.4), channel_id=1, source_target_pairs={{0,1},{1,0},{2,3},{3,2},{4,5},{5,4},{6,7},{7,6},{8,9},{9,8},{10,11... | collective-permute-start | bytes 2359304 | tf_op jit(solution)/shard_map/ppermute | solution.py:228
  98.0 4.2 %collective-permute-start.8 = (bf16[256,1536]{1,0:T(8,128)(2,1)}, bf16[256,1536]{1,0:T(8,128)(2,1)S(1)}, u32[]{:S(2)}, u32[]{:S(2)}) collective-permute-start(bf16[256,1536]{1,0:T(8,128)(2,1)} %collective-permute-done.7.refs_6_), channel_id=1, source_target_pairs={{0,1},{1,0},{2,3},{3,2},{4,5},{5,4},{6,7},{7,6},{8,9},{9,8},{10,11... | collective-permute-start | bytes 2359304 | tf_op jit(solution)/shard_map/ppermute | solution.py:228
  113.6 6.6 %collective-permute-start.17 = (bf16[256,192]{1,0:T(8,128)(2,1)S(1)}, bf16[256,192]{1,0:T(8,128)(2,1)S(1)}, u32[]{:S(2)}, u32[]{:S(2)}) collective-permute-start(bf16[256,192]{1,0:T(8,128)(2,1)S(1)} %get-tuple-element.42), channel_id=1, source_target_pairs={{0,4},{1,5},{2,6},{3,7},{4,8},{5,9},{6,10},{7,11},{8,12},{9,13},{1... | collective-permute-start | bytes 294920 | tf_op jit(solution)/shard_map/ppermute | solution.py:228
  115.5 8.3 %collective-permute-start.18 = (bf16[256,192]{1,0:T(8,128)(2,1)S(1)}, bf16[256,192]{1,0:T(8,128)(2,1)S(1)}, u32[]{:S(2)}, u32[]{:S(2)}) collective-permute-start(bf16[256,192]{1,0:T(8,128)(2,1)S(1)} %get-tuple-element.41), channel_id=1, source_target_pairs={{4,0},{5,1},{6,2},{7,3},{8,4},{9,5},{10,6},{11,7},{12,8},{13,9},{1... | collective-permute-start | bytes 294920 | tf_op jit(solution)/shard_map/ppermute | solution.py:228
  130.8 8.4 %collective-permute-start.20 = (bf16[256,1536]{1,0:T(8,128)(2,1)}, bf16[256,1536]{1,0:T(8,128)(2,1)}, u32[]{:S(2)}, u32[]{:S(2)}) collective-permute-start(bf16[256,1536]{1,0:T(8,128)(2,1)} %get-tuple-element.25), channel_id=1, source_target_pairs={{0,1},{1,0},{2,3},{3,2},{4,5},{5,4},{6,7},{7,6},{8,9},{9,8},{10,11... | collective-permute-start | bytes 2359304 | tf_op jit(solution)/shard_map/ppermute | solution.py:228
  133.9 14.6 %collective-permute-start.22 = (bf16[4,192,384]{2,1,0:T(8,128)(2,1)}, bf16[4,192,384]{2,1,0:T(8,128)(2,1)S(1)}, u32[]{:S(2)}, u32[]{:S(2)}) collective-permute-start(bf16[4,192,384]{2,1,0:T(8,128)(2,1)} %copy-done.11), channel_id=1, source_target_pairs={{0,4},{1,5},{2,6},{3,7},{4,8},{5,9},{6,10},{7,11},{8,12},{9,13},{1... | collective-permute-start | bytes 1769480 | tf_op jit(solution)/shard_map/ppermute | solution.py:228
  135.3 50.4 %collective-permute-start.23 = (bf16[4,192,384]{2,1,0:T(8,128)(2,1)}, bf16[4,192,384]{2,1,0:T(8,128)(2,1)S(1)}, u32[]{:S(2)}, u32[]{:S(2)}) collective-permute-start(bf16[4,192,384]{2,1,0:T(8,128)(2,1)} %copy-done.10), channel_id=1, source_target_pairs={{0,8},{1,9},{2,10},{3,11},{4,12},{5,13},{6,14},{7,15},{8,0},{9,1},... | collective-permute-start | bytes 1769480 | tf_op jit(solution)/shard_map/ppermute | solution.py:228
  135.8 52.1 %collective-permute-start.24 = (bf16[4,192,384]{2,1,0:T(8,128)(2,1)}, bf16[4,192,384]{2,1,0:T(8,128)(2,1)S(1)}, u32[]{:S(2)}, u32[]{:S(2)}) collective-permute-start(bf16[4,192,384]{2,1,0:T(8,128)(2,1)} %copy-done.9), channel_id=1, source_target_pairs={{0,12},{1,13},{2,14},{3,15},{4,0},{5,1},{6,2},{7,3},{8,4},{9,5},{1... | collective-permute-start | bytes 1769480 | tf_op jit(solution)/shard_map/ppermute | solution.py:228
  136.6 69.8 %collective-permute-start.19 = (bf16[256,1536]{1,0:T(8,128)(2,1)}, bf16[256,1536]{1,0:T(8,128)(2,1)}, u32[]{:S(2)}, u32[]{:S(2)}) collective-permute-start(bf16[256,1536]{1,0:T(8,128)(2,1)} %copy-done.8), channel_id=1, source_target_pairs={{0,1},{1,0},{2,3},{3,2},{4,5},{5,4},{6,7},{7,6},{8,9},{9,8},{10,11... | collective-permute-start | bytes 2359304 | tf_op jit(solution)/shard_map/ppermute | solution.py:228
  139.2 55.3 %collective-permute-start.16 = (bf16[256,384]{1,0:T(8,128)(2,1)S(1)}, bf16[256,384]{1,0:T(8,128)(2,1)S(1)}, u32[]{:S(2)}, u32[]{:S(2)}) collective-permute-start(bf16[256,384]{1,0:T(8,128)(2,1)S(1)} %get-tuple-element.50), channel_id=1, source_target_pairs={{0,2},{1,3},{2,0},{3,1},{4,6},{5,7},{6,4},{7,5},{8,10},{9,11},{10,... | collective-permute-start | bytes 589832 | tf_op jit(solution)/shard_map/ppermute | solution.py:228
  148.5 58.0 %collective-permute-start.21 = (bf16[256,1536]{1,0:T(8,128)(2,1)}, bf16[256,1536]{1,0:T(8,128)(2,1)}, u32[]{:S(2)}, u32[]{:S(2)}) collective-permute-start(bf16[256,1536]{1,0:T(8,128)(2,1)} %add_convert_fusion), channel_id=1, source_target_pairs={{0,2},{1,3},{2,0},{3,1},{4,6},{5,7},{6,4},{7,5},{8,10},{9,11},{10,... | collective-permute-start | bytes 2359304 | tf_op jit(solution)/shard_map/ppermute | solution.py:228
  188.4 8.1 %collective-permute-start.25 = (bf16[4,192,96]{2,1,0:T(8,128)(2,1)S(1)}, bf16[4,192,96]{2,1,0:T(8,128)(2,1)S(1)}, u32[]{:S(2)}, u32[]{:S(2)}) collective-permute-start(bf16[4,192,96]{2,1,0:T(8,128)(2,1)S(1)} %get-tuple-element.40), channel_id=1, source_target_pairs={{0,1},{1,0},{2,3},{3,2},{4,5},{5,4},{6,7},{7,6},{8,9},{9,8},{10,11... | collective-permute-start | bytes 442376 | tf_op jit(solution)/shard_map/ppermute | solution.py:228
  188.8 10.9 %collective-permute-start.26 = (bf16[4,192,96]{2,1,0:T(8,128)(2,1)S(1)}, bf16[4,192,96]{2,1,0:T(8,128)(2,1)S(1)}, u32[]{:S(2)}, u32[]{:S(2)}) collective-permute-start(bf16[4,192,96]{2,1,0:T(8,128)(2,1)S(1)} %get-tuple-element.39), channel_id=1, source_target_pairs={{0,2},{1,3},{2,0},{3,1},{4,6},{5,7},{6,4},{7,5},{8,10},{9,11},{10,... | collective-permute-start | bytes 442376 | tf_op jit(solution)/shard_map/ppermute | solution.py:228
  194.6 9.4 %collective-permute-start.27 = (bf16[4,192,96]{2,1,0:T(8,128)(2,1)S(1)}, bf16[4,192,96]{2,1,0:T(8,128)(2,1)S(1)}, u32[]{:S(2)}, u32[]{:S(2)}) collective-permute-start(bf16[4,192,96]{2,1,0:T(8,128)(2,1)S(1)} %get-tuple-element.38), channel_id=1, source_target_pairs={{0,3},{1,2},{2,1},{3,0},{4,7},{5,6},{6,5},{7,4},{8,11},{9,10},{10,... | collective-permute-start | bytes 442376 | tf_op jit(solution)/shard_map/ppermute | solution.py:228
  (20 other events, 280.3 us)

commit v6 on v5

--- a/solution.py
+++ b/solution.py
@@ -60,12 +60,23 @@
 
 
 def started(pairs, sems, first=0):
-    copies = [
-        pltpu.make_async_copy(src, dst, sems.at[first + i])
-        for i, (src, dst) in enumerate(pairs)
-    ]
-    for copy in copies:
-        copy.start()
+    copies = []
+    for i, (src, dst) in enumerate(pairs):
+        sem = sems.at[first + i]
+        if isinstance(src, tuple):
+            chosen, src, other = src
+
+            @pl.when(chosen)
+            def _(src=src, dst=dst, sem=sem):
+                pltpu.make_async_copy(src, dst, sem).start()
+
+            @pl.when(jnp.logical_not(chosen))
+            def _(src=other, dst=dst, sem=sem):
+                pltpu.make_async_copy(src, dst, sem).start()
+
+        else:
+            pltpu.make_async_copy(src, dst, sem).start()
+        copies.append(pltpu.make_async_copy(src, dst, sem))
     return copies
 
 
@@ -74,13 +85,38 @@
         copy.wait()
 
 
-def tap_pairs(pieces, packed):
+def tap_pairs(depth, pieces, packed):
     z, _ = position()
-    depth = len(pieces)
+    if depth == 4:
+        own, two, up, down, passed = pieces
+        return [
+            (own, packed.at[:, z]),
+            (two, packed.at[:, lax.rem(z + 2, 4)]),
+            ((z == 0, passed, up), packed.at[:, lax.rem(z + 3, 4)]),
+            ((z == 3, passed, down), packed.at[:, lax.rem(z + 1, 4)]),
+        ]
     return [
         (piece, packed.at[:, lax.rem(z + depth - d, depth)])
         for d, piece in enumerate(pieces)
     ]
+
+
+def targets(depth, z):
+    if depth == 4:
+        return [
+            jnp.where(z == 0, 3, 0),
+            jnp.where(z < 2, z + 2, z - 2),
+            jnp.minimum(z + 1, 3),
+            jnp.maximum(z - 1, 0),
+            z,
+        ]
+    return [lax.rem(z + d, depth) for d in range(1, depth)] + [z]
+
+
+def target_types(depth):
+    if depth == 4:
+        return [bf16, f32, bf16, bf16, f32]
+    return [bf16] * (depth - 1) + [f32]
 
 
 def unpack(packed, taps):
@@ -95,13 +131,14 @@
 
 
 def weight_kernel(depth, *refs):
-    pieces = refs[:depth]
-    acts = refs[depth : depth + 4]
-    edge, edge_other = refs[depth + 4 : depth + 6]
-    cots = refs[depth + 6 : depth + 10]
-    point = refs[depth + 10]
-    branch, grad = refs[depth + 11 : depth + 13]
-    outs = refs[depth + 13 : -7]
+    count = depth + (depth == 4)
+    pieces = refs[:count]
+    acts = refs[count : count + 4]
+    edge, edge_other = refs[count + 4 : count + 6]
+    cots = refs[count + 6 : count + 10]
+    point = refs[count + 10]
+    branch, grad = refs[count + 11 : count + 13]
+    outs = refs[count + 13 : -7]
     wide, wide_cot, packed, taps, grads, branches, sems = refs[-7:]
     z, q = position()
     rows = acts[0].shape[0]
@@ -112,7 +149,7 @@
             (edge, wide.at[within(5 * (1 - core), rows)]),
             (edge_other, wide.at[within(5 * core, rows)]),
         ]
-        + tap_pairs(pieces, packed),
+        + tap_pairs(depth, pieces, packed),
         sems,
     )
     second = started(
@@ -136,13 +173,14 @@
         grad[here] = value.astype(bf16)
         grads[:, here] = value.T.astype(bf16)
     width = wide.shape[1] // depth
-    for i in range(depth):
+    if len(outs) > 1:
+        where = [within(target, width) for target in targets(depth, z)]
+    else:
+        where = [pl.ds(i * width, width) for i in range(depth)]
+    for i, lanes in enumerate(where):
         if len(outs) > 1:
-            target = lax.rem(z + i + 1, depth)
-            lanes = within(target, width)
-            out = outs[(i + 1) % depth]
+            out = outs[i]
         else:
-            lanes = pl.ds(i * width, width)
             out = outs[0].at[lax.rem(i + depth - z, depth)]
         for k in range(3):
             out[k] = product(
@@ -152,10 +190,11 @@
 
 
 def backward_kernel(depth, *refs):
-    pieces = refs[:depth]
-    low, grad, high = refs[depth : depth + 3]
-    outs = refs[depth + 3 : depth + 7]
-    wide, packed, taps, sems = refs[depth + 7 :]
+    count = depth + (depth == 4)
+    pieces = refs[:count]
+    low, grad, high = refs[count : count + 3]
+    outs = refs[count + 3 : count + 7]
+    wide, packed, taps, sems = refs[count + 7 :]
     _, q = position()
     rows = low.shape[0]
     finish(
@@ -165,7 +204,7 @@
                 (grad, wide.at[pl.ds(rows, 4 * rows)]),
                 (high, wide.at[pl.ds(5 * rows, rows)]),
             ]
-            + tap_pairs(pieces, packed),
+            + tap_pairs(depth, pieces, packed),
             sems,
         )
     )
@@ -254,39 +293,49 @@
     same = in_order(core == 0, got[0], got[1], 2)
     other = in_order(core == 0, got[2], got[3], 2)
     start_piece = in_order(y == 0, same[:, None], other[:, None], 1)
-    pieces = [start_piece] + [to_z(start_piece, d) for d in range(1, depth)]
+
+    def line(value, pairs):
+        return lax.ppermute(
+            value,
+            "seq",
+            [(4 * a + i, 4 * b + i) for a, b in pairs for i in range(4)],
+        )
+
+    if depth == 4:
+        two = to_z(start_piece, 2)
+        up = line(start_piece, [(0, 1), (1, 2), (2, 3)])
+        down = line(start_piece, [(1, 0), (2, 1), (3, 2)])
+        pieces = [start_piece, two, up, down, line(two, [(2, 3), (1, 0)])]
+    else:
+        pieces = [start_piece] + [to_z(start_piece, d) for d in range(1, depth)]
 
     xfull = inputs.astype(f32)
     ratio = lax.rsqrt(jnp.mean(xfull * xfull, axis=-1, keepdims=True) + 1e-06)
     normed = xfull * ratio * norm_gain
     act = gelu_value(normed).astype(bf16)
+    act_late = after(act, start_piece)
+    cot_late = after(cotangent, start_piece)
+    act_across = cross(act_late, 2)
     edge = send(
-        act, lambda i: i + 4 if i % 4 == 3 else i - 4 if i % 4 == 0 else None
-    )
-    edge_across = send(
-        edge, lambda i: i - 2 if i % 4 == 3 else i + 2 if i % 4 == 0 else None
-    )
-    edge = jnp.where(core == y, edge, edge_across)
+        jnp.where(core == y, act_late, act_across),
+        lambda i: i + 4 if i % 2 else i - 4,
+    )
     edge_other = cross(edge, 1)
-
-    def around(value):
-        across = cross(value, 2)
-        return [value, cross(value, 1), across, cross(across, 1)]
-
-    acts = around(act)
-    cots = around(cotangent)
+    cot_across = cross(after(cot_late, act_across), 2)
+    acts = [act_late, cross(act_late, 1), act_across, cross(act_across, 1)]
+    cots = [cot_late, cross(cot_late, 1), cot_across, cross(cot_across, 1)]
     point_rows = cut(point_weight, q * quarter, quarter, 0)
 
     width = channels // depth
     apart = width % 128 == 0
-    outs = [((4, quarter, width), bf16 if d else f32) for d in range(depth)]
+    outs = [((4, quarter, width), t) for t in target_types(depth)]
     if not apart:
         outs = [((depth, 4, quarter, width), f32)]
     branch, pre_grad, *terms = call(
         functools.partial(weight_kernel, depth),
         [((4 * rows, quarter), bf16)] * 2 + outs,
         [*pieces, *acts, edge, edge_other, *cots, point_rows],
-        [pl.ANY] * (depth + 10) + [pltpu.VMEM],
+        [pl.ANY] * (len(pieces) + 10) + [pltpu.VMEM],
         [
             pltpu.VMEM((6 * rows, channels), bf16),
             pltpu.VMEM((4 * rows, channels), bf16),
@@ -300,8 +349,20 @@
         40,
     )
     if not apart:
-        terms = [terms[0][0]] + [terms[0][d].astype(bf16) for d in range(1, depth)]
-    parts = [to_z(terms[d], d) for d in range(1, depth)]
+        terms = [terms[0][d].astype(bf16) for d in range(1, depth)] + [terms[0][0]]
+    if depth == 4:
+        three, two, up, down, total = terms
+        passed = line(three, [(0, 1), (3, 2)])
+        joined = line((two + passed.astype(f32)).astype(bf16), [(1, 3), (2, 0)])
+        parts = [
+            line(two.astype(bf16), [(0, 2), (3, 1)]),
+            line(up, [(0, 1), (1, 2), (2, 3)]),
+            line(down, [(1, 0), (2, 1), (3, 2)]),
+            joined,
+        ]
+    else:
+        total = terms[-1]
+        parts = [to_z(term, d + 1) for d, term in enumerate(terms[:-1])]
 
     grad_low = send(pre_grad[3 * rows :], lambda i: i + 4)
     grad_high = send(pre_grad[:rows], lambda i: i - 4)
@@ -309,7 +370,7 @@
         functools.partial(backward_kernel, depth),
         [((rows, channels), t) for t in (f32, bf16, f32, bf16)],
         [*pieces, grad_low, pre_grad, grad_high],
-        [pl.ANY] * (depth + 3),
+        [pl.ANY] * (len(pieces) + 3),
         [
             pltpu.VMEM((6 * rows, quarter), bf16),
             pltpu.VMEM((3, depth, 2, own, 2 * quarter), bf16),
@@ -335,11 +396,11 @@
     full = in_order(y == 0, keep, cross(cut(chip, 1 - y, 1, 0)[0], 2), 1)
     outputs = (xfull + product(full, point_weight)).astype(bf16)
 
-    total = terms[0]
     for part in parts:
         total = total + part.astype(f32)
     slices = [cut(total, toggled(q, m) * own, own, 2) for m in range(4)]
     slices = slices[:1] + [cross(slices[m].astype(bf16), m) for m in range(1, 4)]
+    slices[3] = after(slices[3], input_grad, outputs)
     dilated_grad, point_grad = call(
         final_kernel,
         [((3, own, hidden), f32), ((hidden, own), f32)],

time: 212 us -> 176 us (0.83)
  the two profiles are of different devices: /device:TPU:9 before, /device:TPU:1 now
where the time goes in v6:
time: 176 us; the launch traced here: 175 us
  waiting for transfers between devices  77.2 us (44%)
  starting transfers between devices  48.1 us (27%)
  Pallas kernels  17.2 us (10%)
  local copies, waits for them, and re-layouts  17.1 us (10%)
  other arithmetic  13 us (7%)
    ppermute x8, waiting for transfers between devices, line(): lax.ppermute(value, 'seq', [(4 * a + i, 4 * b + i) for a, b in pairs for...  51.5 us
    ppermute x22, waiting for transfers between devices, send(): lax.ppermute(value, 'seq', [p for p in pairs if p[1] is not None and 0 <=...  25.7 us
    ppermute x22, starting transfers between devices, send(): lax.ppermute(value, 'seq', [p for p in pairs if p[1] is not None and 0 <=...  24.5 us
    ppermute x8, starting transfers between devices, line(): lax.ppermute(value, 'seq', [(4 * a + i, 4 * b + i) for a, b in pairs for...  23.6 us
    pallas_call x3, Pallas kernels, call(): pl.pallas_call(kernel, out_shape=[jax.ShapeDtypeStruct(s, t) for s, t in...  17.2 us
    unnamed x61, local copies, waits for them, and re-layouts  13.4 us
    select_n x4, other arithmetic, in_order(): jnp.where(first, jnp.concatenate([mine, other], axis), jnp.concatenate([o...  4.61 us
  transfers between devices with their start and end apart: 30, of which 9 were waited for; matrix products, arithmetic and copies ran while one was open for 8% of the time, Pallas kernels for 2%

profile of v6, /device:TPU:1, one launch (start us, length us, event | category | flops | bytes accessed | tf_op | source)
XLA Modules:
  0.0 175.4 jit_solution(17724688972946667893)
XLA Ops:
  0.7 2.3 %dynamic-slice_bitcast_fusion.4 = (bf16[3,1,96,192]{3,2,1,0:T(8,128)(2,1)S(1)}, bf16[3,96,192]{2,1,0:T(8,128)(2,1)}, bf16[3,96,192]{2,1,0:T(8,128)(2,1)}, bf16[3,96,192]{2,1,0:T(8,128)(2,1)S(1)}) fusion(bf16[3,96,768]{2,1,0:T(8,128)(2,1)} %param.7, s32[]{:T(128)S(6)} %select_n.115, s32[]{:T(128)S(6)} %select_n.107, s32[]{:T(128)S(6)} %select_n.106, ...), kind=kLoop, calls=%fused_computation.49 | loop fusion | bytes 884752 | tf_op jit(solution)/shard_map/concatenate | solution.py:283
  3.1 2.7 %collective-permute-start.1 = (bf16[3,96,192]{2,1,0:T(8,128)(2,1)}, bf16[3,96,192]{2,1,0:T(8,128)(2,1)}, u32[]{:S(2)}, u32[]{:S(2)}) collective-permute-start(bf16[3,96,192]{2,1,0:T(8,128)(2,1)} %get-tuple-element.58), channel_id=1, source_target_pairs={{0,2},{1,3},{2,0},{3,1},{4,6},{5,7},{6,4},{7,5},{8,10},{9,11},{10,... | collective-permute-start | bytes 331784 | tf_op jit(solution)/shard_map/ppermute | solution.py:267
  8.0 2.3 %collective-permute-done.1 = bf16[3,96,192]{2,1,0:T(8,128)(2,1)} collective-permute-done((bf16[3,96,192]{2,1,0:T(8,128)(2,1)}, bf16[3,96,192]{2,1,0:T(8,128)(2,1)}, u32[]{:S(2)}, u32[]{:S(2)}) %collective-permute-start.1) | collective-permute-done | bytes 110624 | tf_op jit(solution)/shard_map/ppermute | solution.py:267
  10.4 3.2 %collective-permute-done.2 = bf16[3,96,192]{2,1,0:T(8,128)(2,1)} collective-permute-done((bf16[3,96,192]{2,1,0:T(8,128)(2,1)S(1)}, bf16[3,96,192]{2,1,0:T(8,128)(2,1)}, u32[]{:S(2)}, u32[]{:S(2)}) %collective-permute-start.2) | collective-permute-done | bytes 110624 | tf_op jit(solution)/shard_map/ppermute | solution.py:267
  17.0 2.3 %collective-permute-start.3 = (bf16[3,2,96,384]{3,2,1,0:T(8,128)(2,1)}, bf16[3,2,96,384]{3,2,1,0:T(8,128)(2,1)S(1)}, u32[]{:S(2)}, u32[]{:S(2)}) collective-permute-start(bf16[3,2,96,384]{3,2,1,0:T(8,128)(2,1)} %maximum_select_fusion.refs_0_), channel_id=1, source_target_pairs={{0,8},{1,9},{2,10},{3,11},{4,12},{5,13},{6,14},{7,15},{8,0},{9,1},... | collective-permute-start | bytes 1327112 | tf_op jit(solution)/shard_map/ppermute | solution.py:267
  19.3 15.2 %collective-permute-done.8.refs_7_ = bf16[256,1536]{1,0:T(8,128)(2,1)} collective-permute-done((bf16[256,1536]{1,0:T(8,128)(2,1)S(1)}, bf16[256,1536]{1,0:T(8,128)(2,1)}, u32[]{:S(2)}, u32[]{:S(2)}) %collective-permute-start.8) | collective-permute-done | bytes 786464 | tf_op jit(solution)/shard_map/ppermute | solution.py:267
  37.2 3.3 %collective-permute-start.10 = (bf16[256,1536]{1,0:T(8,128)(2,1)S(1)}, bf16[256,1536]{1,0:T(8,128)(2,1)S(1)}, u32[]{:S(2)}, u32[]{:S(2)}) collective-permute-start(bf16[256,1536]{1,0:T(8,128)(2,1)S(1)} %broadcast_select_fusion), channel_id=1, source_target_pairs={{1,5},{3,7},{4,0},{5,9},{6,2},{7,11},{8,4},{9,13},{10,6},{11,15},{... | collective-permute-start | bytes 2359304 | tf_op jit(solution)/shard_map/ppermute | solution.py:267
  40.4 3.2 %collective-permute-start.4 = (bf16[3,2,96,384]{3,2,1,0:T(8,128)(2,1)S(1)}, bf16[3,2,96,384]{3,2,1,0:T(8,128)(2,1)S(1)}, u32[]{:S(2)}, u32[]{:S(2)}) collective-permute-start(bf16[3,2,96,384]{3,2,1,0:T(8,128)(2,1)S(1)} %copy-done.9), channel_id=1, source_target_pairs={{0,4},{1,5},{2,6},{3,7},{4,8},{5,9},{6,10},{7,11},{8,12},{9,13},{1... | collective-permute-start | bytes 1327112 | tf_op jit(solution)/shard_map/ppermute | solution.py:298
  45.0 13.7 %collective-permute-done.4.refs_2_ = bf16[3,2,96,384]{3,2,1,0:T(8,128)(2,1)S(1)} collective-permute-done((bf16[3,2,96,384]{3,2,1,0:T(8,128)(2,1)S(1)}, bf16[3,2,96,384]{3,2,1,0:T(8,128)(2,1)S(1)}, u32[]{:S(2)}, u32[]{:S(2)}) %collective-permute-start.4) | collective-permute-done | bytes 442400 | tf_op jit(solution)/shard_map/ppermute | solution.py:298
  58.8 2.0 %collective-permute-start.9 = (bf16[256,1536]{1,0:T(8,128)(2,1)}, bf16[256,1536]{1,0:T(8,128)(2,1)S(1)}, u32[]{:S(2)}, u32[]{:S(2)}) collective-permute-start(bf16[256,1536]{1,0:T(8,128)(2,1)} %collective-permute-done.8.refs_7_), channel_id=1, source_target_pairs={{0,1},{1,0},{2,3},{3,2},{4,5},{5,4},{6,7},{7,6},{8,9},{9,8},{10,11... | collective-permute-start | bytes 2359304 | tf_op jit(solution)/shard_map/ppermute | solution.py:267
  62.7 12.2 %collective-permute-done.6.refs_4_ = bf16[3,2,96,384]{3,2,1,0:T(8,128)(2,1)S(1)} collective-permute-done((bf16[3,2,96,384]{3,2,1,0:T(8,128)(2,1)S(1)}, bf16[3,2,96,384]{3,2,1,0:T(8,128)(2,1)S(1)}, u32[]{:S(2)}, u32[]{:S(2)}) %collective-permute-start.6) | collective-permute-done | bytes 442400 | tf_op jit(solution)/shard_map/ppermute | solution.py:298
  75.0 11.8 %shard_map.84 = (bf16[1024,192]{1,0:T(8,128)(2,1)S(1)}, bf16[1024,192]{1,0:T(8,128)(2,1)S(1)}, bf16[4,192,384]{2,1,0:T(8,128)(2,1)S(1)}, f32[4,192,384]{2,1,0:T(...) custom-call(bf16[3,2,96,384]{3,2,1,0:T(8,128)(2,1)S(1)} %copy-done.9, ...), custom_call_target="tpu_custom_call" | custom-call | flops 4831838208 | bytes 15581184 | tf_op jit(solution)/shard_map/pallas_call | solution.py:240
  93.6 5.0 %collective-permute-start.25 = (bf16[4,192,384]{2,1,0:T(8,128)(2,1)}, bf16[4,192,384]{2,1,0:T(8,128)(2,1)}, u32[]{:S(2)}, u32[]{:S(2)}) collective-permute-start(bf16[4,192,384]{2,1,0:T(8,128)(2,1)} %copy-done.15), channel_id=1, source_target_pairs={{0,4},{1,5},{2,6},{3,7},{12,8},{13,9},{14,10},{15,11},{16,20},{17,... | collective-permute-start | bytes 1769480 | tf_op jit(solution)/shard_map/ppermute | solution.py:298
  104.7 3.8 %shard_map.85 = (f32[256,1536]{1,0:T(8,128)S(1)}, bf16[256,1536]{1,0:T(8,128)(2,1)S(1)}, f32[256,1536]{1,0:T(8,128)S(1)}, bf16[256,1536]{1,0:T(8,128)(2,1)}) custom-call(bf16[3,2,96,384]{3,2,1,0:T(8,128)(2,1)S(1)} %copy-done.10, bf16[3,2,96,384]{3,2,1,0:T(8,128)(2,1)S(1)} %copy-done.17, bf16[3,2,96,384]{3,2,1,0:T(8,128)(2,1)S(1)} %copy-done.19, ...), custom_call_target="tpu_custom_call" | custom-call | flops 1811939328 | bytes 7520256 | tf_op jit(solution)/shard_map/pallas_call | solution.py:240
  110.8 1.6 collective-permute-start.20
  113.2 4.1 %collective-permute-start.23 = (bf16[4,192,384]{2,1,0:T(8,128)(2,1)}, bf16[4,192,384]{2,1,0:T(8,128)(2,1)S(1)}, u32[]{:S(2)}, u32[]{:S(2)}) collective-permute-start(bf16[4,192,384]{2,1,0:T(8,128)(2,1)} %copy-done.14), channel_id=1, source_target_pairs={{0,4},{1,5},{2,6},{3,7},{4,8},{5,9},{6,10},{7,11},{8,12},{9,13},{1... | collective-permute-start | bytes 1769480 | tf_op jit(solution)/shard_map/ppermute | solution.py:298
  122.0 5.9 %collective-permute-start.22 = (bf16[4,192,384]{2,1,0:T(8,128)(2,1)S(1)}, bf16[4,192,384]{2,1,0:T(8,128)(2,1)S(1)}, u32[]{:S(2)}, u32[]{:S(2)}) collective-permute-start(bf16[4,192,384]{2,1,0:T(8,128)(2,1)S(1)} %get-tuple-element.51), channel_id=1, source_target_pairs={{0,8},{1,9},{2,10},{3,11},{12,4},{13,5},{14,6},{15,7},{16,24},{17,... | collective-permute-start | bytes 1769480 | tf_op jit(solution)/shard_map/ppermute | solution.py:298
  133.6 1.7 fusion
  135.3 7.0 %collective-permute-done.22 = bf16[4,192,384]{2,1,0:T(8,128)(2,1)S(1)} collective-permute-done((bf16[4,192,384]{2,1,0:T(8,128)(2,1)S(1)}, bf16[4,192,384]{2,1,0:T(8,128)(2,1)S(1)}, u32[]{:S(2)}, u32[]{:S(2)}) %collective-permute-start.22) | collective-permute-done | bytes 589856 | tf_op jit(solution)/shard_map/ppermute | solution.py:298
  142.3 18.5 %collective-permute-done.26 = bf16[4,192,384]{2,1,0:T(8,128)(2,1)S(1)} collective-permute-done((bf16[4,192,384]{2,1,0:T(8,128)(2,1)S(1)}, bf16[4,192,384]{2,1,0:T(8,128)(2,1)S(1)}, u32[]{:S(2)}, u32[]{:S(2)}) %collective-permute-start.26) | collective-permute-done | bytes 589856 | tf_op jit(solution)/shard_map/ppermute | solution.py:298
  161.5 1.8 %collective-permute-start.29 = (bf16[4,192,96]{2,1,0:T(8,128)(2,1)S(1)}, bf16[4,192,96]{2,1,0:T(8,128)(2,1)S(1)}, u32[]{:S(2)}, u32[]{:S(2)}) collective-permute-start(bf16[4,192,96]{2,1,0:T(8,128)(2,1)S(1)} %get-tuple-element.48), channel_id=1, source_target_pairs={{0,3},{1,2},{2,1},{3,0},{4,7},{5,6},{6,5},{7,4},{8,11},{9,10},{10,... | collective-permute-start | bytes 442376 | tf_op jit(solution)/shard_map/ppermute | solution.py:267
  164.8 1.7 fusion.20
  168.0 4.9 %collective-permute-done.28.refs_2_ = bf16[4,192,96]{2,1,0:T(8,128)(2,1)S(1)} collective-permute-done((bf16[4,192,96]{2,1,0:T(8,128)(2,1)S(1)}, bf16[4,192,96]{2,1,0:T(8,128)(2,1)S(1)}, u32[]{:S(2)}, u32[]{:S(2)}) %collective-permute-start.28) | collective-permute-done | bytes 147488 | tf_op jit(solution)/shard_map/ppermute | solution.py:267
  172.9 1.6 shard_map.86
  (122 shorter events, 42.3 us)
Async XLA Ops:
  3.1 7.2 %collective-permute-start.1 = (bf16[3,96,192]{2,1,0:T(8,128)(2,1)}, bf16[3,96,192]{2,1,0:T(8,128)(2,1)}, u32[]{:S(2)}, u32[]{:S(2)}) collective-permute-start(bf16[3,96,192]{2,1,0:T(8,128)(2,1)} %get-tuple-element.58), channel_id=1, source_target_pairs={{0,2},{1,3},{2,0},{3,1},{4,6},{5,7},{6,4},{7,5},{8,10},{9,11},{10,... | collective-permute-start | bytes 331784 | tf_op jit(solution)/shard_map/ppermute | solution.py:267
  5.8 7.7 %collective-permute-start.2 = (bf16[3,96,192]{2,1,0:T(8,128)(2,1)S(1)}, bf16[3,96,192]{2,1,0:T(8,128)(2,1)}, u32[]{:S(2)}, u32[]{:S(2)}) collective-permute-start(bf16[3,96,192]{2,1,0:T(8,128)(2,1)S(1)} %get-tuple-element.60), channel_id=1, source_target_pairs={{0,3},{1,2},{2,1},{3,0},{4,7},{5,6},{6,5},{7,4},{8,11},{9,10},{10,... | collective-permute-start | bytes 331784 | tf_op jit(solution)/shard_map/ppermute | solution.py:267
  15.7 18.8 %collective-permute-start.8 = (bf16[256,1536]{1,0:T(8,128)(2,1)S(1)}, bf16[256,1536]{1,0:T(8,128)(2,1)}, u32[]{:S(2)}, u32[]{:S(2)}) collective-permute-start(bf16[256,1536]{1,0:T(8,128)(2,1)S(1)} %fusion.6.refs_5_), channel_id=1, source_target_pairs={{0,2},{1,3},{2,0},{3,1},{4,6},{5,7},{6,4},{7,5},{8,10},{9,11},{10,... | collective-permute-start | bytes 2359304 | tf_op jit(solution)/shard_map/ppermute | solution.py:267
  17.0 27.9 %collective-permute-start.3 = (bf16[3,2,96,384]{3,2,1,0:T(8,128)(2,1)}, bf16[3,2,96,384]{3,2,1,0:T(8,128)(2,1)S(1)}, u32[]{:S(2)}, u32[]{:S(2)}) collective-permute-start(bf16[3,2,96,384]{3,2,1,0:T(8,128)(2,1)} %maximum_select_fusion.refs_0_), channel_id=1, source_target_pairs={{0,8},{1,9},{2,10},{3,11},{4,12},{5,13},{6,14},{7,15},{8,0},{9,1},... | collective-permute-start | bytes 1327112 | tf_op jit(solution)/shard_map/ppermute | solution.py:267
  34.5 26.3 %collective-permute-start.13 = (bf16[256,1536]{1,0:T(8,128)(2,1)}, bf16[256,1536]{1,0:T(8,128)(2,1)S(1)}, u32[]{:S(2)}, u32[]{:S(2)}) collective-permute-start(bf16[256,1536]{1,0:T(8,128)(2,1)} %refs_11_), channel_id=1, source_target_pairs={{0,2},{1,3},{2,0},{3,1},{4,6},{5,7},{6,4},{7,5},{8,10},{9,11},{10,... | collective-permute-start | bytes 2359304 | tf_op jit(solution)/shard_map/ppermute | solution.py:267
  37.2 23.7 %collective-permute-start.10 = (bf16[256,1536]{1,0:T(8,128)(2,1)S(1)}, bf16[256,1536]{1,0:T(8,128)(2,1)S(1)}, u32[]{:S(2)}, u32[]{:S(2)}) collective-permute-start(bf16[256,1536]{1,0:T(8,128)(2,1)S(1)} %broadcast_select_fusion), channel_id=1, source_target_pairs={{1,5},{3,7},{4,0},{5,9},{6,2},{7,11},{8,4},{9,13},{10,6},{11,15},{... | collective-permute-start | bytes 2359304 | tf_op jit(solution)/shard_map/ppermute | solution.py:267
  40.4 18.3 %collective-permute-start.4 = (bf16[3,2,96,384]{3,2,1,0:T(8,128)(2,1)S(1)}, bf16[3,2,96,384]{3,2,1,0:T(8,128)(2,1)S(1)}, u32[]{:S(2)}, u32[]{:S(2)}) collective-permute-start(bf16[3,2,96,384]{3,2,1,0:T(8,128)(2,1)S(1)} %copy-done.9), channel_id=1, source_target_pairs={{0,4},{1,5},{2,6},{3,7},{4,8},{5,9},{6,10},{7,11},{8,12},{9,13},{1... | collective-permute-start | bytes 1327112 | tf_op jit(solution)/shard_map/ppermute | solution.py:298
  43.6 15.2 %collective-permute-start.5 = (bf16[3,2,96,384]{3,2,1,0:T(8,128)(2,1)S(1)}, bf16[3,2,96,384]{3,2,1,0:T(8,128)(2,1)S(1)}, u32[]{:S(2)}, u32[]{:S(2)}) collective-permute-start(bf16[3,2,96,384]{3,2,1,0:T(8,128)(2,1)S(1)} %copy-done.9), channel_id=1, source_target_pairs={{4,0},{5,1},{6,2},{7,3},{8,4},{9,5},{10,6},{11,7},{12,8},{13,9},{1... | collective-permute-start | bytes 1327112 | tf_op jit(solution)/shard_map/ppermute | solution.py:298
  44.9 16.4 %collective-permute-start.7 = (bf16[256,1536]{1,0:T(8,128)(2,1)S(1)}, bf16[256,1536]{1,0:T(8,128)(2,1)S(1)}, u32[]{:S(2)}, u32[]{:S(2)}) collective-permute-start(bf16[256,1536]{1,0:T(8,128)(2,1)S(1)} %fusion.6.refs_5_), channel_id=1, source_target_pairs={{0,1},{1,0},{2,3},{3,2},{4,5},{5,4},{6,7},{7,6},{8,9},{9,8},{10,11... | collective-permute-start | bytes 2359304 | tf_op jit(solution)/shard_map/ppermute | solution.py:267
  58.8 16.2 %collective-permute-start.9 = (bf16[256,1536]{1,0:T(8,128)(2,1)}, bf16[256,1536]{1,0:T(8,128)(2,1)S(1)}, u32[]{:S(2)}, u32[]{:S(2)}) collective-permute-start(bf16[256,1536]{1,0:T(8,128)(2,1)} %collective-permute-done.8.refs_7_), channel_id=1, source_target_pairs={{0,1},{1,0},{2,3},{3,2},{4,5},{5,4},{6,7},{7,6},{8,9},{9,8},{10,11... | collective-permute-start | bytes 2359304 | tf_op jit(solution)/shard_map/ppermute | solution.py:267
  60.8 14.1 %collective-permute-start.14 = (bf16[256,1536]{1,0:T(8,128)(2,1)S(1)}, bf16[256,1536]{1,0:T(8,128)(2,1)S(1)}, u32[]{:S(2)}, u32[]{:S(2)}) collective-permute-start(bf16[256,1536]{1,0:T(8,128)(2,1)S(1)} %collective-permute-done.13.refs_13_), channel_id=1, source_target_pairs={{0,1},{1,0},{2,3},{3,2},{4,5},{5,4},{6,7},{7,6},{8,9},{9,8},{10,11... | collective-permute-start | bytes 2359304 | tf_op jit(solution)/shard_map/ppermute | solution.py:267
  60.9 14.1 %collective-permute-start.11 = (bf16[256,1536]{1,0:T(8,128)(2,1)S(1)}, bf16[256,1536]{1,0:T(8,128)(2,1)S(1)}, u32[]{:S(2)}, u32[]{:S(2)}) collective-permute-start(bf16[256,1536]{1,0:T(8,128)(2,1)S(1)} %collective-permute-done.10.refs_9_), channel_id=1, source_target_pairs={{0,1},{1,0},{2,3},{3,2},{4,5},{5,4},{6,7},{7,6},{8,9},{9,8},{10,11... | collective-permute-start | bytes 2359304 | tf_op jit(solution)/shard_map/ppermute | solution.py:267
  61.3 13.6 %collective-permute-start.6 = (bf16[3,2,96,384]{3,2,1,0:T(8,128)(2,1)S(1)}, bf16[3,2,96,384]{3,2,1,0:T(8,128)(2,1)S(1)}, u32[]{:S(2)}, u32[]{:S(2)}) collective-permute-start(bf16[3,2,96,384]{3,2,1,0:T(8,128)(2,1)S(1)} %collective-permute-done.3.refs_1_), channel_id=1, source_target_pairs={{8,12},{9,13},{10,14},{11,15},{4,0},{5,1},{6,2},{7,3},{24,28},{25,... | collective-permute-start | bytes 1327112 | tf_op jit(solution)/shard_map/ppermute | solution.py:298
  90.9 7.6 %collective-permute-start.17 = (bf16[256,192]{1,0:T(8,128)(2,1)S(1)}, bf16[256,192]{1,0:T(8,128)(2,1)S(1)}, u32[]{:S(2)}, u32[]{:S(2)}) collective-permute-start(bf16[256,192]{1,0:T(8,128)(2,1)S(1)} %get-tuple-element.54), channel_id=1, source_target_pairs={{0,4},{1,5},{2,6},{3,7},{4,8},{5,9},{6,10},{7,11},{8,12},{9,13},{1... | collective-permute-start | bytes 294920 | tf_op jit(solution)/shard_map/ppermute | solution.py:267
  93.6 27.2 %collective-permute-start.25 = (bf16[4,192,384]{2,1,0:T(8,128)(2,1)}, bf16[4,192,384]{2,1,0:T(8,128)(2,1)}, u32[]{:S(2)}, u32[]{:S(2)}) collective-permute-start(bf16[4,192,384]{2,1,0:T(8,128)(2,1)} %copy-done.15), channel_id=1, source_target_pairs={{0,4},{1,5},{2,6},{3,7},{12,8},{13,9},{14,10},{15,11},{16,20},{17,... | collective-permute-start | bytes 1769480 | tf_op jit(solution)/shard_map/ppermute | solution.py:298
  110.8 17.2 %collective-permute-start.20 = (bf16[256,1536]{1,0:T(8,128)(2,1)}, bf16[256,1536]{1,0:T(8,128)(2,1)}, u32[]{:S(2)}, u32[]{:S(2)}) collective-permute-start(bf16[256,1536]{1,0:T(8,128)(2,1)} %get-tuple-element.33), channel_id=1, source_target_pairs={{0,1},{1,0},{2,3},{3,2},{4,5},{5,4},{6,7},{7,6},{8,9},{9,8},{10,11... | collective-permute-start | bytes 2359304 | tf_op jit(solution)/shard_map/ppermute | solution.py:267
  113.2 19.2 %collective-permute-start.23 = (bf16[4,192,384]{2,1,0:T(8,128)(2,1)}, bf16[4,192,384]{2,1,0:T(8,128)(2,1)S(1)}, u32[]{:S(2)}, u32[]{:S(2)}) collective-permute-start(bf16[4,192,384]{2,1,0:T(8,128)(2,1)} %copy-done.14), channel_id=1, source_target_pairs={{0,4},{1,5},{2,6},{3,7},{4,8},{5,9},{6,10},{7,11},{8,12},{9,13},{1... | collective-permute-start | bytes 1769480 | tf_op jit(solution)/shard_map/ppermute | solution.py:298
  117.3 18.0 %collective-permute-start.24 = (bf16[4,192,384]{2,1,0:T(8,128)(2,1)}, bf16[4,192,384]{2,1,0:T(8,128)(2,1)S(1)}, u32[]{:S(2)}, u32[]{:S(2)}) collective-permute-start(bf16[4,192,384]{2,1,0:T(8,128)(2,1)} %copy-done.13), channel_id=1, source_target_pairs={{4,0},{5,1},{6,2},{7,3},{8,4},{9,5},{10,6},{11,7},{12,8},{13,9},{1... | collective-permute-start | bytes 1769480 | tf_op jit(solution)/shard_map/ppermute | solution.py:298
  120.2 10.5 %collective-permute-start.16 = (bf16[256,384]{1,0:T(8,128)(2,1)S(1)}, bf16[256,384]{1,0:T(8,128)(2,1)S(1)}, u32[]{:S(2)}, u32[]{:S(2)}) collective-permute-start(bf16[256,384]{1,0:T(8,128)(2,1)S(1)} %get-tuple-element.62), channel_id=1, source_target_pairs={{0,2},{1,3},{2,0},{3,1},{4,6},{5,7},{6,4},{7,5},{8,10},{9,11},{10,... | collective-permute-start | bytes 589832 | tf_op jit(solution)/shard_map/ppermute | solution.py:267
  122.0 20.3 %collective-permute-start.22 = (bf16[4,192,384]{2,1,0:T(8,128)(2,1)S(1)}, bf16[4,192,384]{2,1,0:T(8,128)(2,1)S(1)}, u32[]{:S(2)}, u32[]{:S(2)}) collective-permute-start(bf16[4,192,384]{2,1,0:T(8,128)(2,1)S(1)} %get-tuple-element.51), channel_id=1, source_target_pairs={{0,8},{1,9},{2,10},{3,11},{12,4},{13,5},{14,6},{15,7},{16,24},{17,... | collective-permute-start | bytes 1769480 | tf_op jit(solution)/shard_map/ppermute | solution.py:298
  128.0 32.8 %collective-permute-start.26 = (bf16[4,192,384]{2,1,0:T(8,128)(2,1)S(1)}, bf16[4,192,384]{2,1,0:T(8,128)(2,1)S(1)}, u32[]{:S(2)}, u32[]{:S(2)}) collective-permute-start(bf16[4,192,384]{2,1,0:T(8,128)(2,1)S(1)} %get-tuple-element.52), channel_id=1, source_target_pairs={{4,12},{5,13},{6,14},{7,15},{8,0},{9,1},{10,2},{11,3},{20,28},{21,... | collective-permute-start | bytes 1769480 | tf_op jit(solution)/shard_map/ppermute | solution.py:298
  130.8 34.0 %collective-permute-start.19 = (bf16[256,1536]{1,0:T(8,128)(2,1)S(1)}, bf16[256,1536]{1,0:T(8,128)(2,1)S(1)}, u32[]{:S(2)}, u32[]{:S(2)}) collective-permute-start(bf16[256,1536]{1,0:T(8,128)(2,1)S(1)} %get-tuple-element.31), channel_id=1, source_target_pairs={{0,1},{1,0},{2,3},{3,2},{4,5},{5,4},{6,7},{7,6},{8,9},{9,8},{10,11... | collective-permute-start | bytes 2359304 | tf_op jit(solution)/shard_map/ppermute | solution.py:267
  132.3 32.4 %collective-permute-start.21 = (bf16[256,1536]{1,0:T(8,128)(2,1)S(1)}, bf16[256,1536]{1,0:T(8,128)(2,1)S(1)}, u32[]{:S(2)}, u32[]{:S(2)}) collective-permute-start(bf16[256,1536]{1,0:T(8,128)(2,1)S(1)} %add_convert_fusion), channel_id=1, source_target_pairs={{0,2},{1,3},{2,0},{3,1},{4,6},{5,7},{6,4},{7,5},{8,10},{9,11},{10,... | collective-permute-start | bytes 2359304 | tf_op jit(solution)/shard_map/ppermute | solution.py:267
  163.3 9.7 %collective-permute-start.28 = (bf16[4,192,96]{2,1,0:T(8,128)(2,1)S(1)}, bf16[4,192,96]{2,1,0:T(8,128)(2,1)S(1)}, u32[]{:S(2)}, u32[]{:S(2)}) collective-permute-start(bf16[4,192,96]{2,1,0:T(8,128)(2,1)S(1)} %get-tuple-element.49), channel_id=1, source_target_pairs={{0,2},{1,3},{2,0},{3,1},{4,6},{5,7},{6,4},{7,5},{8,10},{9,11},{10,... | collective-permute-start | bytes 442376 | tf_op jit(solution)/shard_map/ppermute | solution.py:267
  (36 other events, 369.1 us)

commit v7 on v6

--- a/solution.py
+++ b/solution.py
@@ -88,12 +88,11 @@
 def tap_pairs(depth, pieces, packed):
     z, _ = position()
     if depth == 4:
-        own, two, up, down, passed = pieces
-        return [
-            (own, packed.at[:, z]),
-            (two, packed.at[:, lax.rem(z + 2, 4)]),
-            ((z == 0, passed, up), packed.at[:, lax.rem(z + 3, 4)]),
-            ((z == 3, passed, down), packed.at[:, lax.rem(z + 1, 4)]),
+        own, *ups = pieces[:4]
+        downs = pieces[4:]
+        return [(own, packed.at[:, z])] + [
+            ((z > j, ups[j], downs[2 - j]), packed.at[:, lax.rem(z + 3 - j, 4)])
+            for j in range(3)
         ]
     return [
         (piece, packed.at[:, lax.rem(z + depth - d, depth)])
@@ -115,7 +114,7 @@
 
 def target_types(depth):
     if depth == 4:
-        return [bf16, f32, bf16, bf16, f32]
+        return [bf16, f32, f32, f32, f32]
     return [bf16] * (depth - 1) + [f32]
 
 
@@ -131,15 +130,19 @@
 
 
 def weight_kernel(depth, *refs):
-    count = depth + (depth == 4)
+    count = depth + 3 * (depth == 4)
     pieces = refs[:count]
     acts = refs[count : count + 4]
     edge, edge_other = refs[count + 4 : count + 6]
     cots = refs[count + 6 : count + 10]
     point = refs[count + 10]
-    branch, grad = refs[count + 11 : count + 13]
-    outs = refs[count + 13 : -7]
-    wide, wide_cot, packed, taps, grads, branches, sems = refs[-7:]
+    refs = refs[count + 11 :]
+    results = (len(refs) - 7) // 2
+    stores, (wide, wide_cot, packed, taps, grads, branches, sems) = (
+        refs[:results],
+        refs[results : results + 7],
+    )
+    branch, grad, *outs = refs[results + 7 :]
     z, q = position()
     rows = acts[0].shape[0]
     core = lax.rem(q, 2)
@@ -157,6 +160,7 @@
         sems,
         len(first),
     )
+    base = len(first) + len(second)
     finish(first)
     unpack(packed, taps)
     finish(second)
@@ -172,6 +176,7 @@
         value = slope * gelu_slope(pre)
         grad[here] = value.astype(bf16)
         grads[:, here] = value.T.astype(bf16)
+    last = started([(grad, stores[1]), (branch, stores[0])], sems, base)
     width = wide.shape[1] // depth
     if len(outs) > 1:
         where = [within(target, width) for target in targets(depth, z)]
@@ -187,14 +192,20 @@
                 grads[...], wide[pl.ds(k * rows, 4 * rows), lanes]
             ).astype(out.dtype)
         out[3] = product(branches[...], wide_cot[:, lanes]).astype(out.dtype)
+        if len(outs) > 1:
+            last += started([(out, stores[2 + i])], sems, base + 2 + i)
+    if len(outs) == 1:
+        last += started([(outs[0], stores[2])], sems, base + 2)
+    finish(last)
 
 
 def backward_kernel(depth, *refs):
-    count = depth + (depth == 4)
+    count = depth + 3 * (depth == 4)
     pieces = refs[:count]
     low, grad, high = refs[count : count + 3]
-    outs = refs[count + 3 : count + 7]
-    wide, packed, taps, sems = refs[count + 7 :]
+    stores = refs[count + 3 : count + 7]
+    wide, packed, taps, sems = refs[count + 7 : count + 11]
+    outs = refs[count + 11 :]
     _, q = position()
     rows = low.shape[0]
     finish(
@@ -209,6 +220,7 @@
         )
     )
     unpack(packed, taps)
+    last = []
     for m in (1, 3, 2, 0):
         part = toggled(q, m)
         total = None
@@ -216,6 +228,8 @@
             term = transposed_product(wide[within(part + 2 - k, rows)], taps[k])
             total = term if total is None else total + term
         outs[m][...] = total.astype(outs[m].dtype)
+        last += started([(outs[m], stores[m])], sems, count + 3 + m)
+    finish(last)
 
 
 def final_kernel(*refs):
@@ -233,7 +247,7 @@
         point[here, :] = held[m, 3]
 
 
-def call(kernel, outs, args, specs, scratch, flops, limit):
+def call(kernel, outs, args, specs, scratch, flops, limit, kept=pltpu.VMEM):
     nbytes = sum(a.size * a.dtype.itemsize for a in args) + sum(
         math.prod(s) * jnp.dtype(t).itemsize for s, t in outs
     )
@@ -241,7 +255,7 @@
         kernel,
         out_shape=[jax.ShapeDtypeStruct(s, t) for s, t in outs],
         in_specs=[pl.BlockSpec(memory_space=m) for m in specs],
-        out_specs=[pl.BlockSpec(memory_space=pltpu.VMEM)] * len(outs),
+        out_specs=[pl.BlockSpec(memory_space=kept)] * len(outs),
         scratch_shapes=scratch,
         compiler_params=pltpu.CompilerParams(vmem_limit_bytes=limit * MIB),
         cost_estimate=pl.CostEstimate(
@@ -302,10 +316,11 @@
         )
 
     if depth == 4:
-        two = to_z(start_piece, 2)
-        up = line(start_piece, [(0, 1), (1, 2), (2, 3)])
-        down = line(start_piece, [(1, 0), (2, 1), (3, 2)])
-        pieces = [start_piece, two, up, down, line(two, [(2, 3), (1, 0)])]
+        ups, downs = [start_piece], [start_piece]
+        for j in range(3):
+            ups.append(line(ups[-1], [(a, a + 1) for a in range(j, 3)]))
+            downs.append(line(downs[-1], [(a + 1, a) for a in range(3 - j)]))
+        pieces = ups + downs[1:]
     else:
         pieces = [start_piece] + [to_z(start_piece, d) for d in range(1, depth)]
 
@@ -316,6 +331,10 @@
     act_late = after(act, start_piece)
     cot_late = after(cotangent, start_piece)
     act_across = cross(act_late, 2)
+    if depth == 4:
+        act_across, pieces[1], pieces[4] = lax.optimization_barrier(
+            (act_across, pieces[1], pieces[4])
+        )
     edge = send(
         jnp.where(core == y, act_late, act_across),
         lambda i: i + 4 if i % 2 else i - 4,
@@ -331,11 +350,12 @@
     outs = [((4, quarter, width), t) for t in target_types(depth)]
     if not apart:
         outs = [((depth, 4, quarter, width), f32)]
+    weight_outs = [((4 * rows, quarter), bf16)] * 2 + outs
     branch, pre_grad, *terms = call(
         functools.partial(weight_kernel, depth),
-        [((4 * rows, quarter), bf16)] * 2 + outs,
+        weight_outs,
         [*pieces, *acts, edge, edge_other, *cots, point_rows],
-        [pl.ANY] * (len(pieces) + 10) + [pltpu.VMEM],
+        [pltpu.HBM] * (len(pieces) + 10) + [pltpu.VMEM],
         [
             pltpu.VMEM((6 * rows, channels), bf16),
             pltpu.VMEM((4 * rows, channels), bf16),
@@ -343,22 +363,26 @@
             pltpu.VMEM((3, channels, quarter), bf16),
             pltpu.VMEM((quarter, 4 * rows), bf16),
             pltpu.VMEM((quarter, 4 * rows), bf16),
-            pltpu.SemaphoreType.DMA((depth + 10,)),
+            pltpu.SemaphoreType.DMA((2 * len(pieces) + 14,)),
+            *[pltpu.VMEM(*out) for out in weight_outs],
         ],
         8 * flops,
         40,
+        pltpu.HBM,
     )
     if not apart:
         terms = [terms[0][d].astype(bf16) for d in range(1, depth)] + [terms[0][0]]
     if depth == 4:
         three, two, up, down, total = terms
-        passed = line(three, [(0, 1), (3, 2)])
-        joined = line((two + passed.astype(f32)).astype(bf16), [(1, 3), (2, 0)])
+        far = line(three, [(0, 1), (3, 2)])
+        joined = (two + far.astype(f32)).astype(bf16)
+        near_up = line(joined, [(0, 1), (1, 2)])
+        near_down = line(joined, [(3, 2), (2, 1)])
+        up = (up + near_up.astype(f32)).astype(bf16)
+        down = (down + near_down.astype(f32)).astype(bf16)
         parts = [
-            line(two.astype(bf16), [(0, 2), (3, 1)]),
             line(up, [(0, 1), (1, 2), (2, 3)]),
             line(down, [(1, 0), (2, 1), (3, 2)]),
-            joined,
         ]
     else:
         total = terms[-1]
@@ -366,19 +390,22 @@
 
     grad_low = send(pre_grad[3 * rows :], lambda i: i + 4)
     grad_high = send(pre_grad[:rows], lambda i: i - 4)
+    share_outs = [((rows, channels), t) for t in (f32, bf16, f32, bf16)]
     shares = call(
         functools.partial(backward_kernel, depth),
-        [((rows, channels), t) for t in (f32, bf16, f32, bf16)],
+        share_outs,
         [*pieces, grad_low, pre_grad, grad_high],
-        [pl.ANY] * (len(pieces) + 3),
+        [pltpu.HBM] * (len(pieces) + 3),
         [
             pltpu.VMEM((6 * rows, quarter), bf16),
             pltpu.VMEM((3, depth, 2, own, 2 * quarter), bf16),
             pltpu.VMEM((3, channels, quarter), bf16),
-            pltpu.SemaphoreType.DMA((depth + 3,)),
+            pltpu.SemaphoreType.DMA((len(pieces) + 7,)),
+            *[pltpu.VMEM(*out) for out in share_outs],
         ],
         3 * flops,
         40,
+        pltpu.HBM,
     )
     mine = shares[0] + cross(shares[1], 1).astype(f32)
     far = shares[2] + cross(shares[3], 1).astype(f32)

time: 176 us -> 168 us (0.955)
  the two profiles are of different devices: /device:TPU:1 before, /device:TPU:9 now
where the time goes in v7:
time: 168 us; the launch traced here: 167 us
  waiting for transfers between devices  64.7 us (39%)
  starting transfers between devices  50.1 us (30%)
  Pallas kernels  20.1 us (12%)
  local copies, waits for them, and re-layouts  15.6 us (9%)
  other arithmetic  13.2 us (8%)
    ppermute x11, waiting for transfers between devices, line(): lax.ppermute(value, 'seq', [(4 * a + i, 4 * b + i) for a, b in pairs for...  36.7 us
    ppermute x21, waiting for transfers between devices, send(): lax.ppermute(value, 'seq', [p for p in pairs if p[1] is not None and 0 <=...  28 us
    ppermute x11, starting transfers between devices, line(): lax.ppermute(value, 'seq', [(4 * a + i, 4 * b + i) for a, b in pairs for...  26 us
    ppermute x21, starting transfers between devices, send(): lax.ppermute(value, 'seq', [p for p in pairs if p[1] is not None and 0 <=...  24.1 us
    pallas_call x3, Pallas kernels, call(): pl.pallas_call(kernel, out_shape=[jax.ShapeDtypeStruct(s, t) for s, t in...  20.1 us
    unnamed x61, local copies, waits for them, and re-layouts  11.9 us
    select_n x4, other arithmetic, in_order(): jnp.where(first, jnp.concatenate([mine, other], axis), jnp.concatenate([o...  4.76 us
  transfers between devices with their start and end apart: 32, of which 16 were waited for; matrix products, arithmetic and copies ran while one was open for 8% of the time, Pallas kernels for 3%

profile of v7, /device:TPU:9, one launch (start us, length us, event | category | flops | bytes accessed | tf_op | source)
XLA Modules:
  0.0 166.6 jit_solution(14909411849766174361)
XLA Ops:
  0.7 2.3 %dynamic-slice_bitcast_fusion.4 = (bf16[3,1,96,192]{3,2,1,0:T(8,128)(2,1)S(1)}, bf16[3,96,192]{2,1,0:T(8,128)(2,1)}, bf16[3,96,192]{2,1,0:T(8,128)(2,1)}, bf16[3,96,192]{2,1,0:T(8,128)(2,1)S(1)}) fusion(bf16[3,96,768]{2,1,0:T(8,128)(2,1)} %param.7, s32[]{:T(128)S(6)} %select_n.115, s32[]{:T(128)S(6)} %select_n.107, s32[]{:T(128)S(6)} %select_n.106, ...), kind=kLoop, calls=%fused_computation.51 | loop fusion | bytes 884752 | tf_op jit(solution)/shard_map/concatenate | solution.py:297
  9.6 3.3 %collective-permute-done.2 = bf16[3,96,192]{2,1,0:T(8,128)(2,1)} collective-permute-done((bf16[3,96,192]{2,1,0:T(8,128)(2,1)S(1)}, bf16[3,96,192]{2,1,0:T(8,128)(2,1)}, u32[]{:S(2)}, u32[]{:S(2)}) %collective-permute-start.2) | collective-permute-done | bytes 110624 | tf_op jit(solution)/shard_map/ppermute | solution.py:281
  16.2 3.2 %collective-permute-start.4 = (bf16[3,2,96,384]{3,2,1,0:T(8,128)(2,1)}, bf16[3,2,96,384]{3,2,1,0:T(8,128)(2,1)}, u32[]{:S(2)}, u32[]{:S(2)}) collective-permute-start(bf16[3,2,96,384]{3,2,1,0:T(8,128)(2,1)} %maximum_select_fusion.refs_0_), channel_id=1, source_target_pairs={{0,4},{1,5},{2,6},{3,7},{4,8},{5,9},{6,10},{7,11},{8,12},{9,13},{1... | collective-permute-start | bytes 1327112 | tf_op jit(solution)/shard_map/ppermute | solution.py:312
  19.4 2.9 %collective-permute-start.5 = (bf16[3,2,96,384]{3,2,1,0:T(8,128)(2,1)}, bf16[3,2,96,384]{3,2,1,0:T(8,128)(2,1)}, u32[]{:S(2)}, u32[]{:S(2)}) collective-permute-start(bf16[3,2,96,384]{3,2,1,0:T(8,128)(2,1)} %maximum_select_fusion.refs_0_), channel_id=1, source_target_pairs={{4,0},{5,1},{6,2},{7,3},{8,4},{9,5},{10,6},{11,7},{12,8},{13,9},{1... | collective-permute-start | bytes 1327112 | tf_op jit(solution)/shard_map/ppermute | solution.py:312
  23.5 6.0 %collective-permute-done.4.refs_1_ = bf16[3,2,96,384]{3,2,1,0:T(8,128)(2,1)} collective-permute-done((bf16[3,2,96,384]{3,2,1,0:T(8,128)(2,1)}, bf16[3,2,96,384]{3,2,1,0:T(8,128)(2,1)}, u32[]{:S(2)}, u32[]{:S(2)}) %collective-permute-start.4) | collective-permute-done | bytes 442400 | tf_op jit(solution)/shard_map/ppermute | solution.py:312
  29.5 2.9 %collective-permute-done.5.refs_4_ = bf16[3,2,96,384]{3,2,1,0:T(8,128)(2,1)} collective-permute-done((bf16[3,2,96,384]{3,2,1,0:T(8,128)(2,1)}, bf16[3,2,96,384]{3,2,1,0:T(8,128)(2,1)}, u32[]{:S(2)}, u32[]{:S(2)}) %collective-permute-start.5) | collective-permute-done | bytes 442400 | tf_op jit(solution)/shard_map/ppermute | solution.py:312
  36.3 3.2 %collective-permute-start.12 = (bf16[256,1536]{1,0:T(8,128)(2,1)S(1)}, bf16[256,1536]{1,0:T(8,128)(2,1)S(1)}, u32[]{:S(2)}, u32[]{:S(2)}) collective-permute-start(bf16[256,1536]{1,0:T(8,128)(2,1)S(1)} %broadcast_select_fusion), channel_id=1, source_target_pairs={{1,5},{3,7},{4,0},{5,9},{6,2},{7,11},{8,4},{9,13},{10,6},{11,15},{... | collective-permute-start | bytes 2359304 | tf_op jit(solution)/shard_map/ppermute | solution.py:281
  39.5 3.2 %collective-permute-start.6 = (bf16[3,2,96,384]{3,2,1,0:T(8,128)(2,1)}, bf16[3,2,96,384]{3,2,1,0:T(8,128)(2,1)S(1)}, u32[]{:S(2)}, u32[]{:S(2)}) collective-permute-start(bf16[3,2,96,384]{3,2,1,0:T(8,128)(2,1)} %collective-permute-done.4.refs_1_), channel_id=1, source_target_pairs={{4,8},{5,9},{6,10},{7,11},{8,12},{9,13},{10,14},{11,15},{20,24},{2... | collective-permute-start | bytes 1327112 | tf_op jit(solution)/shard_map/ppermute | solution.py:312
  44.8 7.2 %collective-permute-done.15.refs_15_ = bf16[256,1536]{1,0:T(8,128)(2,1)S(1)} collective-permute-done((bf16[256,1536]{1,0:T(8,128)(2,1)}, bf16[256,1536]{1,0:T(8,128)(2,1)S(1)}, u32[]{:S(2)}, u32[]{:S(2)}) %collective-permute-start.15) | collective-permute-done | bytes 786464 | tf_op jit(solution)/shard_map/ppermute | solution.py:281
  54.0 4.0 %collective-permute-done.6.refs_2_ = bf16[3,2,96,384]{3,2,1,0:T(8,128)(2,1)S(1)} collective-permute-done((bf16[3,2,96,384]{3,2,1,0:T(8,128)(2,1)}, bf16[3,2,96,384]{3,2,1,0:T(8,128)(2,1)S(1)}, u32[]{:S(2)}, u32[]{:S(2)}) %collective-permute-start.6) | collective-permute-done | bytes 442400 | tf_op jit(solution)/shard_map/ppermute | solution.py:312
  60.2 7.3 %collective-permute-done.9.refs_6_ = bf16[3,2,96,384]{3,2,1,0:T(8,128)(2,1)S(1)} collective-permute-done((bf16[3,2,96,384]{3,2,1,0:T(8,128)(2,1)S(1)}, bf16[3,2,96,384]{3,2,1,0:T(8,128)(2,1)S(1)}, u32[]{:S(2)}, u32[]{:S(2)}) %collective-permute-start.9) | collective-permute-done | bytes 442400 | tf_op jit(solution)/shard_map/ppermute | solution.py:312
  67.5 13.2 %shard_map.84 = (bf16[1024,192]{1,0:T(8,128)(2,1)S(1)}, bf16[1024,192]{1,0:T(8,128)(2,1)S(1)}, bf16[4,192,384]{2,1,0:T(8,128)(2,1)S(1)}, f32[4,192,384]{2,1,0:T(...) custom-call(bf16[3,2,96,384]{3,2,1,0:T(8,128)(2,1)} %maximum_select_fusion.refs_0_, ...), custom_call_target="tpu_custom_call" | custom-call | flops 4831838208 | bytes 17645568 | tf_op jit(solution)/shard_map/pallas_call | solution.py:254
  84.3 4.0 %collective-permute-start.19 = (bf16[256,192]{1,0:T(8,128)(2,1)S(1)}, bf16[256,192]{1,0:T(8,128)(2,1)S(1)}, u32[]{:S(2)}, u32[]{:S(2)}) collective-permute-start(bf16[256,192]{1,0:T(8,128)(2,1)S(1)} %get-tuple-element.58), channel_id=1, source_target_pairs={{0,4},{1,5},{2,6},{3,7},{4,8},{5,9},{6,10},{7,11},{8,12},{9,13},{1... | collective-permute-start | bytes 294920 | tf_op jit(solution)/shard_map/ppermute | solution.py:281
  91.8 3.3 %collective-permute-done.20.refs_9_ = bf16[256,192]{1,0:T(8,128)(2,1)S(1)} collective-permute-done((bf16[256,192]{1,0:T(8,128)(2,1)S(1)}, bf16[256,192]{1,0:T(8,128)(2,1)S(1)}, u32[]{:S(2)}, u32[]{:S(2)}) %collective-permute-start.20) | collective-permute-done | bytes 98336 | tf_op jit(solution)/shard_map/ppermute | solution.py:281
  100.1 5.3 %shard_map.85 = (f32[256,1536]{1,0:T(8,128)S(1)}, bf16[256,1536]{1,0:T(8,128)(2,1)S(1)}, f32[256,1536]{1,0:T(8,128)S(1)}, bf16[256,1536]{1,0:T(8,128)(2,1)}) custom-call(bf16[3,2,96,384]{3,2,1,0:T(8,128)(2,1)} %maximum_select_fusion.refs_0_, bf16[3,2,96,384]{3,2,1,0:T(8,128)(2,1)} %collective-permute-done.4.refs_1_, bf16[3,2,96,384]{3,2,1,0:T(8,128)(2,1)S(1)} %copy-done.16, ...), custom_call_target="tpu_custom_call" | custom-call | flops 1811939328 | bytes 8404992 | tf_op jit(solution)/shard_map/pallas_call | solution.py:254
  115.3 4.0 %collective-permute-start.25 = (bf16[4,192,384]{2,1,0:T(8,128)(2,1)S(1)}, bf16[4,192,384]{2,1,0:T(8,128)(2,1)S(1)}, u32[]{:S(2)}, u32[]{:S(2)}) collective-permute-start(bf16[4,192,384]{2,1,0:T(8,128)(2,1)S(1)} %add_convert_fusion.3), channel_id=1, source_target_pairs={{0,4},{1,5},{2,6},{3,7},{4,8},{5,9},{6,10},{7,11},{16,20},{17,21},... | collective-permute-start | bytes 1769480 | tf_op jit(solution)/shard_map/ppermute | solution.py:312
  123.9 7.6 %collective-permute-done.25 = bf16[4,192,384]{2,1,0:T(8,128)(2,1)S(1)} collective-permute-done((bf16[4,192,384]{2,1,0:T(8,128)(2,1)S(1)}, bf16[4,192,384]{2,1,0:T(8,128)(2,1)S(1)}, u32[]{:S(2)}, u32[]{:S(2)}) %collective-permute-start.25) | collective-permute-done | bytes 589856 | tf_op jit(solution)/shard_map/ppermute | solution.py:312
  131.7 4.2 %collective-permute-start.26 = (bf16[4,192,384]{2,1,0:T(8,128)(2,1)S(1)}, bf16[4,192,384]{2,1,0:T(8,128)(2,1)S(1)}, u32[]{:S(2)}, u32[]{:S(2)}) collective-permute-start(bf16[4,192,384]{2,1,0:T(8,128)(2,1)S(1)} %add_convert_fusion.2), channel_id=1, source_target_pairs={{0,4},{1,5},{2,6},{3,7},{4,8},{5,9},{6,10},{7,11},{8,12},{9,13},{1... | collective-permute-start | bytes 1769480 | tf_op jit(solution)/shard_map/ppermute | solution.py:312
  137.9 2.4 %collective-permute-done.23 = bf16[256,1536]{1,0:T(8,128)(2,1)S(1)} collective-permute-done((bf16[256,1536]{1,0:T(8,128)(2,1)S(1)}, bf16[256,1536]{1,0:T(8,128)(2,1)S(1)}, u32[]{:S(2)}, u32[]{:S(2)}) %collective-permute-start.23) | collective-permute-done | bytes 786464 | tf_op jit(solution)/shard_map/ppermute | solution.py:281
  142.1 5.0 %collective-permute-done.26 = bf16[4,192,384]{2,1,0:T(8,128)(2,1)S(1)} collective-permute-done((bf16[4,192,384]{2,1,0:T(8,128)(2,1)S(1)}, bf16[4,192,384]{2,1,0:T(8,128)(2,1)S(1)}, u32[]{:S(2)}, u32[]{:S(2)}) %collective-permute-start.26) | collective-permute-done | bytes 589856 | tf_op jit(solution)/shard_map/ppermute | solution.py:312
  147.1 4.0 %collective-permute-done.28 = bf16[4,192,384]{2,1,0:T(8,128)(2,1)S(1)} collective-permute-done((bf16[4,192,384]{2,1,0:T(8,128)(2,1)S(1)}, bf16[4,192,384]{2,1,0:T(8,128)(2,1)S(1)}, u32[]{:S(2)}, u32[]{:S(2)}) %collective-permute-start.28) | collective-permute-done | bytes 589856 | tf_op jit(solution)/shard_map/ppermute | solution.py:312
  151.5 2.9 %collective-permute-start.31 = (bf16[4,192,96]{2,1,0:T(8,128)(2,1)S(1)}, bf16[4,192,96]{2,1,0:T(8,128)(2,1)S(1)}, u32[]{:S(2)}, u32[]{:S(2)}) collective-permute-start(bf16[4,192,96]{2,1,0:T(8,128)(2,1)S(1)} %get-tuple-element.54), channel_id=1, source_target_pairs={{0,3},{1,2},{2,1},{3,0},{4,7},{5,6},{6,5},{7,4},{8,11},{9,10},{10,... | collective-permute-start | bytes 442376 | tf_op jit(solution)/shard_map/ppermute | solution.py:281
  157.1 2.4 %collective-permute-done.31.refs_3_ = bf16[4,192,96]{2,1,0:T(8,128)(2,1)S(1)} collective-permute-done((bf16[4,192,96]{2,1,0:T(8,128)(2,1)S(1)}, bf16[4,192,96]{2,1,0:T(8,128)(2,1)S(1)}, u32[]{:S(2)}, u32[]{:S(2)}) %collective-permute-start.31) | collective-permute-done | bytes 147488 | tf_op jit(solution)/shard_map/ppermute | solution.py:281
  159.5 4.6 %collective-permute-done.30.refs_2_ = bf16[4,192,96]{2,1,0:T(8,128)(2,1)S(1)} collective-permute-done((bf16[4,192,96]{2,1,0:T(8,128)(2,1)S(1)}, bf16[4,192,96]{2,1,0:T(8,128)(2,1)S(1)}, u32[]{:S(2)}, u32[]{:S(2)}) %collective-permute-start.30) | collective-permute-done | bytes 147488 | tf_op jit(solution)/shard_map/ppermute | solution.py:281
  (128 shorter events, 57.1 us)
Async XLA Ops:
  14.9 18.9 %collective-permute-start.3 = (bf16[256,1536]{1,0:T(8,128)(2,1)S(1)}, bf16[256,1536]{1,0:T(8,128)(2,1)}, u32[]{:S(2)}, u32[]{:S(2)}) collective-permute-start(bf16[256,1536]{1,0:T(8,128)(2,1)S(1)} %fusion.6.refs_7_), channel_id=1, source_target_pairs={{0,2},{1,3},{2,0},{3,1},{4,6},{5,7},{6,4},{7,5},{8,10},{9,11},{10,... | collective-permute-start | bytes 2359304 | tf_op jit(solution)/shard_map/ppermute | solution.py:281
  16.2 13.3 %collective-permute-start.4 = (bf16[3,2,96,384]{3,2,1,0:T(8,128)(2,1)}, bf16[3,2,96,384]{3,2,1,0:T(8,128)(2,1)}, u32[]{:S(2)}, u32[]{:S(2)}) collective-permute-start(bf16[3,2,96,384]{3,2,1,0:T(8,128)(2,1)} %maximum_select_fusion.refs_0_), channel_id=1, source_target_pairs={{0,4},{1,5},{2,6},{3,7},{4,8},{5,9},{6,10},{7,11},{8,12},{9,13},{1... | collective-permute-start | bytes 1327112 | tf_op jit(solution)/shard_map/ppermute | solution.py:312
  19.4 13.0 %collective-permute-start.5 = (bf16[3,2,96,384]{3,2,1,0:T(8,128)(2,1)}, bf16[3,2,96,384]{3,2,1,0:T(8,128)(2,1)}, u32[]{:S(2)}, u32[]{:S(2)}) collective-permute-start(bf16[3,2,96,384]{3,2,1,0:T(8,128)(2,1)} %maximum_select_fusion.refs_0_), channel_id=1, source_target_pairs={{4,0},{5,1},{6,2},{7,3},{8,4},{9,5},{10,6},{11,7},{12,8},{13,9},{1... | collective-permute-start | bytes 1327112 | tf_op jit(solution)/shard_map/ppermute | solution.py:312
  22.3 22.5 %collective-permute-start.10 = (bf16[256,1536]{1,0:T(8,128)(2,1)S(1)}, bf16[256,1536]{1,0:T(8,128)(2,1)S(1)}, u32[]{:S(2)}, u32[]{:S(2)}) collective-permute-start(bf16[256,1536]{1,0:T(8,128)(2,1)S(1)} %fusion.6.refs_7_), channel_id=1, source_target_pairs={{0,1},{1,0},{2,3},{3,2},{4,5},{5,4},{6,7},{7,6},{8,9},{9,8},{10,11... | collective-permute-start | bytes 2359304 | tf_op jit(solution)/shard_map/ppermute | solution.py:281
  23.5 19.3 %collective-permute-start.14 = (bf16[256,1536]{1,0:T(8,128)(2,1)}, bf16[256,1536]{1,0:T(8,128)(2,1)S(1)}, u32[]{:S(2)}, u32[]{:S(2)}) collective-permute-start(bf16[256,1536]{1,0:T(8,128)(2,1)} %refs_13_), channel_id=1, source_target_pairs={{0,1},{1,0},{2,3},{3,2},{4,5},{5,4},{6,7},{7,6},{8,9},{9,8},{10,11... | collective-permute-start | bytes 2359304 | tf_op jit(solution)/shard_map/ppermute | solution.py:281
  33.9 18.1 %collective-permute-start.15 = (bf16[256,1536]{1,0:T(8,128)(2,1)}, bf16[256,1536]{1,0:T(8,128)(2,1)S(1)}, u32[]{:S(2)}, u32[]{:S(2)}) collective-permute-start(bf16[256,1536]{1,0:T(8,128)(2,1)} %refs_13_), channel_id=1, source_target_pairs={{0,2},{1,3},{2,0},{3,1},{4,6},{5,7},{6,4},{7,5},{8,10},{9,11},{10,... | collective-permute-start | bytes 2359304 | tf_op jit(solution)/shard_map/ppermute | solution.py:281
  36.3 17.7 %collective-permute-start.12 = (bf16[256,1536]{1,0:T(8,128)(2,1)S(1)}, bf16[256,1536]{1,0:T(8,128)(2,1)S(1)}, u32[]{:S(2)}, u32[]{:S(2)}) collective-permute-start(bf16[256,1536]{1,0:T(8,128)(2,1)S(1)} %broadcast_select_fusion), channel_id=1, source_target_pairs={{1,5},{3,7},{4,0},{5,9},{6,2},{7,11},{8,4},{9,13},{10,6},{11,15},{... | collective-permute-start | bytes 2359304 | tf_op jit(solution)/shard_map/ppermute | solution.py:281
  39.5 18.5 %collective-permute-start.6 = (bf16[3,2,96,384]{3,2,1,0:T(8,128)(2,1)}, bf16[3,2,96,384]{3,2,1,0:T(8,128)(2,1)S(1)}, u32[]{:S(2)}, u32[]{:S(2)}) collective-permute-start(bf16[3,2,96,384]{3,2,1,0:T(8,128)(2,1)} %collective-permute-done.4.refs_1_), channel_id=1, source_target_pairs={{4,8},{5,9},{6,10},{7,11},{8,12},{9,13},{10,14},{11,15},{20,24},{2... | collective-permute-start | bytes 1327112 | tf_op jit(solution)/shard_map/ppermute | solution.py:312
  42.8 15.9 %collective-permute-start.8 = (bf16[3,2,96,384]{3,2,1,0:T(8,128)(2,1)}, bf16[3,2,96,384]{3,2,1,0:T(8,128)(2,1)S(1)}, u32[]{:S(2)}, u32[]{:S(2)}) collective-permute-start(bf16[3,2,96,384]{3,2,1,0:T(8,128)(2,1)} %collective-permute-done.5.refs_4_), channel_id=1, source_target_pairs={{4,0},{5,1},{6,2},{7,3},{8,4},{9,5},{10,6},{11,7},{20,16},{21,17},... | collective-permute-start | bytes 1327112 | tf_op jit(solution)/shard_map/ppermute | solution.py:312
  44.7 22.8 %collective-permute-start.11 = (bf16[256,1536]{1,0:T(8,128)(2,1)}, bf16[256,1536]{1,0:T(8,128)(2,1)S(1)}, u32[]{:S(2)}, u32[]{:S(2)}) collective-permute-start(bf16[256,1536]{1,0:T(8,128)(2,1)} %collective-permute-done.3.refs_9_), channel_id=1, source_target_pairs={{0,1},{1,0},{2,3},{3,2},{4,5},{5,4},{6,7},{7,6},{8,9},{9,8},{10,11... | collective-permute-start | bytes 2359304 | tf_op jit(solution)/shard_map/ppermute | solution.py:281
  52.0 15.5 %collective-permute-start.16 = (bf16[256,1536]{1,0:T(8,128)(2,1)S(1)}, bf16[256,1536]{1,0:T(8,128)(2,1)S(1)}, u32[]{:S(2)}, u32[]{:S(2)}) collective-permute-start(bf16[256,1536]{1,0:T(8,128)(2,1)S(1)} %collective-permute-done.15.refs_15_), channel_id=1, source_target_pairs={{0,1},{1,0},{2,3},{3,2},{4,5},{5,4},{6,7},{7,6},{8,9},{9,8},{10,11... | collective-permute-start | bytes 2359304 | tf_op jit(solution)/shard_map/ppermute | solution.py:281
  54.0 13.5 %collective-permute-start.13 = (bf16[256,1536]{1,0:T(8,128)(2,1)S(1)}, bf16[256,1536]{1,0:T(8,128)(2,1)S(1)}, u32[]{:S(2)}, u32[]{:S(2)}) collective-permute-start(bf16[256,1536]{1,0:T(8,128)(2,1)S(1)} %collective-permute-done.12.refs_11_), channel_id=1, source_target_pairs={{0,1},{1,0},{2,3},{3,2},{4,5},{5,4},{6,7},{7,6},{8,9},{9,8},{10,11... | collective-permute-start | bytes 2359304 | tf_op jit(solution)/shard_map/ppermute | solution.py:281
  58.7 8.7 %collective-permute-start.9 = (bf16[3,2,96,384]{3,2,1,0:T(8,128)(2,1)S(1)}, bf16[3,2,96,384]{3,2,1,0:T(8,128)(2,1)S(1)}, u32[]{:S(2)}, u32[]{:S(2)}) collective-permute-start(bf16[3,2,96,384]{3,2,1,0:T(8,128)(2,1)S(1)} %collective-permute-done.8.refs_5_), channel_id=1, source_target_pairs={{4,0},{5,1},{6,2},{7,3},{20,16},{21,17},{22,18},{23,19}} | collective-permute-start | bytes 1327112 | tf_op jit(solution)/shard_map/ppermute | solution.py:312
  90.3 23.8 %collective-permute-start.24 = (bf16[4,192,384]{2,1,0:T(8,128)(2,1)}, bf16[4,192,384]{2,1,0:T(8,128)(2,1)}, u32[]{:S(2)}, u32[]{:S(2)}) collective-permute-start(bf16[4,192,384]{2,1,0:T(8,128)(2,1)} %copy-done.14), channel_id=1, source_target_pairs={{0,4},{1,5},{2,6},{3,7},{12,8},{13,9},{14,10},{15,11},{16,20},{17,... | collective-permute-start | bytes 1769480 | tf_op jit(solution)/shard_map/ppermute | solution.py:312
  107.7 12.8 %collective-permute-start.22 = (bf16[256,1536]{1,0:T(8,128)(2,1)}, bf16[256,1536]{1,0:T(8,128)(2,1)}, u32[]{:S(2)}, u32[]{:S(2)}) collective-permute-start(bf16[256,1536]{1,0:T(8,128)(2,1)} %get-tuple-element.39), channel_id=1, source_target_pairs={{0,1},{1,0},{2,3},{3,2},{4,5},{5,4},{6,7},{7,6},{8,9},{9,8},{10,11... | collective-permute-start | bytes 2359304 | tf_op jit(solution)/shard_map/ppermute | solution.py:281
  110.2 27.7 %collective-permute-start.21 = (bf16[256,1536]{1,0:T(8,128)(2,1)}, bf16[256,1536]{1,0:T(8,128)(2,1)S(1)}, u32[]{:S(2)}, u32[]{:S(2)}) collective-permute-start(bf16[256,1536]{1,0:T(8,128)(2,1)} %copy-done.13), channel_id=1, source_target_pairs={{0,1},{1,0},{2,3},{3,2},{4,5},{5,4},{6,7},{7,6},{8,9},{9,8},{10,11... | collective-permute-start | bytes 2359304 | tf_op jit(solution)/shard_map/ppermute | solution.py:281
  113.4 8.8 %collective-permute-start.18 = (bf16[256,384]{1,0:T(8,128)(2,1)S(1)}, bf16[256,384]{1,0:T(8,128)(2,1)S(1)}, u32[]{:S(2)}, u32[]{:S(2)}) collective-permute-start(bf16[256,384]{1,0:T(8,128)(2,1)S(1)} %get-tuple-element.66), channel_id=1, source_target_pairs={{0,2},{1,3},{2,0},{3,1},{4,6},{5,7},{6,4},{7,5},{8,10},{9,11},{10,... | collective-permute-start | bytes 589832 | tf_op jit(solution)/shard_map/ppermute | solution.py:281
  115.3 16.2 %collective-permute-start.25 = (bf16[4,192,384]{2,1,0:T(8,128)(2,1)S(1)}, bf16[4,192,384]{2,1,0:T(8,128)(2,1)S(1)}, u32[]{:S(2)}, u32[]{:S(2)}) collective-permute-start(bf16[4,192,384]{2,1,0:T(8,128)(2,1)S(1)} %add_convert_fusion.3), channel_id=1, source_target_pairs={{0,4},{1,5},{2,6},{3,7},{4,8},{5,9},{6,10},{7,11},{16,20},{17,21},... | collective-permute-start | bytes 1769480 | tf_op jit(solution)/shard_map/ppermute | solution.py:312
  119.3 16.6 %collective-permute-start.27 = (bf16[4,192,384]{2,1,0:T(8,128)(2,1)S(1)}, bf16[4,192,384]{2,1,0:T(8,128)(2,1)S(1)}, u32[]{:S(2)}, u32[]{:S(2)}) collective-permute-start(bf16[4,192,384]{2,1,0:T(8,128)(2,1)S(1)} %add_convert_fusion.3), channel_id=1, source_target_pairs={{12,8},{13,9},{14,10},{15,11},{8,4},{9,5},{10,6},{11,7},{28,24},{2... | collective-permute-start | bytes 1769480 | tf_op jit(solution)/shard_map/ppermute | solution.py:312
  122.0 18.3 %collective-permute-start.23 = (bf16[256,1536]{1,0:T(8,128)(2,1)S(1)}, bf16[256,1536]{1,0:T(8,128)(2,1)S(1)}, u32[]{:S(2)}, u32[]{:S(2)}) collective-permute-start(bf16[256,1536]{1,0:T(8,128)(2,1)S(1)} %add_convert_fusion), channel_id=1, source_target_pairs={{0,2},{1,3},{2,0},{3,1},{4,6},{5,7},{6,4},{7,5},{8,10},{9,11},{10,... | collective-permute-start | bytes 2359304 | tf_op jit(solution)/shard_map/ppermute | solution.py:281
  131.7 15.4 %collective-permute-start.26 = (bf16[4,192,384]{2,1,0:T(8,128)(2,1)S(1)}, bf16[4,192,384]{2,1,0:T(8,128)(2,1)S(1)}, u32[]{:S(2)}, u32[]{:S(2)}) collective-permute-start(bf16[4,192,384]{2,1,0:T(8,128)(2,1)S(1)} %add_convert_fusion.2), channel_id=1, source_target_pairs={{0,4},{1,5},{2,6},{3,7},{4,8},{5,9},{6,10},{7,11},{8,12},{9,13},{1... | collective-permute-start | bytes 1769480 | tf_op jit(solution)/shard_map/ppermute | solution.py:312
  136.0 15.1 %collective-permute-start.28 = (bf16[4,192,384]{2,1,0:T(8,128)(2,1)S(1)}, bf16[4,192,384]{2,1,0:T(8,128)(2,1)S(1)}, u32[]{:S(2)}, u32[]{:S(2)}) collective-permute-start(bf16[4,192,384]{2,1,0:T(8,128)(2,1)S(1)} %add_convert_fusion.1), channel_id=1, source_target_pairs={{4,0},{5,1},{6,2},{7,3},{8,4},{9,5},{10,6},{11,7},{12,8},{13,9},{1... | collective-permute-start | bytes 1769480 | tf_op jit(solution)/shard_map/ppermute | solution.py:312
  151.5 8.0 %collective-permute-start.31 = (bf16[4,192,96]{2,1,0:T(8,128)(2,1)S(1)}, bf16[4,192,96]{2,1,0:T(8,128)(2,1)S(1)}, u32[]{:S(2)}, u32[]{:S(2)}) collective-permute-start(bf16[4,192,96]{2,1,0:T(8,128)(2,1)S(1)} %get-tuple-element.54), channel_id=1, source_target_pairs={{0,3},{1,2},{2,1},{3,0},{4,7},{5,6},{6,5},{7,4},{8,11},{9,10},{10,... | collective-permute-start | bytes 442376 | tf_op jit(solution)/shard_map/ppermute | solution.py:281
  154.4 9.7 %collective-permute-start.30 = (bf16[4,192,96]{2,1,0:T(8,128)(2,1)S(1)}, bf16[4,192,96]{2,1,0:T(8,128)(2,1)S(1)}, u32[]{:S(2)}, u32[]{:S(2)}) collective-permute-start(bf16[4,192,96]{2,1,0:T(8,128)(2,1)S(1)} %get-tuple-element.55), channel_id=1, source_target_pairs={{0,2},{1,3},{2,0},{3,1},{4,6},{5,7},{6,4},{7,5},{8,10},{9,11},{10,... | collective-permute-start | bytes 442376 | tf_op jit(solution)/shard_map/ppermute | solution.py:281
  (38 other events, 330.3 us)

commit v8 on v7

--- a/solution.py
+++ b/solution.py
@@ -100,22 +100,15 @@
     ]
 
 
-def targets(depth, z):
+def roles(depth, z):
     if depth == 4:
         return [
-            jnp.where(z == 0, 3, 0),
-            jnp.where(z < 2, z + 2, z - 2),
-            jnp.minimum(z + 1, 3),
-            jnp.maximum(z - 1, 0),
-            z,
+            (3 * lax.rem(z + 1, 2), [bf16, f32]),
+            (lax.rem(z + 2, 4), [f32]),
+            (1 + lax.rem(z, 2), [f32]),
+            (z, [f32]),
         ]
-    return [lax.rem(z + d, depth) for d in range(1, depth)] + [z]
-
-
-def target_types(depth):
-    if depth == 4:
-        return [bf16, f32, f32, f32, f32]
-    return [bf16] * (depth - 1) + [f32]
+    return [(lax.rem(z + d, depth), [bf16]) for d in range(1, depth)] + [(z, [f32])]
 
 
 def unpack(packed, taps):
@@ -137,15 +130,19 @@
     cots = refs[count + 6 : count + 10]
     point = refs[count + 10]
     refs = refs[count + 11 :]
-    results = (len(refs) - 7) // 2
-    stores, (wide, wide_cot, packed, taps, grads, branches, sems) = (
+    results = (len(refs) - 8) // 2
+    stores, (wide, wide_cot, packed, taps, grads, branches, slopes, sems) = (
         refs[:results],
-        refs[results : results + 7],
-    )
-    branch, grad, *outs = refs[results + 7 :]
+        refs[results : results + 8],
+    )
+    branch, grad, *outs = refs[results + 8 :]
     z, q = position()
     rows = acts[0].shape[0]
     core = lax.rem(q, 2)
+    second = started(
+        [(cot, wide_cot.at[within(toggled(q, m), rows)]) for m, cot in enumerate(cots)],
+        sems,
+    )
     first = started(
         [(act, wide.at[within(1 + toggled(q, m), rows)]) for m, act in enumerate(acts)]
         + [
@@ -154,48 +151,68 @@
         ]
         + tap_pairs(depth, pieces, packed),
         sems,
-    )
-    second = started(
-        [(cot, wide_cot.at[within(toggled(q, m), rows)]) for m, cot in enumerate(cots)],
-        sems,
-        len(first),
+        len(second),
     )
     base = len(first) + len(second)
-    finish(first)
-    unpack(packed, taps)
     finish(second)
     for part in range(4):
         here = pl.ds(part * rows, rows)
-        slope = transposed_product(wide_cot[here], point[...])
+        slopes[here] = transposed_product(wide_cot[here], point[...])
+    finish(first)
+    unpack(packed, taps)
+    for part in range(4):
+        here = pl.ds(part * rows, rows)
         pre = product(wide[here], taps[0])
         pre = pre + product(wide[pl.ds((part + 1) * rows, rows)], taps[1])
         pre = pre + product(wide[pl.ds((part + 2) * rows, rows)], taps[2])
         value = gelu_value(pre)
         branch[here] = value.astype(bf16)
         branches[:, here] = value.T.astype(bf16)
-        value = slope * gelu_slope(pre)
+        value = slopes[here] * gelu_slope(pre)
         grad[here] = value.astype(bf16)
         grads[:, here] = value.T.astype(bf16)
     last = started([(grad, stores[1]), (branch, stores[0])], sems, base)
     width = wide.shape[1] // depth
-    if len(outs) > 1:
-        where = [within(target, width) for target in targets(depth, z)]
+    if len(outs) == 1:
+        for i in range(depth):
+            lanes = pl.ds(i * width, width)
+            out = outs[0].at[lax.rem(i + depth - z, depth)]
+            for k in range(3):
+                out[k] = product(grads[...], wide[pl.ds(k * rows, 4 * rows), lanes])
+            out[3] = product(branches[...], wide_cot[:, lanes])
+        last += started([(outs[0], stores[2])], sems, base + 2)
     else:
-        where = [pl.ds(i * width, width) for i in range(depth)]
-    for i, lanes in enumerate(where):
-        if len(outs) > 1:
-            out = outs[i]
-        else:
-            out = outs[0].at[lax.rem(i + depth - z, depth)]
-        for k in range(3):
-            out[k] = product(
-                grads[...], wide[pl.ds(k * rows, 4 * rows), lanes]
-            ).astype(out.dtype)
-        out[3] = product(branches[...], wide_cot[:, lanes]).astype(out.dtype)
-        if len(outs) > 1:
-            last += started([(out, stores[2 + i])], sems, base + 2 + i)
-    if len(outs) == 1:
-        last += started([(outs[0], stores[2])], sems, base + 2)
+        i = 0
+        for target, types in roles(depth, z):
+            lanes = within(target, width)
+            same = outs[i : i + len(types)]
+            for k in range(4):
+                if k < 3:
+                    value = product(
+                        grads[...], wide[pl.ds(k * rows, 4 * rows), lanes]
+                    )
+                else:
+                    value = product(branches[...], wide_cot[:, lanes])
+                for out in same:
+                    out[k] = value.astype(out.dtype)
+            i += len(types)
+            if depth != 4:
+                last += started([(same[0], stores[1 + i])], sems, base + 1 + i)
+            elif i == 2:
+                last += started([(outs[0], stores[2])], sems, base + 2)
+            elif i == 3:
+                last += started([(outs[2], stores[3])], sems, base + 3)
+            elif i == 4:
+                last += started(
+                    [
+                        ((z == 2, outs[1], outs[3]), stores[4]),
+                        ((z == 1, outs[1], outs[3]), stores[5]),
+                    ],
+                    sems,
+                    base + 4,
+                )
+            else:
+                last += started([(outs[4], stores[6])], sems, base + 6)
     finish(last)
 
 
@@ -347,7 +364,9 @@
 
     width = channels // depth
     apart = width % 128 == 0
-    outs = [((4, quarter, width), t) for t in target_types(depth)]
+    outs = [
+        ((4, quarter, width), t) for _, types in roles(depth, z) for t in types
+    ]
     if not apart:
         outs = [((depth, 4, quarter, width), f32)]
     weight_outs = [((4 * rows, quarter), bf16)] * 2 + outs
@@ -363,26 +382,27 @@
             pltpu.VMEM((3, channels, quarter), bf16),
             pltpu.VMEM((quarter, 4 * rows), bf16),
             pltpu.VMEM((quarter, 4 * rows), bf16),
-            pltpu.SemaphoreType.DMA((2 * len(pieces) + 14,)),
+            pltpu.VMEM((4 * rows, quarter), f32),
+            pltpu.SemaphoreType.DMA((len(pieces) + 10 + len(weight_outs),)),
             *[pltpu.VMEM(*out) for out in weight_outs],
         ],
         8 * flops,
-        40,
+        60,
         pltpu.HBM,
     )
     if not apart:
         terms = [terms[0][d].astype(bf16) for d in range(1, depth)] + [terms[0][0]]
     if depth == 4:
-        three, two, up, down, total = terms
-        far = line(three, [(0, 1), (3, 2)])
+        far, two, up, down, total = terms
+        far = line(far, [(0, 1), (3, 2)])
         joined = (two + far.astype(f32)).astype(bf16)
         near_up = line(joined, [(0, 1), (1, 2)])
         near_down = line(joined, [(3, 2), (2, 1)])
-        up = (up + near_up.astype(f32)).astype(bf16)
-        down = (down + near_down.astype(f32)).astype(bf16)
+        up = up + near_up.astype(f32)
+        down = down + near_down.astype(f32)
         parts = [
-            line(up, [(0, 1), (1, 2), (2, 3)]),
-            line(down, [(1, 0), (2, 1), (3, 2)]),
+            line(up.astype(bf16), [(0, 1), (1, 2), (2, 3)]),
+            line(down.astype(bf16), [(1, 0), (2, 1), (3, 2)]),
         ]
     else:
         total = terms[-1]
@@ -404,12 +424,14 @@
             *[pltpu.VMEM(*out) for out in share_outs],
         ],
         3 * flops,
-        40,
+        60,
         pltpu.HBM,
     )
+    away = (shares[2] + cross(shares[3], 1).astype(f32)).astype(bf16)
+    arrived = cross(away, 2)
+
     mine = shares[0] + cross(shares[1], 1).astype(f32)
-    far = shares[2] + cross(shares[3], 1).astype(f32)
-    act_grad = mine + cross(far.astype(bf16), 2).astype(f32)
+    act_grad = mine + arrived.astype(f32)
     scaled = act_grad * gelu_slope(normed) * norm_gain
     inner = jnp.mean(scaled * xfull, axis=-1, keepdims=True)
     input_grad = (

time: 168 us -> 162 us (0.964)
  local copies, waits for them, and re-layouts: 15.6 us -> 8.23 us
  starting transfers between devices: 50.1 us -> 54.3 us
  waiting for transfers between devices: 64.7 us -> 61.2 us
    unnamed x61 -> x45, local copies, waits for them, and re-layouts: 11.9 us -> 2.81 us
    ppermute x11, waiting for transfers between devices: 36.7 us -> 32.8 us  [line(): lax.ppermute(value, 'seq', [(4 * a + i, 4 * b + i) for a, b in pairs for...]
    ppermute x21, starting transfers between devices: 24.1 us -> 27.3 us  [send(): lax.ppermute(value, 'seq', [p for p in pairs if p[1] is not None and 0 <=...]
  transfers between devices with their start and end apart: 32 -> 32, of which waited for: 16 -> 16; matrix products, arithmetic and copies ran while one was open for 8% -> 9% of each run, Pallas kernels for 3% -> 4%
where the time goes in v8:
time: 162 us; the launch traced here: 161 us
  waiting for transfers between devices  61.2 us (38%)
  starting transfers between devices  54.3 us (34%)
  Pallas kernels  20 us (12%)
  other arithmetic  14 us (9%)
  local copies, waits for them, and re-layouts  8.23 us (5%)
  matrix products  1.68 us (1%)
    ppermute x11, waiting for transfers between devices, line(): lax.ppermute(value, 'seq', [(4 * a + i, 4 * b + i) for a, b in pairs for...  32.8 us
    ppermute x21, waiting for transfers between devices, send(): lax.ppermute(value, 'seq', [p for p in pairs if p[1] is not None and 0 <=...  28.4 us
    ppermute x21, starting transfers between devices, send(): lax.ppermute(value, 'seq', [p for p in pairs if p[1] is not None and 0 <=...  27.3 us
    ppermute x11, starting transfers between devices, line(): lax.ppermute(value, 'seq', [(4 * a + i, 4 * b + i) for a, b in pairs for...  27.1 us
    pallas_call x3, Pallas kernels, call(): pl.pallas_call(kernel, out_shape=[jax.ShapeDtypeStruct(s, t) for s, t in...  20 us
    select_n x4, other arithmetic, in_order(): jnp.where(first, jnp.concatenate([mine, other], axis), jnp.concatenate([o...  4.62 us
  transfers between devices with their start and end apart: 32, of which 16 were waited for; matrix products, arithmetic and copies ran while one was open for 9% of the time, Pallas kernels for 4%

profile of v8, /device:TPU:9, one launch (start us, length us, event | category | flops | bytes accessed | tf_op | source)
XLA Modules:
  0.0 160.6 jit_solution(8709826011860976789)
XLA Ops:
  0.7 2.3 %dynamic-slice_bitcast_fusion.4 = (bf16[3,1,96,192]{3,2,1,0:T(8,128)(2,1)S(1)}, bf16[3,96,192]{2,1,0:T(8,128)(2,1)}, bf16[3,96,192]{2,1,0:T(8,128)(2,1)}, bf16[3,96,192]{2,1,0:T(8,128)(2,1)S(1)}) fusion(bf16[3,96,768]{2,1,0:T(8,128)(2,1)} %param.7, s32[]{:T(128)S(6)} %select_n.115, s32[]{:T(128)S(6)} %select_n.107, s32[]{:T(128)S(6)} %select_n.106, ...), kind=kLoop, calls=%fused_computation.51 | loop fusion | bytes 884752 | tf_op jit(solution)/shard_map/concatenate | solution.py:314
  9.5 3.3 %collective-permute-done.2 = bf16[3,96,192]{2,1,0:T(8,128)(2,1)} collective-permute-done((bf16[3,96,192]{2,1,0:T(8,128)(2,1)S(1)}, bf16[3,96,192]{2,1,0:T(8,128)(2,1)}, u32[]{:S(2)}, u32[]{:S(2)}) %collective-permute-start.2) | collective-permute-done | bytes 110624 | tf_op jit(solution)/shard_map/ppermute | solution.py:298
  16.2 3.2 %collective-permute-start.4 = (bf16[3,2,96,384]{3,2,1,0:T(8,128)(2,1)}, bf16[3,2,96,384]{3,2,1,0:T(8,128)(2,1)}, u32[]{:S(2)}, u32[]{:S(2)}) collective-permute-start(bf16[3,2,96,384]{3,2,1,0:T(8,128)(2,1)} %maximum_select_fusion.refs_0_), channel_id=1, source_target_pairs={{0,4},{1,5},{2,6},{3,7},{4,8},{5,9},{6,10},{7,11},{8,12},{9,13},{1... | collective-permute-start | bytes 1327112 | tf_op jit(solution)/shard_map/ppermute | solution.py:329
  19.4 2.9 %collective-permute-start.5 = (bf16[3,2,96,384]{3,2,1,0:T(8,128)(2,1)}, bf16[3,2,96,384]{3,2,1,0:T(8,128)(2,1)}, u32[]{:S(2)}, u32[]{:S(2)}) collective-permute-start(bf16[3,2,96,384]{3,2,1,0:T(8,128)(2,1)} %maximum_select_fusion.refs_0_), channel_id=1, source_target_pairs={{4,0},{5,1},{6,2},{7,3},{8,4},{9,5},{10,6},{11,7},{12,8},{13,9},{1... | collective-permute-start | bytes 1327112 | tf_op jit(solution)/shard_map/ppermute | solution.py:329
  23.5 6.0 %collective-permute-done.4.refs_1_ = bf16[3,2,96,384]{3,2,1,0:T(8,128)(2,1)} collective-permute-done((bf16[3,2,96,384]{3,2,1,0:T(8,128)(2,1)}, bf16[3,2,96,384]{3,2,1,0:T(8,128)(2,1)}, u32[]{:S(2)}, u32[]{:S(2)}) %collective-permute-start.4) | collective-permute-done | bytes 442400 | tf_op jit(solution)/shard_map/ppermute | solution.py:329
  29.5 2.9 %collective-permute-done.5.refs_4_ = bf16[3,2,96,384]{3,2,1,0:T(8,128)(2,1)} collective-permute-done((bf16[3,2,96,384]{3,2,1,0:T(8,128)(2,1)}, bf16[3,2,96,384]{3,2,1,0:T(8,128)(2,1)}, u32[]{:S(2)}, u32[]{:S(2)}) %collective-permute-start.5) | collective-permute-done | bytes 442400 | tf_op jit(solution)/shard_map/ppermute | solution.py:329
  36.5 3.2 %collective-permute-start.12 = (bf16[256,1536]{1,0:T(8,128)(2,1)S(1)}, bf16[256,1536]{1,0:T(8,128)(2,1)S(1)}, u32[]{:S(2)}, u32[]{:S(2)}) collective-permute-start(bf16[256,1536]{1,0:T(8,128)(2,1)S(1)} %broadcast_select_fusion), channel_id=1, source_target_pairs={{1,5},{3,7},{4,0},{5,9},{6,2},{7,11},{8,4},{9,13},{10,6},{11,15},{... | collective-permute-start | bytes 2359304 | tf_op jit(solution)/shard_map/ppermute | solution.py:298
  39.8 3.2 %collective-permute-start.6 = (bf16[3,2,96,384]{3,2,1,0:T(8,128)(2,1)}, bf16[3,2,96,384]{3,2,1,0:T(8,128)(2,1)S(1)}, u32[]{:S(2)}, u32[]{:S(2)}) collective-permute-start(bf16[3,2,96,384]{3,2,1,0:T(8,128)(2,1)} %collective-permute-done.4.refs_1_), channel_id=1, source_target_pairs={{4,8},{5,9},{6,10},{7,11},{8,12},{9,13},{10,14},{11,15},{20,24},{2... | collective-permute-start | bytes 1327112 | tf_op jit(solution)/shard_map/ppermute | solution.py:329
  45.9 6.4 %collective-permute-done.15.refs_15_ = bf16[256,1536]{1,0:T(8,128)(2,1)S(1)} collective-permute-done((bf16[256,1536]{1,0:T(8,128)(2,1)}, bf16[256,1536]{1,0:T(8,128)(2,1)S(1)}, u32[]{:S(2)}, u32[]{:S(2)}) %collective-permute-start.15) | collective-permute-done | bytes 786464 | tf_op jit(solution)/shard_map/ppermute | solution.py:298
  55.4 2.9 %collective-permute-done.6.refs_2_ = bf16[3,2,96,384]{3,2,1,0:T(8,128)(2,1)S(1)} collective-permute-done((bf16[3,2,96,384]{3,2,1,0:T(8,128)(2,1)}, bf16[3,2,96,384]{3,2,1,0:T(8,128)(2,1)S(1)}, u32[]{:S(2)}, u32[]{:S(2)}) %collective-permute-start.6) | collective-permute-done | bytes 442400 | tf_op jit(solution)/shard_map/ppermute | solution.py:329
  61.2 5.4 %collective-permute-done.9.refs_6_ = bf16[3,2,96,384]{3,2,1,0:T(8,128)(2,1)S(1)} collective-permute-done((bf16[3,2,96,384]{3,2,1,0:T(8,128)(2,1)S(1)}, bf16[3,2,96,384]{3,2,1,0:T(8,128)(2,1)S(1)}, u32[]{:S(2)}, u32[]{:S(2)}) %collective-permute-start.9) | collective-permute-done | bytes 442400 | tf_op jit(solution)/shard_map/ppermute | solution.py:329
  68.5 12.6 %shard_map.84 = (bf16[1024,192]{1,0:T(8,128)(2,1)}, bf16[1024,192]{1,0:T(8,128)(2,1)}, bf16[4,192,384]{2,1,0:T(8,128)(2,1)}, f32[4,192,384]{2,1,0:T(8,128)}, f32...) custom-call(bf16[3,2,96,384]{3,2,1,0:T(8,128)(2,1)} %maximum_select_fusion.refs_0_, ...), custom_call_target="tpu_custom_call" | custom-call | flops 4831838208 | bytes 17645568 | tf_op jit(solution)/shard_map/pallas_call | solution.py:271
  82.1 6.0 %collective-permute-start.19 = (bf16[256,192]{1,0:T(8,128)(2,1)S(1)}, bf16[256,192]{1,0:T(8,128)(2,1)S(1)}, u32[]{:S(2)}, u32[]{:S(2)}) collective-permute-start(bf16[256,192]{1,0:T(8,128)(2,1)S(1)} %get-tuple-element.58), channel_id=1, source_target_pairs={{0,4},{1,5},{2,6},{3,7},{4,8},{5,9},{6,10},{7,11},{8,12},{9,13},{1... | collective-permute-start | bytes 294920 | tf_op jit(solution)/shard_map/ppermute | solution.py:298
  91.7 4.4 %collective-permute-done.20.refs_9_ = bf16[256,192]{1,0:T(8,128)(2,1)} collective-permute-done((bf16[256,192]{1,0:T(8,128)(2,1)S(1)}, bf16[256,192]{1,0:T(8,128)(2,1)}, u32[]{:S(2)}, u32[]{:S(2)}) %collective-permute-start.20) | collective-permute-done | bytes 98336 | tf_op jit(solution)/shard_map/ppermute | solution.py:298
  96.1 5.7 %shard_map.85 = (f32[256,1536]{1,0:T(8,128)}, bf16[256,1536]{1,0:T(8,128)(2,1)}, f32[256,1536]{1,0:T(8,128)}, bf16[256,1536]{1,0:T(8,128)(2,1)}) custom-call(bf16[3,2,96,384]{3,2,1,0:T(8,128)(2,1)} %maximum_select_fusion.refs_0_, bf16[3,2,96,384]{3,2,1,0:T(8,128)(2,1)} %collective-permute-done.4.refs_1_, bf16[3,2,96,384]{3,2,1,0:T(8,128)(2,1)} %copy-done.17, ...), custom_call_target="tpu_custom_call" | custom-call | flops 1811939328 | bytes 8404992 | tf_op jit(solution)/shard_map/pallas_call | solution.py:271
  107.7 4.8 %collective-permute-start.25 = (bf16[4,192,384]{2,1,0:T(8,128)(2,1)S(1)}, bf16[4,192,384]{2,1,0:T(8,128)(2,1)S(1)}, u32[]{:S(2)}, u32[]{:S(2)}) collective-permute-start(bf16[4,192,384]{2,1,0:T(8,128)(2,1)S(1)} %add_convert_fusion.3), channel_id=1, source_target_pairs={{0,4},{1,5},{2,6},{3,7},{4,8},{5,9},{6,10},{7,11},{16,20},{17,21},... | collective-permute-start | bytes 1769480 | tf_op jit(solution)/shard_map/ppermute | solution.py:329
  117.7 6.8 %collective-permute-done.25 = bf16[4,192,384]{2,1,0:T(8,128)(2,1)S(1)} collective-permute-done((bf16[4,192,384]{2,1,0:T(8,128)(2,1)S(1)}, bf16[4,192,384]{2,1,0:T(8,128)(2,1)S(1)}, u32[]{:S(2)}, u32[]{:S(2)}) %collective-permute-start.25) | collective-permute-done | bytes 589856 | tf_op jit(solution)/shard_map/ppermute | solution.py:329
  124.7 4.2 %collective-permute-start.26 = (bf16[4,192,384]{2,1,0:T(8,128)(2,1)S(1)}, bf16[4,192,384]{2,1,0:T(8,128)(2,1)S(1)}, u32[]{:S(2)}, u32[]{:S(2)}) collective-permute-start(bf16[4,192,384]{2,1,0:T(8,128)(2,1)S(1)} %add_convert_fusion.2), channel_id=1, source_target_pairs={{0,4},{1,5},{2,6},{3,7},{4,8},{5,9},{6,10},{7,11},{8,12},{9,13},{1... | collective-permute-start | bytes 1769480 | tf_op jit(solution)/shard_map/ppermute | solution.py:329
  131.1 2.3 %collective-permute-done.23 = bf16[256,1536]{1,0:T(8,128)(2,1)S(1)} collective-permute-done((bf16[256,1536]{1,0:T(8,128)(2,1)S(1)}, bf16[256,1536]{1,0:T(8,128)(2,1)S(1)}, u32[]{:S(2)}, u32[]{:S(2)}) %collective-permute-start.23) | collective-permute-done | bytes 786464 | tf_op jit(solution)/shard_map/ppermute | solution.py:298
  135.1 4.9 %collective-permute-done.26 = bf16[4,192,384]{2,1,0:T(8,128)(2,1)S(1)} collective-permute-done((bf16[4,192,384]{2,1,0:T(8,128)(2,1)S(1)}, bf16[4,192,384]{2,1,0:T(8,128)(2,1)S(1)}, u32[]{:S(2)}, u32[]{:S(2)}) %collective-permute-start.26) | collective-permute-done | bytes 589856 | tf_op jit(solution)/shard_map/ppermute | solution.py:329
  140.0 4.0 %collective-permute-done.28 = bf16[4,192,384]{2,1,0:T(8,128)(2,1)S(1)} collective-permute-done((bf16[4,192,384]{2,1,0:T(8,128)(2,1)S(1)}, bf16[4,192,384]{2,1,0:T(8,128)(2,1)S(1)}, u32[]{:S(2)}, u32[]{:S(2)}) %collective-permute-start.28) | collective-permute-done | bytes 589856 | tf_op jit(solution)/shard_map/ppermute | solution.py:329
  144.4 3.8 %collective-permute-start.31 = (bf16[4,192,96]{2,1,0:T(8,128)(2,1)S(1)}, bf16[4,192,96]{2,1,0:T(8,128)(2,1)S(1)}, u32[]{:S(2)}, u32[]{:S(2)}) collective-permute-start(bf16[4,192,96]{2,1,0:T(8,128)(2,1)S(1)} %get-tuple-element.54), channel_id=1, source_target_pairs={{0,3},{1,2},{2,1},{3,0},{4,7},{5,6},{6,5},{7,4},{8,11},{9,10},{10,... | collective-permute-start | bytes 442376 | tf_op jit(solution)/shard_map/ppermute | solution.py:298
  150.3 3.6 %collective-permute-done.31.refs_3_ = bf16[4,192,96]{2,1,0:T(8,128)(2,1)S(1)} collective-permute-done((bf16[4,192,96]{2,1,0:T(8,128)(2,1)S(1)}, bf16[4,192,96]{2,1,0:T(8,128)(2,1)S(1)}, u32[]{:S(2)}, u32[]{:S(2)}) %collective-permute-start.31) | collective-permute-done | bytes 147488 | tf_op jit(solution)/shard_map/ppermute | solution.py:298
  153.9 4.2 %collective-permute-done.30.refs_2_ = bf16[4,192,96]{2,1,0:T(8,128)(2,1)S(1)} collective-permute-done((bf16[4,192,96]{2,1,0:T(8,128)(2,1)S(1)}, bf16[4,192,96]{2,1,0:T(8,128)(2,1)S(1)}, u32[]{:S(2)}, u32[]{:S(2)}) %collective-permute-start.30) | collective-permute-done | bytes 147488 | tf_op jit(solution)/shard_map/ppermute | solution.py:298
  (112 shorter events, 50.5 us)
Async XLA Ops:
  14.9 19.2 %collective-permute-start.3 = (bf16[256,1536]{1,0:T(8,128)(2,1)}, bf16[256,1536]{1,0:T(8,128)(2,1)}, u32[]{:S(2)}, u32[]{:S(2)}) collective-permute-start(bf16[256,1536]{1,0:T(8,128)(2,1)} %fusion.6.refs_7_), channel_id=1, source_target_pairs={{0,2},{1,3},{2,0},{3,1},{4,6},{5,7},{6,4},{7,5},{8,10},{9,11},{10,... | collective-permute-start | bytes 2359304 | tf_op jit(solution)/shard_map/ppermute | solution.py:298
  16.2 13.3 %collective-permute-start.4 = (bf16[3,2,96,384]{3,2,1,0:T(8,128)(2,1)}, bf16[3,2,96,384]{3,2,1,0:T(8,128)(2,1)}, u32[]{:S(2)}, u32[]{:S(2)}) collective-permute-start(bf16[3,2,96,384]{3,2,1,0:T(8,128)(2,1)} %maximum_select_fusion.refs_0_), channel_id=1, source_target_pairs={{0,4},{1,5},{2,6},{3,7},{4,8},{5,9},{6,10},{7,11},{8,12},{9,13},{1... | collective-permute-start | bytes 1327112 | tf_op jit(solution)/shard_map/ppermute | solution.py:329
  19.4 13.0 %collective-permute-start.5 = (bf16[3,2,96,384]{3,2,1,0:T(8,128)(2,1)}, bf16[3,2,96,384]{3,2,1,0:T(8,128)(2,1)}, u32[]{:S(2)}, u32[]{:S(2)}) collective-permute-start(bf16[3,2,96,384]{3,2,1,0:T(8,128)(2,1)} %maximum_select_fusion.refs_0_), channel_id=1, source_target_pairs={{4,0},{5,1},{6,2},{7,3},{8,4},{9,5},{10,6},{11,7},{12,8},{13,9},{1... | collective-permute-start | bytes 1327112 | tf_op jit(solution)/shard_map/ppermute | solution.py:329
  22.3 22.7 %collective-permute-start.10 = (bf16[256,1536]{1,0:T(8,128)(2,1)}, bf16[256,1536]{1,0:T(8,128)(2,1)S(1)}, u32[]{:S(2)}, u32[]{:S(2)}) collective-permute-start(bf16[256,1536]{1,0:T(8,128)(2,1)} %fusion.6.refs_7_), channel_id=1, source_target_pairs={{0,1},{1,0},{2,3},{3,2},{4,5},{5,4},{6,7},{7,6},{8,9},{9,8},{10,11... | collective-permute-start | bytes 2359304 | tf_op jit(solution)/shard_map/ppermute | solution.py:298
  23.5 19.5 %collective-permute-start.14 = (bf16[256,1536]{1,0:T(8,128)(2,1)}, bf16[256,1536]{1,0:T(8,128)(2,1)S(1)}, u32[]{:S(2)}, u32[]{:S(2)}) collective-permute-start(bf16[256,1536]{1,0:T(8,128)(2,1)} %refs_13_), channel_id=1, source_target_pairs={{0,1},{1,0},{2,3},{3,2},{4,5},{5,4},{6,7},{7,6},{8,9},{9,8},{10,11... | collective-permute-start | bytes 2359304 | tf_op jit(solution)/shard_map/ppermute | solution.py:298
  34.1 18.1 %collective-permute-start.15 = (bf16[256,1536]{1,0:T(8,128)(2,1)}, bf16[256,1536]{1,0:T(8,128)(2,1)S(1)}, u32[]{:S(2)}, u32[]{:S(2)}) collective-permute-start(bf16[256,1536]{1,0:T(8,128)(2,1)} %refs_13_), channel_id=1, source_target_pairs={{0,2},{1,3},{2,0},{3,1},{4,6},{5,7},{6,4},{7,5},{8,10},{9,11},{10,... | collective-permute-start | bytes 2359304 | tf_op jit(solution)/shard_map/ppermute | solution.py:298
  36.5 17.7 %collective-permute-start.12 = (bf16[256,1536]{1,0:T(8,128)(2,1)S(1)}, bf16[256,1536]{1,0:T(8,128)(2,1)S(1)}, u32[]{:S(2)}, u32[]{:S(2)}) collective-permute-start(bf16[256,1536]{1,0:T(8,128)(2,1)S(1)} %broadcast_select_fusion), channel_id=1, source_target_pairs={{1,5},{3,7},{4,0},{5,9},{6,2},{7,11},{8,4},{9,13},{10,6},{11,15},{... | collective-permute-start | bytes 2359304 | tf_op jit(solution)/shard_map/ppermute | solution.py:298
  39.8 18.5 %collective-permute-start.6 = (bf16[3,2,96,384]{3,2,1,0:T(8,128)(2,1)}, bf16[3,2,96,384]{3,2,1,0:T(8,128)(2,1)S(1)}, u32[]{:S(2)}, u32[]{:S(2)}) collective-permute-start(bf16[3,2,96,384]{3,2,1,0:T(8,128)(2,1)} %collective-permute-done.4.refs_1_), channel_id=1, source_target_pairs={{4,8},{5,9},{6,10},{7,11},{8,12},{9,13},{10,14},{11,15},{20,24},{2... | collective-permute-start | bytes 1327112 | tf_op jit(solution)/shard_map/ppermute | solution.py:329
  43.0 15.9 %collective-permute-start.8 = (bf16[3,2,96,384]{3,2,1,0:T(8,128)(2,1)}, bf16[3,2,96,384]{3,2,1,0:T(8,128)(2,1)S(1)}, u32[]{:S(2)}, u32[]{:S(2)}) collective-permute-start(bf16[3,2,96,384]{3,2,1,0:T(8,128)(2,1)} %collective-permute-done.5.refs_4_), channel_id=1, source_target_pairs={{4,0},{5,1},{6,2},{7,3},{8,4},{9,5},{10,6},{11,7},{20,16},{21,17},... | collective-permute-start | bytes 1327112 | tf_op jit(solution)/shard_map/ppermute | solution.py:329
  45.0 21.6 %collective-permute-start.11 = (bf16[256,1536]{1,0:T(8,128)(2,1)}, bf16[256,1536]{1,0:T(8,128)(2,1)S(1)}, u32[]{:S(2)}, u32[]{:S(2)}) collective-permute-start(bf16[256,1536]{1,0:T(8,128)(2,1)} %collective-permute-done.3.refs_9_), channel_id=1, source_target_pairs={{0,1},{1,0},{2,3},{3,2},{4,5},{5,4},{6,7},{7,6},{8,9},{9,8},{10,11... | collective-permute-start | bytes 2359304 | tf_op jit(solution)/shard_map/ppermute | solution.py:298
  52.2 14.4 %collective-permute-start.16 = (bf16[256,1536]{1,0:T(8,128)(2,1)S(1)}, bf16[256,1536]{1,0:T(8,128)(2,1)S(1)}, u32[]{:S(2)}, u32[]{:S(2)}) collective-permute-start(bf16[256,1536]{1,0:T(8,128)(2,1)S(1)} %collective-permute-done.15.refs_15_), channel_id=1, source_target_pairs={{0,1},{1,0},{2,3},{3,2},{4,5},{5,4},{6,7},{7,6},{8,9},{9,8},{10,11... | collective-permute-start | bytes 2359304 | tf_op jit(solution)/shard_map/ppermute | solution.py:298
  54.3 14.2 %collective-permute-start.13 = (bf16[256,1536]{1,0:T(8,128)(2,1)S(1)}, bf16[256,1536]{1,0:T(8,128)(2,1)}, u32[]{:S(2)}, u32[]{:S(2)}) collective-permute-start(bf16[256,1536]{1,0:T(8,128)(2,1)S(1)} %collective-permute-done.12.refs_11_), channel_id=1, source_target_pairs={{0,1},{1,0},{2,3},{3,2},{4,5},{5,4},{6,7},{7,6},{8,9},{9,8},{10,11... | collective-permute-start | bytes 2359304 | tf_op jit(solution)/shard_map/ppermute | solution.py:298
  82.1 9.6 %collective-permute-start.19 = (bf16[256,192]{1,0:T(8,128)(2,1)S(1)}, bf16[256,192]{1,0:T(8,128)(2,1)S(1)}, u32[]{:S(2)}, u32[]{:S(2)}) collective-permute-start(bf16[256,192]{1,0:T(8,128)(2,1)S(1)} %get-tuple-element.58), channel_id=1, source_target_pairs={{0,4},{1,5},{2,6},{3,7},{4,8},{5,9},{6,10},{7,11},{8,12},{9,13},{1... | collective-permute-start | bytes 294920 | tf_op jit(solution)/shard_map/ppermute | solution.py:298
  90.1 16.3 %collective-permute-start.24 = (bf16[4,192,384]{2,1,0:T(8,128)(2,1)}, bf16[4,192,384]{2,1,0:T(8,128)(2,1)}, u32[]{:S(2)}, u32[]{:S(2)}) collective-permute-start(bf16[4,192,384]{2,1,0:T(8,128)(2,1)} %get-tuple-element.43), channel_id=1, source_target_pairs={{0,4},{1,5},{2,6},{3,7},{12,8},{13,9},{14,10},{15,11},{16,20},{17,... | collective-permute-start | bytes 1769480 | tf_op jit(solution)/shard_map/ppermute | solution.py:329
  101.8 12.0 %collective-permute-start.22 = (bf16[256,1536]{1,0:T(8,128)(2,1)}, bf16[256,1536]{1,0:T(8,128)(2,1)}, u32[]{:S(2)}, u32[]{:S(2)}) collective-permute-start(bf16[256,1536]{1,0:T(8,128)(2,1)} %get-tuple-element.39), channel_id=1, source_target_pairs={{0,1},{1,0},{2,3},{3,2},{4,5},{5,4},{6,7},{7,6},{8,9},{9,8},{10,11... | collective-permute-start | bytes 2359304 | tf_op jit(solution)/shard_map/ppermute | solution.py:298
  103.1 27.9 %collective-permute-start.21 = (bf16[256,1536]{1,0:T(8,128)(2,1)}, bf16[256,1536]{1,0:T(8,128)(2,1)S(1)}, u32[]{:S(2)}, u32[]{:S(2)}) collective-permute-start(bf16[256,1536]{1,0:T(8,128)(2,1)} %get-tuple-element.37), channel_id=1, source_target_pairs={{0,1},{1,0},{2,3},{3,2},{4,5},{5,4},{6,7},{7,6},{8,9},{9,8},{10,11... | collective-permute-start | bytes 2359304 | tf_op jit(solution)/shard_map/ppermute | solution.py:298
  106.3 9.7 %collective-permute-start.18 = (bf16[256,384]{1,0:T(8,128)(2,1)S(1)}, bf16[256,384]{1,0:T(8,128)(2,1)S(1)}, u32[]{:S(2)}, u32[]{:S(2)}) collective-permute-start(bf16[256,384]{1,0:T(8,128)(2,1)S(1)} %get-tuple-element.66), channel_id=1, source_target_pairs={{0,2},{1,3},{2,0},{3,1},{4,6},{5,7},{6,4},{7,5},{8,10},{9,11},{10,... | collective-permute-start | bytes 589832 | tf_op jit(solution)/shard_map/ppermute | solution.py:298
  107.7 16.8 %collective-permute-start.25 = (bf16[4,192,384]{2,1,0:T(8,128)(2,1)S(1)}, bf16[4,192,384]{2,1,0:T(8,128)(2,1)S(1)}, u32[]{:S(2)}, u32[]{:S(2)}) collective-permute-start(bf16[4,192,384]{2,1,0:T(8,128)(2,1)S(1)} %add_convert_fusion.3), channel_id=1, source_target_pairs={{0,4},{1,5},{2,6},{3,7},{4,8},{5,9},{6,10},{7,11},{16,20},{17,21},... | collective-permute-start | bytes 1769480 | tf_op jit(solution)/shard_map/ppermute | solution.py:329
  112.5 16.4 %collective-permute-start.27 = (bf16[4,192,384]{2,1,0:T(8,128)(2,1)S(1)}, bf16[4,192,384]{2,1,0:T(8,128)(2,1)S(1)}, u32[]{:S(2)}, u32[]{:S(2)}) collective-permute-start(bf16[4,192,384]{2,1,0:T(8,128)(2,1)S(1)} %add_convert_fusion.3), channel_id=1, source_target_pairs={{12,8},{13,9},{14,10},{15,11},{8,4},{9,5},{10,6},{11,7},{28,24},{2... | collective-permute-start | bytes 1769480 | tf_op jit(solution)/shard_map/ppermute | solution.py:329
  115.2 18.2 %collective-permute-start.23 = (bf16[256,1536]{1,0:T(8,128)(2,1)S(1)}, bf16[256,1536]{1,0:T(8,128)(2,1)S(1)}, u32[]{:S(2)}, u32[]{:S(2)}) collective-permute-start(bf16[256,1536]{1,0:T(8,128)(2,1)S(1)} %add_convert_fusion), channel_id=1, source_target_pairs={{0,2},{1,3},{2,0},{3,1},{4,6},{5,7},{6,4},{7,5},{8,10},{9,11},{10,... | collective-permute-start | bytes 2359304 | tf_op jit(solution)/shard_map/ppermute | solution.py:298
  124.7 15.3 %collective-permute-start.26 = (bf16[4,192,384]{2,1,0:T(8,128)(2,1)S(1)}, bf16[4,192,384]{2,1,0:T(8,128)(2,1)S(1)}, u32[]{:S(2)}, u32[]{:S(2)}) collective-permute-start(bf16[4,192,384]{2,1,0:T(8,128)(2,1)S(1)} %add_convert_fusion.2), channel_id=1, source_target_pairs={{0,4},{1,5},{2,6},{3,7},{4,8},{5,9},{6,10},{7,11},{8,12},{9,13},{1... | collective-permute-start | bytes 1769480 | tf_op jit(solution)/shard_map/ppermute | solution.py:329
  129.1 14.9 %collective-permute-start.28 = (bf16[4,192,384]{2,1,0:T(8,128)(2,1)S(1)}, bf16[4,192,384]{2,1,0:T(8,128)(2,1)S(1)}, u32[]{:S(2)}, u32[]{:S(2)}) collective-permute-start(bf16[4,192,384]{2,1,0:T(8,128)(2,1)S(1)} %add_convert_fusion.1), channel_id=1, source_target_pairs={{4,0},{5,1},{6,2},{7,3},{8,4},{9,5},{10,6},{11,7},{12,8},{13,9},{1... | collective-permute-start | bytes 1769480 | tf_op jit(solution)/shard_map/ppermute | solution.py:329
  144.4 9.5 %collective-permute-start.31 = (bf16[4,192,96]{2,1,0:T(8,128)(2,1)S(1)}, bf16[4,192,96]{2,1,0:T(8,128)(2,1)S(1)}, u32[]{:S(2)}, u32[]{:S(2)}) collective-permute-start(bf16[4,192,96]{2,1,0:T(8,128)(2,1)S(1)} %get-tuple-element.54), channel_id=1, source_target_pairs={{0,3},{1,2},{2,1},{3,0},{4,7},{5,6},{6,5},{7,4},{8,11},{9,10},{10,... | collective-permute-start | bytes 442376 | tf_op jit(solution)/shard_map/ppermute | solution.py:298
  148.2 9.9 %collective-permute-start.30 = (bf16[4,192,96]{2,1,0:T(8,128)(2,1)S(1)}, bf16[4,192,96]{2,1,0:T(8,128)(2,1)S(1)}, u32[]{:S(2)}, u32[]{:S(2)}) collective-permute-start(bf16[4,192,96]{2,1,0:T(8,128)(2,1)S(1)} %get-tuple-element.55), channel_id=1, source_target_pairs={{0,2},{1,3},{2,0},{3,1},{4,6},{5,7},{6,4},{7,5},{8,10},{9,11},{10,... | collective-permute-start | bytes 442376 | tf_op jit(solution)/shard_map/ppermute | solution.py:298
  (30 other events, 258.7 us)

commit v9 on v8

--- a/solution.py
+++ b/solution.py
@@ -114,11 +114,16 @@
 def unpack(packed, taps):
     _, depth, _, own, width = packed.shape
     quarter = width // 2
-    for k in range(3):
-        for i in range(2 * depth):
-            for core in range(2):
-                taps[k, pl.ds((2 * i + core) * own, own), :] = packed[
-                    k, i // 2, i % 2, :, core * quarter : (core + 1) * quarter
+    _, q = position()
+    y, core = (q // 2, lax.rem(q, 2)) if own % 16 == 0 else (0, 0)
+    for i in range(2 * depth):
+        side = y + (i % 2) * (1 - 2 * y)
+        for half in range(2):
+            start = 2 * (2 * (i // 2) + side) + core + half * (1 - 2 * core)
+            here = within(start, own) if own % 16 == 0 else pl.ds(start * own, own)
+            for k in range(3):
+                taps[k, here, :] = packed[
+                    k, i // 2, i % 2, :, half * quarter : (half + 1) * quarter
                 ]
 
 
@@ -130,7 +135,9 @@
     cots = refs[count + 6 : count + 10]
     point = refs[count + 10]
     refs = refs[count + 11 :]
-    results = (len(refs) - 8) // 2
+    results = (len(refs) - 10) // 2
+    low, high = refs[results : results + 2]
+    refs = refs[:results] + refs[results + 2 :]
     stores, (wide, wide_cot, packed, taps, grads, branches, slopes, sems) = (
         refs[:results],
         refs[results : results + 8],
@@ -172,6 +179,8 @@
         grad[here] = value.astype(bf16)
         grads[:, here] = value.T.astype(bf16)
     last = started([(grad, stores[1]), (branch, stores[0])], sems, base)
+    ends = [(grad.at[pl.ds(3 * rows, rows)], low), (grad.at[pl.ds(0, rows)], high)]
+    last += started(ends, sems, base + len(stores))
     width = wide.shape[1] // depth
     if len(outs) == 1:
         for i in range(depth):
@@ -261,7 +270,7 @@
         here = pl.ds(j * quarter, quarter)
         for k in range(3):
             dilated[k, :, here] = held[m, k].T
-        point[here, :] = held[m, 3]
+        point[:, here] = held[m, 3].T
 
 
 def call(kernel, outs, args, specs, scratch, flops, limit, kept=pltpu.VMEM):
@@ -321,9 +330,14 @@
     inputs = after(inputs, *quarters[1:])
     cotangent = after(cotangent, *quarters[1:])
     got = [quarters[0]] + [cross(quarters[m], m) for m in range(1, 4)]
-    same = in_order(core == 0, got[0], got[1], 2)
-    other = in_order(core == 0, got[2], got[3], 2)
-    start_piece = in_order(y == 0, same[:, None], other[:, None], 1)
+    if own % 16 == 0:
+        same = jnp.concatenate(got[:2], 2)
+        other = jnp.concatenate(got[2:], 2)
+        start_piece = jnp.stack([same, other], 1)
+    else:
+        same = in_order(core == 0, got[0], got[1], 2)
+        other = in_order(core == 0, got[2], got[3], 2)
+        start_piece = in_order(y == 0, same[:, None], other[:, None], 1)
 
     def line(value, pairs):
         return lax.ppermute(
@@ -370,9 +384,9 @@
     if not apart:
         outs = [((depth, 4, quarter, width), f32)]
     weight_outs = [((4 * rows, quarter), bf16)] * 2 + outs
-    branch, pre_grad, *terms = call(
+    *terms, low, high = call(
         functools.partial(weight_kernel, depth),
-        weight_outs,
+        weight_outs + [((rows, quarter), bf16)] * 2,
         [*pieces, *acts, edge, edge_other, *cots, point_rows],
         [pltpu.HBM] * (len(pieces) + 10) + [pltpu.VMEM],
         [
@@ -383,13 +397,14 @@
             pltpu.VMEM((quarter, 4 * rows), bf16),
             pltpu.VMEM((quarter, 4 * rows), bf16),
             pltpu.VMEM((4 * rows, quarter), f32),
-            pltpu.SemaphoreType.DMA((len(pieces) + 10 + len(weight_outs),)),
+            pltpu.SemaphoreType.DMA((len(pieces) + 12 + len(weight_outs),)),
             *[pltpu.VMEM(*out) for out in weight_outs],
         ],
         8 * flops,
         60,
         pltpu.HBM,
     )
+    branch, pre_grad, *terms = terms
     if not apart:
         terms = [terms[0][d].astype(bf16) for d in range(1, depth)] + [terms[0][0]]
     if depth == 4:
@@ -408,8 +423,8 @@
         total = terms[-1]
         parts = [to_z(term, d + 1) for d, term in enumerate(terms[:-1])]
 
-    grad_low = send(pre_grad[3 * rows :], lambda i: i + 4)
-    grad_high = send(pre_grad[:rows], lambda i: i - 4)
+    grad_low = send(low, lambda i: i + 4)
+    grad_high = send(high, lambda i: i - 4)
     share_outs = [((rows, channels), t) for t in (f32, bf16, f32, bf16)]
     shares = call(
         functools.partial(backward_kernel, depth),
@@ -452,14 +467,14 @@
     slices[3] = after(slices[3], input_grad, outputs)
     dilated_grad, point_grad = call(
         final_kernel,
-        [((3, own, hidden), f32), ((hidden, own), f32)],
+        [((3, own, hidden), f32), ((own, hidden), f32)],
         slices,
         [pltpu.VMEM] * 4,
         [pltpu.VMEM((4, 4, quarter, own), f32)],
         1024,
         16,
     )
-    return (outputs, input_grad, dilated_grad, point_grad)
+    return (outputs, input_grad, dilated_grad, point_grad.T)
 
 
 def solution(mesh):

time: 162 us -> 160 us (0.988)
  other arithmetic: 14 us -> 11.8 us
  local copies, waits for them, and re-layouts: 8.23 us -> 6.33 us
  waiting for transfers between devices: 61.2 us -> 63.1 us
  starting transfers between devices: 54.3 us -> 52.5 us
    select_n x4 -> x1, other arithmetic: 4.62 us -> 1.34 us  [in_order(): jnp.where(first, jnp.concatenate([mine, other], axis), jnp.concatenate([o...]
    concatenate x1 -> x0, local copies, waits for them, and re-layouts: 2.35 us -> none  [in_order(): jnp.concatenate([mine, other], axis)]
    dynamic_slice x2 -> x3, local copies, waits for them, and re-layouts: 1.03 us -> 2.68 us  [cut(): return lax.dynamic_slice_in_dim(value, start, length, axis)]
where the time goes in v9:
time: 160 us; the launch traced here: 158 us
  waiting for transfers between devices  63.1 us (39%)
  starting transfers between devices  52.5 us (33%)
  Pallas kernels  21.4 us (13%)
  other arithmetic  11.8 us (7%)
  local copies, waits for them, and re-layouts  6.33 us (4%)
  matrix products  1.68 us (1%)
    ppermute x11, waiting for transfers between devices, line(): lax.ppermute(value, 'seq', [(4 * a + i, 4 * b + i) for a, b in pairs for...  33.9 us
    ppermute x21, waiting for transfers between devices, send(): lax.ppermute(value, 'seq', [p for p in pairs if p[1] is not None and 0 <=...  29.1 us
    ppermute x21, starting transfers between devices, send(): lax.ppermute(value, 'seq', [p for p in pairs if p[1] is not None and 0 <=...  26.4 us
    ppermute x11, starting transfers between devices, line(): lax.ppermute(value, 'seq', [(4 * a + i, 4 * b + i) for a, b in pairs for...  26.1 us
    pallas_call x3, Pallas kernels, call(): pl.pallas_call(kernel, out_shape=[jax.ShapeDtypeStruct(s, t) for s, t in...  21.4 us
  transfers between devices with their start and end apart: 32, of which 16 were waited for; matrix products, arithmetic and copies ran while one was open for 9% of the time, Pallas kernels for 4%

profile of v9, /device:TPU:9, one launch (start us, length us, event | category | flops | bytes accessed | tf_op | source)
XLA Modules:
  0.0 157.9 jit_solution(2942076861920437756)
XLA Ops:
  8.5 3.3 %collective-permute-done.2 = bf16[3,96,192]{2,1,0:T(8,128)(2,1)S(1)} collective-permute-done((bf16[3,96,192]{2,1,0:T(8,128)(2,1)S(1)}, bf16[3,96,192]{2,1,0:T(8,128)(2,1)S(1)}, u32[]{:S(2)}, u32[]{:S(2)}) %collective-permute-start.2) | collective-permute-done | bytes 110624 | tf_op jit(solution)/shard_map/ppermute | solution.py:307
  14.0 3.2 %collective-permute-start.4 = (bf16[3,2,96,384]{3,2,1,0:T(8,128)(2,1)}, bf16[3,2,96,384]{3,2,1,0:T(8,128)(2,1)}, u32[]{:S(2)}, u32[]{:S(2)}) collective-permute-start(bf16[3,2,96,384]{3,2,1,0:T(8,128)(2,1)} %pad_maximum_fusion.refs_0_), channel_id=1, source_target_pairs={{0,4},{1,5},{2,6},{3,7},{4,8},{5,9},{6,10},{7,11},{8,12},{9,13},{1... | collective-permute-start | bytes 1327112 | tf_op jit(solution)/shard_map/ppermute | solution.py:343
  17.2 2.9 %collective-permute-start.5 = (bf16[3,2,96,384]{3,2,1,0:T(8,128)(2,1)}, bf16[3,2,96,384]{3,2,1,0:T(8,128)(2,1)}, u32[]{:S(2)}, u32[]{:S(2)}) collective-permute-start(bf16[3,2,96,384]{3,2,1,0:T(8,128)(2,1)} %pad_maximum_fusion.refs_0_), channel_id=1, source_target_pairs={{4,0},{5,1},{6,2},{7,3},{8,4},{9,5},{10,6},{11,7},{12,8},{13,9},{1... | collective-permute-start | bytes 1327112 | tf_op jit(solution)/shard_map/ppermute | solution.py:343
  21.4 6.1 %collective-permute-done.4.refs_1_ = bf16[3,2,96,384]{3,2,1,0:T(8,128)(2,1)} collective-permute-done((bf16[3,2,96,384]{3,2,1,0:T(8,128)(2,1)}, bf16[3,2,96,384]{3,2,1,0:T(8,128)(2,1)}, u32[]{:S(2)}, u32[]{:S(2)}) %collective-permute-start.4) | collective-permute-done | bytes 442400 | tf_op jit(solution)/shard_map/ppermute | solution.py:343
  27.5 2.9 %collective-permute-done.5.refs_4_ = bf16[3,2,96,384]{3,2,1,0:T(8,128)(2,1)} collective-permute-done((bf16[3,2,96,384]{3,2,1,0:T(8,128)(2,1)}, bf16[3,2,96,384]{3,2,1,0:T(8,128)(2,1)}, u32[]{:S(2)}, u32[]{:S(2)}) %collective-permute-start.5) | collective-permute-done | bytes 442400 | tf_op jit(solution)/shard_map/ppermute | solution.py:343
  34.5 3.2 %collective-permute-start.12 = (bf16[256,1536]{1,0:T(8,128)(2,1)S(1)}, bf16[256,1536]{1,0:T(8,128)(2,1)S(1)}, u32[]{:S(2)}, u32[]{:S(2)}) collective-permute-start(bf16[256,1536]{1,0:T(8,128)(2,1)S(1)} %broadcast_select_fusion), channel_id=1, source_target_pairs={{1,5},{3,7},{4,0},{5,9},{6,2},{7,11},{8,4},{9,13},{10,6},{11,15},{... | collective-permute-start | bytes 2359304 | tf_op jit(solution)/shard_map/ppermute | solution.py:307
  37.7 3.2 %collective-permute-start.6 = (bf16[3,2,96,384]{3,2,1,0:T(8,128)(2,1)}, bf16[3,2,96,384]{3,2,1,0:T(8,128)(2,1)S(1)}, u32[]{:S(2)}, u32[]{:S(2)}) collective-permute-start(bf16[3,2,96,384]{3,2,1,0:T(8,128)(2,1)} %collective-permute-done.4.refs_1_), channel_id=1, source_target_pairs={{4,8},{5,9},{6,10},{7,11},{8,12},{9,13},{10,14},{11,15},{20,24},{2... | collective-permute-start | bytes 1327112 | tf_op jit(solution)/shard_map/ppermute | solution.py:343
  43.7 6.5 %collective-permute-done.15.refs_15_ = bf16[256,1536]{1,0:T(8,128)(2,1)S(1)} collective-permute-done((bf16[256,1536]{1,0:T(8,128)(2,1)}, bf16[256,1536]{1,0:T(8,128)(2,1)S(1)}, u32[]{:S(2)}, u32[]{:S(2)}) %collective-permute-start.15) | collective-permute-done | bytes 786464 | tf_op jit(solution)/shard_map/ppermute | solution.py:307
  50.2 2.0 %collective-permute-start.16 = (bf16[256,1536]{1,0:T(8,128)(2,1)S(1)}, bf16[256,1536]{1,0:T(8,128)(2,1)S(1)}, u32[]{:S(2)}, u32[]{:S(2)}) collective-permute-start(bf16[256,1536]{1,0:T(8,128)(2,1)S(1)} %collective-permute-done.15.refs_15_), channel_id=1, source_target_pairs={{0,1},{1,0},{2,3},{3,2},{4,5},{5,4},{6,7},{7,6},{8,9},{9,8},{10,11... | collective-permute-start | bytes 2359304 | tf_op jit(solution)/shard_map/ppermute | solution.py:307
  53.2 3.0 %collective-permute-done.6.refs_2_ = bf16[3,2,96,384]{3,2,1,0:T(8,128)(2,1)S(1)} collective-permute-done((bf16[3,2,96,384]{3,2,1,0:T(8,128)(2,1)}, bf16[3,2,96,384]{3,2,1,0:T(8,128)(2,1)S(1)}, u32[]{:S(2)}, u32[]{:S(2)}) %collective-permute-start.6) | collective-permute-done | bytes 442400 | tf_op jit(solution)/shard_map/ppermute | solution.py:343
  59.1 5.5 %collective-permute-done.9.refs_6_ = bf16[3,2,96,384]{3,2,1,0:T(8,128)(2,1)S(1)} collective-permute-done((bf16[3,2,96,384]{3,2,1,0:T(8,128)(2,1)S(1)}, bf16[3,2,96,384]{3,2,1,0:T(8,128)(2,1)S(1)}, u32[]{:S(2)}, u32[]{:S(2)}) %collective-permute-start.9) | collective-permute-done | bytes 442400 | tf_op jit(solution)/shard_map/ppermute | solution.py:343
  66.5 13.5 %shard_map.84 = (bf16[1024,192]{1,0:T(8,128)(2,1)}, bf16[1024,192]{1,0:T(8,128)(2,1)}, bf16[4,192,384]{2,1,0:T(8,128)(2,1)}, f32[4,192,384]{2,1,0:T(8,128)}, f32...) custom-call(bf16[3,2,96,384]{3,2,1,0:T(8,128)(2,1)} %pad_maximum_fus, ...), custom_call_target="tpu_custom_call" | custom-call | flops 4831838208 | bytes 17842176 | tf_op jit(solution)/shard_map/pallas_call | solution.py:280
  80.0 5.6 %collective-permute-start.19 = (bf16[256,192]{1,0:T(8,128)(2,1)}, bf16[256,192]{1,0:T(8,128)(2,1)S(1)}, u32[]{:S(2)}, u32[]{:S(2)}) collective-permute-start(bf16[256,192]{1,0:T(8,128)(2,1)} %get-tuple-element.37), channel_id=1, source_target_pairs={{0,4},{1,5},{2,6},{3,7},{4,8},{5,9},{6,10},{7,11},{8,12},{9,13},{1... | collective-permute-start | bytes 294920 | tf_op jit(solution)/shard_map/ppermute | solution.py:307
  89.1 4.7 %collective-permute-done.20.refs_9_ = bf16[256,192]{1,0:T(8,128)(2,1)S(1)} collective-permute-done((bf16[256,192]{1,0:T(8,128)(2,1)}, bf16[256,192]{1,0:T(8,128)(2,1)S(1)}, u32[]{:S(2)}, u32[]{:S(2)}) %collective-permute-start.20) | collective-permute-done | bytes 98336 | tf_op jit(solution)/shard_map/ppermute | solution.py:307
  94.5 6.0 %shard_map.85 = (f32[256,1536]{1,0:T(8,128)}, bf16[256,1536]{1,0:T(8,128)(2,1)}, f32[256,1536]{1,0:T(8,128)}, bf16[256,1536]{1,0:T(8,128)(2,1)}) custom-call(bf16[3,2,96,384]{3,2,1,0:T(8,128)(2,1)} %pad_maximum_fusion.refs_0_, bf16[3,2,96,384]{3,2,1,0:T(8,128)(2,1)} %collective-permute-done.4.refs_1_, bf16[3,2,96,384]{3,2,1,0:T(8,128)(2,1)} %copy-done.17, ...), custom_call_target="tpu_custom_call" | custom-call | flops 1811939328 | bytes 8404992 | tf_op jit(solution)/shard_map/pallas_call | solution.py:280
  106.6 4.1 %collective-permute-start.25 = (bf16[4,192,384]{2,1,0:T(8,128)(2,1)S(1)}, bf16[4,192,384]{2,1,0:T(8,128)(2,1)S(1)}, u32[]{:S(2)}, u32[]{:S(2)}) collective-permute-start(bf16[4,192,384]{2,1,0:T(8,128)(2,1)S(1)} %add_convert_fusion.3), channel_id=1, source_target_pairs={{0,4},{1,5},{2,6},{3,7},{4,8},{5,9},{6,10},{7,11},{16,20},{17,21},... | collective-permute-start | bytes 1769480 | tf_op jit(solution)/shard_map/ppermute | solution.py:343
  115.7 7.3 %collective-permute-done.25 = bf16[4,192,384]{2,1,0:T(8,128)(2,1)S(1)} collective-permute-done((bf16[4,192,384]{2,1,0:T(8,128)(2,1)S(1)}, bf16[4,192,384]{2,1,0:T(8,128)(2,1)S(1)}, u32[]{:S(2)}, u32[]{:S(2)}) %collective-permute-start.25) | collective-permute-done | bytes 589856 | tf_op jit(solution)/shard_map/ppermute | solution.py:343
  123.1 4.1 %collective-permute-start.26 = (bf16[4,192,384]{2,1,0:T(8,128)(2,1)S(1)}, bf16[4,192,384]{2,1,0:T(8,128)(2,1)S(1)}, u32[]{:S(2)}, u32[]{:S(2)}) collective-permute-start(bf16[4,192,384]{2,1,0:T(8,128)(2,1)S(1)} %add_convert_fusion.2), channel_id=1, source_target_pairs={{0,4},{1,5},{2,6},{3,7},{4,8},{5,9},{6,10},{7,11},{8,12},{9,13},{1... | collective-permute-start | bytes 1769480 | tf_op jit(solution)/shard_map/ppermute | solution.py:343
  129.4 2.3 %collective-permute-done.23 = bf16[256,1536]{1,0:T(8,128)(2,1)S(1)} collective-permute-done((bf16[256,1536]{1,0:T(8,128)(2,1)S(1)}, bf16[256,1536]{1,0:T(8,128)(2,1)S(1)}, u32[]{:S(2)}, u32[]{:S(2)}) %collective-permute-start.23) | collective-permute-done | bytes 786464 | tf_op jit(solution)/shard_map/ppermute | solution.py:307
  133.5 5.3 %collective-permute-done.26 = bf16[4,192,384]{2,1,0:T(8,128)(2,1)S(1)} collective-permute-done((bf16[4,192,384]{2,1,0:T(8,128)(2,1)S(1)}, bf16[4,192,384]{2,1,0:T(8,128)(2,1)S(1)}, u32[]{:S(2)}, u32[]{:S(2)}) %collective-permute-start.26) | collective-permute-done | bytes 589856 | tf_op jit(solution)/shard_map/ppermute | solution.py:343
  138.7 3.9 %collective-permute-done.28 = bf16[4,192,384]{2,1,0:T(8,128)(2,1)S(1)} collective-permute-done((bf16[4,192,384]{2,1,0:T(8,128)(2,1)S(1)}, bf16[4,192,384]{2,1,0:T(8,128)(2,1)S(1)}, u32[]{:S(2)}, u32[]{:S(2)}) %collective-permute-start.28) | collective-permute-done | bytes 589856 | tf_op jit(solution)/shard_map/ppermute | solution.py:343
  143.1 3.3 %collective-permute-start.31 = (bf16[4,192,96]{2,1,0:T(8,128)(2,1)S(1)}, bf16[4,192,96]{2,1,0:T(8,128)(2,1)S(1)}, u32[]{:S(2)}, u32[]{:S(2)}) collective-permute-start(bf16[4,192,96]{2,1,0:T(8,128)(2,1)S(1)} %get-tuple-element.54), channel_id=1, source_target_pairs={{0,3},{1,2},{2,1},{3,0},{4,7},{5,6},{6,5},{7,4},{8,11},{9,10},{10,... | collective-permute-start | bytes 442376 | tf_op jit(solution)/shard_map/ppermute | solution.py:307
  148.6 3.2 %collective-permute-done.31.refs_3_ = bf16[4,192,96]{2,1,0:T(8,128)(2,1)S(1)} collective-permute-done((bf16[4,192,96]{2,1,0:T(8,128)(2,1)S(1)}, bf16[4,192,96]{2,1,0:T(8,128)(2,1)S(1)}, u32[]{:S(2)}, u32[]{:S(2)}) %collective-permute-start.31) | collective-permute-done | bytes 147488 | tf_op jit(solution)/shard_map/ppermute | solution.py:307
  151.8 4.2 %collective-permute-done.30.refs_2_ = bf16[4,192,96]{2,1,0:T(8,128)(2,1)S(1)} collective-permute-done((bf16[4,192,96]{2,1,0:T(8,128)(2,1)S(1)}, bf16[4,192,96]{2,1,0:T(8,128)(2,1)S(1)}, u32[]{:S(2)}, u32[]{:S(2)}) %collective-permute-start.30) | collective-permute-done | bytes 147488 | tf_op jit(solution)/shard_map/ppermute | solution.py:307
  (112 shorter events, 47.4 us)
Async XLA Ops:
  12.8 19.2 %collective-permute-start.3 = (bf16[256,1536]{1,0:T(8,128)(2,1)}, bf16[256,1536]{1,0:T(8,128)(2,1)}, u32[]{:S(2)}, u32[]{:S(2)}) collective-permute-start(bf16[256,1536]{1,0:T(8,128)(2,1)} %fusion.6.refs_7_), channel_id=1, source_target_pairs={{0,2},{1,3},{2,0},{3,1},{4,6},{5,7},{6,4},{7,5},{8,10},{9,11},{10,... | collective-permute-start | bytes 2359304 | tf_op jit(solution)/shard_map/ppermute | solution.py:307
  14.0 13.4 %collective-permute-start.4 = (bf16[3,2,96,384]{3,2,1,0:T(8,128)(2,1)}, bf16[3,2,96,384]{3,2,1,0:T(8,128)(2,1)}, u32[]{:S(2)}, u32[]{:S(2)}) collective-permute-start(bf16[3,2,96,384]{3,2,1,0:T(8,128)(2,1)} %pad_maximum_fusion.refs_0_), channel_id=1, source_target_pairs={{0,4},{1,5},{2,6},{3,7},{4,8},{5,9},{6,10},{7,11},{8,12},{9,13},{1... | collective-permute-start | bytes 1327112 | tf_op jit(solution)/shard_map/ppermute | solution.py:343
  17.2 13.1 %collective-permute-start.5 = (bf16[3,2,96,384]{3,2,1,0:T(8,128)(2,1)}, bf16[3,2,96,384]{3,2,1,0:T(8,128)(2,1)}, u32[]{:S(2)}, u32[]{:S(2)}) collective-permute-start(bf16[3,2,96,384]{3,2,1,0:T(8,128)(2,1)} %pad_maximum_fusion.refs_0_), channel_id=1, source_target_pairs={{4,0},{5,1},{6,2},{7,3},{8,4},{9,5},{10,6},{11,7},{12,8},{13,9},{1... | collective-permute-start | bytes 1327112 | tf_op jit(solution)/shard_map/ppermute | solution.py:343
  20.2 22.7 %collective-permute-start.10 = (bf16[256,1536]{1,0:T(8,128)(2,1)}, bf16[256,1536]{1,0:T(8,128)(2,1)S(1)}, u32[]{:S(2)}, u32[]{:S(2)}) collective-permute-start(bf16[256,1536]{1,0:T(8,128)(2,1)} %fusion.6.refs_7_), channel_id=1, source_target_pairs={{0,1},{1,0},{2,3},{3,2},{4,5},{5,4},{6,7},{7,6},{8,9},{9,8},{10,11... | collective-permute-start | bytes 2359304 | tf_op jit(solution)/shard_map/ppermute | solution.py:307
  21.3 19.6 %collective-permute-start.14 = (bf16[256,1536]{1,0:T(8,128)(2,1)}, bf16[256,1536]{1,0:T(8,128)(2,1)S(1)}, u32[]{:S(2)}, u32[]{:S(2)}) collective-permute-start(bf16[256,1536]{1,0:T(8,128)(2,1)} %refs_13_), channel_id=1, source_target_pairs={{0,1},{1,0},{2,3},{3,2},{4,5},{5,4},{6,7},{7,6},{8,9},{9,8},{10,11... | collective-permute-start | bytes 2359304 | tf_op jit(solution)/shard_map/ppermute | solution.py:307
  32.0 18.2 %collective-permute-start.15 = (bf16[256,1536]{1,0:T(8,128)(2,1)}, bf16[256,1536]{1,0:T(8,128)(2,1)S(1)}, u32[]{:S(2)}, u32[]{:S(2)}) collective-permute-start(bf16[256,1536]{1,0:T(8,128)(2,1)} %refs_13_), channel_id=1, source_target_pairs={{0,2},{1,3},{2,0},{3,1},{4,6},{5,7},{6,4},{7,5},{8,10},{9,11},{10,... | collective-permute-start | bytes 2359304 | tf_op jit(solution)/shard_map/ppermute | solution.py:307
  34.5 17.7 %collective-permute-start.12 = (bf16[256,1536]{1,0:T(8,128)(2,1)S(1)}, bf16[256,1536]{1,0:T(8,128)(2,1)S(1)}, u32[]{:S(2)}, u32[]{:S(2)}) collective-permute-start(bf16[256,1536]{1,0:T(8,128)(2,1)S(1)} %broadcast_select_fusion), channel_id=1, source_target_pairs={{1,5},{3,7},{4,0},{5,9},{6,2},{7,11},{8,4},{9,13},{10,6},{11,15},{... | collective-permute-start | bytes 2359304 | tf_op jit(solution)/shard_map/ppermute | solution.py:307
  37.7 18.5 %collective-permute-start.6 = (bf16[3,2,96,384]{3,2,1,0:T(8,128)(2,1)}, bf16[3,2,96,384]{3,2,1,0:T(8,128)(2,1)S(1)}, u32[]{:S(2)}, u32[]{:S(2)}) collective-permute-start(bf16[3,2,96,384]{3,2,1,0:T(8,128)(2,1)} %collective-permute-done.4.refs_1_), channel_id=1, source_target_pairs={{4,8},{5,9},{6,10},{7,11},{8,12},{9,13},{10,14},{11,15},{20,24},{2... | collective-permute-start | bytes 1327112 | tf_op jit(solution)/shard_map/ppermute | solution.py:343
  41.0 15.9 %collective-permute-start.8 = (bf16[3,2,96,384]{3,2,1,0:T(8,128)(2,1)}, bf16[3,2,96,384]{3,2,1,0:T(8,128)(2,1)S(1)}, u32[]{:S(2)}, u32[]{:S(2)}) collective-permute-start(bf16[3,2,96,384]{3,2,1,0:T(8,128)(2,1)} %collective-permute-done.5.refs_4_), channel_id=1, source_target_pairs={{4,0},{5,1},{6,2},{7,3},{8,4},{9,5},{10,6},{11,7},{20,16},{21,17},... | collective-permute-start | bytes 1327112 | tf_op jit(solution)/shard_map/ppermute | solution.py:343
  42.9 21.7 %collective-permute-start.11 = (bf16[256,1536]{1,0:T(8,128)(2,1)}, bf16[256,1536]{1,0:T(8,128)(2,1)S(1)}, u32[]{:S(2)}, u32[]{:S(2)}) collective-permute-start(bf16[256,1536]{1,0:T(8,128)(2,1)} %collective-permute-done.3.refs_9_), channel_id=1, source_target_pairs={{0,1},{1,0},{2,3},{3,2},{4,5},{5,4},{6,7},{7,6},{8,9},{9,8},{10,11... | collective-permute-start | bytes 2359304 | tf_op jit(solution)/shard_map/ppermute | solution.py:307
  50.2 14.4 %collective-permute-start.16 = (bf16[256,1536]{1,0:T(8,128)(2,1)S(1)}, bf16[256,1536]{1,0:T(8,128)(2,1)S(1)}, u32[]{:S(2)}, u32[]{:S(2)}) collective-permute-start(bf16[256,1536]{1,0:T(8,128)(2,1)S(1)} %collective-permute-done.15.refs_15_), channel_id=1, source_target_pairs={{0,1},{1,0},{2,3},{3,2},{4,5},{5,4},{6,7},{7,6},{8,9},{9,8},{10,11... | collective-permute-start | bytes 2359304 | tf_op jit(solution)/shard_map/ppermute | solution.py:307
  52.2 14.3 %collective-permute-start.13 = (bf16[256,1536]{1,0:T(8,128)(2,1)S(1)}, bf16[256,1536]{1,0:T(8,128)(2,1)}, u32[]{:S(2)}, u32[]{:S(2)}) collective-permute-start(bf16[256,1536]{1,0:T(8,128)(2,1)S(1)} %collective-permute-done.12.refs_11_), channel_id=1, source_target_pairs={{0,1},{1,0},{2,3},{3,2},{4,5},{5,4},{6,7},{7,6},{8,9},{9,8},{10,11... | collective-permute-start | bytes 2359304 | tf_op jit(solution)/shard_map/ppermute | solution.py:307
  80.0 9.1 %collective-permute-start.19 = (bf16[256,192]{1,0:T(8,128)(2,1)}, bf16[256,192]{1,0:T(8,128)(2,1)S(1)}, u32[]{:S(2)}, u32[]{:S(2)}) collective-permute-start(bf16[256,192]{1,0:T(8,128)(2,1)} %get-tuple-element.37), channel_id=1, source_target_pairs={{0,4},{1,5},{2,6},{3,7},{4,8},{5,9},{6,10},{7,11},{8,12},{9,13},{1... | collective-permute-start | bytes 294920 | tf_op jit(solution)/shard_map/ppermute | solution.py:307
  87.6 17.6 %collective-permute-start.24 = (bf16[4,192,384]{2,1,0:T(8,128)(2,1)}, bf16[4,192,384]{2,1,0:T(8,128)(2,1)}, u32[]{:S(2)}, u32[]{:S(2)}) collective-permute-start(bf16[4,192,384]{2,1,0:T(8,128)(2,1)} %get-tuple-element.47), channel_id=1, source_target_pairs={{0,4},{1,5},{2,6},{3,7},{12,8},{13,9},{14,10},{15,11},{16,20},{17,... | collective-permute-start | bytes 1769480 | tf_op jit(solution)/shard_map/ppermute | solution.py:343
  100.6 11.4 %collective-permute-start.22 = (bf16[256,1536]{1,0:T(8,128)(2,1)}, bf16[256,1536]{1,0:T(8,128)(2,1)}, u32[]{:S(2)}, u32[]{:S(2)}) collective-permute-start(bf16[256,1536]{1,0:T(8,128)(2,1)} %get-tuple-element.43), channel_id=1, source_target_pairs={{0,1},{1,0},{2,3},{3,2},{4,5},{5,4},{6,7},{7,6},{8,9},{9,8},{10,11... | collective-permute-start | bytes 2359304 | tf_op jit(solution)/shard_map/ppermute | solution.py:307
  101.9 27.5 %collective-permute-start.21 = (bf16[256,1536]{1,0:T(8,128)(2,1)}, bf16[256,1536]{1,0:T(8,128)(2,1)S(1)}, u32[]{:S(2)}, u32[]{:S(2)}) collective-permute-start(bf16[256,1536]{1,0:T(8,128)(2,1)} %get-tuple-element.41), channel_id=1, source_target_pairs={{0,1},{1,0},{2,3},{3,2},{4,5},{5,4},{6,7},{7,6},{8,9},{9,8},{10,11... | collective-permute-start | bytes 2359304 | tf_op jit(solution)/shard_map/ppermute | solution.py:307
  105.1 8.9 %collective-permute-start.18 = (bf16[256,384]{1,0:T(8,128)(2,1)S(1)}, bf16[256,384]{1,0:T(8,128)(2,1)S(1)}, u32[]{:S(2)}, u32[]{:S(2)}) collective-permute-start(bf16[256,384]{1,0:T(8,128)(2,1)S(1)} %get-tuple-element.64), channel_id=1, source_target_pairs={{0,2},{1,3},{2,0},{3,1},{4,6},{5,7},{6,4},{7,5},{8,10},{9,11},{10,... | collective-permute-start | bytes 589832 | tf_op jit(solution)/shard_map/ppermute | solution.py:307
  106.6 16.4 %collective-permute-start.25 = (bf16[4,192,384]{2,1,0:T(8,128)(2,1)S(1)}, bf16[4,192,384]{2,1,0:T(8,128)(2,1)S(1)}, u32[]{:S(2)}, u32[]{:S(2)}) collective-permute-start(bf16[4,192,384]{2,1,0:T(8,128)(2,1)S(1)} %add_convert_fusion.3), channel_id=1, source_target_pairs={{0,4},{1,5},{2,6},{3,7},{4,8},{5,9},{6,10},{7,11},{16,20},{17,21},... | collective-permute-start | bytes 1769480 | tf_op jit(solution)/shard_map/ppermute | solution.py:343
  110.6 16.7 %collective-permute-start.27 = (bf16[4,192,384]{2,1,0:T(8,128)(2,1)S(1)}, bf16[4,192,384]{2,1,0:T(8,128)(2,1)S(1)}, u32[]{:S(2)}, u32[]{:S(2)}) collective-permute-start(bf16[4,192,384]{2,1,0:T(8,128)(2,1)S(1)} %add_convert_fusion.3), channel_id=1, source_target_pairs={{12,8},{13,9},{14,10},{15,11},{8,4},{9,5},{10,6},{11,7},{28,24},{2... | collective-permute-start | bytes 1769480 | tf_op jit(solution)/shard_map/ppermute | solution.py:343
  113.3 18.4 %collective-permute-start.23 = (bf16[256,1536]{1,0:T(8,128)(2,1)S(1)}, bf16[256,1536]{1,0:T(8,128)(2,1)S(1)}, u32[]{:S(2)}, u32[]{:S(2)}) collective-permute-start(bf16[256,1536]{1,0:T(8,128)(2,1)S(1)} %add_convert_fusion), channel_id=1, source_target_pairs={{0,2},{1,3},{2,0},{3,1},{4,6},{5,7},{6,4},{7,5},{8,10},{9,11},{10,... | collective-permute-start | bytes 2359304 | tf_op jit(solution)/shard_map/ppermute | solution.py:307
  123.1 15.6 %collective-permute-start.26 = (bf16[4,192,384]{2,1,0:T(8,128)(2,1)S(1)}, bf16[4,192,384]{2,1,0:T(8,128)(2,1)S(1)}, u32[]{:S(2)}, u32[]{:S(2)}) collective-permute-start(bf16[4,192,384]{2,1,0:T(8,128)(2,1)S(1)} %add_convert_fusion.2), channel_id=1, source_target_pairs={{0,4},{1,5},{2,6},{3,7},{4,8},{5,9},{6,10},{7,11},{8,12},{9,13},{1... | collective-permute-start | bytes 1769480 | tf_op jit(solution)/shard_map/ppermute | solution.py:343
  127.5 15.2 %collective-permute-start.28 = (bf16[4,192,384]{2,1,0:T(8,128)(2,1)S(1)}, bf16[4,192,384]{2,1,0:T(8,128)(2,1)S(1)}, u32[]{:S(2)}, u32[]{:S(2)}) collective-permute-start(bf16[4,192,384]{2,1,0:T(8,128)(2,1)S(1)} %add_convert_fusion.1), channel_id=1, source_target_pairs={{4,0},{5,1},{6,2},{7,3},{8,4},{9,5},{10,6},{11,7},{12,8},{13,9},{1... | collective-permute-start | bytes 1769480 | tf_op jit(solution)/shard_map/ppermute | solution.py:343
  143.1 8.8 %collective-permute-start.31 = (bf16[4,192,96]{2,1,0:T(8,128)(2,1)S(1)}, bf16[4,192,96]{2,1,0:T(8,128)(2,1)S(1)}, u32[]{:S(2)}, u32[]{:S(2)}) collective-permute-start(bf16[4,192,96]{2,1,0:T(8,128)(2,1)S(1)} %get-tuple-element.54), channel_id=1, source_target_pairs={{0,3},{1,2},{2,1},{3,0},{4,7},{5,6},{6,5},{7,4},{8,11},{9,10},{10,... | collective-permute-start | bytes 442376 | tf_op jit(solution)/shard_map/ppermute | solution.py:307
  146.4 9.7 %collective-permute-start.30 = (bf16[4,192,96]{2,1,0:T(8,128)(2,1)S(1)}, bf16[4,192,96]{2,1,0:T(8,128)(2,1)S(1)}, u32[]{:S(2)}, u32[]{:S(2)}) collective-permute-start(bf16[4,192,96]{2,1,0:T(8,128)(2,1)S(1)} %get-tuple-element.55), channel_id=1, source_target_pairs={{0,2},{1,3},{2,0},{3,1},{4,6},{5,7},{6,4},{7,5},{8,10},{9,11},{10,... | collective-permute-start | bytes 442376 | tf_op jit(solution)/shard_map/ppermute | solution.py:307
  (31 other events, 250.8 us)

commit v10 on v9

--- a/solution.py
+++ b/solution.py
@@ -103,9 +103,9 @@
 def roles(depth, z):
     if depth == 4:
         return [
-            (3 * lax.rem(z + 1, 2), [bf16, f32]),
-            (lax.rem(z + 2, 4), [f32]),
-            (1 + lax.rem(z, 2), [f32]),
+            (3 * lax.rem(z + 1, 2), [bf16, bf16]),
+            (lax.rem(z + 2, 4), [bf16]),
+            (1 + lax.rem(z, 2), [bf16]),
             (z, [f32]),
         ]
     return [(lax.rem(z + d, depth), [bf16]) for d in range(1, depth)] + [(z, [f32])]
@@ -410,11 +410,11 @@
     if depth == 4:
         far, two, up, down, total = terms
         far = line(far, [(0, 1), (3, 2)])
-        joined = (two + far.astype(f32)).astype(bf16)
+        joined = (two.astype(f32) + far.astype(f32)).astype(bf16)
         near_up = line(joined, [(0, 1), (1, 2)])
         near_down = line(joined, [(3, 2), (2, 1)])
-        up = up + near_up.astype(f32)
-        down = down + near_down.astype(f32)
+        up = up.astype(f32) + near_up.astype(f32)
+        down = down.astype(f32) + near_down.astype(f32)
         parts = [
             line(up.astype(bf16), [(0, 1), (1, 2), (2, 3)]),
             line(down.astype(bf16), [(1, 0), (2, 1), (3, 2)]),

time: 160 us -> 159 us (level)
  no operation moved by 1% of the time
where the time goes in v10:
time: 159 us; the launch traced here: 157 us
  waiting for transfers between devices  63.2 us (40%)
  starting transfers between devices  52.2 us (33%)
  Pallas kernels  21.1 us (13%)
  other arithmetic  11.8 us (7%)
  local copies, waits for them, and re-layouts  6.37 us (4%)
  matrix products  1.68 us (1%)
    ppermute x11, waiting for transfers between devices, line(): lax.ppermute(value, 'seq', [(4 * a + i, 4 * b + i) for a, b in pairs for...  34.1 us
    ppermute x21, waiting for transfers between devices, send(): lax.ppermute(value, 'seq', [p for p in pairs if p[1] is not None and 0 <=...  29.1 us
    ppermute x21, starting transfers between devices, send(): lax.ppermute(value, 'seq', [p for p in pairs if p[1] is not None and 0 <=...  26.3 us
    ppermute x11, starting transfers between devices, line(): lax.ppermute(value, 'seq', [(4 * a + i, 4 * b + i) for a, b in pairs for...  25.8 us
    pallas_call x3, Pallas kernels, call(): pl.pallas_call(kernel, out_shape=[jax.ShapeDtypeStruct(s, t) for s, t in...  21.1 us
  transfers between devices with their start and end apart: 32, of which 16 were waited for; matrix products, arithmetic and copies ran while one was open for 9% of the time, Pallas kernels for 4%

profile of v10, /device:TPU:9, one launch (start us, length us, event | category | flops | bytes accessed | tf_op | source)
XLA Modules:
  0.0 157.4 jit_solution(1858836126931526876)
XLA Ops:
  8.5 3.3 %collective-permute-done.2 = bf16[3,96,192]{2,1,0:T(8,128)(2,1)S(1)} collective-permute-done((bf16[3,96,192]{2,1,0:T(8,128)(2,1)S(1)}, bf16[3,96,192]{2,1,0:T(8,128)(2,1)S(1)}, u32[]{:S(2)}, u32[]{:S(2)}) %collective-permute-start.2) | collective-permute-done | bytes 110624 | tf_op jit(solution)/shard_map/ppermute | solution.py:307
  14.0 3.2 %collective-permute-start.4 = (bf16[3,2,96,384]{3,2,1,0:T(8,128)(2,1)}, bf16[3,2,96,384]{3,2,1,0:T(8,128)(2,1)}, u32[]{:S(2)}, u32[]{:S(2)}) collective-permute-start(bf16[3,2,96,384]{3,2,1,0:T(8,128)(2,1)} %pad_maximum_fusion.refs_0_), channel_id=1, source_target_pairs={{0,4},{1,5},{2,6},{3,7},{4,8},{5,9},{6,10},{7,11},{8,12},{9,13},{1... | collective-permute-start | bytes 1327112 | tf_op jit(solution)/shard_map/ppermute | solution.py:343
  17.2 2.8 %collective-permute-start.5 = (bf16[3,2,96,384]{3,2,1,0:T(8,128)(2,1)}, bf16[3,2,96,384]{3,2,1,0:T(8,128)(2,1)}, u32[]{:S(2)}, u32[]{:S(2)}) collective-permute-start(bf16[3,2,96,384]{3,2,1,0:T(8,128)(2,1)} %pad_maximum_fusion.refs_0_), channel_id=1, source_target_pairs={{4,0},{5,1},{6,2},{7,3},{8,4},{9,5},{10,6},{11,7},{12,8},{13,9},{1... | collective-permute-start | bytes 1327112 | tf_op jit(solution)/shard_map/ppermute | solution.py:343
  21.3 6.1 %collective-permute-done.4.refs_1_ = bf16[3,2,96,384]{3,2,1,0:T(8,128)(2,1)} collective-permute-done((bf16[3,2,96,384]{3,2,1,0:T(8,128)(2,1)}, bf16[3,2,96,384]{3,2,1,0:T(8,128)(2,1)}, u32[]{:S(2)}, u32[]{:S(2)}) %collective-permute-start.4) | collective-permute-done | bytes 442400 | tf_op jit(solution)/shard_map/ppermute | solution.py:343
  27.4 2.9 %collective-permute-done.5.refs_4_ = bf16[3,2,96,384]{3,2,1,0:T(8,128)(2,1)} collective-permute-done((bf16[3,2,96,384]{3,2,1,0:T(8,128)(2,1)}, bf16[3,2,96,384]{3,2,1,0:T(8,128)(2,1)}, u32[]{:S(2)}, u32[]{:S(2)}) %collective-permute-start.5) | collective-permute-done | bytes 442400 | tf_op jit(solution)/shard_map/ppermute | solution.py:343
  34.5 3.2 %collective-permute-start.12 = (bf16[256,1536]{1,0:T(8,128)(2,1)S(1)}, bf16[256,1536]{1,0:T(8,128)(2,1)S(1)}, u32[]{:S(2)}, u32[]{:S(2)}) collective-permute-start(bf16[256,1536]{1,0:T(8,128)(2,1)S(1)} %broadcast_select_fusion), channel_id=1, source_target_pairs={{1,5},{3,7},{4,0},{5,9},{6,2},{7,11},{8,4},{9,13},{10,6},{11,15},{... | collective-permute-start | bytes 2359304 | tf_op jit(solution)/shard_map/ppermute | solution.py:307
  37.7 3.2 %collective-permute-start.6 = (bf16[3,2,96,384]{3,2,1,0:T(8,128)(2,1)}, bf16[3,2,96,384]{3,2,1,0:T(8,128)(2,1)S(1)}, u32[]{:S(2)}, u32[]{:S(2)}) collective-permute-start(bf16[3,2,96,384]{3,2,1,0:T(8,128)(2,1)} %collective-permute-done.4.refs_1_), channel_id=1, source_target_pairs={{4,8},{5,9},{6,10},{7,11},{8,12},{9,13},{10,14},{11,15},{20,24},{2... | collective-permute-start | bytes 1327112 | tf_op jit(solution)/shard_map/ppermute | solution.py:343
  43.7 6.5 %collective-permute-done.15.refs_15_ = bf16[256,1536]{1,0:T(8,128)(2,1)S(1)} collective-permute-done((bf16[256,1536]{1,0:T(8,128)(2,1)}, bf16[256,1536]{1,0:T(8,128)(2,1)S(1)}, u32[]{:S(2)}, u32[]{:S(2)}) %collective-permute-start.15) | collective-permute-done | bytes 786464 | tf_op jit(solution)/shard_map/ppermute | solution.py:307
  50.2 2.0 %collective-permute-start.16 = (bf16[256,1536]{1,0:T(8,128)(2,1)S(1)}, bf16[256,1536]{1,0:T(8,128)(2,1)S(1)}, u32[]{:S(2)}, u32[]{:S(2)}) collective-permute-start(bf16[256,1536]{1,0:T(8,128)(2,1)S(1)} %collective-permute-done.15.refs_15_), channel_id=1, source_target_pairs={{0,1},{1,0},{2,3},{3,2},{4,5},{5,4},{6,7},{7,6},{8,9},{9,8},{10,11... | collective-permute-start | bytes 2359304 | tf_op jit(solution)/shard_map/ppermute | solution.py:307
  53.2 3.0 %collective-permute-done.6.refs_2_ = bf16[3,2,96,384]{3,2,1,0:T(8,128)(2,1)S(1)} collective-permute-done((bf16[3,2,96,384]{3,2,1,0:T(8,128)(2,1)}, bf16[3,2,96,384]{3,2,1,0:T(8,128)(2,1)S(1)}, u32[]{:S(2)}, u32[]{:S(2)}) %collective-permute-start.6) | collective-permute-done | bytes 442400 | tf_op jit(solution)/shard_map/ppermute | solution.py:343
  59.1 5.5 %collective-permute-done.9.refs_6_ = bf16[3,2,96,384]{3,2,1,0:T(8,128)(2,1)S(1)} collective-permute-done((bf16[3,2,96,384]{3,2,1,0:T(8,128)(2,1)S(1)}, bf16[3,2,96,384]{3,2,1,0:T(8,128)(2,1)S(1)}, u32[]{:S(2)}, u32[]{:S(2)}) %collective-permute-start.9) | collective-permute-done | bytes 442400 | tf_op jit(solution)/shard_map/ppermute | solution.py:343
  66.5 13.2 %shard_map.84 = (bf16[1024,192]{1,0:T(8,128)(2,1)}, bf16[1024,192]{1,0:T(8,128)(2,1)}, bf16[4,192,384]{2,1,0:T(8,128)(2,1)}, bf16[4,192,384]{2,1,0:T(8,128)(2,1)...) custom-call(bf16[3,2,96,384]{3,2,1,0:T(8,128)(2,1)} %pad_maximum_fus, ...), custom_call_target="tpu_custom_call" | custom-call | flops 4831838208 | bytes 16072704 | tf_op jit(solution)/shard_map/pallas_call | solution.py:280
  79.7 5.6 %collective-permute-start.19 = (bf16[256,192]{1,0:T(8,128)(2,1)}, bf16[256,192]{1,0:T(8,128)(2,1)S(1)}, u32[]{:S(2)}, u32[]{:S(2)}) collective-permute-start(bf16[256,192]{1,0:T(8,128)(2,1)} %get-tuple-element.37), channel_id=1, source_target_pairs={{0,4},{1,5},{2,6},{3,7},{4,8},{5,9},{6,10},{7,11},{8,12},{9,13},{1... | collective-permute-start | bytes 294920 | tf_op jit(solution)/shard_map/ppermute | solution.py:307
  88.8 4.8 %collective-permute-done.20.refs_9_ = bf16[256,192]{1,0:T(8,128)(2,1)S(1)} collective-permute-done((bf16[256,192]{1,0:T(8,128)(2,1)}, bf16[256,192]{1,0:T(8,128)(2,1)S(1)}, u32[]{:S(2)}, u32[]{:S(2)}) %collective-permute-start.20) | collective-permute-done | bytes 98336 | tf_op jit(solution)/shard_map/ppermute | solution.py:307
  94.2 6.0 %shard_map.85 = (f32[256,1536]{1,0:T(8,128)}, bf16[256,1536]{1,0:T(8,128)(2,1)}, f32[256,1536]{1,0:T(8,128)}, bf16[256,1536]{1,0:T(8,128)(2,1)}) custom-call(bf16[3,2,96,384]{3,2,1,0:T(8,128)(2,1)} %pad_maximum_fusion.refs_0_, bf16[3,2,96,384]{3,2,1,0:T(8,128)(2,1)} %collective-permute-done.4.refs_1_, bf16[3,2,96,384]{3,2,1,0:T(8,128)(2,1)} %copy-done.17, ...), custom_call_target="tpu_custom_call" | custom-call | flops 1811939328 | bytes 8404992 | tf_op jit(solution)/shard_map/pallas_call | solution.py:280
  106.3 4.0 %collective-permute-start.25 = (bf16[4,192,384]{2,1,0:T(8,128)(2,1)S(1)}, bf16[4,192,384]{2,1,0:T(8,128)(2,1)S(1)}, u32[]{:S(2)}, u32[]{:S(2)}) collective-permute-start(bf16[4,192,384]{2,1,0:T(8,128)(2,1)S(1)} %add_convert_fusion.3), channel_id=1, source_target_pairs={{0,4},{1,5},{2,6},{3,7},{4,8},{5,9},{6,10},{7,11},{16,20},{17,21},... | collective-permute-start | bytes 1769480 | tf_op jit(solution)/shard_map/ppermute | solution.py:343
  115.3 7.4 %collective-permute-done.25 = bf16[4,192,384]{2,1,0:T(8,128)(2,1)S(1)} collective-permute-done((bf16[4,192,384]{2,1,0:T(8,128)(2,1)S(1)}, bf16[4,192,384]{2,1,0:T(8,128)(2,1)S(1)}, u32[]{:S(2)}, u32[]{:S(2)}) %collective-permute-start.25) | collective-permute-done | bytes 589856 | tf_op jit(solution)/shard_map/ppermute | solution.py:343
  122.9 4.0 %collective-permute-start.26 = (bf16[4,192,384]{2,1,0:T(8,128)(2,1)S(1)}, bf16[4,192,384]{2,1,0:T(8,128)(2,1)S(1)}, u32[]{:S(2)}, u32[]{:S(2)}) collective-permute-start(bf16[4,192,384]{2,1,0:T(8,128)(2,1)S(1)} %add_convert_fusion.2), channel_id=1, source_target_pairs={{0,4},{1,5},{2,6},{3,7},{4,8},{5,9},{6,10},{7,11},{8,12},{9,13},{1... | collective-permute-start | bytes 1769480 | tf_op jit(solution)/shard_map/ppermute | solution.py:343
  129.0 2.3 %collective-permute-done.23 = bf16[256,1536]{1,0:T(8,128)(2,1)S(1)} collective-permute-done((bf16[256,1536]{1,0:T(8,128)(2,1)S(1)}, bf16[256,1536]{1,0:T(8,128)(2,1)S(1)}, u32[]{:S(2)}, u32[]{:S(2)}) %collective-permute-start.23) | collective-permute-done | bytes 786464 | tf_op jit(solution)/shard_map/ppermute | solution.py:307
  133.1 5.4 %collective-permute-done.26 = bf16[4,192,384]{2,1,0:T(8,128)(2,1)S(1)} collective-permute-done((bf16[4,192,384]{2,1,0:T(8,128)(2,1)S(1)}, bf16[4,192,384]{2,1,0:T(8,128)(2,1)S(1)}, u32[]{:S(2)}, u32[]{:S(2)}) %collective-permute-start.26) | collective-permute-done | bytes 589856 | tf_op jit(solution)/shard_map/ppermute | solution.py:343
  138.5 3.7 %collective-permute-done.28 = bf16[4,192,384]{2,1,0:T(8,128)(2,1)S(1)} collective-permute-done((bf16[4,192,384]{2,1,0:T(8,128)(2,1)S(1)}, bf16[4,192,384]{2,1,0:T(8,128)(2,1)S(1)}, u32[]{:S(2)}, u32[]{:S(2)}) %collective-permute-start.28) | collective-permute-done | bytes 589856 | tf_op jit(solution)/shard_map/ppermute | solution.py:343
  142.7 3.2 %collective-permute-start.31 = (bf16[4,192,96]{2,1,0:T(8,128)(2,1)S(1)}, bf16[4,192,96]{2,1,0:T(8,128)(2,1)S(1)}, u32[]{:S(2)}, u32[]{:S(2)}) collective-permute-start(bf16[4,192,96]{2,1,0:T(8,128)(2,1)S(1)} %get-tuple-element.54), channel_id=1, source_target_pairs={{0,3},{1,2},{2,1},{3,0},{4,7},{5,6},{6,5},{7,4},{8,11},{9,10},{10,... | collective-permute-start | bytes 442376 | tf_op jit(solution)/shard_map/ppermute | solution.py:307
  148.2 3.1 %collective-permute-done.31.refs_3_ = bf16[4,192,96]{2,1,0:T(8,128)(2,1)S(1)} collective-permute-done((bf16[4,192,96]{2,1,0:T(8,128)(2,1)S(1)}, bf16[4,192,96]{2,1,0:T(8,128)(2,1)S(1)}, u32[]{:S(2)}, u32[]{:S(2)}) %collective-permute-start.31) | collective-permute-done | bytes 147488 | tf_op jit(solution)/shard_map/ppermute | solution.py:307
  151.3 4.2 %collective-permute-done.30.refs_2_ = bf16[4,192,96]{2,1,0:T(8,128)(2,1)S(1)} collective-permute-done((bf16[4,192,96]{2,1,0:T(8,128)(2,1)S(1)}, bf16[4,192,96]{2,1,0:T(8,128)(2,1)S(1)}, u32[]{:S(2)}, u32[]{:S(2)}) %collective-permute-start.30) | collective-permute-done | bytes 147488 | tf_op jit(solution)/shard_map/ppermute | solution.py:307
  (112 shorter events, 47.5 us)
Async XLA Ops:
  12.8 19.2 %collective-permute-start.3 = (bf16[256,1536]{1,0:T(8,128)(2,1)}, bf16[256,1536]{1,0:T(8,128)(2,1)}, u32[]{:S(2)}, u32[]{:S(2)}) collective-permute-start(bf16[256,1536]{1,0:T(8,128)(2,1)} %fusion.6.refs_7_), channel_id=1, source_target_pairs={{0,2},{1,3},{2,0},{3,1},{4,6},{5,7},{6,4},{7,5},{8,10},{9,11},{10,... | collective-permute-start | bytes 2359304 | tf_op jit(solution)/shard_map/ppermute | solution.py:307
  14.0 13.4 %collective-permute-start.4 = (bf16[3,2,96,384]{3,2,1,0:T(8,128)(2,1)}, bf16[3,2,96,384]{3,2,1,0:T(8,128)(2,1)}, u32[]{:S(2)}, u32[]{:S(2)}) collective-permute-start(bf16[3,2,96,384]{3,2,1,0:T(8,128)(2,1)} %pad_maximum_fusion.refs_0_), channel_id=1, source_target_pairs={{0,4},{1,5},{2,6},{3,7},{4,8},{5,9},{6,10},{7,11},{8,12},{9,13},{1... | collective-permute-start | bytes 1327112 | tf_op jit(solution)/shard_map/ppermute | solution.py:343
  17.2 13.1 %collective-permute-start.5 = (bf16[3,2,96,384]{3,2,1,0:T(8,128)(2,1)}, bf16[3,2,96,384]{3,2,1,0:T(8,128)(2,1)}, u32[]{:S(2)}, u32[]{:S(2)}) collective-permute-start(bf16[3,2,96,384]{3,2,1,0:T(8,128)(2,1)} %pad_maximum_fusion.refs_0_), channel_id=1, source_target_pairs={{4,0},{5,1},{6,2},{7,3},{8,4},{9,5},{10,6},{11,7},{12,8},{13,9},{1... | collective-permute-start | bytes 1327112 | tf_op jit(solution)/shard_map/ppermute | solution.py:343
  20.1 22.8 %collective-permute-start.10 = (bf16[256,1536]{1,0:T(8,128)(2,1)}, bf16[256,1536]{1,0:T(8,128)(2,1)S(1)}, u32[]{:S(2)}, u32[]{:S(2)}) collective-permute-start(bf16[256,1536]{1,0:T(8,128)(2,1)} %fusion.6.refs_7_), channel_id=1, source_target_pairs={{0,1},{1,0},{2,3},{3,2},{4,5},{5,4},{6,7},{7,6},{8,9},{9,8},{10,11... | collective-permute-start | bytes 2359304 | tf_op jit(solution)/shard_map/ppermute | solution.py:307
  21.2 19.7 %collective-permute-start.14 = (bf16[256,1536]{1,0:T(8,128)(2,1)}, bf16[256,1536]{1,0:T(8,128)(2,1)S(1)}, u32[]{:S(2)}, u32[]{:S(2)}) collective-permute-start(bf16[256,1536]{1,0:T(8,128)(2,1)} %refs_13_), channel_id=1, source_target_pairs={{0,1},{1,0},{2,3},{3,2},{4,5},{5,4},{6,7},{7,6},{8,9},{9,8},{10,11... | collective-permute-start | bytes 2359304 | tf_op jit(solution)/shard_map/ppermute | solution.py:307
  32.0 18.2 %collective-permute-start.15 = (bf16[256,1536]{1,0:T(8,128)(2,1)}, bf16[256,1536]{1,0:T(8,128)(2,1)S(1)}, u32[]{:S(2)}, u32[]{:S(2)}) collective-permute-start(bf16[256,1536]{1,0:T(8,128)(2,1)} %refs_13_), channel_id=1, source_target_pairs={{0,2},{1,3},{2,0},{3,1},{4,6},{5,7},{6,4},{7,5},{8,10},{9,11},{10,... | collective-permute-start | bytes 2359304 | tf_op jit(solution)/shard_map/ppermute | solution.py:307
  34.5 17.7 %collective-permute-start.12 = (bf16[256,1536]{1,0:T(8,128)(2,1)S(1)}, bf16[256,1536]{1,0:T(8,128)(2,1)S(1)}, u32[]{:S(2)}, u32[]{:S(2)}) collective-permute-start(bf16[256,1536]{1,0:T(8,128)(2,1)S(1)} %broadcast_select_fusion), channel_id=1, source_target_pairs={{1,5},{3,7},{4,0},{5,9},{6,2},{7,11},{8,4},{9,13},{10,6},{11,15},{... | collective-permute-start | bytes 2359304 | tf_op jit(solution)/shard_map/ppermute | solution.py:307
  37.7 18.5 %collective-permute-start.6 = (bf16[3,2,96,384]{3,2,1,0:T(8,128)(2,1)}, bf16[3,2,96,384]{3,2,1,0:T(8,128)(2,1)S(1)}, u32[]{:S(2)}, u32[]{:S(2)}) collective-permute-start(bf16[3,2,96,384]{3,2,1,0:T(8,128)(2,1)} %collective-permute-done.4.refs_1_), channel_id=1, source_target_pairs={{4,8},{5,9},{6,10},{7,11},{8,12},{9,13},{10,14},{11,15},{20,24},{2... | collective-permute-start | bytes 1327112 | tf_op jit(solution)/shard_map/ppermute | solution.py:343
  40.9 15.9 %collective-permute-start.8 = (bf16[3,2,96,384]{3,2,1,0:T(8,128)(2,1)}, bf16[3,2,96,384]{3,2,1,0:T(8,128)(2,1)S(1)}, u32[]{:S(2)}, u32[]{:S(2)}) collective-permute-start(bf16[3,2,96,384]{3,2,1,0:T(8,128)(2,1)} %collective-permute-done.5.refs_4_), channel_id=1, source_target_pairs={{4,0},{5,1},{6,2},{7,3},{8,4},{9,5},{10,6},{11,7},{20,16},{21,17},... | collective-permute-start | bytes 1327112 | tf_op jit(solution)/shard_map/ppermute | solution.py:343
  42.9 21.7 %collective-permute-start.11 = (bf16[256,1536]{1,0:T(8,128)(2,1)}, bf16[256,1536]{1,0:T(8,128)(2,1)S(1)}, u32[]{:S(2)}, u32[]{:S(2)}) collective-permute-start(bf16[256,1536]{1,0:T(8,128)(2,1)} %collective-permute-done.3.refs_9_), channel_id=1, source_target_pairs={{0,1},{1,0},{2,3},{3,2},{4,5},{5,4},{6,7},{7,6},{8,9},{9,8},{10,11... | collective-permute-start | bytes 2359304 | tf_op jit(solution)/shard_map/ppermute | solution.py:307
  50.2 14.4 %collective-permute-start.16 = (bf16[256,1536]{1,0:T(8,128)(2,1)S(1)}, bf16[256,1536]{1,0:T(8,128)(2,1)S(1)}, u32[]{:S(2)}, u32[]{:S(2)}) collective-permute-start(bf16[256,1536]{1,0:T(8,128)(2,1)S(1)} %collective-permute-done.15.refs_15_), channel_id=1, source_target_pairs={{0,1},{1,0},{2,3},{3,2},{4,5},{5,4},{6,7},{7,6},{8,9},{9,8},{10,11... | collective-permute-start | bytes 2359304 | tf_op jit(solution)/shard_map/ppermute | solution.py:307
  52.2 14.3 %collective-permute-start.13 = (bf16[256,1536]{1,0:T(8,128)(2,1)S(1)}, bf16[256,1536]{1,0:T(8,128)(2,1)}, u32[]{:S(2)}, u32[]{:S(2)}) collective-permute-start(bf16[256,1536]{1,0:T(8,128)(2,1)S(1)} %collective-permute-done.12.refs_11_), channel_id=1, source_target_pairs={{0,1},{1,0},{2,3},{3,2},{4,5},{5,4},{6,7},{7,6},{8,9},{9,8},{10,11... | collective-permute-start | bytes 2359304 | tf_op jit(solution)/shard_map/ppermute | solution.py:307
  79.7 9.1 %collective-permute-start.19 = (bf16[256,192]{1,0:T(8,128)(2,1)}, bf16[256,192]{1,0:T(8,128)(2,1)S(1)}, u32[]{:S(2)}, u32[]{:S(2)}) collective-permute-start(bf16[256,192]{1,0:T(8,128)(2,1)} %get-tuple-element.37), channel_id=1, source_target_pairs={{0,4},{1,5},{2,6},{3,7},{4,8},{5,9},{6,10},{7,11},{8,12},{9,13},{1... | collective-permute-start | bytes 294920 | tf_op jit(solution)/shard_map/ppermute | solution.py:307
  87.3 17.7 %collective-permute-start.24 = (bf16[4,192,384]{2,1,0:T(8,128)(2,1)}, bf16[4,192,384]{2,1,0:T(8,128)(2,1)}, u32[]{:S(2)}, u32[]{:S(2)}) collective-permute-start(bf16[4,192,384]{2,1,0:T(8,128)(2,1)} %get-tuple-element.47), channel_id=1, source_target_pairs={{0,4},{1,5},{2,6},{3,7},{12,8},{13,9},{14,10},{15,11},{16,20},{17,... | collective-permute-start | bytes 1769480 | tf_op jit(solution)/shard_map/ppermute | solution.py:343
  100.3 11.3 %collective-permute-start.22 = (bf16[256,1536]{1,0:T(8,128)(2,1)}, bf16[256,1536]{1,0:T(8,128)(2,1)}, u32[]{:S(2)}, u32[]{:S(2)}) collective-permute-start(bf16[256,1536]{1,0:T(8,128)(2,1)} %get-tuple-element.43), channel_id=1, source_target_pairs={{0,1},{1,0},{2,3},{3,2},{4,5},{5,4},{6,7},{7,6},{8,9},{9,8},{10,11... | collective-permute-start | bytes 2359304 | tf_op jit(solution)/shard_map/ppermute | solution.py:307
  101.6 27.4 %collective-permute-start.21 = (bf16[256,1536]{1,0:T(8,128)(2,1)}, bf16[256,1536]{1,0:T(8,128)(2,1)S(1)}, u32[]{:S(2)}, u32[]{:S(2)}) collective-permute-start(bf16[256,1536]{1,0:T(8,128)(2,1)} %get-tuple-element.41), channel_id=1, source_target_pairs={{0,1},{1,0},{2,3},{3,2},{4,5},{5,4},{6,7},{7,6},{8,9},{9,8},{10,11... | collective-permute-start | bytes 2359304 | tf_op jit(solution)/shard_map/ppermute | solution.py:307
  104.9 8.6 %collective-permute-start.18 = (bf16[256,384]{1,0:T(8,128)(2,1)S(1)}, bf16[256,384]{1,0:T(8,128)(2,1)S(1)}, u32[]{:S(2)}, u32[]{:S(2)}) collective-permute-start(bf16[256,384]{1,0:T(8,128)(2,1)S(1)} %get-tuple-element.64), channel_id=1, source_target_pairs={{0,2},{1,3},{2,0},{3,1},{4,6},{5,7},{6,4},{7,5},{8,10},{9,11},{10,... | collective-permute-start | bytes 589832 | tf_op jit(solution)/shard_map/ppermute | solution.py:307
  106.3 16.4 %collective-permute-start.25 = (bf16[4,192,384]{2,1,0:T(8,128)(2,1)S(1)}, bf16[4,192,384]{2,1,0:T(8,128)(2,1)S(1)}, u32[]{:S(2)}, u32[]{:S(2)}) collective-permute-start(bf16[4,192,384]{2,1,0:T(8,128)(2,1)S(1)} %add_convert_fusion.3), channel_id=1, source_target_pairs={{0,4},{1,5},{2,6},{3,7},{4,8},{5,9},{6,10},{7,11},{16,20},{17,21},... | collective-permute-start | bytes 1769480 | tf_op jit(solution)/shard_map/ppermute | solution.py:343
  110.2 16.7 %collective-permute-start.27 = (bf16[4,192,384]{2,1,0:T(8,128)(2,1)S(1)}, bf16[4,192,384]{2,1,0:T(8,128)(2,1)S(1)}, u32[]{:S(2)}, u32[]{:S(2)}) collective-permute-start(bf16[4,192,384]{2,1,0:T(8,128)(2,1)S(1)} %add_convert_fusion.3), channel_id=1, source_target_pairs={{12,8},{13,9},{14,10},{15,11},{8,4},{9,5},{10,6},{11,7},{28,24},{2... | collective-permute-start | bytes 1769480 | tf_op jit(solution)/shard_map/ppermute | solution.py:343
  112.9 18.4 %collective-permute-start.23 = (bf16[256,1536]{1,0:T(8,128)(2,1)S(1)}, bf16[256,1536]{1,0:T(8,128)(2,1)S(1)}, u32[]{:S(2)}, u32[]{:S(2)}) collective-permute-start(bf16[256,1536]{1,0:T(8,128)(2,1)S(1)} %add_convert_fusion), channel_id=1, source_target_pairs={{0,2},{1,3},{2,0},{3,1},{4,6},{5,7},{6,4},{7,5},{8,10},{9,11},{10,... | collective-permute-start | bytes 2359304 | tf_op jit(solution)/shard_map/ppermute | solution.py:307
  122.9 15.6 %collective-permute-start.26 = (bf16[4,192,384]{2,1,0:T(8,128)(2,1)S(1)}, bf16[4,192,384]{2,1,0:T(8,128)(2,1)S(1)}, u32[]{:S(2)}, u32[]{:S(2)}) collective-permute-start(bf16[4,192,384]{2,1,0:T(8,128)(2,1)S(1)} %add_convert_fusion.2), channel_id=1, source_target_pairs={{0,4},{1,5},{2,6},{3,7},{4,8},{5,9},{6,10},{7,11},{8,12},{9,13},{1... | collective-permute-start | bytes 1769480 | tf_op jit(solution)/shard_map/ppermute | solution.py:343
  127.1 15.2 %collective-permute-start.28 = (bf16[4,192,384]{2,1,0:T(8,128)(2,1)S(1)}, bf16[4,192,384]{2,1,0:T(8,128)(2,1)S(1)}, u32[]{:S(2)}, u32[]{:S(2)}) collective-permute-start(bf16[4,192,384]{2,1,0:T(8,128)(2,1)S(1)} %add_convert_fusion.1), channel_id=1, source_target_pairs={{4,0},{5,1},{6,2},{7,3},{8,4},{9,5},{10,6},{11,7},{12,8},{13,9},{1... | collective-permute-start | bytes 1769480 | tf_op jit(solution)/shard_map/ppermute | solution.py:343
  142.7 8.6 %collective-permute-start.31 = (bf16[4,192,96]{2,1,0:T(8,128)(2,1)S(1)}, bf16[4,192,96]{2,1,0:T(8,128)(2,1)S(1)}, u32[]{:S(2)}, u32[]{:S(2)}) collective-permute-start(bf16[4,192,96]{2,1,0:T(8,128)(2,1)S(1)} %get-tuple-element.54), channel_id=1, source_target_pairs={{0,3},{1,2},{2,1},{3,0},{4,7},{5,6},{6,5},{7,4},{8,11},{9,10},{10,... | collective-permute-start | bytes 442376 | tf_op jit(solution)/shard_map/ppermute | solution.py:307
  145.8 9.7 %collective-permute-start.30 = (bf16[4,192,96]{2,1,0:T(8,128)(2,1)S(1)}, bf16[4,192,96]{2,1,0:T(8,128)(2,1)S(1)}, u32[]{:S(2)}, u32[]{:S(2)}) collective-permute-start(bf16[4,192,96]{2,1,0:T(8,128)(2,1)S(1)} %get-tuple-element.55), channel_id=1, source_target_pairs={{0,2},{1,3},{2,0},{3,1},{4,6},{5,7},{6,4},{7,5},{8,10},{9,11},{10,... | collective-permute-start | bytes 442376 | tf_op jit(solution)/shard_map/ppermute | solution.py:307
  (31 other events, 252.4 us)

commit v11 on v9

--- a/solution.py
+++ b/solution.py
@@ -359,7 +359,7 @@
     ratio = lax.rsqrt(jnp.mean(xfull * xfull, axis=-1, keepdims=True) + 1e-06)
     normed = xfull * ratio * norm_gain
     act = gelu_value(normed).astype(bf16)
-    act_late = after(act, start_piece)
+    act_late = after(act, got[1])
     cot_late = after(cotangent, start_piece)
     act_across = cross(act_late, 2)
     if depth == 4:

time: 160 us -> 157 us (0.981)
  waiting for transfers between devices: 63.1 us -> 60.4 us
    ppermute x21, waiting for transfers between devices: 29.1 us -> 26.3 us  [send(): lax.ppermute(value, 'seq', [p for p in pairs if p[1] is not None and 0 <=...]
    ppermute x21, starting transfers between devices: 26.4 us -> 28 us  [send(): lax.ppermute(value, 'seq', [p for p in pairs if p[1] is not None and 0 <=...]
  transfers between devices with their start and end apart: 32 -> 32, of which waited for: 16 -> 15; matrix products, arithmetic and copies ran while one was open for 9% -> 10% of each run, Pallas kernels for 4% -> 4%
where the time goes in v11:
time: 157 us; the launch traced here: 156 us
  waiting for transfers between devices  60.4 us (38%)
  starting transfers between devices  52.8 us (34%)
  Pallas kernels  21.4 us (14%)
  other arithmetic  11.8 us (8%)
  local copies, waits for them, and re-layouts  6.33 us (4%)
  matrix products  1.68 us (1%)
    ppermute x11, waiting for transfers between devices, line(): lax.ppermute(value, 'seq', [(4 * a + i, 4 * b + i) for a, b in pairs for...  34.2 us
    ppermute x21, starting transfers between devices, send(): lax.ppermute(value, 'seq', [p for p in pairs if p[1] is not None and 0 <=...  28 us
    ppermute x21, waiting for transfers between devices, send(): lax.ppermute(value, 'seq', [p for p in pairs if p[1] is not None and 0 <=...  26.3 us
    ppermute x11, starting transfers between devices, line(): lax.ppermute(value, 'seq', [(4 * a + i, 4 * b + i) for a, b in pairs for...  24.8 us
    pallas_call x3, Pallas kernels, call(): pl.pallas_call(kernel, out_shape=[jax.ShapeDtypeStruct(s, t) for s, t in...  21.4 us
  transfers between devices with their start and end apart: 32, of which 15 were waited for; matrix products, arithmetic and copies ran while one was open for 10% of the time, Pallas kernels for 4%

profile of v11, /device:TPU:9, one launch (start us, length us, event | category | flops | bytes accessed | tf_op | source)
XLA Modules:
  0.0 155.6 jit_solution(13600740494550719754)
XLA Ops:
  8.5 3.8 %collective-permute-done.2 = bf16[3,96,192]{2,1,0:T(8,128)(2,1)S(1)} collective-permute-done((bf16[3,96,192]{2,1,0:T(8,128)(2,1)S(1)}, bf16[3,96,192]{2,1,0:T(8,128)(2,1)S(1)}, u32[]{:S(2)}, u32[]{:S(2)}) %collective-permute-start.2) | collective-permute-done | bytes 110624 | tf_op jit(solution)/shard_map/ppermute | solution.py:307
  13.3 3.2 %collective-permute-start.4 = (bf16[3,2,96,384]{3,2,1,0:T(8,128)(2,1)}, bf16[3,2,96,384]{3,2,1,0:T(8,128)(2,1)}, u32[]{:S(2)}, u32[]{:S(2)}) collective-permute-start(bf16[3,2,96,384]{3,2,1,0:T(8,128)(2,1)} %pad_maximum_fusion.refs_0_), channel_id=1, source_target_pairs={{0,4},{1,5},{2,6},{3,7},{4,8},{5,9},{6,10},{7,11},{8,12},{9,13},{1... | collective-permute-start | bytes 1327112 | tf_op jit(solution)/shard_map/ppermute | solution.py:343
  16.5 2.9 %collective-permute-start.5 = (bf16[3,2,96,384]{3,2,1,0:T(8,128)(2,1)}, bf16[3,2,96,384]{3,2,1,0:T(8,128)(2,1)}, u32[]{:S(2)}, u32[]{:S(2)}) collective-permute-start(bf16[3,2,96,384]{3,2,1,0:T(8,128)(2,1)} %pad_maximum_fusion.refs_0_), channel_id=1, source_target_pairs={{4,0},{5,1},{6,2},{7,3},{8,4},{9,5},{10,6},{11,7},{12,8},{13,9},{1... | collective-permute-start | bytes 1327112 | tf_op jit(solution)/shard_map/ppermute | solution.py:343
  20.0 7.4 %collective-permute-done.4.refs_1_ = bf16[3,2,96,384]{3,2,1,0:T(8,128)(2,1)} collective-permute-done((bf16[3,2,96,384]{3,2,1,0:T(8,128)(2,1)}, bf16[3,2,96,384]{3,2,1,0:T(8,128)(2,1)}, u32[]{:S(2)}, u32[]{:S(2)}) %collective-permute-start.4) | collective-permute-done | bytes 442400 | tf_op jit(solution)/shard_map/ppermute | solution.py:343
  27.4 3.0 %collective-permute-done.5.refs_4_ = bf16[3,2,96,384]{3,2,1,0:T(8,128)(2,1)} collective-permute-done((bf16[3,2,96,384]{3,2,1,0:T(8,128)(2,1)}, bf16[3,2,96,384]{3,2,1,0:T(8,128)(2,1)}, u32[]{:S(2)}, u32[]{:S(2)}) %collective-permute-start.5) | collective-permute-done | bytes 442400 | tf_op jit(solution)/shard_map/ppermute | solution.py:343
  32.9 3.2 %collective-permute-start.12 = (bf16[256,1536]{1,0:T(8,128)(2,1)S(1)}, bf16[256,1536]{1,0:T(8,128)(2,1)S(1)}, u32[]{:S(2)}, u32[]{:S(2)}) collective-permute-start(bf16[256,1536]{1,0:T(8,128)(2,1)S(1)} %broadcast_select_fusion), channel_id=1, source_target_pairs={{1,5},{3,7},{4,0},{5,9},{6,2},{7,11},{8,4},{9,13},{10,6},{11,15},{... | collective-permute-start | bytes 2359304 | tf_op jit(solution)/shard_map/ppermute | solution.py:307
  36.1 1.9 %collective-permute-start.6 = (bf16[3,2,96,384]{3,2,1,0:T(8,128)(2,1)}, bf16[3,2,96,384]{3,2,1,0:T(8,128)(2,1)S(1)}, u32[]{:S(2)}, u32[]{:S(2)}) collective-permute-start(bf16[3,2,96,384]{3,2,1,0:T(8,128)(2,1)} %collective-permute-done.4.refs_1_), channel_id=1, source_target_pairs={{4,8},{5,9},{6,10},{7,11},{8,12},{9,13},{10,14},{11,15},{20,24},{2... | collective-permute-start | bytes 1327112 | tf_op jit(solution)/shard_map/ppermute | solution.py:343
  38.0 1.9 %collective-permute-start.8 = (bf16[3,2,96,384]{3,2,1,0:T(8,128)(2,1)}, bf16[3,2,96,384]{3,2,1,0:T(8,128)(2,1)S(1)}, u32[]{:S(2)}, u32[]{:S(2)}) collective-permute-start(bf16[3,2,96,384]{3,2,1,0:T(8,128)(2,1)} %collective-permute-done.5.refs_4_), channel_id=1, source_target_pairs={{4,0},{5,1},{6,2},{7,3},{8,4},{9,5},{10,6},{11,7},{20,16},{21,17},... | collective-permute-start | bytes 1327112 | tf_op jit(solution)/shard_map/ppermute | solution.py:343
  41.9 6.9 %collective-permute-done.15.refs_15_ = bf16[256,1536]{1,0:T(8,128)(2,1)S(1)} collective-permute-done((bf16[256,1536]{1,0:T(8,128)(2,1)}, bf16[256,1536]{1,0:T(8,128)(2,1)S(1)}, u32[]{:S(2)}, u32[]{:S(2)}) %collective-permute-start.15) | collective-permute-done | bytes 786464 | tf_op jit(solution)/shard_map/ppermute | solution.py:307
  52.4 2.1 %collective-permute-done.6.refs_2_ = bf16[3,2,96,384]{3,2,1,0:T(8,128)(2,1)S(1)} collective-permute-done((bf16[3,2,96,384]{3,2,1,0:T(8,128)(2,1)}, bf16[3,2,96,384]{3,2,1,0:T(8,128)(2,1)S(1)}, u32[]{:S(2)}, u32[]{:S(2)}) %collective-permute-start.6) | collective-permute-done | bytes 442400 | tf_op jit(solution)/shard_map/ppermute | solution.py:343
  57.5 4.9 %collective-permute-done.9.refs_6_ = bf16[3,2,96,384]{3,2,1,0:T(8,128)(2,1)S(1)} collective-permute-done((bf16[3,2,96,384]{3,2,1,0:T(8,128)(2,1)S(1)}, bf16[3,2,96,384]{3,2,1,0:T(8,128)(2,1)S(1)}, u32[]{:S(2)}, u32[]{:S(2)}) %collective-permute-start.9) | collective-permute-done | bytes 442400 | tf_op jit(solution)/shard_map/ppermute | solution.py:343
  64.3 13.5 %shard_map.84 = (bf16[1024,192]{1,0:T(8,128)(2,1)}, bf16[1024,192]{1,0:T(8,128)(2,1)}, bf16[4,192,384]{2,1,0:T(8,128)(2,1)}, f32[4,192,384]{2,1,0:T(8,128)}, f32...) custom-call(bf16[3,2,96,384]{3,2,1,0:T(8,128)(2,1)} %pad_maximum_fus, ...), custom_call_target="tpu_custom_call" | custom-call | flops 4831838208 | bytes 17842176 | tf_op jit(solution)/shard_map/pallas_call | solution.py:280
  77.8 6.0 %collective-permute-start.19 = (bf16[256,192]{1,0:T(8,128)(2,1)}, bf16[256,192]{1,0:T(8,128)(2,1)S(1)}, u32[]{:S(2)}, u32[]{:S(2)}) collective-permute-start(bf16[256,192]{1,0:T(8,128)(2,1)} %get-tuple-element.37), channel_id=1, source_target_pairs={{0,4},{1,5},{2,6},{3,7},{4,8},{5,9},{6,10},{7,11},{8,12},{9,13},{1... | collective-permute-start | bytes 294920 | tf_op jit(solution)/shard_map/ppermute | solution.py:307
  87.3 4.5 %collective-permute-done.20.refs_9_ = bf16[256,192]{1,0:T(8,128)(2,1)S(1)} collective-permute-done((bf16[256,192]{1,0:T(8,128)(2,1)}, bf16[256,192]{1,0:T(8,128)(2,1)S(1)}, u32[]{:S(2)}, u32[]{:S(2)}) %collective-permute-start.20) | collective-permute-done | bytes 98336 | tf_op jit(solution)/shard_map/ppermute | solution.py:307
  92.5 6.0 %shard_map.85 = (f32[256,1536]{1,0:T(8,128)}, bf16[256,1536]{1,0:T(8,128)(2,1)}, f32[256,1536]{1,0:T(8,128)}, bf16[256,1536]{1,0:T(8,128)(2,1)}) custom-call(bf16[3,2,96,384]{3,2,1,0:T(8,128)(2,1)} %pad_maximum_fusion.refs_0_, bf16[3,2,96,384]{3,2,1,0:T(8,128)(2,1)} %collective-permute-done.4.refs_1_, bf16[3,2,96,384]{3,2,1,0:T(8,128)(2,1)} %copy-done.17, ...), custom_call_target="tpu_custom_call" | custom-call | flops 1811939328 | bytes 8404992 | tf_op jit(solution)/shard_map/pallas_call | solution.py:280
  105.0 4.0 %collective-permute-start.25 = (bf16[4,192,384]{2,1,0:T(8,128)(2,1)S(1)}, bf16[4,192,384]{2,1,0:T(8,128)(2,1)S(1)}, u32[]{:S(2)}, u32[]{:S(2)}) collective-permute-start(bf16[4,192,384]{2,1,0:T(8,128)(2,1)S(1)} %add_convert_fusion.3), channel_id=1, source_target_pairs={{0,4},{1,5},{2,6},{3,7},{4,8},{5,9},{6,10},{7,11},{16,20},{17,21},... | collective-permute-start | bytes 1769480 | tf_op jit(solution)/shard_map/ppermute | solution.py:343
  113.6 7.6 %collective-permute-done.25 = bf16[4,192,384]{2,1,0:T(8,128)(2,1)S(1)} collective-permute-done((bf16[4,192,384]{2,1,0:T(8,128)(2,1)S(1)}, bf16[4,192,384]{2,1,0:T(8,128)(2,1)S(1)}, u32[]{:S(2)}, u32[]{:S(2)}) %collective-permute-start.25) | collective-permute-done | bytes 589856 | tf_op jit(solution)/shard_map/ppermute | solution.py:343
  121.4 4.2 %collective-permute-start.26 = (bf16[4,192,384]{2,1,0:T(8,128)(2,1)S(1)}, bf16[4,192,384]{2,1,0:T(8,128)(2,1)S(1)}, u32[]{:S(2)}, u32[]{:S(2)}) collective-permute-start(bf16[4,192,384]{2,1,0:T(8,128)(2,1)S(1)} %add_convert_fusion.2), channel_id=1, source_target_pairs={{0,4},{1,5},{2,6},{3,7},{4,8},{5,9},{6,10},{7,11},{8,12},{9,13},{1... | collective-permute-start | bytes 1769480 | tf_op jit(solution)/shard_map/ppermute | solution.py:343
  125.8 1.9 %collective-permute-start.28 = (bf16[4,192,384]{2,1,0:T(8,128)(2,1)S(1)}, bf16[4,192,384]{2,1,0:T(8,128)(2,1)S(1)}, u32[]{:S(2)}, u32[]{:S(2)}) collective-permute-start(bf16[4,192,384]{2,1,0:T(8,128)(2,1)S(1)} %add_convert_fusion.1), channel_id=1, source_target_pairs={{4,0},{5,1},{6,2},{7,3},{8,4},{9,5},{10,6},{11,7},{12,8},{13,9},{1... | collective-permute-start | bytes 1769480 | tf_op jit(solution)/shard_map/ppermute | solution.py:343
  127.7 2.3 %collective-permute-done.23 = bf16[256,1536]{1,0:T(8,128)(2,1)S(1)} collective-permute-done((bf16[256,1536]{1,0:T(8,128)(2,1)S(1)}, bf16[256,1536]{1,0:T(8,128)(2,1)S(1)}, u32[]{:S(2)}, u32[]{:S(2)}) %collective-permute-start.23) | collective-permute-done | bytes 786464 | tf_op jit(solution)/shard_map/ppermute | solution.py:307
  131.8 5.1 %collective-permute-done.26 = bf16[4,192,384]{2,1,0:T(8,128)(2,1)S(1)} collective-permute-done((bf16[4,192,384]{2,1,0:T(8,128)(2,1)S(1)}, bf16[4,192,384]{2,1,0:T(8,128)(2,1)S(1)}, u32[]{:S(2)}, u32[]{:S(2)}) %collective-permute-start.26) | collective-permute-done | bytes 589856 | tf_op jit(solution)/shard_map/ppermute | solution.py:343
  136.9 4.0 %collective-permute-done.28 = bf16[4,192,384]{2,1,0:T(8,128)(2,1)S(1)} collective-permute-done((bf16[4,192,384]{2,1,0:T(8,128)(2,1)S(1)}, bf16[4,192,384]{2,1,0:T(8,128)(2,1)S(1)}, u32[]{:S(2)}, u32[]{:S(2)}) %collective-permute-start.28) | collective-permute-done | bytes 589856 | tf_op jit(solution)/shard_map/ppermute | solution.py:343
  141.3 2.7 %collective-permute-start.31 = (bf16[4,192,96]{2,1,0:T(8,128)(2,1)S(1)}, bf16[4,192,96]{2,1,0:T(8,128)(2,1)S(1)}, u32[]{:S(2)}, u32[]{:S(2)}) collective-permute-start(bf16[4,192,96]{2,1,0:T(8,128)(2,1)S(1)} %get-tuple-element.54), channel_id=1, source_target_pairs={{0,3},{1,2},{2,1},{3,0},{4,7},{5,6},{6,5},{7,4},{8,11},{9,10},{10,... | collective-permute-start | bytes 442376 | tf_op jit(solution)/shard_map/ppermute | solution.py:307
  148.8 4.9 %collective-permute-done.30.refs_2_ = bf16[4,192,96]{2,1,0:T(8,128)(2,1)S(1)} collective-permute-done((bf16[4,192,96]{2,1,0:T(8,128)(2,1)S(1)}, bf16[4,192,96]{2,1,0:T(8,128)(2,1)S(1)}, u32[]{:S(2)}, u32[]{:S(2)}) %collective-permute-start.30) | collective-permute-done | bytes 147488 | tf_op jit(solution)/shard_map/ppermute | solution.py:307
  (112 shorter events, 46.4 us)
Async XLA Ops:
  6.7 23.7 %collective-permute-start.3 = (bf16[256,1536]{1,0:T(8,128)(2,1)}, bf16[256,1536]{1,0:T(8,128)(2,1)}, u32[]{:S(2)}, u32[]{:S(2)}) collective-permute-start(bf16[256,1536]{1,0:T(8,128)(2,1)} %fusion.6.refs_7_), channel_id=1, source_target_pairs={{0,2},{1,3},{2,0},{3,1},{4,6},{5,7},{6,4},{7,5},{8,10},{9,11},{10,... | collective-permute-start | bytes 2359304 | tf_op jit(solution)/shard_map/ppermute | solution.py:307
  13.3 14.1 %collective-permute-start.4 = (bf16[3,2,96,384]{3,2,1,0:T(8,128)(2,1)}, bf16[3,2,96,384]{3,2,1,0:T(8,128)(2,1)}, u32[]{:S(2)}, u32[]{:S(2)}) collective-permute-start(bf16[3,2,96,384]{3,2,1,0:T(8,128)(2,1)} %pad_maximum_fusion.refs_0_), channel_id=1, source_target_pairs={{0,4},{1,5},{2,6},{3,7},{4,8},{5,9},{6,10},{7,11},{8,12},{9,13},{1... | collective-permute-start | bytes 1327112 | tf_op jit(solution)/shard_map/ppermute | solution.py:343
  16.5 13.9 %collective-permute-start.5 = (bf16[3,2,96,384]{3,2,1,0:T(8,128)(2,1)}, bf16[3,2,96,384]{3,2,1,0:T(8,128)(2,1)}, u32[]{:S(2)}, u32[]{:S(2)}) collective-permute-start(bf16[3,2,96,384]{3,2,1,0:T(8,128)(2,1)} %pad_maximum_fusion.refs_0_), channel_id=1, source_target_pairs={{4,0},{5,1},{6,2},{7,3},{8,4},{9,5},{10,6},{11,7},{12,8},{13,9},{1... | collective-permute-start | bytes 1327112 | tf_op jit(solution)/shard_map/ppermute | solution.py:343
  19.4 20.6 %collective-permute-start.10 = (bf16[256,1536]{1,0:T(8,128)(2,1)}, bf16[256,1536]{1,0:T(8,128)(2,1)S(1)}, u32[]{:S(2)}, u32[]{:S(2)}) collective-permute-start(bf16[256,1536]{1,0:T(8,128)(2,1)} %fusion.6.refs_7_), channel_id=1, source_target_pairs={{0,1},{1,0},{2,3},{3,2},{4,5},{5,4},{6,7},{7,6},{8,9},{9,8},{10,11... | collective-permute-start | bytes 2359304 | tf_op jit(solution)/shard_map/ppermute | solution.py:307
  19.8 18.2 %collective-permute-start.14 = (bf16[256,1536]{1,0:T(8,128)(2,1)}, bf16[256,1536]{1,0:T(8,128)(2,1)S(1)}, u32[]{:S(2)}, u32[]{:S(2)}) collective-permute-start(bf16[256,1536]{1,0:T(8,128)(2,1)} %refs_13_), channel_id=1, source_target_pairs={{0,1},{1,0},{2,3},{3,2},{4,5},{5,4},{6,7},{7,6},{8,9},{9,8},{10,11... | collective-permute-start | bytes 2359304 | tf_op jit(solution)/shard_map/ppermute | solution.py:307
  30.4 18.4 %collective-permute-start.15 = (bf16[256,1536]{1,0:T(8,128)(2,1)}, bf16[256,1536]{1,0:T(8,128)(2,1)S(1)}, u32[]{:S(2)}, u32[]{:S(2)}) collective-permute-start(bf16[256,1536]{1,0:T(8,128)(2,1)} %refs_13_), channel_id=1, source_target_pairs={{0,2},{1,3},{2,0},{3,1},{4,6},{5,7},{6,4},{7,5},{8,10},{9,11},{10,... | collective-permute-start | bytes 2359304 | tf_op jit(solution)/shard_map/ppermute | solution.py:307
  32.9 17.7 %collective-permute-start.12 = (bf16[256,1536]{1,0:T(8,128)(2,1)S(1)}, bf16[256,1536]{1,0:T(8,128)(2,1)S(1)}, u32[]{:S(2)}, u32[]{:S(2)}) collective-permute-start(bf16[256,1536]{1,0:T(8,128)(2,1)S(1)} %broadcast_select_fusion), channel_id=1, source_target_pairs={{1,5},{3,7},{4,0},{5,9},{6,2},{7,11},{8,4},{9,13},{10,6},{11,15},{... | collective-permute-start | bytes 2359304 | tf_op jit(solution)/shard_map/ppermute | solution.py:307
  36.1 18.5 %collective-permute-start.6 = (bf16[3,2,96,384]{3,2,1,0:T(8,128)(2,1)}, bf16[3,2,96,384]{3,2,1,0:T(8,128)(2,1)S(1)}, u32[]{:S(2)}, u32[]{:S(2)}) collective-permute-start(bf16[3,2,96,384]{3,2,1,0:T(8,128)(2,1)} %collective-permute-done.4.refs_1_), channel_id=1, source_target_pairs={{4,8},{5,9},{6,10},{7,11},{8,12},{9,13},{10,14},{11,15},{20,24},{2... | collective-permute-start | bytes 1327112 | tf_op jit(solution)/shard_map/ppermute | solution.py:343
  38.0 17.2 %collective-permute-start.8 = (bf16[3,2,96,384]{3,2,1,0:T(8,128)(2,1)}, bf16[3,2,96,384]{3,2,1,0:T(8,128)(2,1)S(1)}, u32[]{:S(2)}, u32[]{:S(2)}) collective-permute-start(bf16[3,2,96,384]{3,2,1,0:T(8,128)(2,1)} %collective-permute-done.5.refs_4_), channel_id=1, source_target_pairs={{4,0},{5,1},{6,2},{7,3},{8,4},{9,5},{10,6},{11,7},{20,16},{21,17},... | collective-permute-start | bytes 1327112 | tf_op jit(solution)/shard_map/ppermute | solution.py:343
  40.0 22.4 %collective-permute-start.11 = (bf16[256,1536]{1,0:T(8,128)(2,1)}, bf16[256,1536]{1,0:T(8,128)(2,1)S(1)}, u32[]{:S(2)}, u32[]{:S(2)}) collective-permute-start(bf16[256,1536]{1,0:T(8,128)(2,1)} %collective-permute-done.3.refs_9_), channel_id=1, source_target_pairs={{0,1},{1,0},{2,3},{3,2},{4,5},{5,4},{6,7},{7,6},{8,9},{9,8},{10,11... | collective-permute-start | bytes 2359304 | tf_op jit(solution)/shard_map/ppermute | solution.py:307
  48.8 13.5 %collective-permute-start.16 = (bf16[256,1536]{1,0:T(8,128)(2,1)S(1)}, bf16[256,1536]{1,0:T(8,128)(2,1)S(1)}, u32[]{:S(2)}, u32[]{:S(2)}) collective-permute-start(bf16[256,1536]{1,0:T(8,128)(2,1)S(1)} %collective-permute-done.15.refs_15_), channel_id=1, source_target_pairs={{0,1},{1,0},{2,3},{3,2},{4,5},{5,4},{6,7},{7,6},{8,9},{9,8},{10,11... | collective-permute-start | bytes 2359304 | tf_op jit(solution)/shard_map/ppermute | solution.py:307
  50.6 13.7 %collective-permute-start.13 = (bf16[256,1536]{1,0:T(8,128)(2,1)S(1)}, bf16[256,1536]{1,0:T(8,128)(2,1)}, u32[]{:S(2)}, u32[]{:S(2)}) collective-permute-start(bf16[256,1536]{1,0:T(8,128)(2,1)S(1)} %collective-permute-done.12.refs_11_), channel_id=1, source_target_pairs={{0,1},{1,0},{2,3},{3,2},{4,5},{5,4},{6,7},{7,6},{8,9},{9,8},{10,11... | collective-permute-start | bytes 2359304 | tf_op jit(solution)/shard_map/ppermute | solution.py:307
  77.8 9.5 %collective-permute-start.19 = (bf16[256,192]{1,0:T(8,128)(2,1)}, bf16[256,192]{1,0:T(8,128)(2,1)S(1)}, u32[]{:S(2)}, u32[]{:S(2)}) collective-permute-start(bf16[256,192]{1,0:T(8,128)(2,1)} %get-tuple-element.37), channel_id=1, source_target_pairs={{0,4},{1,5},{2,6},{3,7},{4,8},{5,9},{6,10},{7,11},{8,12},{9,13},{1... | collective-permute-start | bytes 294920 | tf_op jit(solution)/shard_map/ppermute | solution.py:307
  83.8 8.0 %collective-permute-start.20 = (bf16[256,192]{1,0:T(8,128)(2,1)}, bf16[256,192]{1,0:T(8,128)(2,1)S(1)}, u32[]{:S(2)}, u32[]{:S(2)}) collective-permute-start(bf16[256,192]{1,0:T(8,128)(2,1)} %get-tuple-element.39), channel_id=1, source_target_pairs={{4,0},{5,1},{6,2},{7,3},{8,4},{9,5},{10,6},{11,7},{12,8},{13,9},{1... | collective-permute-start | bytes 294920 | tf_op jit(solution)/shard_map/ppermute | solution.py:307
  85.8 17.9 %collective-permute-start.24 = (bf16[4,192,384]{2,1,0:T(8,128)(2,1)}, bf16[4,192,384]{2,1,0:T(8,128)(2,1)}, u32[]{:S(2)}, u32[]{:S(2)}) collective-permute-start(bf16[4,192,384]{2,1,0:T(8,128)(2,1)} %get-tuple-element.47), channel_id=1, source_target_pairs={{0,4},{1,5},{2,6},{3,7},{12,8},{13,9},{14,10},{15,11},{16,20},{17,... | collective-permute-start | bytes 1769480 | tf_op jit(solution)/shard_map/ppermute | solution.py:343
  98.5 11.8 %collective-permute-start.22 = (bf16[256,1536]{1,0:T(8,128)(2,1)}, bf16[256,1536]{1,0:T(8,128)(2,1)}, u32[]{:S(2)}, u32[]{:S(2)}) collective-permute-start(bf16[256,1536]{1,0:T(8,128)(2,1)} %get-tuple-element.43), channel_id=1, source_target_pairs={{0,1},{1,0},{2,3},{3,2},{4,5},{5,4},{6,7},{7,6},{8,9},{9,8},{10,11... | collective-permute-start | bytes 2359304 | tf_op jit(solution)/shard_map/ppermute | solution.py:307
  100.0 27.7 %collective-permute-start.21 = (bf16[256,1536]{1,0:T(8,128)(2,1)}, bf16[256,1536]{1,0:T(8,128)(2,1)S(1)}, u32[]{:S(2)}, u32[]{:S(2)}) collective-permute-start(bf16[256,1536]{1,0:T(8,128)(2,1)} %get-tuple-element.41), channel_id=1, source_target_pairs={{0,1},{1,0},{2,3},{3,2},{4,5},{5,4},{6,7},{7,6},{8,9},{9,8},{10,11... | collective-permute-start | bytes 2359304 | tf_op jit(solution)/shard_map/ppermute | solution.py:307
  103.3 8.6 %collective-permute-start.18 = (bf16[256,384]{1,0:T(8,128)(2,1)S(1)}, bf16[256,384]{1,0:T(8,128)(2,1)S(1)}, u32[]{:S(2)}, u32[]{:S(2)}) collective-permute-start(bf16[256,384]{1,0:T(8,128)(2,1)S(1)} %get-tuple-element.64), channel_id=1, source_target_pairs={{0,2},{1,3},{2,0},{3,1},{4,6},{5,7},{6,4},{7,5},{8,10},{9,11},{10,... | collective-permute-start | bytes 589832 | tf_op jit(solution)/shard_map/ppermute | solution.py:307
  105.0 16.3 %collective-permute-start.25 = (bf16[4,192,384]{2,1,0:T(8,128)(2,1)S(1)}, bf16[4,192,384]{2,1,0:T(8,128)(2,1)S(1)}, u32[]{:S(2)}, u32[]{:S(2)}) collective-permute-start(bf16[4,192,384]{2,1,0:T(8,128)(2,1)S(1)} %add_convert_fusion.3), channel_id=1, source_target_pairs={{0,4},{1,5},{2,6},{3,7},{4,8},{5,9},{6,10},{7,11},{16,20},{17,21},... | collective-permute-start | bytes 1769480 | tf_op jit(solution)/shard_map/ppermute | solution.py:343
  109.0 16.6 %collective-permute-start.27 = (bf16[4,192,384]{2,1,0:T(8,128)(2,1)S(1)}, bf16[4,192,384]{2,1,0:T(8,128)(2,1)S(1)}, u32[]{:S(2)}, u32[]{:S(2)}) collective-permute-start(bf16[4,192,384]{2,1,0:T(8,128)(2,1)S(1)} %add_convert_fusion.3), channel_id=1, source_target_pairs={{12,8},{13,9},{14,10},{15,11},{8,4},{9,5},{10,6},{11,7},{28,24},{2... | collective-permute-start | bytes 1769480 | tf_op jit(solution)/shard_map/ppermute | solution.py:343
  111.7 18.3 %collective-permute-start.23 = (bf16[256,1536]{1,0:T(8,128)(2,1)S(1)}, bf16[256,1536]{1,0:T(8,128)(2,1)S(1)}, u32[]{:S(2)}, u32[]{:S(2)}) collective-permute-start(bf16[256,1536]{1,0:T(8,128)(2,1)S(1)} %add_convert_fusion), channel_id=1, source_target_pairs={{0,2},{1,3},{2,0},{3,1},{4,6},{5,7},{6,4},{7,5},{8,10},{9,11},{10,... | collective-permute-start | bytes 2359304 | tf_op jit(solution)/shard_map/ppermute | solution.py:307
  121.4 15.5 %collective-permute-start.26 = (bf16[4,192,384]{2,1,0:T(8,128)(2,1)S(1)}, bf16[4,192,384]{2,1,0:T(8,128)(2,1)S(1)}, u32[]{:S(2)}, u32[]{:S(2)}) collective-permute-start(bf16[4,192,384]{2,1,0:T(8,128)(2,1)S(1)} %add_convert_fusion.2), channel_id=1, source_target_pairs={{0,4},{1,5},{2,6},{3,7},{4,8},{5,9},{6,10},{7,11},{8,12},{9,13},{1... | collective-permute-start | bytes 1769480 | tf_op jit(solution)/shard_map/ppermute | solution.py:343
  125.8 15.1 %collective-permute-start.28 = (bf16[4,192,384]{2,1,0:T(8,128)(2,1)S(1)}, bf16[4,192,384]{2,1,0:T(8,128)(2,1)S(1)}, u32[]{:S(2)}, u32[]{:S(2)}) collective-permute-start(bf16[4,192,384]{2,1,0:T(8,128)(2,1)S(1)} %add_convert_fusion.1), channel_id=1, source_target_pairs={{4,0},{5,1},{6,2},{7,3},{8,4},{9,5},{10,6},{11,7},{12,8},{13,9},{1... | collective-permute-start | bytes 1769480 | tf_op jit(solution)/shard_map/ppermute | solution.py:343
  144.0 9.7 %collective-permute-start.30 = (bf16[4,192,96]{2,1,0:T(8,128)(2,1)S(1)}, bf16[4,192,96]{2,1,0:T(8,128)(2,1)S(1)}, u32[]{:S(2)}, u32[]{:S(2)}) collective-permute-start(bf16[4,192,96]{2,1,0:T(8,128)(2,1)S(1)} %get-tuple-element.55), channel_id=1, source_target_pairs={{0,2},{1,3},{2,0},{3,1},{4,6},{5,7},{6,4},{7,5},{8,10},{9,11},{10,... | collective-permute-start | bytes 442376 | tf_op jit(solution)/shard_map/ppermute | solution.py:307
  (31 other events, 249.1 us)
